TPU v7x, 32 devices: a whole 2x2x4 slice. The times are simulated.
32 devices in a mesh: ta: 4 (over x, core), ha: 4 (over z), wa: 2 (over y).
Axes of the slice: x: 2, y: 2, z: 4, core: 2. Of those that a mesh axis runs over, the one named last changes fastest.
Arguments:
- queries: bfloat16 [8, 64, 16, 2048], P('ta', 'ha', 'wa'), may hold values from -16 to 16
- keyvals: bfloat16 [2, 8, 64, 16, 2048], P(None, 'ta', 'ha', 'wa'), may hold values from -6 to 6
- far_frames: int32 [8, 8, 2, 2], P('ta', 'ha', 'wa'), may hold values from 0 to 7, as said below
Outputs:
- attended: bfloat16 [8, 64, 16, 2048], P('ta', 'ha', 'wa')
Inputs may be any that keep to these rules, and one draw needn't show every extreme that they name: far_frames[t, a, b, :] are 2 different frames, each at a distance of 2 or more from t modulo 8.
All inputs are finite; a program needn't handle non-finite values.
Results may differ from a plain program's by a relative error of at most 0.0049.
Values may be sent and summed in bfloat16 or wider, within the bound.
No kernel may reach another device: no remote copies, remote signals or barrier semaphores. Data moves between devices by JAX's collectives and lax.ppermute only.
A program may use at most 192 MiB of HBM per device.

v0:
```python
import jax
import jax.numpy as jnp
from jax import lax
from jax.sharding import PartitionSpec as P

TILE = 8
HEADS = 16
HD = 128
NFAR = 2


def extended_2(cells, sides, width, closed):
    for axis, dim in sides:
        count = lax.axis_size(axis)
        ends = count if closed else count - 1
        head = lax.slice_in_dim(cells, 0, width, axis=dim)
        tail = lax.slice_in_dim(cells, cells.shape[dim] - width, cells.shape[dim], axis=dim)
        cells = jnp.concatenate(
            [
                lax.ppermute(tail, axis, [(i, (i + 1) % count) for i in range(ends)]),
                cells,
                lax.ppermute(head, axis, [((i + 1) % count, i) for i in range(ends)]),
            ],
            axis=dim,
        )
    return cells


def start_at(*values):
    return tuple((jnp.asarray(value).astype(jnp.int32) for value in values))


def widen_space(timed):
    return extended_2(timed, (("ha", 2), ("wa", 3)), TILE, False)


def per_device(queries, keyvals, far_frames):
    frame_count, row_count, column_count, features = queries.shape
    tile_count = row_count // TILE
    scaling = HD ** (-0.5)
    wanted = far_frames[:, :, 0, :]
    shard_rows = lax.all_gather(keyvals, "ta", axis=1, tiled=True)
    piece_count = shard_rows.shape[1]
    frame_ids = jnp.arange(piece_count, dtype=jnp.int32)
    matches = (wanted[:, :, :, None] == frame_ids).astype(jnp.bfloat16)
    blocks = shard_rows.reshape(2, piece_count, tile_count, TILE, column_count, features)
    chosen = jnp.einsum("fanp,kpatwc->kfantwc", matches, blocks, preferred_element_type=jnp.float32)
    far_blocks = chosen.astype(jnp.bfloat16)
    timed = extended_2(keyvals, (("ta", 1),), 1, True)
    extended = widen_space(timed)
    row_base = lax.axis_index("ha") * tile_count
    row_limit = tile_count * lax.axis_size("ha")
    column_tile = lax.axis_index("wa")
    column_limit = lax.axis_size("wa")
    offsets = jnp.arange(3 * TILE, dtype=jnp.int32) // TILE - 1
    column_valid = (column_tile + offsets >= 0) & (column_tile + offsets < column_limit)

    def attend(tile_index):
        frame_at = tile_index // tile_count
        tile_at = tile_index % tile_count
        query_rows = lax.dynamic_slice(
            queries, start_at(frame_at, tile_at * TILE, 0, 0), (1, TILE, column_count, features)
        ).reshape(-1, HEADS, HD)
        window = lax.dynamic_slice(
            extended,
            start_at(0, frame_at, tile_at * TILE, 0, 0),
            (2, 3, 3 * TILE, column_count + 2 * TILE, features),
        )
        distant = lax.dynamic_slice(
            far_blocks,
            start_at(0, frame_at, tile_at, 0, 0, 0, 0),
            (2, 1, 1, NFAR, TILE, column_count, features),
        )
        near_keys = window[0].reshape(-1, HEADS, HD)
        near_values = window[1].reshape(-1, HEADS, HD)
        far_keys = distant[0].reshape(-1, HEADS, HD)
        far_values = distant[1].reshape(-1, HEADS, HD)
        row_valid = (row_base + tile_at + offsets >= 0) & (row_base + tile_at + offsets < row_limit)
        inside = jnp.broadcast_to(
            row_valid[None, :, None] & column_valid[None, None, :],
            (3, 3 * TILE, column_count + 2 * TILE),
        ).reshape(-1)
        near_scores = (
            jnp.einsum("qhd,khd->hqk", query_rows, near_keys, preferred_element_type=jnp.float32)
            * scaling
        )
        near_scores = jnp.where(inside[None, None, :], near_scores, jnp.float32(-1e30))
        far_scores = (
            jnp.einsum("qhd,khd->hqk", query_rows, far_keys, preferred_element_type=jnp.float32)
            * scaling
        )
        peak_score = jnp.maximum(
            jnp.max(near_scores, axis=-1, keepdims=True),
            jnp.max(far_scores, axis=-1, keepdims=True),
        )
        near_exp = jnp.exp(near_scores - peak_score)
        far_exp = jnp.exp(far_scores - peak_score)
        denominator = jnp.sum(near_exp, axis=-1, keepdims=True) + jnp.sum(
            far_exp, axis=-1, keepdims=True
        )
        near_normed = (near_exp / denominator).astype(jnp.bfloat16)
        far_normed = (far_exp / denominator).astype(jnp.bfloat16)
        blended = jnp.einsum(
            "hqk,khd->qhd", near_normed, near_values, preferred_element_type=jnp.float32
        )
        blended = blended + jnp.einsum(
            "hqk,khd->qhd", far_normed, far_values, preferred_element_type=jnp.float32
        )
        return blended.reshape(TILE, column_count, features).astype(jnp.bfloat16)

    tile_outputs = lax.map(attend, jnp.arange(frame_count * tile_count, dtype=jnp.int32))
    return tile_outputs.reshape(frame_count, row_count, column_count, features)


def solution(mesh):
    placed = (P("ta", "ha", "wa", None), P(None, "ta", "ha", "wa", None), P("ta", "ha", "wa", None))
    return jax.shard_map(
        per_device, mesh=mesh, in_specs=placed, out_specs=P("ta", "ha", "wa", None), check_vma=False
    )
```

profile of v0, /device:TPU:0, one launch (start us, length us, event | category | flops | bytes accessed | tf_op | source)
XLA Modules:
  0.0 535.9 jit_solution(17701051988122823325)
XLA Ops:
  10.9 21.0 %collective-permute-done = bf16[2,1,16,8,2048]{4,3,2,1,0:T(8,128)(2,1)S(1)} collective-permute-done((bf16[2,1,16,8,2048]{4,3,2,1,0:T(8,128)(2,1)S(1)}, bf16[2,1,16,8,2048]{4,3,2,1,0:T(8,128)(2,1)S(1)}, u32[]{:S(2)}, u32[]{:S(2)}) %collective-permute-start) | collective-permute-done | bytes 1048608 | tf_op jit(solution)/shard_map/ppermute | solution.py:20
  40.4 5.9 %collective-permute-start.2 = (bf16[2,4,8,8,2048]{4,3,2,1,0:T(8,128)(2,1)}, bf16[2,4,8,8,2048]{4,3,2,1,0:T(8,128)(2,1)}, u32[]{:S(2)}, u32[]{:S(2)}) collective-permute-start(bf16[2,4,8,8,2048]{4,3,2,1,0:T(8,128)(2,1)} %get-tuple-element.184), channel_id=1, source_target_pairs={{0,2},{2,4},{4,6},{1,3},{3,5},{5,7},{8,10},{10,12},{12,14},{9,11},... | collective-permute-start | bytes 6291464 | tf_op jit(solution)/shard_map/ppermute | solution.py:20
  46.3 43.1 %collective-permute-done.3 = bf16[2,4,8,8,2048]{4,3,2,1,0:T(8,128)(2,1)S(1)} collective-permute-done((bf16[2,4,8,8,2048]{4,3,2,1,0:T(8,128)(2,1)}, bf16[2,4,8,8,2048]{4,3,2,1,0:T(8,128)(2,1)S(1)}, u32[]{:S(2)}, u32[]{:S(2)}) %collective-permute-start.3) | collective-permute-done | bytes 2097184 | tf_op jit(solution)/shard_map/ppermute | solution.py:22
  90.6 6.6 %pad_maximum_fusion.1 = bf16[2,4,32,8,2048]{4,3,2,1,0:T(8,128)(2,1)} fusion(bf16[2,4,8,8,2048]{4,3,2,1,0:T(8,128)(2,1)S(1)} %collective-permute-done.3, bf16[2,4,16,8,2048]{4,3,2,1,0:T(8,128)(2,1)} %copy-done, bf16[2,4,8,8,2048]{4,3,2,1,0:T(8,128)(2,1)} %collective-permute-done.2), kind=kLoop, calls=%fused_computation.46 | loop fusion | flops 8388608 | bytes 16777216 | tf_op jit(solution)/shard_map/concatenate | solution.py:18
  98.5 11.0 %collective-permute-start.4 = (bf16[2,4,32,8,2048]{4,3,2,1,0:T(8,128)(2,1)}, bf16[2,4,32,8,2048]{4,3,2,1,0:T(8,128)(2,1)}, u32[]{:S(2)}, u32[]{:S(2)}) collective-permute-start(bf16[2,4,32,8,2048]{4,3,2,1,0:T(8,128)(2,1)} %pad_maximum_fusion.1), channel_id=1, source_target_pairs={{0,1},{2,3},{4,5},{6,7},{8,9},{10,11},{12,13},{14,15},{16,17},{18,... | collective-permute-start | bytes 25165832 | tf_op jit(solution)/shard_map/ppermute | solution.py:20
  109.5 171.9 %collective-permute-done.5 = bf16[2,4,32,8,2048]{4,3,2,1,0:T(8,128)(2,1)} collective-permute-done((bf16[2,4,32,8,2048]{4,3,2,1,0:T(8,128)(2,1)}, bf16[2,4,32,8,2048]{4,3,2,1,0:T(8,128)(2,1)}, u32[]{:S(2)}, u32[]{:S(2)}) %collective-permute-start.5) | collective-permute-done | bytes 8388640 | tf_op jit(solution)/shard_map/ppermute | solution.py:22
  285.7 21.8 %pad_maximum_fusion = bf16[2,4,32,24,2048]{4,3,2,1,0:T(8,128)(2,1)} fusion(bf16[2,4,32,8,2048]{4,3,2,1,0:T(8,128)(2,1)} %collective-permute-done.5, bf16[2,4,8,8,2048]{4,3,2,1,0:T(8,128)(2,1)S(1)} %collective-permute-done.3, bf16[2,4,16,8,2048]{4,3,2,1,0:T(8,128)(2,1)} %copy-done, bf16[2,4,8,8,2048]{4,3,2,1,0:T(8,128)(2,1)} %collective-permute-done.2, ...), kind=kLoop, calls=%fused_computation.45 | loop fusion | flops 125829120 | bytes 50331648 | tf_op jit(solution)/shard_map/concatenate | solution.py:18
  307.6 12.4 %fusion.32 = bf16[2,2,2,2,8,8,2048]{6,3,5,4,0,1,2:T(2,128)(2,1)} fusion(bf16[2,8,2,8,8,2048,1]{5,4,3,2,1,0,6:T(8,128)(2,1)} %bitcast.72, s32[2,2,2]{2,0,1:T(2,128)S(1)} %copy.13), kind=kOutput, calls=%fused_computation.50 | convolution fusion | flops 35651648 | bytes 12582944 | tf_op jit(solution)/shard_map/fanp,kpatwc->kfantwc/dot_general | solution.py:47
  319.9 209.1 %while.13 = (s32[]{:T(128)}, bf16[4,8,8,2048]{3,2,1,0:T(8,128)(2,1)}, s32[4]{0:T(128)S(1)}, bf16[2,4,32,24,2048]{4,3,2,1,0:T(8,128)(2,1)}, s32[]{:T(128)}, /*ind...) while((s32[]{:T(128)}, ...), condition=%wide.region_5.6_spmd.clone, body=%wide.region_0.5_spmd.clone.sunk | while | flops 995490816 | bytes 127479776 | solution.py:111
  322.9 8.4 %constant_dynamic-slice_fusion.6 = (bf16[1,3,24,24,2048]{4,3,2,1,0:T(8,128)(2,1)}, bf16[1,3,24,24,2048]{4,3,2,1,0:T(8,128)(2,1)S(1)}) fusion(bf16[2,4,32,24,2048]{4,3,2,1,0:T(8,128)(2,1)} %get-tuple-element.294, s32[]{:T(128)S(6)} %select_n.118, s32[]{:T(128)S(6)} %select_n.120, s32[]{:T(128)S(6)} %add.155), kind=kLoop, calls=%fused_computation.35.clone.1 | loop fusion | bytes 28311564 | tf_op jit(solution)/shard_map/while/body/eval_jaxpr/slice | solution.py:74
  336.9 8.5 %copy.75 = bf16[216,8,16,128]{3,2,1,0:T(8,128)(2,1)} copy(bf16[216,8,16,128]{3,1,2,0:T(8,128)(2,1)} %bitcast.62) | data formatting | bytes 14155776 | tf_op jit(solution)/shard_map/while
  346.4 10.4 %fusion.52 = (f32[16,64]{1,0:T(8,128)S(1)}, f32[16,64,1728]{2,1,0:T(8,128)}) fusion(pred[1728]{0:T(1024)(128)(4,1)S(1)} %broadcast_in_dim.76, bf16[1728,16,128]{2,1,0:T(8,128)(2,1)} %bitcast.63, bf16[64,16,128]{2,1,0:T(8,128)(2,1)S(1)} %bitcast.66), kind=kOutput, calls=%fused_computation.9.clone.1 | convolution fusion | flops 458292224 | bytes 14423744 | tf_op jit(solution)/shard_map/while/body/eval_jaxpr/qhd,khd->hqk/dot_general | solution.py:84
  375.1 8.4 %constant_dynamic-slice_fusion.6 = (bf16[1,3,24,24,2048]{4,3,2,1,0:T(8,128)(2,1)}, bf16[1,3,24,24,2048]{4,3,2,1,0:T(8,128)(2,1)S(1)}) fusion(bf16[2,4,32,24,2048]{4,3,2,1,0:T(8,128)(2,1)} %get-tuple-element.294, s32[]{:T(128)S(6)} %select_n.118, s32[]{:T(128)S(6)} %select_n.120, s32[]{:T(128)S(6)} %add.155), kind=kLoop, calls=%fused_computation.35.clone.1 | loop fusion | bytes 28311564 | tf_op jit(solution)/shard_map/while/body/eval_jaxpr/slice | solution.py:74
  389.2 8.5 %copy.75 = bf16[216,8,16,128]{3,2,1,0:T(8,128)(2,1)} copy(bf16[216,8,16,128]{3,1,2,0:T(8,128)(2,1)} %bitcast.62) | data formatting | bytes 14155776 | tf_op jit(solution)/shard_map/while
  398.7 10.4 %fusion.52 = (f32[16,64]{1,0:T(8,128)S(1)}, f32[16,64,1728]{2,1,0:T(8,128)}) fusion(pred[1728]{0:T(1024)(128)(4,1)S(1)} %broadcast_in_dim.76, bf16[1728,16,128]{2,1,0:T(8,128)(2,1)} %bitcast.63, bf16[64,16,128]{2,1,0:T(8,128)(2,1)S(1)} %bitcast.66), kind=kOutput, calls=%fused_computation.9.clone.1 | convolution fusion | flops 458292224 | bytes 14423744 | tf_op jit(solution)/shard_map/while/body/eval_jaxpr/qhd,khd->hqk/dot_general | solution.py:84
  417.1 5.6 %fusion.56 = f32[16,128,64]{1,2,0:T(8,128)S(1)} fusion(bf16[1728,16,128]{2,1,0:T(8,128)(2,1)} %bitcast.65, f32[16,64,1728]{2,1,0:T(8,128)S(1)} %bitcast.61, f32[16,64]{1,0:T(8,128)S(1)} %add.160, f32[16,64]{1,0:T(8,128)S(1)} %max.13, pred[1728]{0:T(1024)(128)(4,1)S(1)} %broadcast_in_dim.76), kind=kOutput, calls=%fused_computation.5.clone.1 | convolution fusion | flops 461832192 | bytes 14689984 | tf_op jit(solution)/shard_map/while/body/eval_jaxpr/hqk,khd->qhd/dot_general | solution.py:103
  427.4 8.4 %constant_dynamic-slice_fusion.6 = (bf16[1,3,24,24,2048]{4,3,2,1,0:T(8,128)(2,1)}, bf16[1,3,24,24,2048]{4,3,2,1,0:T(8,128)(2,1)S(1)}) fusion(bf16[2,4,32,24,2048]{4,3,2,1,0:T(8,128)(2,1)} %get-tuple-element.294, s32[]{:T(128)S(6)} %select_n.118, s32[]{:T(128)S(6)} %select_n.120, s32[]{:T(128)S(6)} %add.155), kind=kLoop, calls=%fused_computation.35.clone.1 | loop fusion | bytes 28311564 | tf_op jit(solution)/shard_map/while/body/eval_jaxpr/slice | solution.py:74
  441.5 8.5 %copy.75 = bf16[216,8,16,128]{3,2,1,0:T(8,128)(2,1)} copy(bf16[216,8,16,128]{3,1,2,0:T(8,128)(2,1)} %bitcast.62) | data formatting | bytes 14155776 | tf_op jit(solution)/shard_map/while
  451.0 10.4 %fusion.52 = (f32[16,64]{1,0:T(8,128)S(1)}, f32[16,64,1728]{2,1,0:T(8,128)}) fusion(pred[1728]{0:T(1024)(128)(4,1)S(1)} %broadcast_in_dim.76, bf16[1728,16,128]{2,1,0:T(8,128)(2,1)} %bitcast.63, bf16[64,16,128]{2,1,0:T(8,128)(2,1)S(1)} %bitcast.66), kind=kOutput, calls=%fused_computation.9.clone.1 | convolution fusion | flops 458292224 | bytes 14423744 | tf_op jit(solution)/shard_map/while/body/eval_jaxpr/qhd,khd->hqk/dot_general | solution.py:84
  469.3 5.6 %fusion.56 = f32[16,128,64]{1,2,0:T(8,128)S(1)} fusion(bf16[1728,16,128]{2,1,0:T(8,128)(2,1)} %bitcast.65, f32[16,64,1728]{2,1,0:T(8,128)S(1)} %bitcast.61, f32[16,64]{1,0:T(8,128)S(1)} %add.160, f32[16,64]{1,0:T(8,128)S(1)} %max.13, pred[1728]{0:T(1024)(128)(4,1)S(1)} %broadcast_in_dim.76), kind=kOutput, calls=%fused_computation.5.clone.1 | convolution fusion | flops 461832192 | bytes 14689984 | tf_op jit(solution)/shard_map/while/body/eval_jaxpr/hqk,khd->qhd/dot_general | solution.py:103
  479.7 8.4 %constant_dynamic-slice_fusion.6 = (bf16[1,3,24,24,2048]{4,3,2,1,0:T(8,128)(2,1)}, bf16[1,3,24,24,2048]{4,3,2,1,0:T(8,128)(2,1)S(1)}) fusion(bf16[2,4,32,24,2048]{4,3,2,1,0:T(8,128)(2,1)} %get-tuple-element.294, s32[]{:T(128)S(6)} %select_n.118, s32[]{:T(128)S(6)} %select_n.120, s32[]{:T(128)S(6)} %add.155), kind=kLoop, calls=%fused_computation.35.clone.1 | loop fusion | bytes 28311564 | tf_op jit(solution)/shard_map/while/body/eval_jaxpr/slice | solution.py:74
  493.7 8.5 %copy.75 = bf16[216,8,16,128]{3,2,1,0:T(8,128)(2,1)} copy(bf16[216,8,16,128]{3,1,2,0:T(8,128)(2,1)} %bitcast.62) | data formatting | bytes 14155776 | tf_op jit(solution)/shard_map/while
  503.3 10.4 %fusion.52 = (f32[16,64]{1,0:T(8,128)S(1)}, f32[16,64,1728]{2,1,0:T(8,128)}) fusion(pred[1728]{0:T(1024)(128)(4,1)S(1)} %broadcast_in_dim.76, bf16[1728,16,128]{2,1,0:T(8,128)(2,1)} %bitcast.63, bf16[64,16,128]{2,1,0:T(8,128)(2,1)S(1)} %bitcast.66), kind=kOutput, calls=%fused_computation.9.clone.1 | convolution fusion | flops 458292224 | bytes 14423744 | tf_op jit(solution)/shard_map/while/body/eval_jaxpr/qhd,khd->hqk/dot_general | solution.py:84
  521.6 5.6 %fusion.56 = f32[16,128,64]{1,2,0:T(8,128)S(1)} fusion(bf16[1728,16,128]{2,1,0:T(8,128)(2,1)} %bitcast.65, f32[16,64,1728]{2,1,0:T(8,128)S(1)} %bitcast.61, f32[16,64]{1,0:T(8,128)S(1)} %add.160, f32[16,64]{1,0:T(8,128)S(1)} %max.13, pred[1728]{0:T(1024)(128)(4,1)S(1)} %broadcast_in_dim.76), kind=kOutput, calls=%fused_computation.5.clone.1 | convolution fusion | flops 461832192 | bytes 14689984 | tf_op jit(solution)/shard_map/while/body/eval_jaxpr/hqk,khd->qhd/dot_general | solution.py:103
  (133 shorter events, 92.8 us)
Async XLA Ops:
  6.5 25.4 %copy-start.1 = (bf16[2,2,16,8,2048]{4,3,2,1,0:T(8,128)(2,1)S(1)}, bf16[2,2,16,8,2048]{4,3,2,1,0:T(8,128)(2,1)}, u32[]{:S(2)}) copy-start(bf16[2,2,16,8,2048]{4,3,2,1,0:T(8,128)(2,1)} %param.6) | copy-start | bytes 6291460
  6.5 301.0 %all-gather.2.cloned.1.call-start = ((), (), s32[]{:S(2)}) async-start(), calls=%async_computation | async-start | bytes 10485760 | tf_op jit(solution)/shard_map/all_gather | solution.py:42
  8.4 23.5 %collective-permute-start = (bf16[2,1,16,8,2048]{4,3,2,1,0:T(8,128)(2,1)S(1)}, bf16[2,1,16,8,2048]{4,3,2,1,0:T(8,128)(2,1)S(1)}, u32[]{:S(2)}, u32[]{:S(2)}) collective-permute-start(bf16[2,1,16,8,2048]{4,3,2,1,0:T(8,128)(2,1)S(1)} %get-tuple-element.187), channel_id=1, source_target_pairs={{0,8},{8,16},{16,24},{24,0},{1,9},{9,17},{17,25},{25,1},{2,10},{10... | collective-permute-start | bytes 3145736 | tf_op jit(solution)/shard_map/ppermute | solution.py:20
  8.9 25.5 %collective-permute-start.1 = (bf16[2,1,16,8,2048]{4,3,2,1,0:T(8,128)(2,1)S(1)}, bf16[2,1,16,8,2048]{4,3,2,1,0:T(8,128)(2,1)S(1)}, u32[]{:S(2)}, u32[]{:S(2)}) collective-permute-start(bf16[2,1,16,8,2048]{4,3,2,1,0:T(8,128)(2,1)S(1)} %get-tuple-element.186), channel_id=1, source_target_pairs={{8,0},{16,8},{24,16},{0,24},{9,1},{17,9},{25,17},{1,25},{10,2},{18... | collective-permute-start | bytes 3145736 | tf_op jit(solution)/shard_map/ppermute | solution.py:22
  34.4 2.1 copy-start
  39.1 50.3 %collective-permute-start.3 = (bf16[2,4,8,8,2048]{4,3,2,1,0:T(8,128)(2,1)}, bf16[2,4,8,8,2048]{4,3,2,1,0:T(8,128)(2,1)S(1)}, u32[]{:S(2)}, u32[]{:S(2)}) collective-permute-start(bf16[2,4,8,8,2048]{4,3,2,1,0:T(8,128)(2,1)} %get-tuple-element.185), channel_id=1, source_target_pairs={{2,0},{4,2},{6,4},{3,1},{5,3},{7,5},{10,8},{12,10},{14,12},{11,9},... | collective-permute-start | bytes 6291464 | tf_op jit(solution)/shard_map/ppermute | solution.py:22
  40.4 50.3 %collective-permute-start.2 = (bf16[2,4,8,8,2048]{4,3,2,1,0:T(8,128)(2,1)}, bf16[2,4,8,8,2048]{4,3,2,1,0:T(8,128)(2,1)}, u32[]{:S(2)}, u32[]{:S(2)}) collective-permute-start(bf16[2,4,8,8,2048]{4,3,2,1,0:T(8,128)(2,1)} %get-tuple-element.184), channel_id=1, source_target_pairs={{0,2},{2,4},{4,6},{1,3},{3,5},{5,7},{8,10},{10,12},{12,14},{9,11},... | collective-permute-start | bytes 6291464 | tf_op jit(solution)/shard_map/ppermute | solution.py:20
  46.3 63.3 %copy-start.2 = (s32[2,2,1,2]{3,2,1,0:T(1,128)S(1)}, s32[2,2,1,2]{3,2,1,0:T(1,128)}, u32[]{:S(2)}) copy-start(s32[2,2,1,2]{3,2,1,0:T(1,128)} %param.7) | copy-start | bytes 100
  97.2 184.1 %collective-permute-start.5 = (bf16[2,4,32,8,2048]{4,3,2,1,0:T(8,128)(2,1)}, bf16[2,4,32,8,2048]{4,3,2,1,0:T(8,128)(2,1)}, u32[]{:S(2)}, u32[]{:S(2)}) collective-permute-start(bf16[2,4,32,8,2048]{4,3,2,1,0:T(8,128)(2,1)} %pad_maximum_fusion.1), channel_id=1, source_target_pairs={{1,0},{3,2},{5,4},{7,6},{9,8},{11,10},{13,12},{15,14},{17,16},{19,... | collective-permute-start | bytes 25165832 | tf_op jit(solution)/shard_map/ppermute | solution.py:22
  98.5 187.2 %collective-permute-start.4 = (bf16[2,4,32,8,2048]{4,3,2,1,0:T(8,128)(2,1)}, bf16[2,4,32,8,2048]{4,3,2,1,0:T(8,128)(2,1)}, u32[]{:S(2)}, u32[]{:S(2)}) collective-permute-start(bf16[2,4,32,8,2048]{4,3,2,1,0:T(8,128)(2,1)} %pad_maximum_fusion.1), channel_id=1, source_target_pairs={{0,1},{2,3},{4,5},{6,7},{8,9},{10,11},{12,13},{14,15},{16,17},{18,... | collective-permute-start | bytes 25165832 | tf_op jit(solution)/shard_map/ppermute | solution.py:20
  356.9 7.9 %slice-start = ((s8[7340032]{0:T(1024)(128)(4,1)}), s8[3145728]{0:T(1024)(128)(4,1)S(1)}, s32[]{:S(2)}) async-start(s8[7340032]{0:T(1024)(128)(4,1)} %bitcast.60), calls=%async_computation.1 | async-start | bytes 6291456 | tf_op jit(solution)/shard_map/while
  359.9 4.9 slice-start.1
  409.2 7.9 %slice-start = ((s8[7340032]{0:T(1024)(128)(4,1)}), s8[3145728]{0:T(1024)(128)(4,1)S(1)}, s32[]{:S(2)}) async-start(s8[7340032]{0:T(1024)(128)(4,1)} %bitcast.60), calls=%async_computation.1 | async-start | bytes 6291456 | tf_op jit(solution)/shard_map/while
  412.1 4.9 slice-start.1
  461.4 7.9 %slice-start = ((s8[7340032]{0:T(1024)(128)(4,1)}), s8[3145728]{0:T(1024)(128)(4,1)S(1)}, s32[]{:S(2)}) async-start(s8[7340032]{0:T(1024)(128)(4,1)} %bitcast.60), calls=%async_computation.1 | async-start | bytes 6291456 | tf_op jit(solution)/shard_map/while
  464.4 4.9 slice-start.1
  513.7 7.9 %slice-start = ((s8[7340032]{0:T(1024)(128)(4,1)}), s8[3145728]{0:T(1024)(128)(4,1)S(1)}, s32[]{:S(2)}) async-start(s8[7340032]{0:T(1024)(128)(4,1)} %bitcast.60), calls=%async_computation.1 | async-start | bytes 6291456 | tf_op jit(solution)/shard_map/while
  516.7 4.9 slice-start.1
Sparse Core Ops, SparseCore 0:
  46.4 57.7 all-gather.1
where the time goes:
time: 538 us; the launch traced here: 536 us
  waiting for transfers between devices  244 us (45%)
  local copies, waits for them, and re-layouts  118 us (22%)
  matrix products  80.8 us (15%)
  other arithmetic  48.2 us (9%)
  starting transfers between devices  21.9 us (4%)
  between operations  13.5 us (3%)
  loops' own time  9.89 us (2%)
    ppermute x3, waiting for transfers between devices, extended_2(): lax.ppermute(head, axis, [((i + 1) % count, i) for i in range(ends)])  217 us
    while x48, local copies, waits for them, and re-layouts  62.2 us
    dot_general x4, matrix products, attend(): jnp.einsum('qhd,khd->hqk', query_rows, near_keys, preferred_element_type=...  41.8 us
    slice x4, local copies, waits for them, and re-layouts, attend(): near_keys = window[0].reshape(-1, HEADS, HD)  33.5 us
    concatenate x2, other arithmetic, extended_2(): jnp.concatenate([lax.ppermute(tail, axis, [(i, (i + 1) % count) for i in...  28.4 us
    ppermute x3, waiting for transfers between devices, extended_2(): lax.ppermute(tail, axis, [(i, (i + 1) % count) for i in range(ends)])  26.6 us
    dot_general x4, matrix products, attend(): jnp.einsum('hqk,khd->qhd', near_normed, near_values, preferred_element_ty...  22.6 us
    reduce_sum x4, other arithmetic, attend(): jnp.sum(near_exp, axis=-1, keepdims=True)  17.8 us
  transfers between devices with their start and end apart: 7, of which 6 were waited for; matrix products, arithmetic and copies ran while one was open for 5% of the time, Pallas kernels for 0%

commit v1 on v0

v1 whole, which is shorter than its diff:
```python
import functools

import jax
import jax.numpy as jnp
from jax import lax
from jax.experimental import pallas as pl
from jax.experimental.pallas import tpu as pltpu
from jax.sharding import PartitionSpec as P

TILE = 8
HEADS = 16
HD = 128
NFAR = 2
CHUNKS = 2
SPOT = TILE * TILE
NEGATIVE = -1e30
EXP_SCALE = HD ** (-0.5) * 1.4426950408889634


def contract_last(left, right):
    return lax.dot_general(left, right, (((1,), (1,)), ((), ())), preferred_element_type=jnp.float32)


def attention_kernel(frames, heads, own, first, far_ref, valid_ref, kv_ref, top_ref, bottom_ref, q_ref, out_ref):
    groups, columns = kv_ref.shape[0], kv_ref.shape[1]
    total = groups * frames
    ones = jnp.ones((2 * columns * SPOT, HD), jnp.bfloat16)

    def with_ones(values):
        return jnp.concatenate([values, ones[: values.shape[0]]], axis=1)

    def attend(t, h):
        group, frame = t // frames, t % frames
        queries = [
            jnp.concatenate([q_ref[group, b, h, frame, a * SPOT : (a + 1) * SPOT] for b in range(own)], axis=0)
            for a in range(2)
        ]
        both = jnp.concatenate(queries, axis=0)
        near = [((t + step + total) % total) for step in (-1, 0, 1)]
        near = [(f // frames, f % frames) for f in near]
        split = own == columns
        pieces = [list(range(columns))] if split else [[e] for e in range(columns)]

        def column_valid(piece):
            if split or 0 < piece[0] < columns - 1:
                return None
            return valid_ref[2 if piece[0] == 0 else 3] > 0

        def gather(ref, kind, spot, piece):
            return jnp.concatenate([ref[spot[0], e, h, kind, spot[1]] for e in piece], axis=0)

        blocks = [[], []]
        for spot in near:
            for piece in pieces:
                valid = column_valid(piece)
                scores = contract_last(both, gather(kv_ref, 0, spot, piece))
                values = with_ones(gather(kv_ref, 1, spot, piece))
                half = own * SPOT
                blocks[0].append((valid, scores[:half], values))
                blocks[1].append((valid, scores[half:], values))
        for a, ref in ((0, top_ref), (1, bottom_ref)):
            row_valid = valid_ref[a] > 0
            for spot in near:
                for piece in pieces:
                    valid = column_valid(piece)
                    valid = row_valid if valid is None else jnp.logical_and(valid, row_valid)
                    scores = contract_last(queries[a], gather(ref, 0, spot, piece))
                    blocks[a].append((valid, scores, with_ones(gather(ref, 1, spot, piece))))
        for a in range(2):
            far_scores, far_values = [], []
            for b in range(own):
                keys, values = [], []
                for j in range(NFAR):
                    f = far_ref[((t * 2 + a) * own + b) * NFAR + j]
                    tokens = pl.ds(a * SPOT, SPOT)
                    keys.append(kv_ref[f // frames, first + b, h, 0, f % frames, tokens])
                    values.append(kv_ref[f // frames, first + b, h, 1, f % frames, tokens])
                far_scores.append(contract_last(queries[a][b * SPOT : (b + 1) * SPOT], jnp.concatenate(keys, axis=0)))
                far_values.append(with_ones(jnp.concatenate(values, axis=0)))
            far_all = jnp.concatenate(far_scores, axis=0)
            peak = jnp.max(far_all, axis=-1, keepdims=True)
            for valid, scores, _ in blocks[a]:
                block_peak = jnp.max(scores, axis=-1, keepdims=True)
                if valid is not None:
                    block_peak = jnp.where(valid, block_peak, NEGATIVE)
                peak = jnp.maximum(peak, block_peak)
            weights = jnp.exp2((far_all - peak) * EXP_SCALE).astype(jnp.bfloat16)
            summed = jnp.concatenate(
                [
                    jnp.dot(weights[b * SPOT : (b + 1) * SPOT], far_values[b], preferred_element_type=jnp.float32)
                    for b in range(own)
                ],
                axis=0,
            )
            for valid, scores, values in blocks[a]:
                shift = peak if valid is None else jnp.where(valid, peak, -NEGATIVE)
                weights = jnp.exp2((scores - shift) * EXP_SCALE).astype(jnp.bfloat16)
                summed = summed + jnp.dot(weights, values, preferred_element_type=jnp.float32)
            result = (summed[:, :HD] / summed[:, HD:]).astype(out_ref.dtype)
            for b in range(own):
                out_ref[group, b, h, frame, a * SPOT : (a + 1) * SPOT] = result[b * SPOT : (b + 1) * SPOT]

    def step(t, carry):
        for h in range(heads):
            attend(t, h)
        return carry

    lax.fori_loop(0, total, step, 0)


def attention(far, valid, kv, top, bottom, q, first):
    groups, own, heads, frames = q.shape[:4]
    body = functools.partial(attention_kernel, frames, heads, own, first)
    keys = 2 * SPOT * own * (9 * kv.shape[1] + NFAR) * SPOT * groups * frames * heads
    in_vmem = pl.BlockSpec(memory_space=pltpu.VMEM)
    in_smem = pl.BlockSpec(memory_space=pltpu.SMEM)
    return pl.pallas_call(
        body,
        out_shape=jax.ShapeDtypeStruct(q.shape, q.dtype),
        in_specs=[in_smem, in_smem, in_vmem, in_vmem, in_vmem, in_vmem],
        out_specs=in_vmem,
        compiler_params=pltpu.CompilerParams(vmem_limit_bytes=40 * 1024 * 1024),
        cost_estimate=pl.CostEstimate(flops=keys * HD * 4, bytes_accessed=4 << 20, transcendentals=keys),
    )(far, valid, kv, top, bottom, q)


def per_device(queries, keyvals, far_frames):
    frames, rows, columns, _ = queries.shape
    tokens = rows * columns
    ta_size, ha_size, wa_size = lax.axis_size("ta"), lax.axis_size("ha"), lax.axis_size("wa")
    paired = wa_size == 2
    group = ("ta", "wa") if paired else ("ta",)
    own = wa_size if paired else 1
    members = ta_size * own
    heads = HEADS // (members * CHUNKS)
    ha, wa = lax.axis_index("ha"), lax.axis_index("wa")
    up = [(i, i + 1) for i in range(ha_size - 1)]
    down = [(i + 1, i) for i in range(ha_size - 1)]
    valid = jnp.stack([ha > 0, ha < ha_size - 1, wa > 0, wa < wa_size - 1]).astype(jnp.int32)

    far = lax.all_gather(far_frames[:, :, 0, :], group, axis=0, tiled=False)
    far = far.reshape(ta_size, own, frames, 2, NFAR).transpose(0, 2, 3, 1, 4).reshape(-1)

    kv_split = keyvals.reshape(2, frames, tokens, members, CHUNKS, heads, HD).transpose(4, 3, 5, 0, 1, 2, 6)
    q_split = queries.reshape(frames, tokens, members, CHUNKS, heads, HD).transpose(3, 2, 4, 0, 1, 5)

    def exchange(value):
        return lax.all_to_all(value, group, split_axis=0, concat_axis=0, tiled=True)

    outs = []
    for chunk in range(CHUNKS):
        kv = exchange(kv_split[chunk]).reshape(ta_size, own, heads, 2, frames, tokens, HD)
        first = 0
        if not paired:
            left = lax.ppermute(kv, "wa", [(i, i + 1) for i in range(wa_size - 1)])
            right = lax.ppermute(kv, "wa", [(i + 1, i) for i in range(wa_size - 1)])
            kv = jnp.concatenate([left, kv, right], axis=1)
            first = 1
        top = lax.ppermute(kv[..., tokens - SPOT :, :], "ha", up)
        bottom = lax.ppermute(kv[..., :SPOT, :], "ha", down)
        q = exchange(q_split[chunk]).reshape(ta_size, own, heads, frames, tokens, HD)
        out = attention(far, valid, kv, top, bottom, q, first)
        outs.append(exchange(out.reshape(members, heads, frames, tokens, HD)))
    merged = jnp.stack(outs).transpose(3, 4, 1, 0, 2, 5)
    return merged.reshape(queries.shape)


def solution(mesh):
    placed = (P("ta", "ha", "wa", None), P(None, "ta", "ha", "wa", None), P("ta", "ha", "wa", None))
    return jax.shard_map(
        per_device, mesh=mesh, in_specs=placed, out_specs=P("ta", "ha", "wa", None), check_vma=False
    )
```

time: 538 us -> 124 us (0.23)
  waiting for transfers between devices: 244 us -> 12 us
  local copies, waits for them, and re-layouts: 118 us -> 24.5 us
  matrix products: 80.8 us -> 0 us
  other arithmetic: 48.2 us -> 1.22 us
  blocking collectives: 0 us -> 31.8 us
  Pallas kernels: 0 us -> 22 us
  between operations: 13.5 us -> 0.15 us
  loops' own time: 9.89 us -> 0 us
  starting transfers between devices: 21.9 us -> 31.5 us
    ppermute x6 -> x4, waiting for transfers between devices: 244 us -> 0.01 us  [the longest x2 0.01 us: per_device(): top = lax.ppermute(kv[..., tokens - SPOT:, :], 'ha', up)]
    dot_general x17 -> x0, matrix products: 80.8 us -> none  [the longest x4 41.8 us: attend(): jnp.einsum('qhd,khd->hqk', query_rows, near_keys, preferred_element_type=...]
    while x48 -> x0, local copies, waits for them, and re-layouts: 62.2 us -> none
    slice x10 -> x8, local copies, waits for them, and re-layouts: 46.4 us -> 15.9 us  [the longest x3 8.22 us: per_device(): kv_split[chunk]]
    concatenate x2 -> x0, other arithmetic: 28.4 us -> none  [extended_2(): jnp.concatenate([lax.ppermute(tail, axis, [(i, (i + 1) % count) for i in...]
    pallas_call x0 -> x2, Pallas kernels: none -> 22 us  [attention(): pl.pallas_call(body, out_shape=jax.ShapeDtypeStruct(q.shape, q.dtype), in...]
    all_to_all x0 -> x5, starting transfers between devices: none -> 20.3 us  [exchange(): return lax.all_to_all(value, group, split_axis=0, concat_axis=0, tiled=True)]
    reduce_sum x8 -> x0, other arithmetic: 19.4 us -> none  [the longest x4 17.8 us: attend(): jnp.sum(near_exp, axis=-1, keepdims=True)]
  transfers between devices with their start and end apart: 7 -> 9, of which waited for: 6 -> 2; matrix products, arithmetic and copies ran while one was open for 5% -> 13% of each run, Pallas kernels for 0% -> 18%
where the time goes in v1:
time: 124 us; the launch traced here: 123 us
  blocking collectives  31.8 us (26%)
  starting transfers between devices  31.5 us (25%)
  local copies, waits for them, and re-layouts  24.5 us (20%)
  Pallas kernels  22 us (18%)
  waiting for transfers between devices  12 us (10%)
    pallas_call x2, Pallas kernels, attention(): pl.pallas_call(body, out_shape=jax.ShapeDtypeStruct(q.shape, q.dtype), in...  22 us
    all_to_all x5, starting transfers between devices, exchange(): return lax.all_to_all(value, group, split_axis=0, concat_axis=0, tiled=True)  20.3 us
    all_gather x1, blocking collectives, per_device(): far = lax.all_gather(far_frames[:, :, 0, :], group, axis=0, tiled=False)  19 us
    all_to_all x1, blocking collectives, exchange(): return lax.all_to_all(value, group, split_axis=0, concat_axis=0, tiled=True)  12.8 us
    all_to_all x5, waiting for transfers between devices, exchange(): return lax.all_to_all(value, group, split_axis=0, concat_axis=0, tiled=True)  12 us
    ppermute x2, starting transfers between devices, per_device(): top = lax.ppermute(kv[..., tokens - SPOT:, :], 'ha', up)  8.57 us
    slice x3, local copies, waits for them, and re-layouts, per_device(): kv_split[chunk]  8.22 us
    slice x3, local copies, waits for them, and re-layouts, per_device(): q_split[chunk]  5.51 us
  transfers between devices with their start and end apart: 9, of which 2 were waited for; matrix products, arithmetic and copies ran while one was open for 13% of the time, Pallas kernels for 18%

profile of v1, /device:TPU:0, one launch (start us, length us, event | category | flops | bytes accessed | tf_op | source)
XLA Modules:
  0.0 123.1 jit_solution(5133999723261892312)
XLA Ops:
  0.0 1.8 %reshape.37 = bf16[2,128,8,2,1,128]{5,3,2,1,0,4:T(2,128)(2,1)S(1)} reshape(bf16[2,16,8,2048]{3,2,1,0:T(8,128)(2,1)} %param.3) | data formatting | bytes 2097152 | tf_op jit(solution)/shard_map/reshape | solution.py:145
  1.8 2.3 %fusion.1 = (bf16[1,8,1,2,128,128]{5,0,1,4,3,2:T(2,128)(2,1)S(1)}, bf16[1,8,1,2,128,128]{5,0,1,4,3,2:T(2,128)(2,1)}) fusion(bf16[2,8,1,2,128,128]{5,0,1,4,3,2:T(2,128)(2,1)S(1)} %bitcast.60), kind=kLoop, calls=%fused_computation.7 | loop fusion | bytes 2097152 | tf_op jit(solution)/shard_map/slice | solution.py:161
  5.1 5.2 %all-to-all-start.1 = ((bf16[8,1,2,128,128]{4,3,2,1,0:T(8,128)(2,1)}), bf16[8,1,2,128,128]{4,3,2,1,0:T(8,128)(2,1)S(1)}, u32[]{:S(2)}, u32[]{:S(2)}) async-start(bf16[8,1,2,128,128]{4,3,2,1,0:T(8,128)(2,1)} %bitcast.50), calls=%async_computation.1 | async-start | bytes 1048576 | tf_op jit(solution)/shard_map/all_to_all | solution.py:148
  10.2 3.2 %reshape.35 = bf16[2,2,128,8,2,1,128]{6,4,3,2,1,0,5:T(2,128)(2,1)S(1)} reshape(bf16[2,2,16,8,2048]{4,3,2,1,0:T(8,128)(2,1)} %param.4) | data formatting | bytes 4194304 | tf_op jit(solution)/shard_map/reshape | solution.py:144
  13.5 3.9 %fusion = (bf16[1,8,1,2,2,128,128]{6,0,1,5,4,3,2:T(2,128)(2,1)S(1)}, bf16[1,8,1,2,2,128,128]{6,0,1,5,4,3,2:T(2,128)(2,1)}) fusion(bf16[2,8,1,2,2,128,128]{6,0,1,5,4,3,2:T(2,128)(2,1)S(1)} %bitcast.59), kind=kLoop, calls=%fused_computation.6 | loop fusion | bytes 4194304 | tf_op jit(solution)/shard_map/slice | solution.py:152
  17.3 1.4 %copy.52 = bf16[1,8,1,2,2,128,128]{6,5,4,3,1,2,0:T(8,128)(2,1)} copy(bf16[1,8,1,2,2,128,128]{6,0,1,5,4,3,2:T(2,128)(2,1)S(1)} %get-tuple-element.5) | data formatting | bytes 2097152 | tf_op jit(solution)/shard_map/slice | solution.py:152
  19.1 3.8 %all-to-all-start = ((bf16[8,1,2,2,128,128]{5,4,3,2,1,0:T(8,128)(2,1)}), bf16[8,1,2,2,128,128]{5,4,3,2,1,0:T(8,128)(2,1)S(1)}, u32[]{:S(2)}, u32[]{:S(2)}) async-start(bf16[8,1,2,2,128,128]{5,4,3,2,1,0:T(8,128)(2,1)} %bitcast.48), calls=%async_computation | async-start | bytes 2097152 | tf_op jit(solution)/shard_map/all_to_all | solution.py:148
  22.9 3.0 %copy.51 = bf16[1,8,1,2,2,128,128]{6,5,4,3,1,2,0:T(8,128)(2,1)} copy(bf16[1,8,1,2,2,128,128]{6,0,1,5,4,3,2:T(2,128)(2,1)} %get-tuple-element.6) | data formatting | bytes 2097152 | tf_op jit(solution)/shard_map/slice | solution.py:152
  25.9 11.6 %all-to-all-done = bf16[8,1,2,2,128,128]{5,4,3,2,1,0:T(8,128)(2,1)S(1)} async-done(((bf16[8,1,2,2,128,128]{5,4,3,2,1,0:T(8,128)(2,1)}), bf16[8,1,2,2,128,128]{5,4,3,2,1,0:T(8,128)(2,1)S(1)}, u32[]{:S(2)}, u32[]{:S(2)}) %all-to-all-start) | async-done | bytes 1048608 | tf_op jit(solution)/shard_map/all_to_all | solution.py:148
  37.5 3.7 %all-to-all-start.3 = ((bf16[8,1,2,2,128,128]{5,4,3,2,1,0:T(8,128)(2,1)}), bf16[8,1,2,2,128,128]{5,4,3,2,1,0:T(8,128)(2,1)S(1)}, u32[]{:S(2)}, u32[]{:S(2)}) async-start(bf16[8,1,2,2,128,128]{5,4,3,2,1,0:T(8,128)(2,1)} %bitcast.61), calls=%async_computation.3 | async-start | bytes 2097152 | tf_op jit(solution)/shard_map/all_to_all | solution.py:148
  42.3 4.3 %collective-permute-start = (bf16[4,2,1,2,2,64,128]{6,5,4,3,2,1,0:T(8,128)(2,1)}, bf16[4,2,1,2,2,64,128]{6,5,4,3,2,1,0:T(8,128)(2,1)}, u32[]{:S(2)}, u32[]{:S(2)}) collective-permute-start(bf16[4,2,1,2,2,64,128]{6,5,4,3,2,1,0:T(8,128)(2,1)} %get-tuple-element.10), channel_id=1, source_target_pairs={{0,2},{2,4},{4,6},{1,3},{3,5},{5,7},{8,10},{10,12},{12,14},{9,11},... | collective-permute-start | bytes 1572872 | tf_op jit(solution)/shard_map/ppermute | solution.py:159
  46.6 1.3 %collective-permute-start.1 = (bf16[4,2,1,2,2,64,128]{6,5,4,3,2,1,0:T(8,128)(2,1)}, bf16[4,2,1,2,2,64,128]{6,5,4,3,2,1,0:T(8,128)(2,1)}, u32[]{:S(2)}, u32[]{:S(2)}) collective-permute-start(bf16[4,2,1,2,2,64,128]{6,5,4,3,2,1,0:T(8,128)(2,1)} %get-tuple-element.9), channel_id=1, source_target_pairs={{2,0},{4,2},{6,4},{3,1},{5,3},{7,5},{10,8},{12,10},{14,12},{11,9},... | collective-permute-start | bytes 1572872 | tf_op jit(solution)/shard_map/ppermute | solution.py:160
  47.9 19.0 %all-gather = s32[16,2,1,2]{3,1,2,0:T(2,128)S(1)} all-gather(s32[2,2,1,2]{3,1,2,0:T(2,128)S(1)} %bitcast.65), channel_id=2, replica_groups=mesh['ta'=4,'ha'=4,'wa'=2] {'ta','wa'}, dimensions={0}, use_global_device_ids=true | all-gather | bytes 288 | tf_op jit(solution)/shard_map/all_gather | solution.py:141
  67.0 2.2 %copy.53 = bf16[1,8,1,2,128,128]{5,4,3,1,2,0:T(8,128)(2,1)} copy(bf16[1,8,1,2,128,128]{5,0,1,4,3,2:T(2,128)(2,1)} %get-tuple-element.8) | data formatting | bytes 1048576 | tf_op jit(solution)/shard_map/slice | solution.py:161
  69.2 3.5 %all-to-all-start.4 = ((bf16[8,1,2,128,128]{4,3,2,1,0:T(8,128)(2,1)}), bf16[8,1,2,128,128]{4,3,2,1,0:T(8,128)(2,1)S(1)}, u32[]{:S(2)}, u32[]{:S(2)}) async-start(bf16[8,1,2,128,128]{4,3,2,1,0:T(8,128)(2,1)} %bitcast.62), calls=%async_computation.4 | async-start | bytes 1048576 | tf_op jit(solution)/shard_map/all_to_all | solution.py:148
  73.8 4.3 %collective-permute-start.2 = (bf16[4,2,1,2,2,64,128]{6,5,4,3,2,1,0:T(8,128)(2,1)}, bf16[4,2,1,2,2,64,128]{6,5,4,3,2,1,0:T(8,128)(2,1)}, u32[]{:S(2)}, u32[]{:S(2)}) collective-permute-start(bf16[4,2,1,2,2,64,128]{6,5,4,3,2,1,0:T(8,128)(2,1)} %get-tuple-element.12), channel_id=1, source_target_pairs={{0,2},{2,4},{4,6},{1,3},{3,5},{5,7},{8,10},{10,12},{12,14},{9,11},... | collective-permute-start | bytes 1572872 | tf_op jit(solution)/shard_map/ppermute | solution.py:159
  78.1 1.3 %collective-permute-start.3 = (bf16[4,2,1,2,2,64,128]{6,5,4,3,2,1,0:T(8,128)(2,1)}, bf16[4,2,1,2,2,64,128]{6,5,4,3,2,1,0:T(8,128)(2,1)}, u32[]{:S(2)}, u32[]{:S(2)}) collective-permute-start(bf16[4,2,1,2,2,64,128]{6,5,4,3,2,1,0:T(8,128)(2,1)} %get-tuple-element.11), channel_id=1, source_target_pairs={{2,0},{4,2},{6,4},{3,1},{5,3},{7,5},{10,8},{12,10},{14,12},{11,9},... | collective-permute-start | bytes 1572872 | tf_op jit(solution)/shard_map/ppermute | solution.py:160
  79.5 11.0 %shard_map.37 = bf16[4,2,1,2,128,128]{5,4,3,2,1,0:T(8,128)(2,1)S(1)} custom-call(s32[64]{0:T(128)S(1)} %reshape.34.far_ref, s32[4]{0:T(128)S(1)} %add_convert_fusion.valid_ref, bf16[4,2,1,2,2,128,128]{6,5,4,3,2,1,0:T(8,128)(2,1)S(1)} %bitcast.54, bf16[4,2,1,2,2,64,128]{6,5,4,3,2,1,0:T(8,128)(2,1)} %collective-permute-done.top_ref, ...), custom_call_target="tpu_custom_call" | custom-call | flops 1342177280 | bytes 4194304 | tf_op jit(solution)/shard_map/pallas_call | solution.py:117
  91.3 4.1 %all-to-all-start.2 = ((bf16[8,1,2,128,128]{4,3,2,1,0:T(8,128)(2,1)}), bf16[8,1,2,128,128]{4,3,2,1,0:T(8,128)(2,1)}, u32[]{:S(2)}, u32[]{:S(2)}) async-start(bf16[8,1,2,128,128]{4,3,2,1,0:T(8,128)(2,1)} %bitcast.57), calls=%async_computation.2 | async-start | bytes 1048576 | tf_op jit(solution)/shard_map/all_to_all | solution.py:148
  95.4 11.0 %shard_map.38 = bf16[4,2,1,2,128,128]{5,4,3,2,1,0:T(8,128)(2,1)S(1)} custom-call(s32[64]{0:T(128)S(1)} %reshape.34.far_ref, s32[4]{0:T(128)S(1)} %add_convert_fusion.valid_ref, bf16[4,2,1,2,2,128,128]{6,5,4,3,2,1,0:T(8,128)(2,1)S(1)} %bitcast.52, bf16[4,2,1,2,2,64,128]{6,5,4,3,2,1,0:T(8,128)(2,1)} %collective-permute-done.2.top_ref, ...), custom_call_target="tpu_custom_call" | custom-call | flops 1342177280 | bytes 4194304 | tf_op jit(solution)/shard_map/pallas_call | solution.py:117
  106.4 12.8 %all_to_all.30 = bf16[8,1,2,128,128]{4,3,2,1,0:T(8,128)(2,1)S(1)} all-to-all(bf16[8,1,2,128,128]{4,3,2,1,0:T(8,128)(2,1)S(1)} %bitcast.58), channel_id=1, replica_groups=mesh['ta'=4,'ha'=4,'wa'=2] {'ta','wa'}, dimensions={0} | all-to-all | bytes 1048576 | tf_op jit(solution)/shard_map/all_to_all | solution.py:148
  119.2 1.1 maximum_bitcast_fusion
  120.4 1.1 copy.44
  121.5 1.6 %reshape.43 = bf16[2,16,8,2048]{3,2,1,0:T(8,128)(2,1)} reshape(bf16[2,128,8,2,1,128]{5,3,2,1,0,4:T(2,128)(2,1)S(1)} %copy.44) | data formatting | bytes 2097152 | tf_op jit(solution)/shard_map/reshape | solution.py:165
  (18 shorter events, 4.5 us)
Async XLA Ops:
  5.1 14.0 %all-to-all-start.1 = ((bf16[8,1,2,128,128]{4,3,2,1,0:T(8,128)(2,1)}), bf16[8,1,2,128,128]{4,3,2,1,0:T(8,128)(2,1)S(1)}, u32[]{:S(2)}, u32[]{:S(2)}) async-start(bf16[8,1,2,128,128]{4,3,2,1,0:T(8,128)(2,1)} %bitcast.50), calls=%async_computation.1 | async-start | bytes 1048576 | tf_op jit(solution)/shard_map/all_to_all | solution.py:148
  19.1 18.4 %all-to-all-start = ((bf16[8,1,2,2,128,128]{5,4,3,2,1,0:T(8,128)(2,1)}), bf16[8,1,2,2,128,128]{5,4,3,2,1,0:T(8,128)(2,1)S(1)}, u32[]{:S(2)}, u32[]{:S(2)}) async-start(bf16[8,1,2,2,128,128]{5,4,3,2,1,0:T(8,128)(2,1)} %bitcast.48), calls=%async_computation | async-start | bytes 2097152 | tf_op jit(solution)/shard_map/all_to_all | solution.py:148
  37.5 10.4 %copy-start.1 = (s32[2,2,1,2]{3,2,1,0:T(1,128)S(1)}, s32[2,2,1,2]{3,2,1,0:T(1,128)}, u32[]{:S(2)}) copy-start(s32[2,2,1,2]{3,2,1,0:T(1,128)} %param.5) | copy-start | bytes 100
  37.5 31.8 %all-to-all-start.3 = ((bf16[8,1,2,2,128,128]{5,4,3,2,1,0:T(8,128)(2,1)}), bf16[8,1,2,2,128,128]{5,4,3,2,1,0:T(8,128)(2,1)S(1)}, u32[]{:S(2)}, u32[]{:S(2)}) async-start(bf16[8,1,2,2,128,128]{5,4,3,2,1,0:T(8,128)(2,1)} %bitcast.61), calls=%async_computation.3 | async-start | bytes 2097152 | tf_op jit(solution)/shard_map/all_to_all | solution.py:148
  42.3 37.2 %collective-permute-start = (bf16[4,2,1,2,2,64,128]{6,5,4,3,2,1,0:T(8,128)(2,1)}, bf16[4,2,1,2,2,64,128]{6,5,4,3,2,1,0:T(8,128)(2,1)}, u32[]{:S(2)}, u32[]{:S(2)}) collective-permute-start(bf16[4,2,1,2,2,64,128]{6,5,4,3,2,1,0:T(8,128)(2,1)} %get-tuple-element.10), channel_id=1, source_target_pairs={{0,2},{2,4},{4,6},{1,3},{3,5},{5,7},{8,10},{10,12},{12,14},{9,11},... | collective-permute-start | bytes 1572872 | tf_op jit(solution)/shard_map/ppermute | solution.py:159
  46.6 32.9 %collective-permute-start.1 = (bf16[4,2,1,2,2,64,128]{6,5,4,3,2,1,0:T(8,128)(2,1)}, bf16[4,2,1,2,2,64,128]{6,5,4,3,2,1,0:T(8,128)(2,1)}, u32[]{:S(2)}, u32[]{:S(2)}) collective-permute-start(bf16[4,2,1,2,2,64,128]{6,5,4,3,2,1,0:T(8,128)(2,1)} %get-tuple-element.9), channel_id=1, source_target_pairs={{2,0},{4,2},{6,4},{3,1},{5,3},{7,5},{10,8},{12,10},{14,12},{11,9},... | collective-permute-start | bytes 1572872 | tf_op jit(solution)/shard_map/ppermute | solution.py:160
  69.2 22.0 %all-to-all-start.4 = ((bf16[8,1,2,128,128]{4,3,2,1,0:T(8,128)(2,1)}), bf16[8,1,2,128,128]{4,3,2,1,0:T(8,128)(2,1)S(1)}, u32[]{:S(2)}, u32[]{:S(2)}) async-start(bf16[8,1,2,128,128]{4,3,2,1,0:T(8,128)(2,1)} %bitcast.62), calls=%async_computation.4 | async-start | bytes 1048576 | tf_op jit(solution)/shard_map/all_to_all | solution.py:148
  73.8 21.6 %collective-permute-start.2 = (bf16[4,2,1,2,2,64,128]{6,5,4,3,2,1,0:T(8,128)(2,1)}, bf16[4,2,1,2,2,64,128]{6,5,4,3,2,1,0:T(8,128)(2,1)}, u32[]{:S(2)}, u32[]{:S(2)}) collective-permute-start(bf16[4,2,1,2,2,64,128]{6,5,4,3,2,1,0:T(8,128)(2,1)} %get-tuple-element.12), channel_id=1, source_target_pairs={{0,2},{2,4},{4,6},{1,3},{3,5},{5,7},{8,10},{10,12},{12,14},{9,11},... | collective-permute-start | bytes 1572872 | tf_op jit(solution)/shard_map/ppermute | solution.py:159
  78.1 17.3 %collective-permute-start.3 = (bf16[4,2,1,2,2,64,128]{6,5,4,3,2,1,0:T(8,128)(2,1)}, bf16[4,2,1,2,2,64,128]{6,5,4,3,2,1,0:T(8,128)(2,1)}, u32[]{:S(2)}, u32[]{:S(2)}) collective-permute-start(bf16[4,2,1,2,2,64,128]{6,5,4,3,2,1,0:T(8,128)(2,1)} %get-tuple-element.11), channel_id=1, source_target_pairs={{2,0},{4,2},{6,4},{3,1},{5,3},{7,5},{10,8},{12,10},{14,12},{11,9},... | collective-permute-start | bytes 1572872 | tf_op jit(solution)/shard_map/ppermute | solution.py:160
  90.5 0.8 copy-start
  91.3 15.2 %all-to-all-start.2 = ((bf16[8,1,2,128,128]{4,3,2,1,0:T(8,128)(2,1)}), bf16[8,1,2,128,128]{4,3,2,1,0:T(8,128)(2,1)}, u32[]{:S(2)}, u32[]{:S(2)}) async-start(bf16[8,1,2,128,128]{4,3,2,1,0:T(8,128)(2,1)} %bitcast.57), calls=%async_computation.2 | async-start | bytes 1048576 | tf_op jit(solution)/shard_map/all_to_all | solution.py:148

commit v2 on v0

v2 whole, which is shorter than its diff:
```python
import functools

import jax
import jax.numpy as jnp
from jax import lax
from jax.experimental import pallas as pl
from jax.experimental.pallas import tpu as pltpu
from jax.sharding import PartitionSpec as P

TILE = 8
HEADS = 16
HD = 128
NFAR = 2
SPOT = TILE * TILE
NEGATIVE = -1e30
EXP_SCALE = HD ** (-0.5) * 1.4426950408889634
VMEM_LIMIT = 48 * 1024 * 1024


def contract_last(left, right):
    return lax.dot_general(left, right, (((1,), (1,)), ((), ())), preferred_element_type=jnp.float32)


def with_ones(values):
    return jnp.concatenate([values, jnp.ones_like(values)], axis=1)


def head_lanes(h):
    return pl.ds(pl.multiple_of(h * HD, HD), HD)


def lane_index(rows):
    return lax.broadcasted_iota(jnp.int32, (rows, HD), 1)


def near_kernel(sides, meta_ref, own_ref, ext_ref, top_ref, bottom_ref, ext_top_ref, ext_bottom_ref, *refs):
    q_refs, out_refs, sum_refs = refs[:sides], refs[sides : 2 * sides], refs[2 * sides :]
    frame, ext_at = meta_ref[0], meta_ref[1]
    valid = (meta_ref[2] > 0, meta_ref[3] > 0)
    half = sides * SPOT

    def middle(kind, lanes):
        parts = [own_ref[kind, 0, :, lanes], own_ref[kind, 1, :, lanes], ext_ref[kind, ext_at, :, lanes]]
        return jnp.concatenate(parts, axis=0)

    def halo(a, kind, lanes):
        ref, ext = ((top_ref, ext_top_ref), (bottom_ref, ext_bottom_ref))[a]
        return jnp.concatenate([ref[kind, 0, :, lanes], ref[kind, 1, :, lanes], ext[kind, 0, :, lanes]], axis=0)

    def step(h, carry):
        lanes = head_lanes(h)
        queries = [
            jnp.concatenate([ref[frame, a * SPOT : (a + 1) * SPOT, lanes] for ref in q_refs], axis=0) for a in range(2)
        ]
        middle_scores = contract_last(jnp.concatenate(queries, axis=0), middle(0, lanes))
        middle_values = with_ones(middle(1, lanes))
        for a in range(2):
            near = middle_scores[a * half : (a + 1) * half]
            edge = contract_last(queries[a], halo(a, 0, lanes))
            edge_peak = jnp.where(valid[a], jnp.max(edge, axis=-1, keepdims=True), NEGATIVE)
            peak = jnp.maximum(jnp.max(near, axis=-1, keepdims=True), edge_peak)
            near_weights = jnp.exp2((near - peak) * EXP_SCALE).astype(jnp.bfloat16)
            edge_weights = jnp.exp2((edge - jnp.where(valid[a], peak, -NEGATIVE)) * EXP_SCALE).astype(jnp.bfloat16)
            summed = jnp.dot(near_weights, middle_values, preferred_element_type=jnp.float32)
            summed = summed + jnp.dot(
                edge_weights, with_ones(halo(a, 1, lanes)), preferred_element_type=jnp.float32
            )
            total = summed[:, HD:]
            result = summed[:, :HD] / total
            log_sum = peak * EXP_SCALE + jnp.log2(total)
            for s in range(sides):
                tokens, rows = slice(a * SPOT, (a + 1) * SPOT), slice(s * SPOT, (s + 1) * SPOT)
                out_refs[s][tokens, lanes] = result[rows].astype(out_refs[s].dtype)
                sum_refs[s][tokens, :] = jnp.where(lane_index(SPOT) == h, log_sum[rows], sum_refs[s][tokens, :])
        return carry

    for ref in sum_refs:
        ref[...] = jnp.zeros_like(ref)
    lax.fori_loop(0, HEADS, step, 0)


def near_attention(meta, own, ext, top, bottom, ext_top, ext_bottom, queries, out_dtypes):
    sides = len(queries)
    tokens, features = queries[0].shape[1:]
    in_vmem = pl.BlockSpec(memory_space=pltpu.VMEM)
    scores = sides * HEADS * tokens * 9 * SPOT
    outs = [jax.ShapeDtypeStruct((tokens, features), dtype) for dtype in out_dtypes]
    sums = [jax.ShapeDtypeStruct((tokens, HD), jnp.float32) for _ in out_dtypes]
    return pl.pallas_call(
        functools.partial(near_kernel, sides),
        out_shape=outs + sums,
        in_specs=[pl.BlockSpec(memory_space=pltpu.SMEM)] + [in_vmem] * (6 + sides),
        out_specs=[in_vmem] * (2 * sides),
        compiler_params=pltpu.CompilerParams(vmem_limit_bytes=VMEM_LIMIT),
        cost_estimate=pl.CostEstimate(flops=scores * HD * 4, bytes_accessed=8 << 20, transcendentals=scores),
    )(meta, own, ext, top, bottom, ext_top, ext_bottom, *queries)


def far_kernel(meta_ref, code_ref, q_ref, core_ref, cross_ref, last_ref, corner_ref, corner_last_ref, *refs):
    near_refs, near_sums, out_ref, sum_ref, held, sems = refs[:2], refs[2:4], refs[4], refs[5], refs[6], refs[7]
    sources = [(core_ref, 0), (core_ref, 1), (cross_ref, 0), (last_ref, 0), (corner_ref, 0), (corner_last_ref, 0)]

    def for_copies(action):
        for f in range(2):
            for a in range(2):
                for j in range(NFAR):
                    slot = (f * 2 + a) * NFAR + j
                    for code, (ref, at) in enumerate(sources):

                        @pl.when(code_ref[slot] == code)
                        def _(ref=ref, at=at, f=f, a=a, j=j, slot=slot):
                            copy = pltpu.make_async_copy(
                                ref.at[:, at, pl.ds(a * SPOT, SPOT), :],
                                held.at[:, f * 2 + a, pl.ds(j * SPOT, SPOT), :],
                                sems.at[slot],
                            )
                            action(copy)

    for_copies(lambda copy: copy.start())
    for_copies(lambda copy: copy.wait())

    def step(h, carry):
        lanes = head_lanes(h)
        for early in range(2):
            frame = meta_ref[early]
            for a in range(2):
                tokens = slice(a * SPOT, (a + 1) * SPOT)
                scores = contract_last(q_ref[frame, tokens, lanes], held[0, frame * 2 + a, :, lanes])
                peak = jnp.max(scores, axis=-1, keepdims=True)
                weights = jnp.exp2((scores - peak) * EXP_SCALE).astype(jnp.bfloat16)
                values = with_ones(held[1, frame * 2 + a, :, lanes])
                summed = jnp.dot(weights, values, preferred_element_type=jnp.float32)
                mask = lane_index(SPOT) == h
                near_sum = jnp.max(
                    jnp.where(mask, near_sums[early][tokens, :], NEGATIVE), axis=-1, keepdims=True
                )
                far_peak = peak * EXP_SCALE
                top = jnp.maximum(near_sum, far_peak)
                near_scale, far_scale = jnp.exp2(near_sum - top), jnp.exp2(far_peak - top)
                total = near_scale + far_scale * summed[:, HD:]
                joined = near_scale * near_refs[early][tokens, lanes] + far_scale * summed[:, :HD]
                out_ref[early, tokens, lanes] = joined / total
                sum_ref[early, tokens, :] = jnp.where(mask, top + jnp.log2(total), sum_ref[early, tokens, :])
        return carry

    sum_ref[...] = jnp.zeros_like(sum_ref)
    lax.fori_loop(0, HEADS, step, 0)


def far_attention(meta, code, queries, buffers, near):
    tokens, features = queries.shape[1:]
    in_vmem = pl.BlockSpec(memory_space=pltpu.VMEM)
    in_smem = pl.BlockSpec(memory_space=pltpu.SMEM)
    scores = HEADS * 2 * tokens * NFAR * SPOT
    return pl.pallas_call(
        far_kernel,
        out_shape=[
            jax.ShapeDtypeStruct((2, tokens, features), jnp.float32),
            jax.ShapeDtypeStruct((2, tokens, HD), jnp.float32),
        ],
        in_specs=[in_smem, in_smem, in_vmem] + [pl.BlockSpec(memory_space=pl.ANY)] * 5 + [in_vmem] * 4,
        out_specs=[in_vmem] * 2,
        scratch_shapes=[
            pltpu.VMEM((2, 4, NFAR * SPOT, features), jnp.bfloat16),
            pltpu.SemaphoreType.DMA((4 * NFAR,)),
        ],
        compiler_params=pltpu.CompilerParams(vmem_limit_bytes=VMEM_LIMIT),
        cost_estimate=pl.CostEstimate(flops=scores * HD * 4, bytes_accessed=8 << 20, transcendentals=scores),
    )(meta, code, queries, *buffers, *near)


def finish_kernel(sides, meta_ref, own_ref, own_sum_ref, *refs):
    parts, sums, out_ref = refs[: 2 * sides], refs[2 * sides : 4 * sides], refs[4 * sides]
    for early in range(2):
        logs = [own_sum_ref[early]]
        for s in range(sides):
            logs.append(jnp.where(meta_ref[2 + s] > 0, sums[early * sides + s][...], NEGATIVE))
        top = functools.reduce(jnp.maximum, logs)
        scales = [jnp.exp2(value - top) for value in logs]
        total = functools.reduce(jnp.add, scales)
        scales = [value / total for value in scales]
        for h in range(HEADS):
            lanes = slice(h * HD, (h + 1) * HD)
            joined = scales[0][:, h : h + 1] * own_ref[early, :, lanes]
            for s in range(sides):
                joined = joined + scales[1 + s][:, h : h + 1] * parts[early * sides + s][:, lanes].astype(jnp.float32)
            out_ref[meta_ref[early], :, lanes] = joined.astype(out_ref.dtype)


def finish(meta, own, own_sum, parts, sums):
    sides = len(parts) // 2
    in_vmem = pl.BlockSpec(memory_space=pltpu.VMEM)
    return pl.pallas_call(
        functools.partial(finish_kernel, sides),
        out_shape=jax.ShapeDtypeStruct(own.shape, jnp.bfloat16),
        in_specs=[pl.BlockSpec(memory_space=pltpu.SMEM)] + [in_vmem] * (2 + 4 * sides),
        out_specs=in_vmem,
        compiler_params=pltpu.CompilerParams(vmem_limit_bytes=VMEM_LIMIT),
        cost_estimate=pl.CostEstimate(flops=own.size * 8, bytes_accessed=5 << 20, transcendentals=0),
    )(meta, own, own_sum, *parts, *sums)


def per_device(queries, keyvals, far_frames):
    shape = queries.shape
    frames, rows, columns, features = shape
    tokens = rows * columns
    ta_size, ha_size, wa_size = lax.axis_size("ta"), lax.axis_size("ha"), lax.axis_size("wa")
    ta, ha, wa = lax.axis_index("ta"), lax.axis_index("ha"), lax.axis_index("wa")
    parity = ta % 2
    queries = queries.reshape(frames, tokens, features)
    keyvals = keyvals.reshape(2, frames, tokens, features)

    core_pairs = [(i, i ^ 1) for i in range(ta_size)]
    cross_pairs = [(i, ta_size - 1 - i) for i in range(ta_size)]
    up = [(i, i + 1) for i in range(ha_size - 1)]
    down = [(i + 1, i) for i in range(ha_size - 1)]
    if wa_size == 2:
        ways = [([(0, 1), (1, 0)], [(0, 1), (1, 0)], wa >= 0)]
    else:
        right = [(i, i + 1) for i in range(wa_size - 1)]
        left = [(i + 1, i) for i in range(wa_size - 1)]
        ways = [(right, left, wa < wa_size - 1), (left, right, wa > 0)]

    def frame_of(value, index):
        return lax.dynamic_slice_in_dim(value, index, 1, axis=1)

    def halo_rows(value):
        top = lax.ppermute(value[:, :, tokens - SPOT :], "ha", up)
        return top, lax.ppermute(value[:, :, :SPOT], "ha", down)

    cross = lax.ppermute(frame_of(keyvals, parity), "ta", cross_pairs)
    top, bottom = halo_rows(keyvals)
    visitors = [lax.ppermute(queries, "wa", there) for there, _, _ in ways]
    core = lax.ppermute(keyvals, "ta", core_pairs)
    inner_top, inner_bottom = frame_of(top, 1 - parity), frame_of(bottom, 1 - parity)
    core_top = lax.ppermute(inner_top, "ta", core_pairs)
    core_bottom = lax.ppermute(inner_bottom, "ta", core_pairs)
    cross_top, cross_bottom = halo_rows(cross)
    last_frame, cross = lax.optimization_barrier((frame_of(keyvals, 1 - parity), cross))
    last = lax.ppermute(last_frame, "ta", cross_pairs)
    corner = lax.ppermute(cross, "ta", core_pairs)
    corner_last = lax.ppermute(last, "ta", core_pairs)

    has_top, has_bottom = ha > 0, ha < ha_size - 1

    def as_meta(*values):
        return jnp.stack([jnp.asarray(value).astype(jnp.int32) for value in values])

    dtypes = [jnp.bfloat16] * len(ways) + [jnp.float32]
    q_sides = visitors + [queries]
    early = near_attention(
        as_meta(1 - parity, parity, has_top, has_bottom),
        keyvals, core, top, bottom, core_top, core_bottom, q_sides, dtypes,
    )
    late = near_attention(
        as_meta(parity, 0, has_top, has_bottom),
        keyvals, cross, top, bottom, cross_top, cross_bottom, q_sides, dtypes,
    )
    sides = len(ways) + 1

    def send_back(near):
        parts = [lax.ppermute(near[s], "wa", back) for s, (_, back, _) in enumerate(ways)]
        return parts, [lax.ppermute(near[sides + s], "wa", back) for s, (_, back, _) in enumerate(ways)]

    early_parts, early_sums = send_back(early)
    late_parts, late_sums = send_back(late)

    wanted = far_frames[:, :, 0, :]
    owner, place = wanted // frames, wanted % frames
    inner = (place != owner % 2).astype(jnp.int32)
    code = jnp.where(owner == ta ^ 1, place, jnp.where(owner == ta_size - 1 - ta, 2 + inner, 4 + inner))
    own, own_sum = far_attention(
        as_meta(1 - parity, parity),
        code.reshape(-1).astype(jnp.int32),
        queries,
        (core, cross, last, corner, corner_last),
        (early[sides - 1], late[sides - 1], early[2 * sides - 1], late[2 * sides - 1]),
    )
    meta = as_meta(1 - parity, parity, *[valid for _, _, valid in ways])
    out = finish(meta, own, own_sum, early_parts + late_parts, early_sums + late_sums)
    return out.reshape(shape)


def solution(mesh):
    placed = (P("ta", "ha", "wa", None), P(None, "ta", "ha", "wa", None), P("ta", "ha", "wa", None))
    return jax.shard_map(
        per_device, mesh=mesh, in_specs=placed, out_specs=P("ta", "ha", "wa", None), check_vma=False
    )
```

time: 538 us -> 121 us (0.22)
  waiting for transfers between devices: 244 us -> 29.2 us
  local copies, waits for them, and re-layouts: 118 us -> 16.3 us
  matrix products: 80.8 us -> 0 us
  Pallas kernels: 0 us -> 51.9 us
  other arithmetic: 48.2 us -> 1.03 us
  between operations: 13.5 us -> 0.17 us
  loops' own time: 9.89 us -> 0 us
    ppermute x6 -> x16, waiting for transfers between devices: 244 us -> 29.2 us  [the longest x1 15 us: per_device(): cross = lax.ppermute(frame_of(keyvals, parity), 'ta', cross_pairs)]
    dot_general x17 -> x0, matrix products: 80.8 us -> none  [the longest x4 41.8 us: attend(): jnp.einsum('qhd,khd->hqk', query_rows, near_keys, preferred_element_type=...]
    while x48 -> x0, local copies, waits for them, and re-layouts: 62.2 us -> none
    pallas_call x0 -> x4, Pallas kernels: none -> 51.9 us  [the longest x2 26.1 us: near_attention(): pl.pallas_call(functools.partial(near_kernel, sides), out_shape=outs + su...]
    slice x10 -> x2, local copies, waits for them, and re-layouts: 46.4 us -> 1.75 us  [halo_rows(): return (top, lax.ppermute(value[:, :, :SPOT], 'ha', down))]
    concatenate x2 -> x0, other arithmetic: 28.4 us -> none  [extended_2(): jnp.concatenate([lax.ppermute(tail, axis, [(i, (i + 1) % count) for i in...]
    reduce_sum x8 -> x0, other arithmetic: 19.4 us -> none  [the longest x4 17.8 us: attend(): jnp.sum(near_exp, axis=-1, keepdims=True)]
    another operation x1 -> x0, loops' own time: 9.89 us -> none  [per_device(): lax.map(attend, jnp.arange(frame_count * tile_count, dtype=jnp.int32))]
  transfers between devices with their start and end apart: 7 -> 16, of which waited for: 6 -> 4; matrix products, arithmetic and copies ran while one was open for 5% -> 4% of each run, Pallas kernels for 0% -> 40%
where the time goes in v2:
time: 121 us; the launch traced here: 120 us
  Pallas kernels  51.9 us (43%)
  waiting for transfers between devices  29.2 us (24%)
  starting transfers between devices  21.9 us (18%)
  local copies, waits for them, and re-layouts  16.3 us (13%)
    pallas_call x2, Pallas kernels, near_attention(): pl.pallas_call(functools.partial(near_kernel, sides), out_shape=outs + su...  26.1 us
    pallas_call x1, Pallas kernels, far_attention(): pl.pallas_call(far_kernel, out_shape=[jax.ShapeDtypeStruct((2, tokens, fe...  22.4 us
    ppermute x1, waiting for transfers between devices, per_device(): cross = lax.ppermute(frame_of(keyvals, parity), 'ta', cross_pairs)  15 us
    ppermute x2, waiting for transfers between devices, halo_rows(): top = lax.ppermute(value[:, :, tokens - SPOT:], 'ha', up)  11.6 us
    unnamed x35, local copies, waits for them, and re-layouts  11.1 us
    ppermute x2, starting transfers between devices, halo_rows(): top = lax.ppermute(value[:, :, tokens - SPOT:], 'ha', up)  7.95 us
    pallas_call x1, Pallas kernels, finish(): pl.pallas_call(functools.partial(finish_kernel, sides), out_shape=jax.Sha...  3.37 us
    dynamic_slice x3, local copies, waits for them, and re-layouts, frame_of(): return lax.dynamic_slice_in_dim(value, index, 1, axis=1)  3.36 us
  transfers between devices with their start and end apart: 16, of which 4 were waited for; matrix products, arithmetic and copies ran while one was open for 4% of the time, Pallas kernels for 40%

profile of v2, /device:TPU:0, one launch (start us, length us, event | category | flops | bytes accessed | tf_op | source)
XLA Modules:
  0.0 120.4 jit_solution(1021566981582467083)
XLA Ops:
  0.0 1.7 %constant_dynamic-slice_fusion.2 = (bf16[2,1,128,2048]{3,2,1,0:T(8,128)(2,1)S(1)}, bf16[2,1,128,2048]{3,2,1,0:T(8,128)(2,1)S(1)}) fusion(bf16[2,2,128,2048]{3,2,1,0:T(8,128)(2,1)} %bitcast.4.own_ref, s32[]{:T(128)S(6)} %select_n.48, s32[]{:T(128)S(6)} %select_n.47), kind=kLoop, calls=%fused_computation.13 | loop fusion | bytes 4194312 | tf_op jit(solution)/shard_map/dynamic_slice | solution.py:225
  1.7 2.4 %collective-permute-start.1 = (bf16[2,1,128,2048]{3,2,1,0:T(8,128)(2,1)S(1)}, bf16[2,1,128,2048]{3,2,1,0:T(8,128)(2,1)S(1)}, u32[]{:S(2)}, u32[]{:S(2)}) collective-permute-start(bf16[2,1,128,2048]{3,2,1,0:T(8,128)(2,1)S(1)} %get-tuple-element.31), channel_id=1, source_target_pairs={{0,24},{8,16},{16,8},{24,0},{1,25},{9,17},{17,9},{25,1},{2,26},{10... | collective-permute-start | bytes 3145736 | tf_op jit(solution)/shard_map/ppermute | solution.py:231
  4.1 1.7 %fusion.1 = (bf16[2,2,64,2048]{3,2,1,0:T(8,128)(2,1)S(1)}, bf16[2,2,64,2048]{3,2,1,0:T(8,128)(2,1)S(1)}) fusion(bf16[2,2,128,2048]{3,2,1,0:T(8,128)(2,1)} %bitcast.4.own_ref), kind=kLoop, calls=%fused_computation.20 | loop fusion | bytes 4194304 | tf_op jit(solution)/shard_map/slice | solution.py:229
  5.8 3.5 %collective-permute-start.5 = (bf16[2,2,64,2048]{3,2,1,0:T(8,128)(2,1)S(1)}, bf16[2,2,64,2048]{3,2,1,0:T(8,128)(2,1)S(1)}, u32[]{:S(2)}, u32[]{:S(2)}) collective-permute-start(bf16[2,2,64,2048]{3,2,1,0:T(8,128)(2,1)S(1)} %get-tuple-element.30), channel_id=1, source_target_pairs={{0,2},{2,4},{4,6},{1,3},{3,5},{5,7},{8,10},{10,12},{12,14},{9,11},... | collective-permute-start | bytes 3145736 | tf_op jit(solution)/shard_map/ppermute | solution.py:228
  9.4 1.3 %collective-permute-start.6 = (bf16[2,2,64,2048]{3,2,1,0:T(8,128)(2,1)S(1)}, bf16[2,2,64,2048]{3,2,1,0:T(8,128)(2,1)S(1)}, u32[]{:S(2)}, u32[]{:S(2)}) collective-permute-start(bf16[2,2,64,2048]{3,2,1,0:T(8,128)(2,1)S(1)} %get-tuple-element.29), channel_id=1, source_target_pairs={{2,0},{4,2},{6,4},{3,1},{5,3},{7,5},{10,8},{12,10},{14,12},{11,9},... | collective-permute-start | bytes 3145736 | tf_op jit(solution)/shard_map/ppermute | solution.py:229
  11.1 1.5 %collective-permute-start.9 = (bf16[2,128,2048]{2,1,0:T(8,128)(2,1)S(1)}, bf16[2,128,2048]{2,1,0:T(8,128)(2,1)S(1)}, u32[]{:S(2)}, u32[]{:S(2)}) collective-permute-start(bf16[2,128,2048]{2,1,0:T(8,128)(2,1)S(1)} %bitcast.10), channel_id=1, source_target_pairs={{0,1},{1,0},{2,3},{3,2},{4,5},{5,4},{6,7},{7,6},{8,9},{9,8},{10,11... | collective-permute-start | bytes 3145736 | tf_op jit(solution)/shard_map/ppermute | solution.py:233
  12.7 15.0 %collective-permute-done.1.ext_ref.cross_ref = bf16[2,1,128,2048]{3,2,1,0:T(8,128)(2,1)S(1)} collective-permute-done((bf16[2,1,128,2048]{3,2,1,0:T(8,128)(2,1)S(1)}, bf16[2,1,128,2048]{3,2,1,0:T(8,128)(2,1)S(1)}, u32[]{:S(2)}, u32[]{:S(2)}) %collective-permute-start.1) | collective-permute-done | bytes 1048608 | tf_op jit(solution)/shard_map/ppermute | solution.py:231
  27.7 2.2 %collective-permute-start.2 = (bf16[2,1,128,2048]{3,2,1,0:T(8,128)(2,1)S(1)}, bf16[2,1,128,2048]{3,2,1,0:T(8,128)(2,1)}, u32[]{:S(2)}, u32[]{:S(2)}) collective-permute-start(bf16[2,1,128,2048]{3,2,1,0:T(8,128)(2,1)S(1)} %get-tuple-element.18), channel_id=1, source_target_pairs={{0,24},{8,16},{16,8},{24,0},{1,25},{9,17},{17,9},{25,1},{2,26},{10... | collective-permute-start | bytes 3145736 | tf_op jit(solution)/shard_map/ppermute | solution.py:240
  30.0 2.6 %collective-permute-done.5.top_ref = bf16[2,2,64,2048]{3,2,1,0:T(8,128)(2,1)S(1)} collective-permute-done((bf16[2,2,64,2048]{3,2,1,0:T(8,128)(2,1)S(1)}, bf16[2,2,64,2048]{3,2,1,0:T(8,128)(2,1)S(1)}, u32[]{:S(2)}, u32[]{:S(2)}) %collective-permute-start.5) | collective-permute-done | bytes 1048608 | tf_op jit(solution)/shard_map/ppermute | solution.py:228
  32.5 4.4 %collective-permute-start.10 = (bf16[2,1,64,2048]{3,2,1,0:T(8,128)(2,1)S(1)}, bf16[2,1,64,2048]{3,2,1,0:T(8,128)(2,1)S(1)}, u32[]{:S(2)}, u32[]{:S(2)}) collective-permute-start(bf16[2,1,64,2048]{3,2,1,0:T(8,128)(2,1)S(1)} %get-tuple-element.34), channel_id=1, source_target_pairs={{0,2},{2,4},{4,6},{1,3},{3,5},{5,7},{8,10},{10,12},{12,14},{9,11},... | collective-permute-start | bytes 1572872 | tf_op jit(solution)/shard_map/ppermute | solution.py:228
  37.0 1.3 %collective-permute-start.11 = (bf16[2,1,64,2048]{3,2,1,0:T(8,128)(2,1)S(1)}, bf16[2,1,64,2048]{3,2,1,0:T(8,128)(2,1)S(1)}, u32[]{:S(2)}, u32[]{:S(2)}) collective-permute-start(bf16[2,1,64,2048]{3,2,1,0:T(8,128)(2,1)S(1)} %get-tuple-element.33), channel_id=1, source_target_pairs={{2,0},{4,2},{6,4},{3,1},{5,3},{7,5},{10,8},{12,10},{14,12},{11,9},... | collective-permute-start | bytes 1572872 | tf_op jit(solution)/shard_map/ppermute | solution.py:229
  39.2 9.0 %collective-permute-done.10.ext_top_ref = bf16[2,1,64,2048]{3,2,1,0:T(8,128)(2,1)S(1)} collective-permute-done((bf16[2,1,64,2048]{3,2,1,0:T(8,128)(2,1)S(1)}, bf16[2,1,64,2048]{3,2,1,0:T(8,128)(2,1)S(1)}, u32[]{:S(2)}, u32[]{:S(2)}) %collective-permute-start.10) | collective-permute-done | bytes 524320 | tf_op jit(solution)/shard_map/ppermute | solution.py:228
  49.8 2.5 %collective-permute-done.11.ext_bottom_ref = bf16[2,1,64,2048]{3,2,1,0:T(8,128)(2,1)S(1)} collective-permute-done((bf16[2,1,64,2048]{3,2,1,0:T(8,128)(2,1)S(1)}, bf16[2,1,64,2048]{3,2,1,0:T(8,128)(2,1)S(1)}, u32[]{:S(2)}, u32[]{:S(2)}) %collective-permute-start.11) | collective-permute-done | bytes 524320 | tf_op jit(solution)/shard_map/ppermute | solution.py:229
  53.9 1.2 %copy-done.3 = bf16[2,2,64,2048]{3,2,1,0:T(8,128)(2,1)S(1)} copy-done((bf16[2,2,64,2048]{3,2,1,0:T(8,128)(2,1)S(1)}, bf16[2,2,64,2048]{3,2,1,0:T(8,128)(2,1)}, u32[]{:S(2)}) %copy-start.3) | copy-done | bytes 1048600
  55.1 1.0 copy-done.13
  56.1 1.0 copy-done.15
  57.2 12.9 %shard_map.38 = (bf16[128,2048]{1,0:T(8,128)(2,1)}, f32[128,2048]{1,0:T(8,128)S(1)}, f32[128,128]{1,0:T(8,128)S(1)}, f32[128,128]{1,0:T(8,128)S(1)}) custom-call(s32[4]{0:T(128)S(1)} %add_add_fusion.1.meta_ref, bf16[2,2,128,2048]{3,2,1,0:T(8,128)(2,1)} %bitcast.4.own_ref, bf16[2,1,128,2048]{3,2,1,0:T(8,128)(2,1)S(1)} %collective-permute-done.1.ext_ref.cross_ref, ...), custom_call_target="tpu_custom_call" | custom-call | flops 1207959552 | bytes 8388608 | tf_op jit(solution)/shard_map/pallas_call | solution.py:89
  70.1 1.1 copy-done.8
  72.0 1.8 %collective-permute-start.13 = (bf16[128,2048]{1,0:T(8,128)(2,1)}, bf16[128,2048]{1,0:T(8,128)(2,1)}, u32[]{:S(2)}, u32[]{:S(2)}) collective-permute-start(bf16[128,2048]{1,0:T(8,128)(2,1)} %get-tuple-element.26), channel_id=1, source_target_pairs={{0,1},{1,0},{2,3},{3,2},{4,5},{5,4},{6,7},{7,6},{8,9},{9,8},{10,11... | collective-permute-start | bytes 1572872 | tf_op jit(solution)/shard_map/ppermute | solution.py:262
  74.9 13.2 %shard_map.37 = (bf16[128,2048]{1,0:T(8,128)(2,1)}, f32[128,2048]{1,0:T(8,128)S(1)}, f32[128,128]{1,0:T(8,128)S(1)}, f32[128,128]{1,0:T(8,128)S(1)}) custom-call(s32[4]{0:T(128)S(1)} %add_add_fusion.meta_ref, bf16[2,2,128,2048]{3,2,1,0:T(8,128)(2,1)} %bitcast.4.own_ref, bf16[2,2,128,2048]{3,2,1,0:T(8,128)(2,1)} %collective-permute-done.ext_ref.core_ref, ...), custom_call_target="tpu_custom_call" | custom-call | flops 1207959552 | bytes 8388608 | tf_op jit(solution)/shard_map/pallas_call | solution.py:89
  90.8 1.8 %collective-permute-start.15 = (f32[128,128]{1,0:T(8,128)S(1)}, f32[128,128]{1,0:T(8,128)S(1)}, u32[]{:S(2)}, u32[]{:S(2)}) collective-permute-start(f32[128,128]{1,0:T(8,128)S(1)} %get-tuple-element.28), channel_id=1, source_target_pairs={{0,1},{1,0},{2,3},{3,2},{4,5},{5,4},{6,7},{7,6},{8,9},{9,8},{10,11... | collective-permute-start | bytes 196616 | tf_op jit(solution)/shard_map/ppermute | solution.py:263
  93.0 22.4 %shard_map.39 = (f32[2,128,2048]{2,1,0:T(8,128)}, f32[2,128,128]{2,1,0:T(8,128)S(1)}) custom-call(s32[2]{0:T(128)S(1)} %pad_add_fusion.1.meta_ref, s32[8]{0:T(128)S(1)} %compare_select_fusion.3.code_ref, bf16[2,128,2048]{2,1,0:T(8,128)(2,1)S(1)} %bitcast.11, bf16[2,2,128,2048]{3,2,1,0:T(8,128)(2,1)} %collective-permute-done.ext_ref.core_ref, ...), custom_call_target="tpu_custom_call" | custom-call | flops 268435456 | bytes 8388608 | tf_op jit(solution)/shard_map/pallas_call | solution.py:155
  115.5 1.6 %copy-done.7 = f32[2,128,2048]{2,1,0:T(8,128)S(1)} copy-done((f32[2,128,2048]{2,1,0:T(8,128)S(1)}, f32[2,128,2048]{2,1,0:T(8,128)}, u32[]{:S(2)}) %copy-start.7) | copy-done | bytes 2097176
  117.0 3.4 %shard_map.40 = bf16[2,128,2048]{2,1,0:T(8,128)(2,1)} custom-call(s32[3]{0:T(128)S(1)} %pad_add_fusion.meta_ref, f32[2,128,2048]{2,1,0:T(8,128)S(1)} %copy-done.7, f32[2,128,128]{2,1,0:T(8,128)S(1)} %get-tuple-element.24.own_sum_ref, bf16[128,2048]{1,0:T(8,128)(2,1)S(1)} %collective-permute-done.12.refs_0_, ...), custom_call_target="tpu_custom_call" | custom-call | flops 4194304 | bytes 5242880 | tf_op jit(solution)/shard_map/pallas_call | solution.py:193
  (59 shorter events, 9.6 us)
Async XLA Ops:
  1.7 9.5 %copy-start = (bf16[2,16,8,2048]{3,2,1,0:T(8,128)(2,1)S(1)}, bf16[2,16,8,2048]{3,2,1,0:T(8,128)(2,1)}, u32[]{:S(2)}) copy-start(bf16[2,16,8,2048]{3,2,1,0:T(8,128)(2,1)} %param.3) | copy-start | bytes 3145732
  1.7 26.0 %collective-permute-start.1 = (bf16[2,1,128,2048]{3,2,1,0:T(8,128)(2,1)S(1)}, bf16[2,1,128,2048]{3,2,1,0:T(8,128)(2,1)S(1)}, u32[]{:S(2)}, u32[]{:S(2)}) collective-permute-start(bf16[2,1,128,2048]{3,2,1,0:T(8,128)(2,1)S(1)} %get-tuple-element.31), channel_id=1, source_target_pairs={{0,24},{8,16},{16,8},{24,0},{1,25},{9,17},{17,9},{25,1},{2,26},{10... | collective-permute-start | bytes 3145736 | tf_op jit(solution)/shard_map/ppermute | solution.py:231
  5.8 26.7 %collective-permute-start.5 = (bf16[2,2,64,2048]{3,2,1,0:T(8,128)(2,1)S(1)}, bf16[2,2,64,2048]{3,2,1,0:T(8,128)(2,1)S(1)}, u32[]{:S(2)}, u32[]{:S(2)}) collective-permute-start(bf16[2,2,64,2048]{3,2,1,0:T(8,128)(2,1)S(1)} %get-tuple-element.30), channel_id=1, source_target_pairs={{0,2},{2,4},{4,6},{1,3},{3,5},{5,7},{8,10},{10,12},{12,14},{9,11},... | collective-permute-start | bytes 3145736 | tf_op jit(solution)/shard_map/ppermute | solution.py:228
  9.4 27.6 %collective-permute-start.6 = (bf16[2,2,64,2048]{3,2,1,0:T(8,128)(2,1)S(1)}, bf16[2,2,64,2048]{3,2,1,0:T(8,128)(2,1)S(1)}, u32[]{:S(2)}, u32[]{:S(2)}) collective-permute-start(bf16[2,2,64,2048]{3,2,1,0:T(8,128)(2,1)S(1)} %get-tuple-element.29), channel_id=1, source_target_pairs={{2,0},{4,2},{6,4},{3,1},{5,3},{7,5},{10,8},{12,10},{14,12},{11,9},... | collective-permute-start | bytes 3145736 | tf_op jit(solution)/shard_map/ppermute | solution.py:229
  10.7 63.2 %collective-permute-start = (bf16[2,2,128,2048]{3,2,1,0:T(8,128)(2,1)}, bf16[2,2,128,2048]{3,2,1,0:T(8,128)(2,1)}, u32[]{:S(2)}, u32[]{:S(2)}) collective-permute-start(bf16[2,2,128,2048]{3,2,1,0:T(8,128)(2,1)} %bitcast.4.own_ref), channel_id=1, source_target_pairs={{0,8},{8,0},{16,24},{24,16},{1,9},{9,1},{17,25},{25,17},{2,10},{10... | collective-permute-start | bytes 6291464 | tf_op jit(solution)/shard_map/ppermute | solution.py:234
  11.1 28.0 %collective-permute-start.9 = (bf16[2,128,2048]{2,1,0:T(8,128)(2,1)S(1)}, bf16[2,128,2048]{2,1,0:T(8,128)(2,1)S(1)}, u32[]{:S(2)}, u32[]{:S(2)}) collective-permute-start(bf16[2,128,2048]{2,1,0:T(8,128)(2,1)S(1)} %bitcast.10), channel_id=1, source_target_pairs={{0,1},{1,0},{2,3},{3,2},{4,5},{5,4},{6,7},{7,6},{8,9},{9,8},{10,11... | collective-permute-start | bytes 3145736 | tf_op jit(solution)/shard_map/ppermute | solution.py:233
  27.7 25.5 %collective-permute-start.2 = (bf16[2,1,128,2048]{3,2,1,0:T(8,128)(2,1)S(1)}, bf16[2,1,128,2048]{3,2,1,0:T(8,128)(2,1)}, u32[]{:S(2)}, u32[]{:S(2)}) collective-permute-start(bf16[2,1,128,2048]{3,2,1,0:T(8,128)(2,1)S(1)} %get-tuple-element.18), channel_id=1, source_target_pairs={{0,24},{8,16},{16,8},{24,0},{1,25},{9,17},{17,9},{25,1},{2,26},{10... | collective-permute-start | bytes 3145736 | tf_op jit(solution)/shard_map/ppermute | solution.py:240
  32.5 15.6 %collective-permute-start.10 = (bf16[2,1,64,2048]{3,2,1,0:T(8,128)(2,1)S(1)}, bf16[2,1,64,2048]{3,2,1,0:T(8,128)(2,1)S(1)}, u32[]{:S(2)}, u32[]{:S(2)}) collective-permute-start(bf16[2,1,64,2048]{3,2,1,0:T(8,128)(2,1)S(1)} %get-tuple-element.34), channel_id=1, source_target_pairs={{0,2},{2,4},{4,6},{1,3},{3,5},{5,7},{8,10},{10,12},{12,14},{9,11},... | collective-permute-start | bytes 1572872 | tf_op jit(solution)/shard_map/ppermute | solution.py:228
  37.0 12.0 %copy-start.2 = (bf16[2,2,64,2048]{3,2,1,0:T(8,128)(2,1)}, bf16[2,2,64,2048]{3,2,1,0:T(8,128)(2,1)S(1)}, u32[]{:S(2)}) copy-start(bf16[2,2,64,2048]{3,2,1,0:T(8,128)(2,1)S(1)} %collective-permute-done.6.bottom_ref) | copy-start | bytes 3145732
  37.0 15.4 %collective-permute-start.11 = (bf16[2,1,64,2048]{3,2,1,0:T(8,128)(2,1)S(1)}, bf16[2,1,64,2048]{3,2,1,0:T(8,128)(2,1)S(1)}, u32[]{:S(2)}, u32[]{:S(2)}) collective-permute-start(bf16[2,1,64,2048]{3,2,1,0:T(8,128)(2,1)S(1)} %get-tuple-element.33), channel_id=1, source_target_pairs={{2,0},{4,2},{6,4},{3,1},{5,3},{7,5},{10,8},{12,10},{14,12},{11,9},... | collective-permute-start | bytes 1572872 | tf_op jit(solution)/shard_map/ppermute | solution.py:229
  39.2 10.7 %copy-start.5 = (bf16[2,128,2048]{2,1,0:T(8,128)(2,1)}, bf16[2,128,2048]{2,1,0:T(8,128)(2,1)S(1)}, u32[]{:S(2)}) copy-start(bf16[2,128,2048]{2,1,0:T(8,128)(2,1)S(1)} %collective-permute-done.9.refs_0_) | copy-start | bytes 3145732
  39.2 32.0 %collective-permute-start.7 = (bf16[2,1,64,2048]{3,2,1,0:T(8,128)(2,1)}, bf16[2,1,64,2048]{3,2,1,0:T(8,128)(2,1)S(1)}, u32[]{:S(2)}, u32[]{:S(2)}) collective-permute-start(bf16[2,1,64,2048]{3,2,1,0:T(8,128)(2,1)} %constant_dynamic-slice_fusion.1), channel_id=1, source_target_pairs={{0,8},{8,0},{16,24},{24,16},{1,9},{9,1},{17,25},{25,17},{2,10},{10... | collective-permute-start | bytes 1572872 | tf_op jit(solution)/shard_map/ppermute | solution.py:236
  49.0 43.6 %collective-permute-start.3 = (bf16[2,1,128,2048]{3,2,1,0:T(8,128)(2,1)S(1)}, bf16[2,1,128,2048]{3,2,1,0:T(8,128)(2,1)}, u32[]{:S(2)}, u32[]{:S(2)}) collective-permute-start(bf16[2,1,128,2048]{3,2,1,0:T(8,128)(2,1)S(1)} %collective-permute-done.1.ext_ref.cross_ref), channel_id=1, source_target_pairs={{0,8},{8,0},{16,24},{24,16},{1,9},{9,1},{17,25},{25,17},{2,10},{10... | collective-permute-start | bytes 3145736 | tf_op jit(solution)/shard_map/ppermute | solution.py:241
  53.2 20.6 %collective-permute-start.8 = (bf16[2,1,64,2048]{3,2,1,0:T(8,128)(2,1)}, bf16[2,1,64,2048]{3,2,1,0:T(8,128)(2,1)}, u32[]{:S(2)}, u32[]{:S(2)}) collective-permute-start(bf16[2,1,64,2048]{3,2,1,0:T(8,128)(2,1)} %constant_dynamic-slice_fusion), channel_id=1, source_target_pairs={{0,8},{8,0},{16,24},{24,16},{1,9},{9,1},{17,25},{25,17},{2,10},{10... | collective-permute-start | bytes 1572872 | tf_op jit(solution)/shard_map/ppermute | solution.py:237
  53.2 39.8 %collective-permute-start.4 = (bf16[2,1,128,2048]{3,2,1,0:T(8,128)(2,1)}, bf16[2,1,128,2048]{3,2,1,0:T(8,128)(2,1)}, u32[]{:S(2)}, u32[]{:S(2)}) collective-permute-start(bf16[2,1,128,2048]{3,2,1,0:T(8,128)(2,1)} %collective-permute-done.2.last_ref), channel_id=1, source_target_pairs={{0,8},{8,0},{16,24},{24,16},{1,9},{9,1},{17,25},{25,17},{2,10},{10... | collective-permute-start | bytes 3145736 | tf_op jit(solution)/shard_map/ppermute | solution.py:242
  57.2 16.7 %copy-start.4 = (bf16[2,2,64,2048]{3,2,1,0:T(8,128)(2,1)S(1)}, bf16[2,2,64,2048]{3,2,1,0:T(8,128)(2,1)}, u32[]{:S(2)}) copy-start(bf16[2,2,64,2048]{3,2,1,0:T(8,128)(2,1)} %copy-done.2) | copy-start | bytes 3145732
  57.2 16.7 %copy-start.6 = (bf16[2,128,2048]{2,1,0:T(8,128)(2,1)S(1)}, bf16[2,128,2048]{2,1,0:T(8,128)(2,1)}, u32[]{:S(2)}) copy-start(bf16[2,128,2048]{2,1,0:T(8,128)(2,1)} %copy-done.5) | copy-start | bytes 3145732
  72.0 21.0 %copy-start.1 = (bf16[2,16,8,2048]{3,2,1,0:T(8,128)(2,1)S(1)}, bf16[2,16,8,2048]{3,2,1,0:T(8,128)(2,1)}, u32[]{:S(2)}) copy-start(bf16[2,16,8,2048]{3,2,1,0:T(8,128)(2,1)} %param.3) | copy-start | bytes 3145732
  72.0 43.4 %collective-permute-start.13 = (bf16[128,2048]{1,0:T(8,128)(2,1)}, bf16[128,2048]{1,0:T(8,128)(2,1)}, u32[]{:S(2)}, u32[]{:S(2)}) collective-permute-start(bf16[128,2048]{1,0:T(8,128)(2,1)} %get-tuple-element.26), channel_id=1, source_target_pairs={{0,1},{1,0},{2,3},{3,2},{4,5},{5,4},{6,7},{7,6},{8,9},{9,8},{10,11... | collective-permute-start | bytes 1572872 | tf_op jit(solution)/shard_map/ppermute | solution.py:262
  74.9 15.1 %copy-start.16 = (s32[2,2,1,2]{3,2,1,0:T(1,128)S(1)}, s32[2,2,1,2]{3,2,1,0:T(1,128)}, u32[]{:S(2)}) copy-start(s32[2,2,1,2]{3,2,1,0:T(1,128)} %param.5) | copy-start | bytes 100
  89.1 26.4 %collective-permute-start.12 = (bf16[128,2048]{1,0:T(8,128)(2,1)}, bf16[128,2048]{1,0:T(8,128)(2,1)S(1)}, u32[]{:S(2)}, u32[]{:S(2)}) collective-permute-start(bf16[128,2048]{1,0:T(8,128)(2,1)} %get-tuple-element.25), channel_id=1, source_target_pairs={{0,1},{1,0},{2,3},{3,2},{4,5},{5,4},{6,7},{7,6},{8,9},{9,8},{10,11... | collective-permute-start | bytes 1572872 | tf_op jit(solution)/shard_map/ppermute | solution.py:262
  90.8 24.6 %collective-permute-start.15 = (f32[128,128]{1,0:T(8,128)S(1)}, f32[128,128]{1,0:T(8,128)S(1)}, u32[]{:S(2)}, u32[]{:S(2)}) collective-permute-start(f32[128,128]{1,0:T(8,128)S(1)} %get-tuple-element.28), channel_id=1, source_target_pairs={{0,1},{1,0},{2,3},{3,2},{4,5},{5,4},{6,7},{7,6},{8,9},{9,8},{10,11... | collective-permute-start | bytes 196616 | tf_op jit(solution)/shard_map/ppermute | solution.py:263
  92.7 22.8 %collective-permute-start.14 = (f32[128,128]{1,0:T(8,128)S(1)}, f32[128,128]{1,0:T(8,128)S(1)}, u32[]{:S(2)}, u32[]{:S(2)}) collective-permute-start(f32[128,128]{1,0:T(8,128)S(1)} %get-tuple-element.27), channel_id=1, source_target_pairs={{0,1},{1,0},{2,3},{3,2},{4,5},{5,4},{6,7},{7,6},{8,9},{9,8},{10,11... | collective-permute-start | bytes 196616 | tf_op jit(solution)/shard_map/ppermute | solution.py:263
  115.5 1.6 %copy-start.7 = (f32[2,128,2048]{2,1,0:T(8,128)S(1)}, f32[2,128,2048]{2,1,0:T(8,128)}, u32[]{:S(2)}) copy-start(f32[2,128,2048]{2,1,0:T(8,128)} %get-tuple-element.23.own_ref) | copy-start | bytes 6291460
  (9 other events, 8.9 us)

commit v3 on v2

--- a/solution.py
+++ b/solution.py
@@ -14,7 +14,8 @@
 SPOT = TILE * TILE
 NEGATIVE = -1e30
 EXP_SCALE = HD ** (-0.5) * 1.4426950408889634
-VMEM_LIMIT = 48 * 1024 * 1024
+VMEM_LIMIT = 20 * 1024 * 1024
+GROUP = 4
 
 
 def contract_last(left, right):
@@ -47,36 +48,56 @@
         ref, ext = ((top_ref, ext_top_ref), (bottom_ref, ext_bottom_ref))[a]
         return jnp.concatenate([ref[kind, 0, :, lanes], ref[kind, 1, :, lanes], ext[kind, 0, :, lanes]], axis=0)
 
-    def step(h, carry):
-        lanes = head_lanes(h)
-        queries = [
-            jnp.concatenate([ref[frame, a * SPOT : (a + 1) * SPOT, lanes] for ref in q_refs], axis=0) for a in range(2)
-        ]
-        middle_scores = contract_last(jnp.concatenate(queries, axis=0), middle(0, lanes))
-        middle_values = with_ones(middle(1, lanes))
-        for a in range(2):
-            near = middle_scores[a * half : (a + 1) * half]
-            edge = contract_last(queries[a], halo(a, 0, lanes))
-            edge_peak = jnp.where(valid[a], jnp.max(edge, axis=-1, keepdims=True), NEGATIVE)
-            peak = jnp.maximum(jnp.max(near, axis=-1, keepdims=True), edge_peak)
-            near_weights = jnp.exp2((near - peak) * EXP_SCALE).astype(jnp.bfloat16)
-            edge_weights = jnp.exp2((edge - jnp.where(valid[a], peak, -NEGATIVE)) * EXP_SCALE).astype(jnp.bfloat16)
-            summed = jnp.dot(near_weights, middle_values, preferred_element_type=jnp.float32)
-            summed = summed + jnp.dot(
-                edge_weights, with_ones(halo(a, 1, lanes)), preferred_element_type=jnp.float32
-            )
-            total = summed[:, HD:]
-            result = summed[:, :HD] / total
-            log_sum = peak * EXP_SCALE + jnp.log2(total)
-            for s in range(sides):
-                tokens, rows = slice(a * SPOT, (a + 1) * SPOT), slice(s * SPOT, (s + 1) * SPOT)
-                out_refs[s][tokens, lanes] = result[rows].astype(out_refs[s].dtype)
-                sum_refs[s][tokens, :] = jnp.where(lane_index(SPOT) == h, log_sum[rows], sum_refs[s][tokens, :])
-        return carry
-
-    for ref in sum_refs:
-        ref[...] = jnp.zeros_like(ref)
-    lax.fori_loop(0, HEADS, step, 0)
+    def step(group, carry):
+        members = [head_lanes(group * GROUP + i) for i in range(GROUP)]
+        scores = []
+        for lanes in members:
+            queries = [
+                jnp.concatenate([ref[frame, a * SPOT : (a + 1) * SPOT, lanes] for ref in q_refs], axis=0)
+                for a in range(2)
+            ]
+            near = contract_last(jnp.concatenate(queries, axis=0), middle(0, lanes))
+            edges = [contract_last(queries[a], halo(a, 0, lanes)) for a in range(2)]
+            scores.append([(near[a * half : (a + 1) * half], edges[a]) for a in range(2)])
+        weights = []
+        for pairs in scores:
+            for a, (near, edge) in enumerate(pairs):
+                best = functools.reduce(jnp.maximum, [near[:, i * HD : (i + 1) * HD] for i in range(3)])
+                edge_best = jnp.maximum(edge[:, : 2 * SPOT], jnp.concatenate([edge[:, 2 * SPOT :]] * 2, axis=1))
+                best = jnp.maximum(best, jnp.where(valid[a], edge_best, NEGATIVE))
+                peak = jnp.max(best, axis=-1, keepdims=True)
+                shift = jnp.where(valid[a], peak, -NEGATIVE)
+                weights.append(
+                    (
+                        peak,
+                        jnp.exp2((near - peak) * EXP_SCALE).astype(jnp.bfloat16),
+                        jnp.exp2((edge - shift) * EXP_SCALE).astype(jnp.bfloat16),
+                    )
+                )
+        peaks, totals = [carry_value for carry_value in carry[0]], [carry_value for carry_value in carry[1]]
+        for i, lanes in enumerate(members):
+            mask = lane_index(half) == group * GROUP + i
+            middle_values = with_ones(middle(1, lanes))
+            for a in range(2):
+                peak, near, edge = weights[2 * i + a]
+                summed = jnp.dot(near, middle_values, preferred_element_type=jnp.float32)
+                summed = summed + jnp.dot(edge, with_ones(halo(a, 1, lanes)), preferred_element_type=jnp.float32)
+                total = summed[:, HD:]
+                result = summed[:, :HD] / total
+                peaks[a] = jnp.where(mask, peak, peaks[a])
+                totals[a] = jnp.where(mask, total, totals[a])
+                for s in range(sides):
+                    rows = slice(s * SPOT, (s + 1) * SPOT)
+                    out_refs[s][a * SPOT : (a + 1) * SPOT, lanes] = result[rows].astype(out_refs[s].dtype)
+        return tuple(peaks), tuple(totals)
+
+    zeros = tuple(jnp.zeros((half, HD), jnp.float32) for _ in range(2))
+    ones = tuple(jnp.ones((half, HD), jnp.float32) for _ in range(2))
+    peaks, totals = lax.fori_loop(0, HEADS // GROUP, step, (zeros, ones))
+    for a in range(2):
+        log_sum = peaks[a] * EXP_SCALE + jnp.log2(totals[a])
+        for s in range(sides):
+            sum_refs[s][a * SPOT : (a + 1) * SPOT, :] = log_sum[s * SPOT : (s + 1) * SPOT]
 
 
 def near_attention(meta, own, ext, top, bottom, ext_top, ext_bottom, queries, out_dtypes):
@@ -119,32 +140,37 @@
     for_copies(lambda copy: copy.start())
     for_copies(lambda copy: copy.wait())
 
-    def step(h, carry):
-        lanes = head_lanes(h)
-        for early in range(2):
-            frame = meta_ref[early]
-            for a in range(2):
-                tokens = slice(a * SPOT, (a + 1) * SPOT)
-                scores = contract_last(q_ref[frame, tokens, lanes], held[0, frame * 2 + a, :, lanes])
-                peak = jnp.max(scores, axis=-1, keepdims=True)
-                weights = jnp.exp2((scores - peak) * EXP_SCALE).astype(jnp.bfloat16)
-                values = with_ones(held[1, frame * 2 + a, :, lanes])
-                summed = jnp.dot(weights, values, preferred_element_type=jnp.float32)
-                mask = lane_index(SPOT) == h
-                near_sum = jnp.max(
-                    jnp.where(mask, near_sums[early][tokens, :], NEGATIVE), axis=-1, keepdims=True
-                )
-                far_peak = peak * EXP_SCALE
-                top = jnp.maximum(near_sum, far_peak)
-                near_scale, far_scale = jnp.exp2(near_sum - top), jnp.exp2(far_peak - top)
-                total = near_scale + far_scale * summed[:, HD:]
-                joined = near_scale * near_refs[early][tokens, lanes] + far_scale * summed[:, :HD]
-                out_ref[early, tokens, lanes] = joined / total
-                sum_ref[early, tokens, :] = jnp.where(mask, top + jnp.log2(total), sum_ref[early, tokens, :])
-        return carry
-
-    sum_ref[...] = jnp.zeros_like(sum_ref)
-    lax.fori_loop(0, HEADS, step, 0)
+    units = [(early, a) for early in range(2) for a in range(2)]
+    collected = [jnp.zeros((SPOT, HD), jnp.float32) for _ in units]
+    for first in range(0, HEADS, GROUP):
+        work = [(h, u) for h in range(first, first + GROUP) for u in range(len(units))]
+        scores = []
+        for h, u in work:
+            early, a = units[u]
+            frame, lanes = meta_ref[early], slice(h * HD, (h + 1) * HD)
+            queries = q_ref[frame, a * SPOT : (a + 1) * SPOT, lanes]
+            scores.append(contract_last(queries, held[0, frame * 2 + a, :, lanes]))
+        peaks = [jnp.max(value, axis=-1, keepdims=True) for value in scores]
+        weights = [
+            jnp.exp2((value - peak) * EXP_SCALE).astype(jnp.bfloat16) for value, peak in zip(scores, peaks)
+        ]
+        for (h, u), weight, peak in zip(work, weights, peaks):
+            early, a = units[u]
+            frame, lanes = meta_ref[early], slice(h * HD, (h + 1) * HD)
+            tokens = slice(a * SPOT, (a + 1) * SPOT)
+            summed = jnp.dot(
+                weight, with_ones(held[1, frame * 2 + a, :, lanes]), preferred_element_type=jnp.float32
+            )
+            near_sum = near_sums[early][tokens, h : h + 1]
+            far_peak = peak * EXP_SCALE
+            top = jnp.maximum(near_sum, far_peak)
+            near_scale, far_scale = jnp.exp2(near_sum - top), jnp.exp2(far_peak - top)
+            total = near_scale + far_scale * summed[:, HD:]
+            joined = near_scale * near_refs[early][tokens, lanes] + far_scale * summed[:, :HD]
+            out_ref[early, tokens, lanes] = joined / total
+            collected[u] = jnp.where(lane_index(SPOT) == h, top + jnp.log2(total), collected[u])
+    for (early, a), value in zip(units, collected):
+        sum_ref[early, a * SPOT : (a + 1) * SPOT, :] = value
 
 
 def far_attention(meta, code, queries, buffers, near):
@@ -252,8 +278,10 @@
         as_meta(1 - parity, parity, has_top, has_bottom),
         keyvals, core, top, bottom, core_top, core_bottom, q_sides, dtypes,
     )
+    late_meta, early_first = lax.optimization_barrier((as_meta(parity, 0, has_top, has_bottom), early[0]))
+    early = [early_first] + list(early[1:])
     late = near_attention(
-        as_meta(parity, 0, has_top, has_bottom),
+        late_meta,
         keyvals, cross, top, bottom, cross_top, cross_bottom, q_sides, dtypes,
     )
     sides = len(ways) + 1

time: 121 us -> 109 us (0.901)
  Pallas kernels: 51.9 us -> 24.8 us
  waiting for transfers between devices: 29.2 us -> 42.3 us
  local copies, waits for them, and re-layouts: 16.3 us -> 18.8 us
    pallas_call x1, Pallas kernels: 22.4 us -> 6.31 us  [far_attention(): pl.pallas_call(far_kernel, out_shape=[jax.ShapeDtypeStruct((2, tokens, fe...]
    ppermute x2, waiting for transfers between devices: 0.01 us -> 14 us  [send_back(): lax.ppermute(near[sides + s], 'wa', back)]
    pallas_call x2, Pallas kernels: 26.1 us -> 15.5 us  [near_attention(): pl.pallas_call(functools.partial(near_kernel, sides), out_shape=outs + su...]
    ppermute x2, waiting for transfers between devices: 11.6 us -> 1.05 us  [halo_rows(): top = lax.ppermute(value[:, :, tokens - SPOT:], 'ha', up)]
    ppermute x1, waiting for transfers between devices: 0.01 us -> 6.58 us  [per_device(): last = lax.ppermute(last_frame, 'ta', cross_pairs)]
    unnamed x35 -> x39, local copies, waits for them, and re-layouts: 11.1 us -> 14.4 us
    ppermute x2, waiting for transfers between devices: 2.51 us -> 4.09 us  [halo_rows(): return (top, lax.ppermute(value[:, :, :SPOT], 'ha', down))]
    ppermute x1, waiting for transfers between devices: 15 us -> 16.6 us  [per_device(): cross = lax.ppermute(frame_of(keyvals, parity), 'ta', cross_pairs)]
  transfers between devices with their start and end apart: 16 -> 16, of which waited for: 4 -> 6; matrix products, arithmetic and copies ran while one was open for 4% -> 4% of each run, Pallas kernels for 40% -> 20%
where the time goes in v3:
time: 109 us
  waiting for transfers between devices  42.3 us (39%)
  Pallas kernels  24.8 us (23%)
  starting transfers between devices  22 us (20%)
  local copies, waits for them, and re-layouts  18.8 us (17%)
    ppermute x1, waiting for transfers between devices, per_device(): cross = lax.ppermute(frame_of(keyvals, parity), 'ta', cross_pairs)  16.6 us
    pallas_call x2, Pallas kernels, near_attention(): pl.pallas_call(functools.partial(near_kernel, sides), out_shape=outs + su...  15.5 us
    unnamed x39, local copies, waits for them, and re-layouts  14.4 us
    ppermute x2, waiting for transfers between devices, send_back(): lax.ppermute(near[sides + s], 'wa', back)  14 us
    ppermute x2, starting transfers between devices, halo_rows(): top = lax.ppermute(value[:, :, tokens - SPOT:], 'ha', up)  7.75 us
    ppermute x1, waiting for transfers between devices, per_device(): last = lax.ppermute(last_frame, 'ta', cross_pairs)  6.58 us
    pallas_call x1, Pallas kernels, far_attention(): pl.pallas_call(far_kernel, out_shape=[jax.ShapeDtypeStruct((2, tokens, fe...  6.31 us
    ppermute x2, waiting for transfers between devices, halo_rows(): return (top, lax.ppermute(value[:, :, :SPOT], 'ha', down))  4.09 us
  transfers between devices with their start and end apart: 16, of which 6 were waited for; matrix products, arithmetic and copies ran while one was open for 4% of the time, Pallas kernels for 20%

profile of v3, /device:TPU:0, one launch (start us, length us, event | category | flops | bytes accessed | tf_op | source)
XLA Modules:
  0.0 108.9 jit_solution(3756133239046894183)
XLA Ops:
  0.0 1.8 %constant_dynamic-slice_fusion.2 = (bf16[2,1,128,2048]{3,2,1,0:T(8,128)(2,1)S(1)}, bf16[2,1,128,2048]{3,2,1,0:T(8,128)(2,1)S(1)}) fusion(bf16[2,2,128,2048]{3,2,1,0:T(8,128)(2,1)} %bitcast.8, s32[]{:T(128)S(6)} %select_n.48, s32[]{:T(128)S(6)} %select_n.47), kind=kLoop, calls=%fused_computation.13 | loop fusion | bytes 4194312 | tf_op jit(solution)/shard_map/dynamic_slice | solution.py:251
  1.8 2.4 %collective-permute-start.1 = (bf16[2,1,128,2048]{3,2,1,0:T(8,128)(2,1)S(1)}, bf16[2,1,128,2048]{3,2,1,0:T(8,128)(2,1)}, u32[]{:S(2)}, u32[]{:S(2)}) collective-permute-start(bf16[2,1,128,2048]{3,2,1,0:T(8,128)(2,1)S(1)} %get-tuple-element.35), channel_id=1, source_target_pairs={{0,24},{8,16},{16,8},{24,0},{1,25},{9,17},{17,9},{25,1},{2,26},{10... | collective-permute-start | bytes 3145736 | tf_op jit(solution)/shard_map/ppermute | solution.py:257
  4.4 3.5 %collective-permute-start.5 = (bf16[2,2,64,2048]{3,2,1,0:T(8,128)(2,1)S(1)}, bf16[2,2,64,2048]{3,2,1,0:T(8,128)(2,1)S(1)}, u32[]{:S(2)}, u32[]{:S(2)}) collective-permute-start(bf16[2,2,64,2048]{3,2,1,0:T(8,128)(2,1)S(1)} %get-tuple-element.34), channel_id=1, source_target_pairs={{0,2},{2,4},{4,6},{1,3},{3,5},{5,7},{8,10},{10,12},{12,14},{9,11},... | collective-permute-start | bytes 3145736 | tf_op jit(solution)/shard_map/ppermute | solution.py:254
  8.0 1.3 %collective-permute-start.6 = (bf16[2,2,64,2048]{3,2,1,0:T(8,128)(2,1)S(1)}, bf16[2,2,64,2048]{3,2,1,0:T(8,128)(2,1)S(1)}, u32[]{:S(2)}, u32[]{:S(2)}) collective-permute-start(bf16[2,2,64,2048]{3,2,1,0:T(8,128)(2,1)S(1)} %get-tuple-element.33), channel_id=1, source_target_pairs={{2,0},{4,2},{6,4},{3,1},{5,3},{7,5},{10,8},{12,10},{14,12},{11,9},... | collective-permute-start | bytes 3145736 | tf_op jit(solution)/shard_map/ppermute | solution.py:255
  9.8 1.5 %collective-permute-start.9 = (bf16[2,128,2048]{2,1,0:T(8,128)(2,1)S(1)}, bf16[2,128,2048]{2,1,0:T(8,128)(2,1)S(1)}, u32[]{:S(2)}, u32[]{:S(2)}) collective-permute-start(bf16[2,128,2048]{2,1,0:T(8,128)(2,1)S(1)} %bitcast.13), channel_id=1, source_target_pairs={{0,1},{1,0},{2,3},{3,2},{4,5},{5,4},{6,7},{7,6},{8,9},{9,8},{10,11... | collective-permute-start | bytes 3145736 | tf_op jit(solution)/shard_map/ppermute | solution.py:259
  11.3 16.6 %collective-permute-done.1.ext_ref.cross_ref = bf16[2,1,128,2048]{3,2,1,0:T(8,128)(2,1)} collective-permute-done((bf16[2,1,128,2048]{3,2,1,0:T(8,128)(2,1)S(1)}, bf16[2,1,128,2048]{3,2,1,0:T(8,128)(2,1)}, u32[]{:S(2)}, u32[]{:S(2)}) %collective-permute-start.1) | collective-permute-done | bytes 1048608 | tf_op jit(solution)/shard_map/ppermute | solution.py:257
  27.8 2.3 %collective-permute-start.2 = (bf16[2,1,128,2048]{3,2,1,0:T(8,128)(2,1)S(1)}, bf16[2,1,128,2048]{3,2,1,0:T(8,128)(2,1)}, u32[]{:S(2)}, u32[]{:S(2)}) collective-permute-start(bf16[2,1,128,2048]{3,2,1,0:T(8,128)(2,1)S(1)} %get-tuple-element.20), channel_id=1, source_target_pairs={{0,24},{8,16},{16,8},{24,0},{1,25},{9,17},{17,9},{25,1},{2,26},{10... | collective-permute-start | bytes 3145736 | tf_op jit(solution)/shard_map/ppermute | solution.py:266
  31.3 4.1 %collective-permute-done.6.bottom_ref = bf16[2,2,64,2048]{3,2,1,0:T(8,128)(2,1)S(1)} collective-permute-done((bf16[2,2,64,2048]{3,2,1,0:T(8,128)(2,1)S(1)}, bf16[2,2,64,2048]{3,2,1,0:T(8,128)(2,1)S(1)}, u32[]{:S(2)}, u32[]{:S(2)}) %collective-permute-start.6) | collective-permute-done | bytes 1048608 | tf_op jit(solution)/shard_map/ppermute | solution.py:255
  37.4 2.3 %fusion.2 = (bf16[2,1,64,2048]{3,2,1,0:T(8,128)(2,1)}, bf16[2,1,64,2048]{3,2,1,0:T(8,128)(2,1)}) fusion(bf16[2,1,128,2048]{3,2,1,0:T(8,128)(2,1)} %collective-permute-done.1.ext_ref.cross_ref), kind=kLoop, calls=%fused_computation.21 | loop fusion | bytes 2097152 | tf_op jit(solution)/shard_map/slice | solution.py:255
  40.6 4.2 %collective-permute-start.10 = (bf16[2,1,64,2048]{3,2,1,0:T(8,128)(2,1)}, bf16[2,1,64,2048]{3,2,1,0:T(8,128)(2,1)}, u32[]{:S(2)}, u32[]{:S(2)}) collective-permute-start(bf16[2,1,64,2048]{3,2,1,0:T(8,128)(2,1)} %get-tuple-element.38), channel_id=1, source_target_pairs={{0,2},{2,4},{4,6},{1,3},{3,5},{5,7},{8,10},{10,12},{12,14},{9,11},... | collective-permute-start | bytes 1572872 | tf_op jit(solution)/shard_map/ppermute | solution.py:254
  45.6 1.3 %collective-permute-start.11 = (bf16[2,1,64,2048]{3,2,1,0:T(8,128)(2,1)}, bf16[2,1,64,2048]{3,2,1,0:T(8,128)(2,1)}, u32[]{:S(2)}, u32[]{:S(2)}) collective-permute-start(bf16[2,1,64,2048]{3,2,1,0:T(8,128)(2,1)} %get-tuple-element.37), channel_id=1, source_target_pairs={{2,0},{4,2},{6,4},{3,1},{5,3},{7,5},{10,8},{12,10},{14,12},{11,9},... | collective-permute-start | bytes 1572872 | tf_op jit(solution)/shard_map/ppermute | solution.py:255
  46.8 6.6 %collective-permute-done.2.last_ref = bf16[2,1,128,2048]{3,2,1,0:T(8,128)(2,1)} collective-permute-done((bf16[2,1,128,2048]{3,2,1,0:T(8,128)(2,1)S(1)}, bf16[2,1,128,2048]{3,2,1,0:T(8,128)(2,1)}, u32[]{:S(2)}, u32[]{:S(2)}) %collective-permute-start.2) | collective-permute-done | bytes 1048608 | tf_op jit(solution)/shard_map/ppermute | solution.py:266
  54.1 1.2 %copy-done.3 = bf16[2,2,64,2048]{3,2,1,0:T(8,128)(2,1)S(1)} copy-done((bf16[2,2,64,2048]{3,2,1,0:T(8,128)(2,1)S(1)}, bf16[2,2,64,2048]{3,2,1,0:T(8,128)(2,1)}, u32[]{:S(2)}) %copy-start.3) | copy-done | bytes 1048600
  55.4 1.2 %copy-done.6 = bf16[2,2,64,2048]{3,2,1,0:T(8,128)(2,1)S(1)} copy-done((bf16[2,2,64,2048]{3,2,1,0:T(8,128)(2,1)S(1)}, bf16[2,2,64,2048]{3,2,1,0:T(8,128)(2,1)}, u32[]{:S(2)}) %copy-start.6) | copy-done | bytes 1048600
  56.6 1.2 %copy-done.8 = bf16[2,128,2048]{2,1,0:T(8,128)(2,1)S(1)} copy-done((bf16[2,128,2048]{2,1,0:T(8,128)(2,1)S(1)}, bf16[2,128,2048]{2,1,0:T(8,128)(2,1)}, u32[]{:S(2)}) %copy-start.8) | copy-done | bytes 1048600
  59.9 7.9 %shard_map.37 = (bf16[128,2048]{1,0:T(8,128)(2,1)}, f32[128,2048]{1,0:T(8,128)S(1)}, f32[128,128]{1,0:T(8,128)S(1)}, f32[128,128]{1,0:T(8,128)S(1)}) custom-call(s32[4]{0:T(128)S(1)} %get-tuple-element.39.meta_ref, bf16[2,2,128,2048]{3,2,1,0:T(8,128)(2,1)S(1)} %bitcast.11, bf16[2,2,128,2048]{3,2,1,0:T(8,128)(2,1)} %collective-permute-done.ext_ref.core_ref, ...), custom_call_target="tpu_custom_call" | custom-call | flops 1207959552 | bytes 8388608 | tf_op jit(solution)/shard_map/pallas_call | solution.py:110
  68.9 7.6 %shard_map.38 = (bf16[128,2048]{1,0:T(8,128)(2,1)}, f32[128,2048]{1,0:T(8,128)S(1)}, f32[128,128]{1,0:T(8,128)S(1)}, f32[128,128]{1,0:T(8,128)S(1)}) custom-call(s32[4]{0:T(128)S(1)} %get-tuple-element.23.meta_ref, bf16[2,2,128,2048]{3,2,1,0:T(8,128)(2,1)S(1)} %bitcast.12, bf16[2,1,128,2048]{3,2,1,0:T(8,128)(2,1)} %collective-permute-done.1.ext_ref.cross_ref, ...), custom_call_target="tpu_custom_call" | custom-call | flops 1207959552 | bytes 8388608 | tf_op jit(solution)/shard_map/pallas_call | solution.py:110
  77.5 2.0 %collective-permute-start.13 = (bf16[128,2048]{1,0:T(8,128)(2,1)}, bf16[128,2048]{1,0:T(8,128)(2,1)S(1)}, u32[]{:S(2)}, u32[]{:S(2)}) collective-permute-start(bf16[128,2048]{1,0:T(8,128)(2,1)} %get-tuple-element.30), channel_id=1, source_target_pairs={{0,1},{1,0},{2,3},{3,2},{4,5},{5,4},{6,7},{7,6},{8,9},{9,8},{10,11... | collective-permute-start | bytes 1572872 | tf_op jit(solution)/shard_map/ppermute | solution.py:290
  81.0 2.1 %collective-permute-start.15 = (f32[128,128]{1,0:T(8,128)S(1)}, f32[128,128]{1,0:T(8,128)S(1)}, u32[]{:S(2)}, u32[]{:S(2)}) collective-permute-start(f32[128,128]{1,0:T(8,128)S(1)} %get-tuple-element.32), channel_id=1, source_target_pairs={{0,1},{1,0},{2,3},{3,2},{4,5},{5,4},{6,7},{7,6},{8,9},{9,8},{10,11... | collective-permute-start | bytes 196616 | tf_op jit(solution)/shard_map/ppermute | solution.py:291
  83.3 1.2 %copy-done.11 = f32[128,2048]{1,0:T(8,128)S(1)} copy-done((f32[128,2048]{1,0:T(8,128)S(1)}, f32[128,2048]{1,0:T(8,128)}, u32[]{:S(2)}) %copy-start.11) | copy-done | bytes 1048600
  84.5 1.2 %copy-done.13 = f32[128,2048]{1,0:T(8,128)S(1)} copy-done((f32[128,2048]{1,0:T(8,128)S(1)}, f32[128,2048]{1,0:T(8,128)}, u32[]{:S(2)}) %copy-start.13) | copy-done | bytes 1048600
  85.7 6.3 %shard_map.39 = (f32[2,128,2048]{2,1,0:T(8,128)S(1)}, f32[2,128,128]{2,1,0:T(8,128)S(1)}) custom-call(s32[2]{0:T(128)S(1)} %pad_add_fusion.1.meta_ref, s32[8]{0:T(128)S(1)} %compare_select_fusion.3.code_ref, bf16[2,128,2048]{2,1,0:T(8,128)(2,1)S(1)} %bitcast.16, bf16[2,2,128,2048]{3,2,1,0:T(8,128)(2,1)} %collective-permute-done.ext_ref.core_ref, ...), custom_call_target="tpu_custom_call" | custom-call | flops 268435456 | bytes 8388608 | tf_op jit(solution)/shard_map/pallas_call | solution.py:181
  92.0 13.1 %collective-permute-done.15.refs_3_ = f32[128,128]{1,0:T(8,128)S(1)} collective-permute-done((f32[128,128]{1,0:T(8,128)S(1)}, f32[128,128]{1,0:T(8,128)S(1)}, u32[]{:S(2)}, u32[]{:S(2)}) %collective-permute-start.15) | collective-permute-done | bytes 65568 | tf_op jit(solution)/shard_map/ppermute | solution.py:291
  106.0 2.9 %shard_map.40 = bf16[2,128,2048]{2,1,0:T(8,128)(2,1)} custom-call(s32[3]{0:T(128)S(1)} %pad_add_fusion.meta_ref, f32[2,128,2048]{2,1,0:T(8,128)S(1)} %get-tuple-element.27.own_ref, f32[2,128,128]{2,1,0:T(8,128)S(1)} %get-tuple-element.28.own_sum_ref, bf16[128,2048]{1,0:T(8,128)(2,1)S(1)} %collective-permute-done.12.refs_0_, ...), custom_call_target="tpu_custom_call" | custom-call | flops 4194304 | bytes 5242880 | tf_op jit(solution)/shard_map/pallas_call | solution.py:219
  (62 shorter events, 12.8 us)
Async XLA Ops:
  0.0 4.3 %copy-start = (bf16[2,2,16,8,2048]{4,3,2,1,0:T(8,128)(2,1)S(1)}, bf16[2,2,16,8,2048]{4,3,2,1,0:T(8,128)(2,1)}, u32[]{:S(2)}) copy-start(bf16[2,2,16,8,2048]{4,3,2,1,0:T(8,128)(2,1)} %param.4) | copy-start | bytes 6291460
  1.8 7.9 %copy-start.1 = (bf16[2,16,8,2048]{3,2,1,0:T(8,128)(2,1)S(1)}, bf16[2,16,8,2048]{3,2,1,0:T(8,128)(2,1)}, u32[]{:S(2)}) copy-start(bf16[2,16,8,2048]{3,2,1,0:T(8,128)(2,1)} %param.3) | copy-start | bytes 3145732
  1.8 26.0 %collective-permute-start.1 = (bf16[2,1,128,2048]{3,2,1,0:T(8,128)(2,1)S(1)}, bf16[2,1,128,2048]{3,2,1,0:T(8,128)(2,1)}, u32[]{:S(2)}, u32[]{:S(2)}) collective-permute-start(bf16[2,1,128,2048]{3,2,1,0:T(8,128)(2,1)S(1)} %get-tuple-element.35), channel_id=1, source_target_pairs={{0,24},{8,16},{16,8},{24,0},{1,25},{9,17},{17,9},{25,1},{2,26},{10... | collective-permute-start | bytes 3145736 | tf_op jit(solution)/shard_map/ppermute | solution.py:257
  4.4 26.7 %collective-permute-start.5 = (bf16[2,2,64,2048]{3,2,1,0:T(8,128)(2,1)S(1)}, bf16[2,2,64,2048]{3,2,1,0:T(8,128)(2,1)S(1)}, u32[]{:S(2)}, u32[]{:S(2)}) collective-permute-start(bf16[2,2,64,2048]{3,2,1,0:T(8,128)(2,1)S(1)} %get-tuple-element.34), channel_id=1, source_target_pairs={{0,2},{2,4},{4,6},{1,3},{3,5},{5,7},{8,10},{10,12},{12,14},{9,11},... | collective-permute-start | bytes 3145736 | tf_op jit(solution)/shard_map/ppermute | solution.py:254
  8.0 27.4 %collective-permute-start.6 = (bf16[2,2,64,2048]{3,2,1,0:T(8,128)(2,1)S(1)}, bf16[2,2,64,2048]{3,2,1,0:T(8,128)(2,1)S(1)}, u32[]{:S(2)}, u32[]{:S(2)}) collective-permute-start(bf16[2,2,64,2048]{3,2,1,0:T(8,128)(2,1)S(1)} %get-tuple-element.33), channel_id=1, source_target_pairs={{2,0},{4,2},{6,4},{3,1},{5,3},{7,5},{10,8},{12,10},{14,12},{11,9},... | collective-permute-start | bytes 3145736 | tf_op jit(solution)/shard_map/ppermute | solution.py:255
  9.3 44.8 %collective-permute-start = (bf16[2,2,128,2048]{3,2,1,0:T(8,128)(2,1)S(1)}, bf16[2,2,128,2048]{3,2,1,0:T(8,128)(2,1)}, u32[]{:S(2)}, u32[]{:S(2)}) collective-permute-start(bf16[2,2,128,2048]{3,2,1,0:T(8,128)(2,1)S(1)} %bitcast.10), channel_id=1, source_target_pairs={{0,8},{8,0},{16,24},{24,16},{1,9},{9,1},{17,25},{25,17},{2,10},{10... | collective-permute-start | bytes 6291464 | tf_op jit(solution)/shard_map/ppermute | solution.py:260
  9.8 25.8 %collective-permute-start.9 = (bf16[2,128,2048]{2,1,0:T(8,128)(2,1)S(1)}, bf16[2,128,2048]{2,1,0:T(8,128)(2,1)S(1)}, u32[]{:S(2)}, u32[]{:S(2)}) collective-permute-start(bf16[2,128,2048]{2,1,0:T(8,128)(2,1)S(1)} %bitcast.13), channel_id=1, source_target_pairs={{0,1},{1,0},{2,3},{3,2},{4,5},{5,4},{6,7},{7,6},{8,9},{9,8},{10,11... | collective-permute-start | bytes 3145736 | tf_op jit(solution)/shard_map/ppermute | solution.py:259
  27.8 25.6 %collective-permute-start.2 = (bf16[2,1,128,2048]{3,2,1,0:T(8,128)(2,1)S(1)}, bf16[2,1,128,2048]{3,2,1,0:T(8,128)(2,1)}, u32[]{:S(2)}, u32[]{:S(2)}) collective-permute-start(bf16[2,1,128,2048]{3,2,1,0:T(8,128)(2,1)S(1)} %get-tuple-element.20), channel_id=1, source_target_pairs={{0,24},{8,16},{16,8},{24,0},{1,25},{9,17},{17,9},{25,1},{2,26},{10... | collective-permute-start | bytes 3145736 | tf_op jit(solution)/shard_map/ppermute | solution.py:266
  31.2 4.4 %copy-start.2 = (bf16[2,2,64,2048]{3,2,1,0:T(8,128)(2,1)}, bf16[2,2,64,2048]{3,2,1,0:T(8,128)(2,1)S(1)}, u32[]{:S(2)}) copy-start(bf16[2,2,64,2048]{3,2,1,0:T(8,128)(2,1)S(1)} %collective-permute-done.5.top_ref) | copy-start | bytes 3145732
  31.2 8.5 %collective-permute-start.7 = (bf16[2,1,64,2048]{3,2,1,0:T(8,128)(2,1)S(1)}, bf16[2,1,64,2048]{3,2,1,0:T(8,128)(2,1)S(1)}, u32[]{:S(2)}, u32[]{:S(2)}) collective-permute-start(bf16[2,1,64,2048]{3,2,1,0:T(8,128)(2,1)S(1)} %constant_dynamic-slice_fusion.1), channel_id=1, source_target_pairs={{0,8},{8,0},{16,24},{24,16},{1,9},{9,1},{17,25},{25,17},{2,10},{10... | collective-permute-start | bytes 1572872 | tf_op jit(solution)/shard_map/ppermute | solution.py:262
  35.4 9.4 %collective-permute-start.8 = (bf16[2,1,64,2048]{3,2,1,0:T(8,128)(2,1)S(1)}, bf16[2,1,64,2048]{3,2,1,0:T(8,128)(2,1)S(1)}, u32[]{:S(2)}, u32[]{:S(2)}) collective-permute-start(bf16[2,1,64,2048]{3,2,1,0:T(8,128)(2,1)S(1)} %constant_dynamic-slice_fusion), channel_id=1, source_target_pairs={{0,8},{8,0},{16,24},{24,16},{1,9},{9,1},{17,25},{25,17},{2,10},{10... | collective-permute-start | bytes 1572872 | tf_op jit(solution)/shard_map/ppermute | solution.py:263
  37.4 45.7 %collective-permute-start.3 = (bf16[2,1,128,2048]{3,2,1,0:T(8,128)(2,1)}, bf16[2,1,128,2048]{3,2,1,0:T(8,128)(2,1)}, u32[]{:S(2)}, u32[]{:S(2)}) collective-permute-start(bf16[2,1,128,2048]{3,2,1,0:T(8,128)(2,1)} %collective-permute-done.1.ext_ref.cross_ref), channel_id=1, source_target_pairs={{0,8},{8,0},{16,24},{24,16},{1,9},{9,1},{17,25},{25,17},{2,10},{10... | collective-permute-start | bytes 3145736 | tf_op jit(solution)/shard_map/ppermute | solution.py:267
  40.6 28.3 %collective-permute-start.10 = (bf16[2,1,64,2048]{3,2,1,0:T(8,128)(2,1)}, bf16[2,1,64,2048]{3,2,1,0:T(8,128)(2,1)}, u32[]{:S(2)}, u32[]{:S(2)}) collective-permute-start(bf16[2,1,64,2048]{3,2,1,0:T(8,128)(2,1)} %get-tuple-element.38), channel_id=1, source_target_pairs={{0,2},{2,4},{4,6},{1,3},{3,5},{5,7},{8,10},{10,12},{12,14},{9,11},... | collective-permute-start | bytes 1572872 | tf_op jit(solution)/shard_map/ppermute | solution.py:254
  45.6 23.3 %collective-permute-start.11 = (bf16[2,1,64,2048]{3,2,1,0:T(8,128)(2,1)}, bf16[2,1,64,2048]{3,2,1,0:T(8,128)(2,1)}, u32[]{:S(2)}, u32[]{:S(2)}) collective-permute-start(bf16[2,1,64,2048]{3,2,1,0:T(8,128)(2,1)} %get-tuple-element.37), channel_id=1, source_target_pairs={{2,0},{4,2},{6,4},{3,1},{5,3},{7,5},{10,8},{12,10},{14,12},{11,9},... | collective-permute-start | bytes 1572872 | tf_op jit(solution)/shard_map/ppermute | solution.py:255
  53.4 29.8 %collective-permute-start.4 = (bf16[2,1,128,2048]{3,2,1,0:T(8,128)(2,1)}, bf16[2,1,128,2048]{3,2,1,0:T(8,128)(2,1)}, u32[]{:S(2)}, u32[]{:S(2)}) collective-permute-start(bf16[2,1,128,2048]{3,2,1,0:T(8,128)(2,1)} %collective-permute-done.2.last_ref), channel_id=1, source_target_pairs={{0,8},{8,0},{16,24},{24,16},{1,9},{9,1},{17,25},{25,17},{2,10},{10... | collective-permute-start | bytes 3145736 | tf_op jit(solution)/shard_map/ppermute | solution.py:268
  54.1 1.2 %copy-start.3 = (bf16[2,2,64,2048]{3,2,1,0:T(8,128)(2,1)S(1)}, bf16[2,2,64,2048]{3,2,1,0:T(8,128)(2,1)}, u32[]{:S(2)}) copy-start(bf16[2,2,64,2048]{3,2,1,0:T(8,128)(2,1)} %copy-done.2) | copy-start | bytes 3145732
  59.9 9.0 %copy-start.4 = (bf16[2,2,64,2048]{3,2,1,0:T(8,128)(2,1)S(1)}, bf16[2,2,64,2048]{3,2,1,0:T(8,128)(2,1)}, u32[]{:S(2)}) copy-start(bf16[2,2,64,2048]{3,2,1,0:T(8,128)(2,1)} %copy-done.2) | copy-start | bytes 3145732
  59.9 9.0 %copy-start.9 = (bf16[2,128,2048]{2,1,0:T(8,128)(2,1)S(1)}, bf16[2,128,2048]{2,1,0:T(8,128)(2,1)}, u32[]{:S(2)}) copy-start(bf16[2,128,2048]{2,1,0:T(8,128)(2,1)} %copy-done.7) | copy-start | bytes 3145732
  68.9 11.3 %copy-start.18 = (s32[2,2,1,2]{3,2,1,0:T(1,128)S(1)}, s32[2,2,1,2]{3,2,1,0:T(1,128)}, u32[]{:S(2)}) copy-start(s32[2,2,1,2]{3,2,1,0:T(1,128)} %param.5) | copy-start | bytes 100
  77.5 28.5 %collective-permute-start.13 = (bf16[128,2048]{1,0:T(8,128)(2,1)}, bf16[128,2048]{1,0:T(8,128)(2,1)S(1)}, u32[]{:S(2)}, u32[]{:S(2)}) collective-permute-start(bf16[128,2048]{1,0:T(8,128)(2,1)} %get-tuple-element.30), channel_id=1, source_target_pairs={{0,1},{1,0},{2,3},{3,2},{4,5},{5,4},{6,7},{7,6},{8,9},{9,8},{10,11... | collective-permute-start | bytes 1572872 | tf_op jit(solution)/shard_map/ppermute | solution.py:290
  79.5 26.5 %collective-permute-start.12 = (bf16[128,2048]{1,0:T(8,128)(2,1)}, bf16[128,2048]{1,0:T(8,128)(2,1)S(1)}, u32[]{:S(2)}, u32[]{:S(2)}) collective-permute-start(bf16[128,2048]{1,0:T(8,128)(2,1)} %get-tuple-element.29), channel_id=1, source_target_pairs={{0,1},{1,0},{2,3},{3,2},{4,5},{5,4},{6,7},{7,6},{8,9},{9,8},{10,11... | collective-permute-start | bytes 1572872 | tf_op jit(solution)/shard_map/ppermute | solution.py:290
  81.0 24.1 %collective-permute-start.15 = (f32[128,128]{1,0:T(8,128)S(1)}, f32[128,128]{1,0:T(8,128)S(1)}, u32[]{:S(2)}, u32[]{:S(2)}) collective-permute-start(f32[128,128]{1,0:T(8,128)S(1)} %get-tuple-element.32), channel_id=1, source_target_pairs={{0,1},{1,0},{2,3},{3,2},{4,5},{5,4},{6,7},{7,6},{8,9},{9,8},{10,11... | collective-permute-start | bytes 196616 | tf_op jit(solution)/shard_map/ppermute | solution.py:291
  83.1 22.9 %collective-permute-start.14 = (f32[128,128]{1,0:T(8,128)S(1)}, f32[128,128]{1,0:T(8,128)S(1)}, u32[]{:S(2)}, u32[]{:S(2)}) collective-permute-start(f32[128,128]{1,0:T(8,128)S(1)} %get-tuple-element.31), channel_id=1, source_target_pairs={{0,1},{1,0},{2,3},{3,2},{4,5},{5,4},{6,7},{7,6},{8,9},{9,8},{10,11... | collective-permute-start | bytes 196616 | tf_op jit(solution)/shard_map/ppermute | solution.py:291
  83.3 1.2 %copy-start.11 = (f32[128,2048]{1,0:T(8,128)S(1)}, f32[128,2048]{1,0:T(8,128)}, u32[]{:S(2)}) copy-start(f32[128,2048]{1,0:T(8,128)} %copy-done.10) | copy-start | bytes 3145732
  (11 other events, 11.5 us)

commit v4 on v3

v4 whole, which is shorter than its diff:
```python
import functools

import jax
import jax.numpy as jnp
from jax import lax
from jax.experimental import pallas as pl
from jax.experimental.pallas import tpu as pltpu
from jax.sharding import PartitionSpec as P

TILE = 8
HEADS = 16
HD = 128
NFAR = 2
SPOT = TILE * TILE
NEGATIVE = -1e30
EXP_SCALE = HD ** (-0.5) * 1.4426950408889634
VMEM_LIMIT = 24 * 1024 * 1024
GROUP = 4
FINISH_COST = 4 << 30
LATE_COST = 16 << 30


def contract_last(left, right):
    return lax.dot_general(left, right, (((1,), (1,)), ((), ())), preferred_element_type=jnp.float32)


def with_ones(values):
    return jnp.concatenate([values, jnp.ones_like(values)], axis=1)


def lane_index(rows):
    return lax.broadcasted_iota(jnp.int32, (rows, HD), 1)


def split_sums(value):
    high = value.astype(jnp.bfloat16).astype(jnp.float32)
    rest = value - high
    middle = rest.astype(jnp.bfloat16).astype(jnp.float32)
    low = rest - middle
    return (high + pltpu.roll(middle, HEADS, 1) + pltpu.roll(low, 2 * HEADS, 1)).astype(jnp.bfloat16)


def join_sums(value):
    terms = value.astype(jnp.float32)
    return terms + (pltpu.roll(terms, HD - HEADS, 1) + pltpu.roll(terms, HD - 2 * HEADS, 1))


def near_kernel(sides, meta_ref, own_ref, ext_ref, top_ref, bottom_ref, *refs):
    ext_halos, refs = (refs[:2], refs[2:4]), refs[4:]
    q_refs, out_refs, own_sum_ref, log_ref = refs[:sides], refs[sides : 2 * sides], refs[2 * sides], refs[2 * sides + 1]
    group = pl.program_id(0)
    valid = (meta_ref[2] > 0, meta_ref[3] > 0)
    half = sides * SPOT

    def middle(kind, lanes):
        parts = [own_ref[kind, 0, :, lanes], own_ref[kind, 1, :, lanes], ext_ref[kind, 0, :, lanes]]
        return jnp.concatenate(parts, axis=0)

    def halo(a, kind, lanes):
        ref, ext = (top_ref, bottom_ref)[a], ext_halos[a][kind]
        return jnp.concatenate([ref[kind, 0, :, lanes], ref[kind, 1, :, lanes], ext[0, 0, :, lanes]], axis=0)

    members = [slice(i * HD, (i + 1) * HD) for i in range(GROUP)]
    scores = []
    for lanes in members:
        queries = [
            jnp.concatenate([ref[0, a * SPOT : (a + 1) * SPOT, lanes] for ref in q_refs], axis=0) for a in range(2)
        ]
        near = contract_last(jnp.concatenate(queries, axis=0), middle(0, lanes))
        edges = [contract_last(queries[a], halo(a, 0, lanes)) for a in range(2)]
        scores.append([(near[a * half : (a + 1) * half], edges[a]) for a in range(2)])
    weights = []
    for pairs in scores:
        for a, (near, edge) in enumerate(pairs):
            best = functools.reduce(jnp.maximum, [near[:, i * HD : (i + 1) * HD] for i in range(3)])
            edge_best = jnp.maximum(edge[:, : 2 * SPOT], jnp.concatenate([edge[:, 2 * SPOT :]] * 2, axis=1))
            best = jnp.maximum(best, jnp.where(valid[a], edge_best, NEGATIVE))
            peak = jnp.max(best, axis=-1, keepdims=True)
            shift = jnp.where(valid[a], peak, -NEGATIVE)
            weights.append(
                (
                    peak,
                    jnp.exp2((near - peak) * EXP_SCALE).astype(jnp.bfloat16),
                    jnp.exp2((edge - shift) * EXP_SCALE).astype(jnp.bfloat16),
                )
            )
    peaks = [jnp.zeros((half, HD), jnp.float32) for _ in range(2)]
    totals = [jnp.ones((half, HD), jnp.float32) for _ in range(2)]
    for i, lanes in enumerate(members):
        mask = lane_index(half) == group * GROUP + i
        middle_values = with_ones(middle(1, lanes))
        for a in range(2):
            peak, near, edge = weights[2 * i + a]
            summed = jnp.dot(near, middle_values, preferred_element_type=jnp.float32)
            summed = summed + jnp.dot(edge, with_ones(halo(a, 1, lanes)), preferred_element_type=jnp.float32)
            total = summed[:, HD:]
            result = summed[:, :HD] / total
            peaks[a] = jnp.where(mask, peak, peaks[a])
            totals[a] = jnp.where(mask, total, totals[a])
            for s in range(sides):
                rows = slice(s * SPOT, (s + 1) * SPOT)
                at = pl.ds(pl.multiple_of((group * GROUP + i) * HD, HD), HD)
                out_refs[s][a * SPOT : (a + 1) * SPOT, at] = result[rows].astype(out_refs[s].dtype)

    @pl.when(group == 0)
    def _():
        log_ref[...] = jnp.zeros_like(log_ref)

    for a in range(2):
        log_sum = peaks[a] * EXP_SCALE + jnp.log2(totals[a])
        for s in range(sides):
            log_ref[s, a * SPOT : (a + 1) * SPOT, :] += log_sum[s * SPOT : (s + 1) * SPOT]

    @pl.when(group == pl.num_programs(0) - 1)
    def _():
        own_sum_ref[...] = log_ref[sides - 1]
        for s in range(sides - 1):
            out_refs[s][:, HEADS * HD :] = split_sums(log_ref[s])


def near_attention(meta, own, ext, top, bottom, ext_halos, queries, cost):
    sides = len(queries)
    tokens, features = queries[0].shape[1:]
    width = GROUP * HD
    outs = [jax.ShapeDtypeStruct((tokens, features + HD), jnp.bfloat16) for _ in queries[1:]]
    outs += [jax.ShapeDtypeStruct((tokens, features), jnp.float32), jax.ShapeDtypeStruct((tokens, HD), jnp.float32)]

    def block(value, count, at):
        return pl.BlockSpec((2, count, value.shape[2], width), lambda g, meta: (0, at(meta), 0, g))

    def first(meta):
        return 0

    in_specs = [block(own, 2, first), block(ext, 1, lambda meta: meta[1])]
    in_specs += [block(top, 2, first), block(bottom, 2, first)]
    for _, lead in ext_halos:
        in_specs.append(pl.BlockSpec((1, 1, SPOT, width), lambda g, meta, lead=lead: (lead, 0, 0, g)))
    in_specs += [pl.BlockSpec((1, tokens, width), lambda g, meta: (meta[0], 0, g)) for _ in queries]
    out_specs = [pl.BlockSpec(out.shape, lambda g, meta: (0, 0)) for out in outs]
    return pl.pallas_call(
        functools.partial(near_kernel, sides),
        out_shape=outs,
        grid_spec=pltpu.PrefetchScalarGridSpec(
            num_scalar_prefetch=1,
            grid=(HEADS // GROUP,),
            in_specs=in_specs,
            out_specs=out_specs,
            scratch_shapes=[pltpu.VMEM((sides, tokens, HD), jnp.float32)],
        ),
        compiler_params=pltpu.CompilerParams(vmem_limit_bytes=VMEM_LIMIT),
        cost_estimate=pl.CostEstimate(flops=cost, bytes_accessed=1, transcendentals=0),
    )(meta, own, ext, top, bottom, *[value for value, _ in ext_halos], *queries)


def far_kernel(meta_ref, code_ref, q_ref, core_ref, cross_ref, last_ref, corner_ref, corner_last_ref, *refs):
    near_refs, near_sums, out_ref, sum_ref, held, sems = refs[:2], refs[2:4], refs[4], refs[5], refs[6], refs[7]
    sources = [(core_ref, 0), (core_ref, 1), (cross_ref, 0), (last_ref, 0), (corner_ref, 0), (corner_last_ref, 0)]

    def for_copies(first, action):
        lanes = pl.ds(first * HD, GROUP * HD)
        for f in range(2):
            for a in range(2):
                for j in range(NFAR):
                    slot = (f * 2 + a) * NFAR + j
                    for code, (ref, at) in enumerate(sources):

                        @pl.when(code_ref[slot] == code)
                        def _(ref=ref, at=at, f=f, a=a, j=j, slot=slot):
                            copy = pltpu.make_async_copy(
                                ref.at[:, at, pl.ds(a * SPOT, SPOT), lanes],
                                held.at[:, f * 2 + a, pl.ds(j * SPOT, SPOT), lanes],
                                sems.at[slot, first // GROUP],
                            )
                            action(copy)

    for first in range(0, HEADS, GROUP):
        for_copies(first, lambda copy: copy.start())

    units = [(early, a) for early in range(2) for a in range(2)]
    collected = [jnp.zeros((SPOT, HD), jnp.float32) for _ in units]
    for first in range(0, HEADS, GROUP):
        for_copies(first, lambda copy: copy.wait())
        work = [(h, u) for h in range(first, first + GROUP) for u in range(len(units))]
        scores = []
        for h, u in work:
            early, a = units[u]
            frame, lanes = meta_ref[early], slice(h * HD, (h + 1) * HD)
            queries = q_ref[frame, a * SPOT : (a + 1) * SPOT, lanes]
            scores.append(contract_last(queries, held[0, frame * 2 + a, :, lanes]))
        peaks = [jnp.max(value, axis=-1, keepdims=True) for value in scores]
        weights = [
            jnp.exp2((value - peak) * EXP_SCALE).astype(jnp.bfloat16) for value, peak in zip(scores, peaks)
        ]
        for (h, u), weight, peak in zip(work, weights, peaks):
            early, a = units[u]
            frame, lanes = meta_ref[early], slice(h * HD, (h + 1) * HD)
            tokens = slice(a * SPOT, (a + 1) * SPOT)
            summed = jnp.dot(
                weight, with_ones(held[1, frame * 2 + a, :, lanes]), preferred_element_type=jnp.float32
            )
            near_sum = near_sums[early][tokens, h : h + 1]
            far_peak = peak * EXP_SCALE
            top = jnp.maximum(near_sum, far_peak)
            near_scale, far_scale = jnp.exp2(near_sum - top), jnp.exp2(far_peak - top)
            total = near_scale + far_scale * summed[:, HD:]
            joined = near_scale * near_refs[early][tokens, lanes] + far_scale * summed[:, :HD]
            out_ref[early, tokens, lanes] = joined / total
            collected[u] = jnp.where(lane_index(SPOT) == h, top + jnp.log2(total), collected[u])
    for (early, a), value in zip(units, collected):
        sum_ref[early, a * SPOT : (a + 1) * SPOT, :] = value


def far_attention(meta, code, queries, buffers, near):
    tokens, features = queries.shape[1:]
    in_vmem = pl.BlockSpec(memory_space=pltpu.VMEM)
    in_smem = pl.BlockSpec(memory_space=pltpu.SMEM)
    scores = HEADS * 2 * tokens * NFAR * SPOT
    return pl.pallas_call(
        far_kernel,
        out_shape=[
            jax.ShapeDtypeStruct((2, tokens, features), jnp.float32),
            jax.ShapeDtypeStruct((2, tokens, HD), jnp.float32),
        ],
        in_specs=[in_smem, in_smem, in_vmem] + [pl.BlockSpec(memory_space=pl.ANY)] * 5 + [in_vmem] * 4,
        out_specs=[in_vmem] * 2,
        scratch_shapes=[
            pltpu.VMEM((2, 4, NFAR * SPOT, features), jnp.bfloat16),
            pltpu.SemaphoreType.DMA((4 * NFAR, HEADS // GROUP)),
        ],
        compiler_params=pltpu.CompilerParams(vmem_limit_bytes=VMEM_LIMIT),
        cost_estimate=pl.CostEstimate(flops=1, bytes_accessed=1, transcendentals=0),
    )(meta, code, queries, *buffers, *near)


def finish_kernel(sides, aliased, meta_ref, own_ref, own_sum_ref, *refs):
    parts, out_ref = refs[:sides], refs[sides + aliased]
    logs = [own_sum_ref[0]]
    for s in range(sides):
        logs.append(jnp.where(meta_ref[1 + s] > 0, join_sums(parts[s][:, HEADS * HD :]), NEGATIVE))
    top = functools.reduce(jnp.maximum, logs)
    scales = [jnp.exp2(value - top) for value in logs]
    total = functools.reduce(jnp.add, scales)
    scales = [value / total for value in scales]
    for h in range(HEADS):
        lanes = slice(h * HD, (h + 1) * HD)
        joined = scales[0][:, h : h + 1] * own_ref[0, :, lanes]
        for s in range(sides):
            joined = joined + scales[1 + s][:, h : h + 1] * parts[s][:, lanes].astype(jnp.float32)
        out_ref[0, :, lanes] = joined.astype(out_ref.dtype)


def finish(meta, at, own, own_sum, parts, earlier, cost):
    sides, rows = len(parts), 32
    _, tokens, features = own.shape
    in_specs = [
        pl.BlockSpec((1, rows, features), lambda i, meta: (at, i, 0)),
        pl.BlockSpec((1, rows, HD), lambda i, meta: (at, i, 0)),
    ]
    in_specs += [pl.BlockSpec((rows, features + HD), lambda i, meta: (i, 0)) for _ in parts]
    extra = () if earlier is None else (earlier,)
    in_specs += [pl.BlockSpec(memory_space=pl.ANY) for _ in extra]
    return pl.pallas_call(
        functools.partial(finish_kernel, sides, len(extra)),
        out_shape=jax.ShapeDtypeStruct(own.shape, jnp.bfloat16),
        grid_spec=pltpu.PrefetchScalarGridSpec(
            num_scalar_prefetch=1,
            grid=(tokens // rows,),
            in_specs=in_specs,
            out_specs=pl.BlockSpec((1, rows, features), lambda i, meta: (meta[0], i, 0)),
        ),
        input_output_aliases={} if earlier is None else {3 + sides: 0},
        compiler_params=pltpu.CompilerParams(vmem_limit_bytes=VMEM_LIMIT),
        cost_estimate=pl.CostEstimate(flops=cost, bytes_accessed=1, transcendentals=0),
    )(meta, own, own_sum, *parts, *extra)


def per_device(queries, keyvals, far_frames):
    shape = queries.shape
    frames, rows, columns, features = shape
    tokens = rows * columns
    ta_size, ha_size, wa_size = lax.axis_size("ta"), lax.axis_size("ha"), lax.axis_size("wa")
    ta, ha, wa = lax.axis_index("ta"), lax.axis_index("ha"), lax.axis_index("wa")
    parity = ta % 2
    queries = queries.reshape(frames, tokens, features)
    keyvals = keyvals.reshape(2, frames, tokens, features)

    core_pairs = [(i, i ^ 1) for i in range(ta_size)]
    cross_pairs = [(i, ta_size - 1 - i) for i in range(ta_size)]
    up = [(i, i + 1) for i in range(ha_size - 1)]
    down = [(i + 1, i) for i in range(ha_size - 1)]
    if wa_size == 2:
        ways = [([(0, 1), (1, 0)], [(0, 1), (1, 0)], wa >= 0)]
    else:
        right = [(i, i + 1) for i in range(wa_size - 1)]
        left = [(i + 1, i) for i in range(wa_size - 1)]
        ways = [(right, left, wa < wa_size - 1), (left, right, wa > 0)]

    def frame_of(value, index):
        return lax.dynamic_slice_in_dim(value, index, 1, axis=1)

    visitors = [lax.ppermute(queries, "wa", there) for there, _, _ in ways]
    last_rows, first_rows, held = lax.optimization_barrier(
        (keyvals[:, :, tokens - SPOT :], keyvals[:, :, :SPOT], keyvals)
    )
    top = lax.ppermute(last_rows, "ha", up)
    bottom = lax.ppermute(first_rows, "ha", down)
    cross = lax.ppermute(frame_of(held, parity), "ta", cross_pairs)
    core = lax.ppermute(keyvals, "ta", core_pairs)
    core_top = lax.ppermute(frame_of(top, 1 - parity), "ta", core_pairs)
    core_bottom = lax.ppermute(frame_of(bottom, 1 - parity), "ta", core_pairs)
    last_frame, cross, core_top, core_bottom = lax.optimization_barrier(
        (frame_of(keyvals, 1 - parity), cross, core_top, core_bottom)
    )
    last = lax.ppermute(last_frame, "ta", cross_pairs)
    cross_top = lax.ppermute(cross[:, :, tokens - SPOT :], "ha", up)
    cross_bottom = lax.ppermute(cross[:, :, :SPOT], "ha", down)
    core_halos = [(value, kind) for value in (core_top, core_bottom) for kind in range(2)]
    cross_halos = [(value, kind) for value in (cross_top, cross_bottom) for kind in range(2)]

    has_top, has_bottom = ha > 0, ha < ha_size - 1

    def as_meta(*values):
        return jnp.stack([jnp.asarray(value).astype(jnp.int32) for value in values])

    q_sides = visitors + [queries]
    early = near_attention(
        as_meta(1 - parity, parity, has_top, has_bottom),
        keyvals, core, top, bottom, core_halos, q_sides, 1,
    )
    late_meta, _ = lax.optimization_barrier((as_meta(parity, 0, has_top, has_bottom), early[0]))
    late = near_attention(
        late_meta,
        keyvals, cross, top, bottom, cross_halos, q_sides, LATE_COST,
    )
    early_parts = [lax.ppermute(early[s], "wa", back) for s, (_, back, _) in enumerate(ways)]
    late_results, early_parts, cross, last = lax.optimization_barrier((late[: len(ways)], early_parts, cross, last))
    late_parts = [lax.ppermute(late_results[s], "wa", back) for s, (_, back, _) in enumerate(ways)]
    corner = lax.ppermute(cross, "ta", core_pairs)
    corner_last = lax.ppermute(last, "ta", core_pairs)

    wanted = far_frames[:, :, 0, :]
    owner, place = wanted // frames, wanted % frames
    inner = (place != owner % 2).astype(jnp.int32)
    code = jnp.where(owner == ta ^ 1, place, jnp.where(owner == ta_size - 1 - ta, 2 + inner, 4 + inner))
    own, own_sum = far_attention(
        as_meta(1 - parity, parity),
        code.reshape(-1).astype(jnp.int32),
        queries,
        (core, cross, last, corner, corner_last),
        (early[-2], late[-2], early[-1], late[-1]),
    )
    exists = [valid for _, _, valid in ways]
    out = finish(as_meta(1 - parity, *exists), 0, own, own_sum, early_parts, None, FINISH_COST)
    out = finish(as_meta(parity, *exists), 1, own, own_sum, late_parts, out, 1)
    return out.reshape(shape)


def solution(mesh):
    placed = (P("ta", "ha", "wa", None), P(None, "ta", "ha", "wa", None), P("ta", "ha", "wa", None))
    return jax.shard_map(
        per_device, mesh=mesh, in_specs=placed, out_specs=P("ta", "ha", "wa", None), check_vma=False
    )
```

time: 109 us -> 110 us (level)
  Pallas kernels: 24.8 us -> 29.3 us
  waiting for transfers between devices: 42.3 us -> 38.8 us
    ppermute x1, waiting for transfers between devices: 0.01 us -> 13 us  [per_device(): visitors = [lax.ppermute(queries, 'wa', there) for there, _, _ in ways]]
    ppermute x11 -> x9, waiting for transfers between devices: 35.7 us -> 25.1 us  [the longest x1 17.7 us: per_device(): top = lax.ppermute(last_rows, 'ha', up)]
    ppermute x1, waiting for transfers between devices: 6.58 us -> 0.01 us  [per_device(): last = lax.ppermute(last_frame, 'ta', cross_pairs)]
    unnamed x39 -> x27, local copies, waits for them, and re-layouts: 14.4 us -> 10.3 us
    pallas_call x1, Pallas kernels: 6.31 us -> 8.89 us  [far_attention(): pl.pallas_call(far_kernel, out_shape=[jax.ShapeDtypeStruct((2, tokens, fe...]
    dynamic_slice x3 -> x4, local copies, waits for them, and re-layouts: 1.9 us -> 4.35 us  [frame_of(): return lax.dynamic_slice_in_dim(value, index, 1, axis=1)]
    pallas_call x3 -> x4, Pallas kernels: 18.5 us -> 20.4 us  [the longest x2 14.7 us: near_attention(): pl.pallas_call(functools.partial(near_kernel, sides), out_shape=outs, gri...]
    slice x2, local copies, waits for them, and re-layouts: 2.44 us -> 4.39 us  [the longest x1 3.3 us: per_device(): keyvals[:, :, :SPOT]]
  transfers between devices with their start and end apart: 16 -> 14, of which waited for: 6 -> 6; matrix products, arithmetic and copies ran while one was open for 4% -> 6% of each run, Pallas kernels for 20% -> 24%
where the time goes in v4:
time: 110 us
  waiting for transfers between devices  38.8 us (35%)
  Pallas kernels  29.3 us (27%)
  starting transfers between devices  21.5 us (20%)
  local copies, waits for them, and re-layouts  19.2 us (17%)
    ppermute x1, waiting for transfers between devices, per_device(): top = lax.ppermute(last_rows, 'ha', up)  17.7 us
    pallas_call x2, Pallas kernels, near_attention(): pl.pallas_call(functools.partial(near_kernel, sides), out_shape=outs, gri...  14.7 us
    ppermute x1, waiting for transfers between devices, per_device(): visitors = [lax.ppermute(queries, 'wa', there) for there, _, _ in ways]  13 us
    unnamed x27, local copies, waits for them, and re-layouts  10.3 us
    pallas_call x1, Pallas kernels, far_attention(): pl.pallas_call(far_kernel, out_shape=[jax.ShapeDtypeStruct((2, tokens, fe...  8.89 us
    ppermute x1, starting transfers between devices, per_device(): top = lax.ppermute(last_rows, 'ha', up)  5.91 us
    pallas_call x2, Pallas kernels, finish(): pl.pallas_call(functools.partial(finish_kernel, sides, len(extra)), out_s...  5.71 us
    ppermute x1, starting transfers between devices, per_device(): cross_top = lax.ppermute(cross[:, :, tokens - SPOT:], 'ha', up)  5.37 us
  transfers between devices with their start and end apart: 14, of which 6 were waited for; matrix products, arithmetic and copies ran while one was open for 6% of the time, Pallas kernels for 24%

profile of v4, /device:TPU:0, one launch (start us, length us, event | category | flops | bytes accessed | tf_op | source)
XLA Modules:
  0.0 109.9 jit_solution(495326616766675781)
XLA Ops:
  0.0 3.3 %fusion.1 = (bf16[2,2,64,2048]{3,2,1,0:T(8,128)(2,1)}, bf16[2,2,64,2048]{3,2,1,0:T(8,128)(2,1)}) fusion(bf16[2,2,128,2048]{3,2,1,0:T(8,128)(2,1)} %bitcast.8), kind=kLoop, calls=%fused_computation.21 | loop fusion | bytes 4194304 | tf_op jit(solution)/shard_map/slice | solution.py:303
  3.3 5.9 %collective-permute-start.1 = (bf16[2,2,64,2048]{3,2,1,0:T(8,128)(2,1)}, bf16[2,2,64,2048]{3,2,1,0:T(8,128)(2,1)}, u32[]{:S(2)}, u32[]{:S(2)}) collective-permute-start(bf16[2,2,64,2048]{3,2,1,0:T(8,128)(2,1)} %get-tuple-element.25), channel_id=1, source_target_pairs={{0,2},{2,4},{4,6},{1,3},{3,5},{5,7},{8,10},{10,12},{12,14},{9,11},... | collective-permute-start | bytes 3145736 | tf_op jit(solution)/shard_map/ppermute | solution.py:305
  9.2 1.3 %collective-permute-start.2 = (bf16[2,2,64,2048]{3,2,1,0:T(8,128)(2,1)}, bf16[2,2,64,2048]{3,2,1,0:T(8,128)(2,1)}, u32[]{:S(2)}, u32[]{:S(2)}) collective-permute-start(bf16[2,2,64,2048]{3,2,1,0:T(8,128)(2,1)} %get-tuple-element.26), channel_id=1, source_target_pairs={{2,0},{4,2},{6,4},{3,1},{5,3},{7,5},{10,8},{12,10},{14,12},{11,9},... | collective-permute-start | bytes 3145736 | tf_op jit(solution)/shard_map/ppermute | solution.py:306
  10.6 1.1 constant_dynamic-slice_fusion.2
  11.7 1.6 %collective-permute-start.3 = (bf16[2,1,128,2048]{3,2,1,0:T(8,128)(2,1)}, bf16[2,1,128,2048]{3,2,1,0:T(8,128)(2,1)S(1)}, u32[]{:S(2)}, u32[]{:S(2)}) collective-permute-start(bf16[2,1,128,2048]{3,2,1,0:T(8,128)(2,1)} %constant_dynamic-slice_fusion.2), channel_id=1, source_target_pairs={{0,24},{8,16},{16,8},{24,0},{1,25},{9,17},{17,9},{25,1},{2,26},{10... | collective-permute-start | bytes 3145736 | tf_op jit(solution)/shard_map/ppermute | solution.py:307
  13.3 17.7 %collective-permute-done.1.top_ref = bf16[2,2,64,2048]{3,2,1,0:T(8,128)(2,1)} collective-permute-done((bf16[2,2,64,2048]{3,2,1,0:T(8,128)(2,1)}, bf16[2,2,64,2048]{3,2,1,0:T(8,128)(2,1)}, u32[]{:S(2)}, u32[]{:S(2)}) %collective-permute-start.1) | collective-permute-done | bytes 1048608 | tf_op jit(solution)/shard_map/ppermute | solution.py:305
  32.1 3.9 %collective-permute-done.2.bottom_ref = bf16[2,2,64,2048]{3,2,1,0:T(8,128)(2,1)} collective-permute-done((bf16[2,2,64,2048]{3,2,1,0:T(8,128)(2,1)}, bf16[2,2,64,2048]{3,2,1,0:T(8,128)(2,1)}, u32[]{:S(2)}, u32[]{:S(2)}) %collective-permute-start.2) | collective-permute-done | bytes 1048608 | tf_op jit(solution)/shard_map/ppermute | solution.py:306
  36.0 1.1 constant_dynamic-slice_fusion
  37.2 1.6 %collective-permute-start.6 = (bf16[2,128,2048]{2,1,0:T(8,128)(2,1)}, bf16[2,128,2048]{2,1,0:T(8,128)(2,1)}, u32[]{:S(2)}, u32[]{:S(2)}) collective-permute-start(bf16[2,128,2048]{2,1,0:T(8,128)(2,1)} %bitcast.3.refs_5_.q_ref), channel_id=1, source_target_pairs={{0,1},{1,0},{2,3},{3,2},{4,5},{5,4},{6,7},{7,6},{8,9},{9,8},{10,11... | collective-permute-start | bytes 3145736 | tf_op jit(solution)/shard_map/ppermute | solution.py:301
  38.8 1.1 %constant_dynamic-slice_fusion.3 = bf16[2,1,128,2048]{3,2,1,0:T(8,128)(2,1)} fusion(bf16[2,2,128,2048]{3,2,1,0:T(8,128)(2,1)S(1)} %bitcast.11, s32[]{:T(128)S(6)} %select_n.47), kind=kLoop, calls=%fused_computation.14 | loop fusion | bytes 2097156 | tf_op jit(solution)/shard_map/dynamic_slice | solution.py:299
  41.6 1.1 fusion.2
  42.7 1.3 %collective-permute-start.8 = (bf16[2,1,64,2048]{3,2,1,0:T(8,128)(2,1)}, bf16[2,1,64,2048]{3,2,1,0:T(8,128)(2,1)}, u32[]{:S(2)}, u32[]{:S(2)}) collective-permute-start(bf16[2,1,64,2048]{3,2,1,0:T(8,128)(2,1)} %get-tuple-element.47), channel_id=1, source_target_pairs={{2,0},{4,2},{6,4},{3,1},{5,3},{7,5},{10,8},{12,10},{14,12},{11,9},... | collective-permute-start | bytes 1572872 | tf_op jit(solution)/shard_map/ppermute | solution.py:316
  44.0 5.4 %collective-permute-start.7 = (bf16[2,1,64,2048]{3,2,1,0:T(8,128)(2,1)}, bf16[2,1,64,2048]{3,2,1,0:T(8,128)(2,1)}, u32[]{:S(2)}, u32[]{:S(2)}) collective-permute-start(bf16[2,1,64,2048]{3,2,1,0:T(8,128)(2,1)} %get-tuple-element.48), channel_id=1, source_target_pairs={{0,2},{2,4},{4,6},{1,3},{3,5},{5,7},{8,10},{10,12},{12,14},{9,11},... | collective-permute-start | bytes 1572872 | tf_op jit(solution)/shard_map/ppermute | solution.py:315
  50.1 13.0 %collective-permute-done.6.refs_4_ = bf16[2,128,2048]{2,1,0:T(8,128)(2,1)} collective-permute-done((bf16[2,128,2048]{2,1,0:T(8,128)(2,1)}, bf16[2,128,2048]{2,1,0:T(8,128)(2,1)}, u32[]{:S(2)}, u32[]{:S(2)}) %collective-permute-start.6) | collective-permute-done | bytes 1048608 | tf_op jit(solution)/shard_map/ppermute | solution.py:301
  65.2 7.3 %shard_map.37 = (bf16[128,2176]{1,0:T(8,128)(2,1)S(1)}, f32[128,2048]{1,0:T(8,128)S(1)}, f32[128,128]{1,0:T(8,128)S(1)}) custom-call(s32[4]{0:T(128)S(1)} %get-tuple-element.50.meta_ref, bf16[2,2,128,2048]{3,2,1,0:T(8,128)(2,1)S(1)} %bitcast.12, bf16[2,2,128,2048]{3,2,1,0:T(8,128)(2,1)} %collective-permute-done.ext_ref.core_ref, ...), custom_call_target="tpu_custom_call" | custom-call | flops 1 | bytes 1 | tf_op jit(solution)/shard_map/pallas_call | solution.py:140
  73.5 1.5 %collective-permute-start.9 = (bf16[128,2176]{1,0:T(8,128)(2,1)S(1)}, bf16[128,2176]{1,0:T(8,128)(2,1)S(1)}, u32[]{:S(2)}, u32[]{:S(2)}) collective-permute-start(bf16[128,2176]{1,0:T(8,128)(2,1)S(1)} %get-tuple-element.30), channel_id=1, source_target_pairs={{0,1},{1,0},{2,3},{3,2},{4,5},{5,4},{6,7},{7,6},{8,9},{9,8},{10,11... | collective-permute-start | bytes 1671176 | tf_op jit(solution)/shard_map/ppermute | solution.py:335
  75.0 7.4 %shard_map.38 = (bf16[128,2176]{1,0:T(8,128)(2,1)S(1)}, f32[128,2048]{1,0:T(8,128)S(1)}, f32[128,128]{1,0:T(8,128)S(1)}) custom-call(s32[4]{0:T(128)S(1)} %get-tuple-element.31.meta_ref, bf16[2,2,128,2048]{3,2,1,0:T(8,128)(2,1)S(1)} %bitcast.13, bf16[2,1,128,2048]{3,2,1,0:T(8,128)(2,1)S(1)} %collective-permute-done.3.ext_ref.cross_ref, ...), custom_call_target="tpu_custom_call" | custom-call | flops 17179869184 | bytes 1 | tf_op jit(solution)/shard_map/pallas_call | solution.py:140
  84.2 3.5 %collective-permute-done.9.refs_0_ = bf16[128,2176]{1,0:T(8,128)(2,1)S(1)} collective-permute-done((bf16[128,2176]{1,0:T(8,128)(2,1)S(1)}, bf16[128,2176]{1,0:T(8,128)(2,1)S(1)}, u32[]{:S(2)}, u32[]{:S(2)}) %collective-permute-start.9) | collective-permute-done | bytes 557088 | tf_op jit(solution)/shard_map/ppermute | solution.py:335
  90.4 1.6 %collective-permute-start.13 = (bf16[128,2176]{1,0:T(8,128)(2,1)}, bf16[128,2176]{1,0:T(8,128)(2,1)S(1)}, u32[]{:S(2)}, u32[]{:S(2)}) collective-permute-start(bf16[128,2176]{1,0:T(8,128)(2,1)} %copy-done.11), channel_id=1, source_target_pairs={{0,1},{1,0},{2,3},{3,2},{4,5},{5,4},{6,7},{7,6},{8,9},{9,8},{10,11... | collective-permute-start | bytes 1671176 | tf_op jit(solution)/shard_map/ppermute | solution.py:337
  92.9 1.2 %copy-done.6 = f32[128,2048]{1,0:T(8,128)S(1)} copy-done((f32[128,2048]{1,0:T(8,128)S(1)}, f32[128,2048]{1,0:T(8,128)}, u32[]{:S(2)}) %copy-start.6) | copy-done | bytes 1048600
  94.1 1.2 %copy-done.8 = f32[128,2048]{1,0:T(8,128)S(1)} copy-done((f32[128,2048]{1,0:T(8,128)S(1)}, f32[128,2048]{1,0:T(8,128)}, u32[]{:S(2)}) %copy-start.8) | copy-done | bytes 1048600
  95.3 8.9 %shard_map.39 = (f32[2,128,2048]{2,1,0:T(8,128)S(1)}, f32[2,128,128]{2,1,0:T(8,128)S(1)}) custom-call(s32[2]{0:T(128)S(1)} %pad_add_fusion.1.meta_ref, s32[8]{0:T(128)S(1)} %compare_select_fusion.3.code_ref, bf16[2,128,2048]{2,1,0:T(8,128)(2,1)} %bitcast.3.refs_5_.q_ref, bf16[2,2,128,2048]{3,2,1,0:T(8,128)(2,1)} %collective-permute-done.ext_ref.core_ref, ...), custom_call_target="tpu_custom_call" | custom-call | flops 1 | bytes 1 | tf_op jit(solution)/shard_map/pallas_call | solution.py:218
  104.2 2.9 %shard_map.40.refs_1_ = bf16[2,128,2048]{2,1,0:T(8,128)(2,1)} custom-call(s32[2]{0:T(128)S(1)} %pad_add_fusion.2.meta_ref, f32[2,128,2048]{2,1,0:T(8,128)S(1)} %get-tuple-element.41.own_ref, f32[2,128,128]{2,1,0:T(8,128)S(1)} %get-tuple-element.42.own_sum_ref, bf16[128,2176]{1,0:T(8,128)(2,1)S(1)} %copy-done.10), custom_call_target="tpu_custom_call" | custom-call | flops 4294967296 | bytes 1 | tf_op jit(solution)/shard_map/pallas_call | solution.py:262
  107.1 2.9 %shard_map.41 = bf16[2,128,2048]{2,1,0:T(8,128)(2,1)} custom-call(s32[2]{0:T(128)S(1)} %pad_add_fusion.meta_ref, f32[2,128,2048]{2,1,0:T(8,128)S(1)} %get-tuple-element.41.own_ref, f32[2,128,128]{2,1,0:T(8,128)S(1)} %get-tuple-element.42.own_sum_ref, bf16[128,2176]{1,0:T(8,128)(2,1)S(1)} %collective-permute-done.13.refs_0_, ...), custom_call_target="tpu_custom_call", output_to_operand_aliasing={{}: (4, {})} | custom-call | flops 1 | bytes 1 | tf_op jit(solution)/shard_map/pallas_call | solution.py:262
  (49 shorter events, 12.2 us)
Async XLA Ops:
  0.0 10.5 %copy-start = (bf16[2,2,16,8,2048]{4,3,2,1,0:T(8,128)(2,1)S(1)}, bf16[2,2,16,8,2048]{4,3,2,1,0:T(8,128)(2,1)}, u32[]{:S(2)}) copy-start(bf16[2,2,16,8,2048]{4,3,2,1,0:T(8,128)(2,1)} %param.4) | copy-start | bytes 6291460
  3.3 27.6 %collective-permute-start.1 = (bf16[2,2,64,2048]{3,2,1,0:T(8,128)(2,1)}, bf16[2,2,64,2048]{3,2,1,0:T(8,128)(2,1)}, u32[]{:S(2)}, u32[]{:S(2)}) collective-permute-start(bf16[2,2,64,2048]{3,2,1,0:T(8,128)(2,1)} %get-tuple-element.25), channel_id=1, source_target_pairs={{0,2},{2,4},{4,6},{1,3},{3,5},{5,7},{8,10},{10,12},{12,14},{9,11},... | collective-permute-start | bytes 3145736 | tf_op jit(solution)/shard_map/ppermute | solution.py:305
  9.2 26.8 %collective-permute-start.2 = (bf16[2,2,64,2048]{3,2,1,0:T(8,128)(2,1)}, bf16[2,2,64,2048]{3,2,1,0:T(8,128)(2,1)}, u32[]{:S(2)}, u32[]{:S(2)}) collective-permute-start(bf16[2,2,64,2048]{3,2,1,0:T(8,128)(2,1)} %get-tuple-element.26), channel_id=1, source_target_pairs={{2,0},{4,2},{6,4},{3,1},{5,3},{7,5},{10,8},{12,10},{14,12},{11,9},... | collective-permute-start | bytes 3145736 | tf_op jit(solution)/shard_map/ppermute | solution.py:306
  10.5 52.6 %collective-permute-start = (bf16[2,2,128,2048]{3,2,1,0:T(8,128)(2,1)S(1)}, bf16[2,2,128,2048]{3,2,1,0:T(8,128)(2,1)}, u32[]{:S(2)}, u32[]{:S(2)}) collective-permute-start(bf16[2,2,128,2048]{3,2,1,0:T(8,128)(2,1)S(1)} %bitcast.9), channel_id=1, source_target_pairs={{0,8},{8,0},{16,24},{24,16},{1,9},{9,1},{17,25},{25,17},{2,10},{10... | collective-permute-start | bytes 6291464 | tf_op jit(solution)/shard_map/ppermute | solution.py:308
  11.7 28.2 %collective-permute-start.3 = (bf16[2,1,128,2048]{3,2,1,0:T(8,128)(2,1)}, bf16[2,1,128,2048]{3,2,1,0:T(8,128)(2,1)S(1)}, u32[]{:S(2)}, u32[]{:S(2)}) collective-permute-start(bf16[2,1,128,2048]{3,2,1,0:T(8,128)(2,1)} %constant_dynamic-slice_fusion.2), channel_id=1, source_target_pairs={{0,24},{8,16},{16,8},{24,0},{1,25},{9,17},{17,9},{25,1},{2,26},{10... | collective-permute-start | bytes 3145736 | tf_op jit(solution)/shard_map/ppermute | solution.py:307
  32.0 7.9 %collective-permute-start.4 = (bf16[2,1,64,2048]{3,2,1,0:T(8,128)(2,1)S(1)}, bf16[2,1,64,2048]{3,2,1,0:T(8,128)(2,1)S(1)}, u32[]{:S(2)}, u32[]{:S(2)}) collective-permute-start(bf16[2,1,64,2048]{3,2,1,0:T(8,128)(2,1)S(1)} %constant_dynamic-slice_fusion.1), channel_id=1, source_target_pairs={{0,8},{8,0},{16,24},{24,16},{1,9},{9,1},{17,25},{25,17},{2,10},{10... | collective-permute-start | bytes 1572872 | tf_op jit(solution)/shard_map/ppermute | solution.py:309
  37.1 3.6 %collective-permute-start.5 = (bf16[2,1,64,2048]{3,2,1,0:T(8,128)(2,1)S(1)}, bf16[2,1,64,2048]{3,2,1,0:T(8,128)(2,1)S(1)}, u32[]{:S(2)}, u32[]{:S(2)}) collective-permute-start(bf16[2,1,64,2048]{3,2,1,0:T(8,128)(2,1)S(1)} %constant_dynamic-slice_fusion), channel_id=1, source_target_pairs={{0,8},{8,0},{16,24},{24,16},{1,9},{9,1},{17,25},{25,17},{2,10},{10... | collective-permute-start | bytes 1572872 | tf_op jit(solution)/shard_map/ppermute | solution.py:310
  37.2 25.9 %collective-permute-start.6 = (bf16[2,128,2048]{2,1,0:T(8,128)(2,1)}, bf16[2,128,2048]{2,1,0:T(8,128)(2,1)}, u32[]{:S(2)}, u32[]{:S(2)}) collective-permute-start(bf16[2,128,2048]{2,1,0:T(8,128)(2,1)} %bitcast.3.refs_5_.q_ref), channel_id=1, source_target_pairs={{0,1},{1,0},{2,3},{3,2},{4,5},{5,4},{6,7},{7,6},{8,9},{9,8},{10,11... | collective-permute-start | bytes 3145736 | tf_op jit(solution)/shard_map/ppermute | solution.py:301
  40.7 0.9 copy-start.3
  42.7 32.3 %collective-permute-start.8 = (bf16[2,1,64,2048]{3,2,1,0:T(8,128)(2,1)}, bf16[2,1,64,2048]{3,2,1,0:T(8,128)(2,1)}, u32[]{:S(2)}, u32[]{:S(2)}) collective-permute-start(bf16[2,1,64,2048]{3,2,1,0:T(8,128)(2,1)} %get-tuple-element.47), channel_id=1, source_target_pairs={{2,0},{4,2},{6,4},{3,1},{5,3},{7,5},{10,8},{12,10},{14,12},{11,9},... | collective-permute-start | bytes 1572872 | tf_op jit(solution)/shard_map/ppermute | solution.py:316
  44.0 31.1 %collective-permute-start.7 = (bf16[2,1,64,2048]{3,2,1,0:T(8,128)(2,1)}, bf16[2,1,64,2048]{3,2,1,0:T(8,128)(2,1)}, u32[]{:S(2)}, u32[]{:S(2)}) collective-permute-start(bf16[2,1,64,2048]{3,2,1,0:T(8,128)(2,1)} %get-tuple-element.48), channel_id=1, source_target_pairs={{0,2},{2,4},{4,6},{1,3},{3,5},{5,7},{8,10},{10,12},{12,14},{9,11},... | collective-permute-start | bytes 1572872 | tf_op jit(solution)/shard_map/ppermute | solution.py:315
  49.4 34.8 %collective-permute-start.10 = (bf16[2,1,128,2048]{3,2,1,0:T(8,128)(2,1)}, bf16[2,1,128,2048]{3,2,1,0:T(8,128)(2,1)}, u32[]{:S(2)}, u32[]{:S(2)}) collective-permute-start(bf16[2,1,128,2048]{3,2,1,0:T(8,128)(2,1)} %constant_dynamic-slice_fusion.3), channel_id=1, source_target_pairs={{0,24},{8,16},{16,8},{24,0},{1,25},{9,17},{17,9},{25,1},{2,26},{10... | collective-permute-start | bytes 3145736 | tf_op jit(solution)/shard_map/ppermute | solution.py:314
  63.1 1.0 copy-start.2
  64.1 1.0 copy-start.4
  72.5 1.0 copy-start.5
  73.5 14.2 %collective-permute-start.9 = (bf16[128,2176]{1,0:T(8,128)(2,1)S(1)}, bf16[128,2176]{1,0:T(8,128)(2,1)S(1)}, u32[]{:S(2)}, u32[]{:S(2)}) collective-permute-start(bf16[128,2176]{1,0:T(8,128)(2,1)S(1)} %get-tuple-element.30), channel_id=1, source_target_pairs={{0,1},{1,0},{2,3},{3,2},{4,5},{5,4},{6,7},{7,6},{8,9},{9,8},{10,11... | collective-permute-start | bytes 1671176 | tf_op jit(solution)/shard_map/ppermute | solution.py:335
  75.0 14.6 %copy-start.12 = (s32[2,2,1,2]{3,2,1,0:T(1,128)S(1)}, s32[2,2,1,2]{3,2,1,0:T(1,128)}, u32[]{:S(2)}) copy-start(s32[2,2,1,2]{3,2,1,0:T(1,128)} %param.5) | copy-start | bytes 100
  82.4 1.0 copy-start.7
  88.5 4.1 %collective-permute-start.11 = (bf16[2,1,128,2048]{3,2,1,0:T(8,128)(2,1)S(1)}, bf16[2,1,128,2048]{3,2,1,0:T(8,128)(2,1)S(1)}, u32[]{:S(2)}, u32[]{:S(2)}) collective-permute-start(bf16[2,1,128,2048]{3,2,1,0:T(8,128)(2,1)S(1)} %collective-permute-done.3.ext_ref.cross_ref), channel_id=1, source_target_pairs={{0,8},{8,0},{16,24},{24,16},{1,9},{9,1},{17,25},{25,17},{2,10},{10... | collective-permute-start | bytes 3145736 | tf_op jit(solution)/shard_map/ppermute | solution.py:338
  88.5 4.4 %collective-permute-start.12 = (bf16[2,1,128,2048]{3,2,1,0:T(8,128)(2,1)}, bf16[2,1,128,2048]{3,2,1,0:T(8,128)(2,1)S(1)}, u32[]{:S(2)}, u32[]{:S(2)}) collective-permute-start(bf16[2,1,128,2048]{3,2,1,0:T(8,128)(2,1)} %collective-permute-done.10.last_ref), channel_id=1, source_target_pairs={{0,8},{8,0},{16,24},{24,16},{1,9},{9,1},{17,25},{25,17},{2,10},{10... | collective-permute-start | bytes 3145736 | tf_op jit(solution)/shard_map/ppermute | solution.py:339
  90.4 16.7 %collective-permute-start.13 = (bf16[128,2176]{1,0:T(8,128)(2,1)}, bf16[128,2176]{1,0:T(8,128)(2,1)S(1)}, u32[]{:S(2)}, u32[]{:S(2)}) collective-permute-start(bf16[128,2176]{1,0:T(8,128)(2,1)} %copy-done.11), channel_id=1, source_target_pairs={{0,1},{1,0},{2,3},{3,2},{4,5},{5,4},{6,7},{7,6},{8,9},{9,8},{10,11... | collective-permute-start | bytes 1671176 | tf_op jit(solution)/shard_map/ppermute | solution.py:337
  92.9 1.2 %copy-start.6 = (f32[128,2048]{1,0:T(8,128)S(1)}, f32[128,2048]{1,0:T(8,128)}, u32[]{:S(2)}) copy-start(f32[128,2048]{1,0:T(8,128)} %copy-done.5) | copy-start | bytes 3145732
  94.1 1.2 %copy-start.8 = (f32[128,2048]{1,0:T(8,128)S(1)}, f32[128,2048]{1,0:T(8,128)}, u32[]{:S(2)}) copy-start(f32[128,2048]{1,0:T(8,128)} %copy-done.7) | copy-start | bytes 3145732
  95.3 8.9 %copy-start.10 = (bf16[128,2176]{1,0:T(8,128)(2,1)S(1)}, bf16[128,2176]{1,0:T(8,128)(2,1)}, u32[]{:S(2)}) copy-start(bf16[128,2176]{1,0:T(8,128)(2,1)} %copy-done.9) | copy-start | bytes 1671172
  (3 other events, 2.4 us)

commit v5 on v4

v5 whole, which is shorter than its diff:
```python
import functools

import jax
import jax.numpy as jnp
from jax import lax
from jax.experimental import pallas as pl
from jax.experimental.pallas import tpu as pltpu
from jax.sharding import PartitionSpec as P

TILE = 8
HEADS = 16
HD = 128
NFAR = 2
SPOT = TILE * TILE
NEGATIVE = -1e30
EXP_SCALE = HD ** (-0.5) * 1.4426950408889634
VMEM_LIMIT = 16 * 1024 * 1024
GROUP = 4
FINISH_COST = 4 << 30
LATE_COST = 7 << 30


def contract_last(left, right):
    return lax.dot_general(left, right, (((1,), (1,)), ((), ())), preferred_element_type=jnp.float32)


def with_ones(values):
    return jnp.concatenate([values, jnp.ones_like(values)], axis=1)


def lane_index(rows):
    return lax.broadcasted_iota(jnp.int32, (rows, HD), 1)


def split_sums(value):
    high = value.astype(jnp.bfloat16).astype(jnp.float32)
    rest = value - high
    middle = rest.astype(jnp.bfloat16).astype(jnp.float32)
    low = rest - middle
    return (high + pltpu.roll(middle, HEADS, 1) + pltpu.roll(low, 2 * HEADS, 1)).astype(jnp.bfloat16)


def join_sums(value):
    terms = value.astype(jnp.float32)
    return terms + (pltpu.roll(terms, HD - HEADS, 1) + pltpu.roll(terms, HD - 2 * HEADS, 1))


def kernel_cost(flops):
    return pl.CostEstimate(flops=flops, bytes_accessed=1, transcendentals=0)


def cut_kernel(keyvals_ref, last_rows_ref, first_rows_ref, outer_last_ref, outer_first_ref, inner_ref, sems):
    outer = lax.axis_index("ta") % 2
    first, last = pl.ds(0, SPOT), pl.ds(SPOT, SPOT)
    pieces = [
        (keyvals_ref.at[:, :, last], last_rows_ref),
        (keyvals_ref.at[:, :, first], first_rows_ref),
        (keyvals_ref.at[:, outer, last], outer_last_ref),
        (keyvals_ref.at[:, outer, first], outer_first_ref),
        (keyvals_ref.at[:, 1 - outer], inner_ref),
    ]
    copies = [pltpu.make_async_copy(source, target, sems.at[i]) for i, (source, target) in enumerate(pieces)]
    for copy in copies:
        copy.start()
    for copy in copies:
        copy.wait()


def cut(keyvals):
    two, frames, tokens, features = keyvals.shape
    shapes = [(two, frames, SPOT, features)] * 2 + [(two, SPOT, features)] * 2 + [(two, tokens, features)]
    return pl.pallas_call(
        cut_kernel,
        out_shape=[jax.ShapeDtypeStruct(shape, keyvals.dtype) for shape in shapes],
        in_specs=[pl.BlockSpec(memory_space=pl.ANY)],
        out_specs=[pl.BlockSpec(memory_space=pltpu.VMEM)] * 5,
        scratch_shapes=[pltpu.SemaphoreType.DMA((5,))],
        compiler_params=pltpu.CompilerParams(vmem_limit_bytes=VMEM_LIMIT),
        cost_estimate=kernel_cost(1),
    )(keyvals)


def near_kernel(sides, early, has_rows, own_ref, top_ref, bottom_ref, *refs):
    parity = lax.axis_index("ta") % 2
    ha = lax.axis_index("ha")
    valid = (ha > 0, ha < has_rows - 1)
    if early:
        ext_ref, ext_top_ref, ext_bottom_ref, refs = refs[0], refs[1], refs[2], refs[3:]
        frame = 1 - parity
    else:
        ext_first_ref, ext_last_ref, ext_top_ref, ext_bottom_ref, refs = refs[0], refs[1], refs[2], refs[3], refs[4:]
        frame = parity
    q_refs, out_refs, own_sum_ref, log_ref = refs[:sides], refs[sides : 2 * sides], refs[2 * sides], refs[2 * sides + 1]
    group = pl.program_id(0)
    half = sides * SPOT

    def middle(kind, lanes):
        parts = [own_ref[kind, 0, :, lanes], own_ref[kind, 1, :, lanes]]
        if early:
            parts.append(ext_ref[kind, parity, :, lanes])
        else:
            parts += [ext_first_ref[kind, :, lanes], ext_last_ref[kind, :, lanes]]
        return jnp.concatenate(parts, axis=0)

    def halo(a, kind, lanes):
        ref, ext = ((top_ref, ext_top_ref), (bottom_ref, ext_bottom_ref))[a]
        third = ext[kind, parity, :, lanes] if early else ext[kind, :, lanes]
        return jnp.concatenate([ref[kind, 0, :, lanes], ref[kind, 1, :, lanes], third], axis=0)

    members = [slice(i * HD, (i + 1) * HD) for i in range(GROUP)]
    scores = []
    for lanes in members:
        queries = [
            jnp.concatenate([ref[frame, a * SPOT : (a + 1) * SPOT, lanes] for ref in q_refs], axis=0) for a in range(2)
        ]
        near = contract_last(jnp.concatenate(queries, axis=0), middle(0, lanes))
        edges = [contract_last(queries[a], halo(a, 0, lanes)) for a in range(2)]
        scores.append([(near[a * half : (a + 1) * half], edges[a]) for a in range(2)])
    weights = []
    for pairs in scores:
        for a, (near, edge) in enumerate(pairs):
            best = functools.reduce(jnp.maximum, [near[:, i * HD : (i + 1) * HD] for i in range(3)])
            edge_best = jnp.maximum(edge[:, : 2 * SPOT], jnp.concatenate([edge[:, 2 * SPOT :]] * 2, axis=1))
            best = jnp.maximum(best, jnp.where(valid[a], edge_best, NEGATIVE))
            peak = jnp.max(best, axis=-1, keepdims=True)
            shift = jnp.where(valid[a], peak, -NEGATIVE)
            weights.append(
                (
                    peak,
                    jnp.exp2((near - peak) * EXP_SCALE).astype(jnp.bfloat16),
                    jnp.exp2((edge - shift) * EXP_SCALE).astype(jnp.bfloat16),
                )
            )
    peaks = [jnp.zeros((half, HD), jnp.float32) for _ in range(2)]
    totals = [jnp.ones((half, HD), jnp.float32) for _ in range(2)]
    for i, lanes in enumerate(members):
        mask = lane_index(half) == group * GROUP + i
        middle_values = with_ones(middle(1, lanes))
        for a in range(2):
            peak, near, edge = weights[2 * i + a]
            summed = jnp.dot(near, middle_values, preferred_element_type=jnp.float32)
            summed = summed + jnp.dot(edge, with_ones(halo(a, 1, lanes)), preferred_element_type=jnp.float32)
            total = summed[:, HD:]
            result = summed[:, :HD] / total
            peaks[a] = jnp.where(mask, peak, peaks[a])
            totals[a] = jnp.where(mask, total, totals[a])
            for s in range(sides):
                rows = slice(s * SPOT, (s + 1) * SPOT)
                at = pl.ds(pl.multiple_of((group * GROUP + i) * HD, HD), HD)
                out_refs[s][a * SPOT : (a + 1) * SPOT, at] = result[rows].astype(out_refs[s].dtype)

    @pl.when(group == 0)
    def _():
        log_ref[...] = jnp.zeros_like(log_ref)

    for a in range(2):
        log_sum = peaks[a] * EXP_SCALE + jnp.log2(totals[a])
        for s in range(sides):
            log_ref[s, a * SPOT : (a + 1) * SPOT, :] += log_sum[s * SPOT : (s + 1) * SPOT]

    @pl.when(group == pl.num_programs(0) - 1)
    def _():
        own_sum_ref[...] = log_ref[sides - 1]
        for s in range(sides - 1):
            out_refs[s][:, HEADS * HD :] = split_sums(log_ref[s])


def near_attention(early, has_rows, own, top, bottom, third, queries, cost):
    sides = len(queries)
    tokens, features = queries[0].shape[1:]
    width = GROUP * HD
    operands = [own, top, bottom, *third, *queries]
    outs = [jax.ShapeDtypeStruct((tokens, features + HD), jnp.bfloat16) for _ in queries[1:]]
    outs += [jax.ShapeDtypeStruct((tokens, features), jnp.float32), jax.ShapeDtypeStruct((tokens, HD), jnp.float32)]

    def lanes_of_group(value):
        lead = value.ndim - 1
        return pl.BlockSpec(value.shape[:-1] + (width,), lambda g: (0,) * lead + (g,))

    return pl.pallas_call(
        functools.partial(near_kernel, sides, early, has_rows),
        out_shape=outs,
        grid=(HEADS // GROUP,),
        in_specs=[lanes_of_group(value) for value in operands],
        out_specs=[pl.BlockSpec(out.shape, lambda g: (0, 0)) for out in outs],
        scratch_shapes=[pltpu.VMEM((sides, tokens, HD), jnp.float32)],
        compiler_params=pltpu.CompilerParams(vmem_limit_bytes=VMEM_LIMIT),
        cost_estimate=kernel_cost(cost),
    )(*operands)


def far_kernel(members, far_ref, q_ref, core_ref, cross_first_ref, cross_last_ref, last_ref, *refs):
    corner_first_ref, corner_last_ref, corner_inner_ref, *refs = refs
    near_refs, near_sums, out_ref, sum_ref, held, sems = refs[:2], refs[2:4], refs[4], refs[5], refs[6], refs[7]
    ta = lax.axis_index("ta")
    parity = ta % 2

    def for_copies(first, action):
        lanes = pl.ds(first * HD, GROUP * HD)
        for f in range(2):
            for a in range(2):
                rows = pl.ds(a * SPOT, SPOT)
                by_rows = (cross_first_ref, cross_last_ref)[a], (corner_first_ref, corner_last_ref)[a]
                for j in range(NFAR):
                    slot = (f * 2 + a) * NFAR + j
                    wanted = far_ref[f, a, 0, j]
                    owner, place = wanted // 2, wanted % 2
                    inner = place != owner % 2
                    is_core, is_cross = owner == ta + 1 - 2 * parity, owner == members - 1 - ta
                    is_corner = jnp.logical_not(jnp.logical_or(is_core, is_cross))
                    sources = [
                        (jnp.logical_and(is_core, place == 0), core_ref.at[:, 0, rows, lanes]),
                        (jnp.logical_and(is_core, place == 1), core_ref.at[:, 1, rows, lanes]),
                        (jnp.logical_and(is_cross, jnp.logical_not(inner)), by_rows[0].at[:, :, lanes]),
                        (jnp.logical_and(is_cross, inner), last_ref.at[:, rows, lanes]),
                        (jnp.logical_and(is_corner, jnp.logical_not(inner)), by_rows[1].at[:, :, lanes]),
                        (jnp.logical_and(is_corner, inner), corner_inner_ref.at[:, rows, lanes]),
                    ]
                    for chosen, source in sources:

                        @pl.when(chosen)
                        def _(source=source, f=f, a=a, j=j, slot=slot):
                            copy = pltpu.make_async_copy(
                                source,
                                held.at[:, f * 2 + a, pl.ds(j * SPOT, SPOT), lanes],
                                sems.at[slot, first // GROUP],
                            )
                            action(copy)

    for first in range(0, HEADS, GROUP):
        for_copies(first, lambda copy: copy.start())

    units = [(early, a) for early in range(2) for a in range(2)]
    frames = (1 - parity, parity)
    collected = [jnp.zeros((SPOT, HD), jnp.float32) for _ in units]
    for first in range(0, HEADS, GROUP):
        for_copies(first, lambda copy: copy.wait())
        work = [(h, u) for h in range(first, first + GROUP) for u in range(len(units))]
        scores = []
        for h, u in work:
            early, a = units[u]
            frame, lanes = frames[early], slice(h * HD, (h + 1) * HD)
            queries = q_ref[frame, a * SPOT : (a + 1) * SPOT, lanes]
            scores.append(contract_last(queries, held[0, frame * 2 + a, :, lanes]))
        peaks = [jnp.max(value, axis=-1, keepdims=True) for value in scores]
        weights = [
            jnp.exp2((value - peak) * EXP_SCALE).astype(jnp.bfloat16) for value, peak in zip(scores, peaks)
        ]
        for (h, u), weight, peak in zip(work, weights, peaks):
            early, a = units[u]
            frame, lanes = frames[early], slice(h * HD, (h + 1) * HD)
            tokens = slice(a * SPOT, (a + 1) * SPOT)
            summed = jnp.dot(
                weight, with_ones(held[1, frame * 2 + a, :, lanes]), preferred_element_type=jnp.float32
            )
            near_sum = near_sums[early][tokens, h : h + 1]
            far_peak = peak * EXP_SCALE
            top = jnp.maximum(near_sum, far_peak)
            near_scale, far_scale = jnp.exp2(near_sum - top), jnp.exp2(far_peak - top)
            total = near_scale + far_scale * summed[:, HD:]
            joined = near_scale * near_refs[early][tokens, lanes] + far_scale * summed[:, :HD]
            out_ref[early, tokens, lanes] = joined / total
            collected[u] = jnp.where(lane_index(SPOT) == h, top + jnp.log2(total), collected[u])
    for (early, a), value in zip(units, collected):
        sum_ref[early, a * SPOT : (a + 1) * SPOT, :] = value


def far_attention(members, far_frames, queries, buffers, near):
    tokens, features = queries.shape[1:]
    in_vmem = pl.BlockSpec(memory_space=pltpu.VMEM)
    in_specs = [pl.BlockSpec(memory_space=pltpu.SMEM), in_vmem]
    in_specs += [pl.BlockSpec(memory_space=pl.ANY)] * len(buffers) + [in_vmem] * len(near)
    return pl.pallas_call(
        functools.partial(far_kernel, members),
        out_shape=[
            jax.ShapeDtypeStruct((2, tokens, features), jnp.float32),
            jax.ShapeDtypeStruct((2, tokens, HD), jnp.float32),
        ],
        in_specs=in_specs,
        out_specs=[in_vmem] * 2,
        scratch_shapes=[
            pltpu.VMEM((2, 4, NFAR * SPOT, features), jnp.bfloat16),
            pltpu.SemaphoreType.DMA((4 * NFAR, HEADS // GROUP)),
        ],
        compiler_params=pltpu.CompilerParams(vmem_limit_bytes=VMEM_LIMIT),
        cost_estimate=kernel_cost(1),
    )(far_frames, queries, *buffers, *near)


def finish_kernel(sides, columns, early, own_ref, own_sum_ref, *refs):
    parts, refs = refs[:sides], refs[sides:]
    wa = lax.axis_index("wa")
    logs = [own_sum_ref[0]]
    for s in range(sides):
        value = join_sums(parts[s][:, HEADS * HD :])
        if columns > 2:
            value = jnp.where(wa < columns - 1 if s == 0 else wa > 0, value, NEGATIVE)
        logs.append(value)
    top = functools.reduce(jnp.maximum, logs)
    scales = [jnp.exp2(value - top) for value in logs]
    total = functools.reduce(jnp.add, scales)
    scales = [value / total for value in scales]
    if not early:
        parity = lax.axis_index("ta") % 2
        refs[1][1 - parity] = refs[0][...]
    for h in range(HEADS):
        lanes = slice(h * HD, (h + 1) * HD)
        joined = scales[0][:, h : h + 1] * own_ref[0, :, lanes]
        for s in range(sides):
            joined = joined + scales[1 + s][:, h : h + 1] * parts[s][:, lanes].astype(jnp.float32)
        if early:
            refs[0][:, lanes] = joined.astype(jnp.bfloat16)
        else:
            refs[1][parity, :, lanes] = joined.astype(jnp.bfloat16)


def finish(columns, own, own_sum, parts, early_out, cost):
    sides, rows = len(parts), 32
    frames, tokens, features = own.shape
    early = early_out is None
    at = 0 if early else 1
    in_specs = [
        pl.BlockSpec((1, rows, features), lambda i: (at, i, 0)),
        pl.BlockSpec((1, rows, HD), lambda i: (at, i, 0)),
    ]
    in_specs += [pl.BlockSpec((rows, features + HD), lambda i: (i, 0)) for _ in parts]
    one_frame = pl.BlockSpec((rows, features), lambda i: (i, 0))
    if early:
        extra, out_spec, out_shape = (), one_frame, (tokens, features)
    else:
        extra, out_spec = (early_out,), pl.BlockSpec((frames, rows, features), lambda i: (0, i, 0))
        in_specs.append(one_frame)
        out_shape = own.shape
    return pl.pallas_call(
        functools.partial(finish_kernel, sides, columns, early),
        out_shape=jax.ShapeDtypeStruct(out_shape, jnp.bfloat16),
        grid=(tokens // rows,),
        in_specs=in_specs,
        out_specs=out_spec,
        compiler_params=pltpu.CompilerParams(vmem_limit_bytes=VMEM_LIMIT),
        cost_estimate=kernel_cost(cost),
    )(own, own_sum, *parts, *extra)


def per_device(queries, keyvals, far_frames):
    shape = queries.shape
    frames, rows, columns, features = shape
    tokens = rows * columns
    ta_size, ha_size, wa_size = lax.axis_size("ta"), lax.axis_size("ha"), lax.axis_size("wa")
    queries = queries.reshape(frames, tokens, features)
    keyvals = keyvals.reshape(2, frames, tokens, features)

    core_pairs = [(i, i ^ 1) for i in range(ta_size)]
    cross_pairs = [(i, ta_size - 1 - i) for i in range(ta_size)]
    up = [(i, i + 1) for i in range(ha_size - 1)]
    down = [(i + 1, i) for i in range(ha_size - 1)]
    if wa_size == 2:
        ways = [([(0, 1), (1, 0)], [(0, 1), (1, 0)])]
    else:
        right = [(i, i + 1) for i in range(wa_size - 1)]
        left = [(i + 1, i) for i in range(wa_size - 1)]
        ways = [(right, left), (left, right)]
    tie = lax.optimization_barrier

    visitors = [lax.ppermute(queries, "wa", there) for there, _ in ways]
    core = lax.ppermute(keyvals, "ta", core_pairs)
    last_rows, first_rows, outer_last, outer_first, inner = cut(keyvals)
    top = lax.ppermute(last_rows, "ha", up)
    bottom = lax.ppermute(first_rows, "ha", down)
    cross_last = lax.ppermute(outer_last, "ta", cross_pairs)
    outer_first, core = tie((outer_first, core))
    cross_first = lax.ppermute(outer_first, "ta", cross_pairs)
    top, bottom, visitors, cross_first, cross_last = tie((top, bottom, visitors, cross_first, cross_last))
    core_top = lax.ppermute(top, "ta", core_pairs)
    core_bottom = lax.ppermute(bottom, "ta", core_pairs)
    inner, cross_first, cross_last, core_top, core_bottom = tie((inner, cross_first, cross_last, core_top, core_bottom))
    cross_top = lax.ppermute(cross_last, "ha", up)
    cross_bottom = lax.ppermute(cross_first, "ha", down)
    last = lax.ppermute(inner, "ta", cross_pairs)

    q_sides = visitors + [queries]
    early = near_attention(
        True, ha_size, keyvals, top, bottom, (core, core_top, core_bottom), q_sides, 1
    )
    early_parts = [lax.ppermute(early[s], "wa", back) for s, (_, back) in enumerate(ways)]
    cross_top, cross_bottom, _ = tie((cross_top, cross_bottom, early[0]))
    late = near_attention(
        False, ha_size, keyvals, top, bottom, (cross_first, cross_last, cross_top, cross_bottom), q_sides, LATE_COST
    )
    late_results, early_parts, cross_first, cross_last, last = tie(
        (late[: len(ways)], early_parts, cross_first, cross_last, last)
    )
    late_parts = [lax.ppermute(late_results[s], "wa", back) for s, (_, back) in enumerate(ways)]
    corner_first = lax.ppermute(cross_first, "ta", core_pairs)
    corner_last = lax.ppermute(cross_last, "ta", core_pairs)
    corner_inner = lax.ppermute(last, "ta", core_pairs)
    own, own_sum = far_attention(
        ta_size,
        far_frames,
        queries,
        (core, cross_first, cross_last, last, corner_first, corner_last, corner_inner),
        (early[-2], late[-2], early[-1], late[-1]),
    )
    out = finish(wa_size, own, own_sum, early_parts, None, FINISH_COST)
    out = finish(wa_size, own, own_sum, late_parts, out, 1)
    return out.reshape(shape)


def solution(mesh):
    placed = (P("ta", "ha", "wa", None), P(None, "ta", "ha", "wa", None), P("ta", "ha", "wa", None))
    return jax.shard_map(
        per_device, mesh=mesh, in_specs=placed, out_specs=P("ta", "ha", "wa", None), check_vma=False
    )
```

time: 110 us -> 89.5 us (0.81)
  local copies, waits for them, and re-layouts: 19.2 us -> 1.6 us
  waiting for transfers between devices: 38.8 us -> 44.6 us
  Pallas kernels: 29.3 us -> 23.9 us
  starting transfers between devices: 21.5 us -> 19.1 us
    ppermute x9 -> x11, waiting for transfers between devices: 13.7 us -> 29.2 us  [the longest x1 12.3 us: per_device(): cross_last = lax.ppermute(outer_last, 'ta', cross_pairs)]
    ppermute x1, waiting for transfers between devices: 17.7 us -> 4.18 us  [per_device(): top = lax.ppermute(last_rows, 'ha', up)]
    unnamed x27 -> x6, local copies, waits for them, and re-layouts: 10.3 us -> 1.6 us
    pallas_call x5 -> x6, Pallas kernels: 29.3 us -> 23.9 us  [the longest x2 12 us: near_attention(): pl.pallas_call(functools.partial(near_kernel, sides, early, has_rows), ou...]
    slice x2 -> x0, local copies, waits for them, and re-layouts: 4.39 us -> none  [the longest x1 3.3 us: per_device(): keyvals[:, :, :SPOT]]
    dynamic_slice x4 -> x0, local copies, waits for them, and re-layouts: 4.35 us -> none  [frame_of(): return lax.dynamic_slice_in_dim(value, index, 1, axis=1)]
    ppermute x1, starting transfers between devices: 5.91 us -> 3.55 us  [per_device(): top = lax.ppermute(last_rows, 'ha', up)]
    ppermute x1, waiting for transfers between devices: 0.01 us -> 2.13 us  [per_device(): lax.ppermute(late_results[s], 'wa', back)]
  transfers between devices with their start and end apart: 14 -> 16, of which waited for: 6 -> 13; matrix products, arithmetic and copies ran while one was open for 6% -> 0% of each run, Pallas kernels for 24% -> 24%
where the time goes in v5:
time: 89.5 us; the launch traced here: 89.3 us
  waiting for transfers between devices  44.6 us (50%)
  Pallas kernels  23.9 us (27%)
  starting transfers between devices  19.1 us (21%)
  local copies, waits for them, and re-layouts  1.6 us (2%)
    ppermute x1, waiting for transfers between devices, per_device(): cross_last = lax.ppermute(outer_last, 'ta', cross_pairs)  12.3 us
    pallas_call x2, Pallas kernels, near_attention(): pl.pallas_call(functools.partial(near_kernel, sides, early, has_rows), ou...  12 us
    pallas_call x1, Pallas kernels, far_attention(): pl.pallas_call(functools.partial(far_kernel, members), out_shape=[jax.Sha...  7.92 us
    ppermute x1, starting transfers between devices, per_device(): cross_top = lax.ppermute(cross_last, 'ha', up)  5.07 us
    ppermute x1, waiting for transfers between devices, per_device(): lax.ppermute(early[s], 'wa', back)  4.86 us
    ppermute x1, waiting for transfers between devices, per_device(): bottom = lax.ppermute(first_rows, 'ha', down)  4.18 us
    ppermute x1, waiting for transfers between devices, per_device(): top = lax.ppermute(last_rows, 'ha', up)  4.18 us
    pallas_call x2, Pallas kernels, finish(): pl.pallas_call(functools.partial(finish_kernel, sides, columns, early), o...  3.71 us
  transfers between devices with their start and end apart: 16, of which 13 were waited for; matrix products, arithmetic and copies ran while one was open for 0% of the time, Pallas kernels for 24%

profile of v5, /device:TPU:0, one launch (start us, length us, event | category | flops | bytes accessed | tf_op | source)
XLA Modules:
  0.0 89.3 jit_solution(540621673486406923)
XLA Ops:
  0.5 2.5 %collective-permute-start.3 = (bf16[2,128,2048]{2,1,0:T(8,128)(2,1)}, bf16[2,128,2048]{2,1,0:T(8,128)(2,1)S(1)}, u32[]{:S(2)}, u32[]{:S(2)}) collective-permute-start(bf16[2,128,2048]{2,1,0:T(8,128)(2,1)} %bitcast.7), channel_id=1, source_target_pairs={{0,1},{1,0},{2,3},{3,2},{4,5},{5,4},{6,7},{7,6},{8,9},{9,8},{10,11... | collective-permute-start | bytes 3145736 | tf_op jit(solution)/shard_map/ppermute | solution.py:365
  3.0 1.6 %copy-done = bf16[2,2,16,8,2048]{4,3,2,1,0:T(8,128)(2,1)S(1)} copy-done((bf16[2,2,16,8,2048]{4,3,2,1,0:T(8,128)(2,1)S(1)}, bf16[2,2,16,8,2048]{4,3,2,1,0:T(8,128)(2,1)}, u32[]{:S(2)}) %copy-start) | copy-done | bytes 2097176
  4.9 3.5 %collective-permute-start.1 = (bf16[2,2,64,2048]{3,2,1,0:T(8,128)(2,1)S(1)}, bf16[2,2,64,2048]{3,2,1,0:T(8,128)(2,1)S(1)}, u32[]{:S(2)}, u32[]{:S(2)}) collective-permute-start(bf16[2,2,64,2048]{3,2,1,0:T(8,128)(2,1)S(1)} %get-tuple-element.39), channel_id=1, source_target_pairs={{0,2},{2,4},{4,6},{1,3},{3,5},{5,7},{8,10},{10,12},{12,14},{9,11},... | collective-permute-start | bytes 3145736 | tf_op jit(solution)/shard_map/ppermute | solution.py:368
  8.5 1.3 %collective-permute-start.2 = (bf16[2,2,64,2048]{3,2,1,0:T(8,128)(2,1)S(1)}, bf16[2,2,64,2048]{3,2,1,0:T(8,128)(2,1)S(1)}, u32[]{:S(2)}, u32[]{:S(2)}) collective-permute-start(bf16[2,2,64,2048]{3,2,1,0:T(8,128)(2,1)S(1)} %get-tuple-element.40), channel_id=1, source_target_pairs={{2,0},{4,2},{6,4},{3,1},{5,3},{7,5},{10,8},{12,10},{14,12},{11,9},... | collective-permute-start | bytes 3145736 | tf_op jit(solution)/shard_map/ppermute | solution.py:369
  9.8 1.1 %collective-permute-start.5 = (bf16[2,64,2048]{2,1,0:T(8,128)(2,1)S(1)}, bf16[2,64,2048]{2,1,0:T(8,128)(2,1)S(1)}, u32[]{:S(2)}, u32[]{:S(2)}) collective-permute-start(bf16[2,64,2048]{2,1,0:T(8,128)(2,1)S(1)} %get-tuple-element.42), channel_id=1, source_target_pairs={{0,24},{8,16},{16,8},{24,0},{1,25},{9,17},{17,9},{25,1},{2,26},{10... | collective-permute-start | bytes 1572872 | tf_op jit(solution)/shard_map/ppermute | solution.py:370
  11.6 12.3 %collective-permute-done.5.refs_1_.cross_last_ref = bf16[2,64,2048]{2,1,0:T(8,128)(2,1)S(1)} collective-permute-done((bf16[2,64,2048]{2,1,0:T(8,128)(2,1)S(1)}, bf16[2,64,2048]{2,1,0:T(8,128)(2,1)S(1)}, u32[]{:S(2)}, u32[]{:S(2)}) %collective-permute-start.5) | collective-permute-done | bytes 524320 | tf_op jit(solution)/shard_map/ppermute | solution.py:370
  23.9 3.1 %collective-permute-done.3.refs_3_.refs_4_ = bf16[2,128,2048]{2,1,0:T(8,128)(2,1)S(1)} collective-permute-done((bf16[2,128,2048]{2,1,0:T(8,128)(2,1)}, bf16[2,128,2048]{2,1,0:T(8,128)(2,1)S(1)}, u32[]{:S(2)}, u32[]{:S(2)}) %collective-permute-start.3) | collective-permute-done | bytes 1048608 | tf_op jit(solution)/shard_map/ppermute | solution.py:365
  27.0 4.2 %collective-permute-done.1.top_ref = bf16[2,2,64,2048]{3,2,1,0:T(8,128)(2,1)S(1)} collective-permute-done((bf16[2,2,64,2048]{3,2,1,0:T(8,128)(2,1)S(1)}, bf16[2,2,64,2048]{3,2,1,0:T(8,128)(2,1)S(1)}, u32[]{:S(2)}, u32[]{:S(2)}) %collective-permute-start.1) | collective-permute-done | bytes 1048608 | tf_op jit(solution)/shard_map/ppermute | solution.py:368
  31.2 4.2 %collective-permute-done.2.bottom_ref = bf16[2,2,64,2048]{3,2,1,0:T(8,128)(2,1)S(1)} collective-permute-done((bf16[2,2,64,2048]{3,2,1,0:T(8,128)(2,1)S(1)}, bf16[2,2,64,2048]{3,2,1,0:T(8,128)(2,1)S(1)}, u32[]{:S(2)}, u32[]{:S(2)}) %collective-permute-start.2) | collective-permute-done | bytes 1048608 | tf_op jit(solution)/shard_map/ppermute | solution.py:369
  35.9 2.1 %collective-permute-done.6.refs_1_ = bf16[2,2,64,2048]{3,2,1,0:T(8,128)(2,1)S(1)} collective-permute-done((bf16[2,2,64,2048]{3,2,1,0:T(8,128)(2,1)S(1)}, bf16[2,2,64,2048]{3,2,1,0:T(8,128)(2,1)S(1)}, u32[]{:S(2)}, u32[]{:S(2)}) %collective-permute-start.6) | collective-permute-done | bytes 1048608 | tf_op jit(solution)/shard_map/ppermute | solution.py:374
  38.0 1.5 %collective-permute-done.7.refs_2_ = bf16[2,2,64,2048]{3,2,1,0:T(8,128)(2,1)S(1)} collective-permute-done((bf16[2,2,64,2048]{3,2,1,0:T(8,128)(2,1)S(1)}, bf16[2,2,64,2048]{3,2,1,0:T(8,128)(2,1)S(1)}, u32[]{:S(2)}, u32[]{:S(2)}) %collective-permute-start.7) | collective-permute-done | bytes 1048608 | tf_op jit(solution)/shard_map/ppermute | solution.py:375
  39.5 1.3 %collective-permute-start.9 = (bf16[2,64,2048]{2,1,0:T(8,128)(2,1)S(1)}, bf16[2,64,2048]{2,1,0:T(8,128)(2,1)S(1)}, u32[]{:S(2)}, u32[]{:S(2)}) collective-permute-start(bf16[2,64,2048]{2,1,0:T(8,128)(2,1)S(1)} %collective-permute-done.4.refs_0_.cross_first_ref), channel_id=1, source_target_pairs={{2,0},{4,2},{6,4},{3,1},{5,3},{7,5},{10,8},{12,10},{14,12},{11,9},... | collective-permute-start | bytes 1572872 | tf_op jit(solution)/shard_map/ppermute | solution.py:378
  40.8 5.1 %collective-permute-start.8 = (bf16[2,64,2048]{2,1,0:T(8,128)(2,1)S(1)}, bf16[2,64,2048]{2,1,0:T(8,128)(2,1)S(1)}, u32[]{:S(2)}, u32[]{:S(2)}) collective-permute-start(bf16[2,64,2048]{2,1,0:T(8,128)(2,1)S(1)} %collective-permute-done.5.refs_1_.cross_last_ref), channel_id=1, source_target_pairs={{0,2},{2,4},{4,6},{1,3},{3,5},{5,7},{8,10},{10,12},{12,14},{9,11},... | collective-permute-start | bytes 1572872 | tf_op jit(solution)/shard_map/ppermute | solution.py:377
  46.8 6.0 %shard_map.38 = (bf16[128,2176]{1,0:T(8,128)(2,1)S(1)}, f32[128,2048]{1,0:T(8,128)S(1)}, f32[128,128]{1,0:T(8,128)S(1)}) custom-call(bf16[2,2,128,2048]{3,2,1,0:T(8,128)(2,1)S(1)} %bitcast.5, bf16[2,2,64,2048]{3,2,1,0:T(8,128)(2,1)S(1)} %collective-permute-done.1.top_ref, bf16[2,2,64,2048]{3,2,1,0:T(8,128)(2,1)S(1)} %collective-permute-done.2.bottom_ref, ...), custom_call_target="tpu_custom_call" | custom-call | flops 1 | bytes 1 | tf_op jit(solution)/shard_map/pallas_call | solution.py:180
  53.5 2.7 %collective-permute-done.9.refs_3_ = bf16[2,64,2048]{2,1,0:T(8,128)(2,1)S(1)} collective-permute-done((bf16[2,64,2048]{2,1,0:T(8,128)(2,1)S(1)}, bf16[2,64,2048]{2,1,0:T(8,128)(2,1)S(1)}, u32[]{:S(2)}, u32[]{:S(2)}) %collective-permute-start.9) | collective-permute-done | bytes 524320 | tf_op jit(solution)/shard_map/ppermute | solution.py:378
  56.2 1.2 %collective-permute-done.8.refs_2_ = bf16[2,64,2048]{2,1,0:T(8,128)(2,1)S(1)} collective-permute-done((bf16[2,64,2048]{2,1,0:T(8,128)(2,1)S(1)}, bf16[2,64,2048]{2,1,0:T(8,128)(2,1)S(1)}, u32[]{:S(2)}, u32[]{:S(2)}) %collective-permute-start.8) | collective-permute-done | bytes 524320 | tf_op jit(solution)/shard_map/ppermute | solution.py:377
  57.3 5.9 %shard_map.39 = (bf16[128,2176]{1,0:T(8,128)(2,1)S(1)}, f32[128,2048]{1,0:T(8,128)S(1)}, f32[128,128]{1,0:T(8,128)S(1)}) custom-call(bf16[2,2,128,2048]{3,2,1,0:T(8,128)(2,1)S(1)} %bitcast.6, bf16[2,2,64,2048]{3,2,1,0:T(8,128)(2,1)S(1)} %collective-permute-done.1.top_ref, bf16[2,2,64,2048]{3,2,1,0:T(8,128)(2,1)S(1)} %collective-permute-done.2.bottom_ref, ...), custom_call_target="tpu_custom_call" | custom-call | flops 7516192768 | bytes 1 | tf_op jit(solution)/shard_map/pallas_call | solution.py:180
  63.3 4.9 %collective-permute-done.10.refs_0_ = bf16[128,2176]{1,0:T(8,128)(2,1)S(1)} collective-permute-done((bf16[128,2176]{1,0:T(8,128)(2,1)S(1)}, bf16[128,2176]{1,0:T(8,128)(2,1)S(1)}, u32[]{:S(2)}, u32[]{:S(2)}) %collective-permute-start.10) | collective-permute-done | bytes 557088 | tf_op jit(solution)/shard_map/ppermute | solution.py:385
  68.1 3.2 %collective-permute-done.11.last_ref = bf16[2,128,2048]{2,1,0:T(8,128)(2,1)S(1)} collective-permute-done((bf16[2,128,2048]{2,1,0:T(8,128)(2,1)S(1)}, bf16[2,128,2048]{2,1,0:T(8,128)(2,1)S(1)}, u32[]{:S(2)}, u32[]{:S(2)}) %collective-permute-start.11) | collective-permute-done | bytes 1048608 | tf_op jit(solution)/shard_map/ppermute | solution.py:379
  72.6 2.2 %collective-permute-done.12.refs_0_ = bf16[2,64,2048]{2,1,0:T(8,128)(2,1)S(1)} collective-permute-done((bf16[2,64,2048]{2,1,0:T(8,128)(2,1)S(1)}, bf16[2,64,2048]{2,1,0:T(8,128)(2,1)S(1)}, u32[]{:S(2)}, u32[]{:S(2)}) %collective-permute-start.12) | collective-permute-done | bytes 524320 | tf_op jit(solution)/shard_map/ppermute | solution.py:394
  75.6 7.9 %shard_map.40 = (f32[2,128,2048]{2,1,0:T(8,128)S(1)}, f32[2,128,128]{2,1,0:T(8,128)S(1)}) custom-call(s32[2,2,1,2]{3,2,1,0:T(1,128)S(1)} %copy-done.2, bf16[2,128,2048]{2,1,0:T(8,128)(2,1)S(1)} %bitcast.10, bf16[2,2,128,2048]{3,2,1,0:T(8,128)(2,1)S(1)} %collective-permute-done.refs_0_.core_ref, ...), custom_call_target="tpu_custom_call" | custom-call | flops 1 | bytes 1 | tf_op jit(solution)/shard_map/pallas_call | solution.py:273
  83.5 1.3 %shard_map.41.refs_1_ = bf16[128,2048]{1,0:T(8,128)(2,1)S(1)} custom-call(f32[2,128,2048]{2,1,0:T(8,128)S(1)} %get-tuple-element.65.own_ref, f32[2,128,128]{2,1,0:T(8,128)S(1)} %get-tuple-element.66.own_sum_ref, bf16[128,2176]{1,0:T(8,128)(2,1)S(1)} %collective-permute-done.10.refs_0_), custom_call_target="tpu_custom_call" | custom-call | flops 4294967296 | bytes 1 | tf_op jit(solution)/shard_map/pallas_call | solution.py:334
  84.8 2.1 %collective-permute-done.15.refs_0_ = bf16[128,2176]{1,0:T(8,128)(2,1)S(1)} collective-permute-done((bf16[128,2176]{1,0:T(8,128)(2,1)S(1)}, bf16[128,2176]{1,0:T(8,128)(2,1)S(1)}, u32[]{:S(2)}, u32[]{:S(2)}) %collective-permute-start.15) | collective-permute-done | bytes 557088 | tf_op jit(solution)/shard_map/ppermute | solution.py:393
  86.9 2.4 %shard_map.42 = bf16[2,128,2048]{2,1,0:T(8,128)(2,1)} custom-call(f32[2,128,2048]{2,1,0:T(8,128)S(1)} %get-tuple-element.65.own_ref, f32[2,128,128]{2,1,0:T(8,128)S(1)} %get-tuple-element.66.own_sum_ref, bf16[128,2176]{1,0:T(8,128)(2,1)S(1)} %collective-permute-done.15.refs_0_, bf16[128,2048]{1,0:T(8,128)(2,1)S(1)} %shard_map.41.refs_1_), custom_call_target="tpu_custom_call" | custom-call | flops 1 | bytes 1 | tf_op jit(solution)/shard_map/pallas_call | solution.py:334
  (20 shorter events, 5.4 us)
Async XLA Ops:
  0.0 10.9 %collective-permute-start = (bf16[2,2,128,2048]{3,2,1,0:T(8,128)(2,1)}, bf16[2,2,128,2048]{3,2,1,0:T(8,128)(2,1)S(1)}, u32[]{:S(2)}, u32[]{:S(2)}) collective-permute-start(bf16[2,2,128,2048]{3,2,1,0:T(8,128)(2,1)} %bitcast.3), channel_id=1, source_target_pairs={{0,8},{8,0},{16,24},{24,16},{1,9},{9,1},{17,25},{25,17},{2,10},{10... | collective-permute-start | bytes 6291464 | tf_op jit(solution)/shard_map/ppermute | solution.py:366
  0.5 26.6 %collective-permute-start.3 = (bf16[2,128,2048]{2,1,0:T(8,128)(2,1)}, bf16[2,128,2048]{2,1,0:T(8,128)(2,1)S(1)}, u32[]{:S(2)}, u32[]{:S(2)}) collective-permute-start(bf16[2,128,2048]{2,1,0:T(8,128)(2,1)} %bitcast.7), channel_id=1, source_target_pairs={{0,1},{1,0},{2,3},{3,2},{4,5},{5,4},{6,7},{7,6},{8,9},{9,8},{10,11... | collective-permute-start | bytes 3145736 | tf_op jit(solution)/shard_map/ppermute | solution.py:365
  3.0 1.6 %copy-start = (bf16[2,2,16,8,2048]{4,3,2,1,0:T(8,128)(2,1)S(1)}, bf16[2,2,16,8,2048]{4,3,2,1,0:T(8,128)(2,1)}, u32[]{:S(2)}) copy-start(bf16[2,2,16,8,2048]{4,3,2,1,0:T(8,128)(2,1)} %param.4) | copy-start | bytes 6291460
  4.6 42.3 %copy-start.1 = (bf16[2,16,8,2048]{3,2,1,0:T(8,128)(2,1)S(1)}, bf16[2,16,8,2048]{3,2,1,0:T(8,128)(2,1)}, u32[]{:S(2)}) copy-start(bf16[2,16,8,2048]{3,2,1,0:T(8,128)(2,1)} %param.3) | copy-start | bytes 3145732
  4.9 26.3 %collective-permute-start.1 = (bf16[2,2,64,2048]{3,2,1,0:T(8,128)(2,1)S(1)}, bf16[2,2,64,2048]{3,2,1,0:T(8,128)(2,1)S(1)}, u32[]{:S(2)}, u32[]{:S(2)}) collective-permute-start(bf16[2,2,64,2048]{3,2,1,0:T(8,128)(2,1)S(1)} %get-tuple-element.39), channel_id=1, source_target_pairs={{0,2},{2,4},{4,6},{1,3},{3,5},{5,7},{8,10},{10,12},{12,14},{9,11},... | collective-permute-start | bytes 3145736 | tf_op jit(solution)/shard_map/ppermute | solution.py:368
  8.5 26.9 %collective-permute-start.2 = (bf16[2,2,64,2048]{3,2,1,0:T(8,128)(2,1)S(1)}, bf16[2,2,64,2048]{3,2,1,0:T(8,128)(2,1)S(1)}, u32[]{:S(2)}, u32[]{:S(2)}) collective-permute-start(bf16[2,2,64,2048]{3,2,1,0:T(8,128)(2,1)S(1)} %get-tuple-element.40), channel_id=1, source_target_pairs={{2,0},{4,2},{6,4},{3,1},{5,3},{7,5},{10,8},{12,10},{14,12},{11,9},... | collective-permute-start | bytes 3145736 | tf_op jit(solution)/shard_map/ppermute | solution.py:369
  9.8 14.2 %collective-permute-start.5 = (bf16[2,64,2048]{2,1,0:T(8,128)(2,1)S(1)}, bf16[2,64,2048]{2,1,0:T(8,128)(2,1)S(1)}, u32[]{:S(2)}, u32[]{:S(2)}) collective-permute-start(bf16[2,64,2048]{2,1,0:T(8,128)(2,1)S(1)} %get-tuple-element.42), channel_id=1, source_target_pairs={{0,24},{8,16},{16,8},{24,0},{1,25},{9,17},{17,9},{25,1},{2,26},{10... | collective-permute-start | bytes 1572872 | tf_op jit(solution)/shard_map/ppermute | solution.py:370
  10.9 24.5 %collective-permute-start.4 = (bf16[2,64,2048]{2,1,0:T(8,128)(2,1)S(1)}, bf16[2,64,2048]{2,1,0:T(8,128)(2,1)S(1)}, u32[]{:S(2)}, u32[]{:S(2)}) collective-permute-start(bf16[2,64,2048]{2,1,0:T(8,128)(2,1)S(1)} %get-tuple-element.41), channel_id=1, source_target_pairs={{0,24},{8,16},{16,8},{24,0},{1,25},{9,17},{17,9},{25,1},{2,26},{10... | collective-permute-start | bytes 1572872 | tf_op jit(solution)/shard_map/ppermute | solution.py:372
  35.4 2.7 %collective-permute-start.6 = (bf16[2,2,64,2048]{3,2,1,0:T(8,128)(2,1)S(1)}, bf16[2,2,64,2048]{3,2,1,0:T(8,128)(2,1)S(1)}, u32[]{:S(2)}, u32[]{:S(2)}) collective-permute-start(bf16[2,2,64,2048]{3,2,1,0:T(8,128)(2,1)S(1)} %collective-permute-done.1.top_ref), channel_id=1, source_target_pairs={{0,8},{8,0},{16,24},{24,16},{1,9},{9,1},{17,25},{25,17},{2,10},{10... | collective-permute-start | bytes 3145736 | tf_op jit(solution)/shard_map/ppermute | solution.py:374
  35.4 4.1 %collective-permute-start.7 = (bf16[2,2,64,2048]{3,2,1,0:T(8,128)(2,1)S(1)}, bf16[2,2,64,2048]{3,2,1,0:T(8,128)(2,1)S(1)}, u32[]{:S(2)}, u32[]{:S(2)}) collective-permute-start(bf16[2,2,64,2048]{3,2,1,0:T(8,128)(2,1)S(1)} %collective-permute-done.2.bottom_ref), channel_id=1, source_target_pairs={{0,8},{8,0},{16,24},{24,16},{1,9},{9,1},{17,25},{25,17},{2,10},{10... | collective-permute-start | bytes 3145736 | tf_op jit(solution)/shard_map/ppermute | solution.py:375
  39.5 16.6 %collective-permute-start.9 = (bf16[2,64,2048]{2,1,0:T(8,128)(2,1)S(1)}, bf16[2,64,2048]{2,1,0:T(8,128)(2,1)S(1)}, u32[]{:S(2)}, u32[]{:S(2)}) collective-permute-start(bf16[2,64,2048]{2,1,0:T(8,128)(2,1)S(1)} %collective-permute-done.4.refs_0_.cross_first_ref), channel_id=1, source_target_pairs={{2,0},{4,2},{6,4},{3,1},{5,3},{7,5},{10,8},{12,10},{14,12},{11,9},... | collective-permute-start | bytes 1572872 | tf_op jit(solution)/shard_map/ppermute | solution.py:378
  40.8 16.5 %collective-permute-start.8 = (bf16[2,64,2048]{2,1,0:T(8,128)(2,1)S(1)}, bf16[2,64,2048]{2,1,0:T(8,128)(2,1)S(1)}, u32[]{:S(2)}, u32[]{:S(2)}) collective-permute-start(bf16[2,64,2048]{2,1,0:T(8,128)(2,1)S(1)} %collective-permute-done.5.refs_1_.cross_last_ref), channel_id=1, source_target_pairs={{0,2},{2,4},{4,6},{1,3},{3,5},{5,7},{8,10},{10,12},{12,14},{9,11},... | collective-permute-start | bytes 1572872 | tf_op jit(solution)/shard_map/ppermute | solution.py:377
  45.9 25.5 %collective-permute-start.11 = (bf16[2,128,2048]{2,1,0:T(8,128)(2,1)S(1)}, bf16[2,128,2048]{2,1,0:T(8,128)(2,1)S(1)}, u32[]{:S(2)}, u32[]{:S(2)}) collective-permute-start(bf16[2,128,2048]{2,1,0:T(8,128)(2,1)S(1)} %get-tuple-element.57), channel_id=1, source_target_pairs={{0,24},{8,16},{16,8},{24,0},{1,25},{9,17},{17,9},{25,1},{2,26},{10... | collective-permute-start | bytes 3145736 | tf_op jit(solution)/shard_map/ppermute | solution.py:379
  52.9 22.7 %copy-start.2 = (s32[2,2,1,2]{3,2,1,0:T(1,128)S(1)}, s32[2,2,1,2]{3,2,1,0:T(1,128)}, u32[]{:S(2)}) copy-start(s32[2,2,1,2]{3,2,1,0:T(1,128)} %far_ref.1) | copy-start | bytes 100
  52.9 15.3 %collective-permute-start.10 = (bf16[128,2176]{1,0:T(8,128)(2,1)S(1)}, bf16[128,2176]{1,0:T(8,128)(2,1)S(1)}, u32[]{:S(2)}, u32[]{:S(2)}) collective-permute-start(bf16[128,2176]{1,0:T(8,128)(2,1)S(1)} %get-tuple-element.53), channel_id=1, source_target_pairs={{0,1},{1,0},{2,3},{3,2},{4,5},{5,4},{6,7},{7,6},{8,9},{9,8},{10,11... | collective-permute-start | bytes 1671176 | tf_op jit(solution)/shard_map/ppermute | solution.py:385
  71.4 4.2 %collective-permute-start.14 = (bf16[2,128,2048]{2,1,0:T(8,128)(2,1)S(1)}, bf16[2,128,2048]{2,1,0:T(8,128)(2,1)S(1)}, u32[]{:S(2)}, u32[]{:S(2)}) collective-permute-start(bf16[2,128,2048]{2,1,0:T(8,128)(2,1)S(1)} %collective-permute-done.11.last_ref), channel_id=1, source_target_pairs={{0,8},{8,0},{16,24},{24,16},{1,9},{9,1},{17,25},{25,17},{2,10},{10... | collective-permute-start | bytes 3145736 | tf_op jit(solution)/shard_map/ppermute | solution.py:396
  71.5 3.3 %collective-permute-start.12 = (bf16[2,64,2048]{2,1,0:T(8,128)(2,1)S(1)}, bf16[2,64,2048]{2,1,0:T(8,128)(2,1)S(1)}, u32[]{:S(2)}, u32[]{:S(2)}) collective-permute-start(bf16[2,64,2048]{2,1,0:T(8,128)(2,1)S(1)} %collective-permute-done.4.refs_0_.cross_first_ref), channel_id=1, source_target_pairs={{0,8},{8,0},{16,24},{24,16},{1,9},{9,1},{17,25},{25,17},{2,10},{10... | collective-permute-start | bytes 1572872 | tf_op jit(solution)/shard_map/ppermute | solution.py:394
  71.9 3.6 %collective-permute-start.13 = (bf16[2,64,2048]{2,1,0:T(8,128)(2,1)S(1)}, bf16[2,64,2048]{2,1,0:T(8,128)(2,1)S(1)}, u32[]{:S(2)}, u32[]{:S(2)}) collective-permute-start(bf16[2,64,2048]{2,1,0:T(8,128)(2,1)S(1)} %collective-permute-done.5.refs_1_.cross_last_ref), channel_id=1, source_target_pairs={{0,8},{8,0},{16,24},{24,16},{1,9},{9,1},{17,25},{25,17},{2,10},{10... | collective-permute-start | bytes 1572872 | tf_op jit(solution)/shard_map/ppermute | solution.py:395
  72.0 14.9 %collective-permute-start.15 = (bf16[128,2176]{1,0:T(8,128)(2,1)S(1)}, bf16[128,2176]{1,0:T(8,128)(2,1)S(1)}, u32[]{:S(2)}, u32[]{:S(2)}) collective-permute-start(bf16[128,2176]{1,0:T(8,128)(2,1)S(1)} %get-tuple-element.67), channel_id=1, source_target_pairs={{0,1},{1,0},{2,3},{3,2},{4,5},{5,4},{6,7},{7,6},{8,9},{9,8},{10,11... | collective-permute-start | bytes 1671176 | tf_op jit(solution)/shard_map/ppermute | solution.py:393

commit v6 on v5

--- a/solution.py
+++ b/solution.py
@@ -16,8 +16,8 @@
 EXP_SCALE = HD ** (-0.5) * 1.4426950408889634
 VMEM_LIMIT = 16 * 1024 * 1024
 GROUP = 4
-FINISH_COST = 4 << 30
-LATE_COST = 7 << 30
+FINISH_COST = 1
+LATE_COST = 8 << 30
 
 
 def contract_last(left, right):
@@ -49,7 +49,8 @@
     return pl.CostEstimate(flops=flops, bytes_accessed=1, transcendentals=0)
 
 
-def cut_kernel(keyvals_ref, last_rows_ref, first_rows_ref, outer_last_ref, outer_first_ref, inner_ref, sems):
+def cut_kernel(keyvals_ref, last_rows_ref, first_rows_ref, outer_last_ref, outer_first_ref, *refs):
+    inner_keys_ref, inner_values_ref, sems = refs
     outer = lax.axis_index("ta") % 2
     first, last = pl.ds(0, SPOT), pl.ds(SPOT, SPOT)
     pieces = [
@@ -57,7 +58,8 @@
         (keyvals_ref.at[:, :, first], first_rows_ref),
         (keyvals_ref.at[:, outer, last], outer_last_ref),
         (keyvals_ref.at[:, outer, first], outer_first_ref),
-        (keyvals_ref.at[:, 1 - outer], inner_ref),
+        (keyvals_ref.at[0, 1 - outer], inner_keys_ref),
+        (keyvals_ref.at[1, 1 - outer], inner_values_ref),
     ]
     copies = [pltpu.make_async_copy(source, target, sems.at[i]) for i, (source, target) in enumerate(pieces)]
     for copy in copies:
@@ -68,19 +70,19 @@
 
 def cut(keyvals):
     two, frames, tokens, features = keyvals.shape
-    shapes = [(two, frames, SPOT, features)] * 2 + [(two, SPOT, features)] * 2 + [(two, tokens, features)]
+    shapes = [(two, frames, SPOT, features)] * 2 + [(two, SPOT, features)] * 2 + [(tokens, features)] * 2
     return pl.pallas_call(
         cut_kernel,
         out_shape=[jax.ShapeDtypeStruct(shape, keyvals.dtype) for shape in shapes],
         in_specs=[pl.BlockSpec(memory_space=pl.ANY)],
-        out_specs=[pl.BlockSpec(memory_space=pltpu.VMEM)] * 5,
-        scratch_shapes=[pltpu.SemaphoreType.DMA((5,))],
+        out_specs=[pl.BlockSpec(memory_space=pltpu.VMEM)] * 6,
+        scratch_shapes=[pltpu.SemaphoreType.DMA((6,))],
         compiler_params=pltpu.CompilerParams(vmem_limit_bytes=VMEM_LIMIT),
         cost_estimate=kernel_cost(1),
     )(keyvals)
 
 
-def near_kernel(sides, early, has_rows, own_ref, top_ref, bottom_ref, *refs):
+def near_kernel(sides, early, home, has_rows, own_ref, top_ref, bottom_ref, *refs):
     parity = lax.axis_index("ta") % 2
     ha = lax.axis_index("ha")
     valid = (ha > 0, ha < has_rows - 1)
@@ -90,7 +92,7 @@
     else:
         ext_first_ref, ext_last_ref, ext_top_ref, ext_bottom_ref, refs = refs[0], refs[1], refs[2], refs[3], refs[4:]
         frame = parity
-    q_refs, out_refs, own_sum_ref, log_ref = refs[:sides], refs[sides : 2 * sides], refs[2 * sides], refs[2 * sides + 1]
+    q_refs, out_refs, refs, log_ref = refs[:sides], refs[sides : 2 * sides], refs[2 * sides : -1], refs[-1]
     group = pl.program_id(0)
     half = sides * SPOT
 
@@ -160,25 +162,29 @@
 
     @pl.when(group == pl.num_programs(0) - 1)
     def _():
-        own_sum_ref[...] = log_ref[sides - 1]
-        for s in range(sides - 1):
-            out_refs[s][:, HEADS * HD :] = split_sums(log_ref[s])
-
-
-def near_attention(early, has_rows, own, top, bottom, third, queries, cost):
+        if home:
+            refs[0][...] = log_ref[0]
+        else:
+            for s in range(sides):
+                out_refs[s][:, HEADS * HD :] = split_sums(log_ref[s])
+
+
+def near_attention(early, home, has_rows, own, top, bottom, third, queries, cost):
     sides = len(queries)
     tokens, features = queries[0].shape[1:]
     width = GROUP * HD
     operands = [own, top, bottom, *third, *queries]
-    outs = [jax.ShapeDtypeStruct((tokens, features + HD), jnp.bfloat16) for _ in queries[1:]]
-    outs += [jax.ShapeDtypeStruct((tokens, features), jnp.float32), jax.ShapeDtypeStruct((tokens, HD), jnp.float32)]
+    if home:
+        outs = [jax.ShapeDtypeStruct((tokens, lanes), jnp.float32) for lanes in (features, HD)]
+    else:
+        outs = [jax.ShapeDtypeStruct((tokens, features + HD), jnp.bfloat16) for _ in queries]
 
     def lanes_of_group(value):
         lead = value.ndim - 1
         return pl.BlockSpec(value.shape[:-1] + (width,), lambda g: (0,) * lead + (g,))
 
     return pl.pallas_call(
-        functools.partial(near_kernel, sides, early, has_rows),
+        functools.partial(near_kernel, sides, early, home, has_rows),
         out_shape=outs,
         grid=(HEADS // GROUP,),
         in_specs=[lanes_of_group(value) for value in operands],
@@ -189,52 +195,51 @@
     )(*operands)
 
 
-def far_kernel(members, far_ref, q_ref, core_ref, cross_first_ref, cross_last_ref, last_ref, *refs):
-    corner_first_ref, corner_last_ref, corner_inner_ref, *refs = refs
+def far_kernel(members, far_ref, q_ref, core_ref, cross_first_ref, cross_last_ref, *refs):
+    last_refs, corner_first_ref, corner_last_ref, corner_inner_refs, refs = refs[:2], refs[2], refs[3], refs[4:6], refs[6:]
     near_refs, near_sums, out_ref, sum_ref, held, sems = refs[:2], refs[2:4], refs[4], refs[5], refs[6], refs[7]
     ta = lax.axis_index("ta")
     parity = ta % 2
 
-    def for_copies(first, action):
-        lanes = pl.ds(first * HD, GROUP * HD)
-        for f in range(2):
-            for a in range(2):
-                rows = pl.ds(a * SPOT, SPOT)
-                by_rows = (cross_first_ref, cross_last_ref)[a], (corner_first_ref, corner_last_ref)[a]
-                for j in range(NFAR):
-                    slot = (f * 2 + a) * NFAR + j
-                    wanted = far_ref[f, a, 0, j]
-                    owner, place = wanted // 2, wanted % 2
-                    inner = place != owner % 2
-                    is_core, is_cross = owner == ta + 1 - 2 * parity, owner == members - 1 - ta
-                    is_corner = jnp.logical_not(jnp.logical_or(is_core, is_cross))
-                    sources = [
-                        (jnp.logical_and(is_core, place == 0), core_ref.at[:, 0, rows, lanes]),
-                        (jnp.logical_and(is_core, place == 1), core_ref.at[:, 1, rows, lanes]),
-                        (jnp.logical_and(is_cross, jnp.logical_not(inner)), by_rows[0].at[:, :, lanes]),
-                        (jnp.logical_and(is_cross, inner), last_ref.at[:, rows, lanes]),
-                        (jnp.logical_and(is_corner, jnp.logical_not(inner)), by_rows[1].at[:, :, lanes]),
-                        (jnp.logical_and(is_corner, inner), corner_inner_ref.at[:, rows, lanes]),
-                    ]
-                    for chosen, source in sources:
-
-                        @pl.when(chosen)
-                        def _(source=source, f=f, a=a, j=j, slot=slot):
-                            copy = pltpu.make_async_copy(
-                                source,
-                                held.at[:, f * 2 + a, pl.ds(j * SPOT, SPOT), lanes],
-                                sems.at[slot, first // GROUP],
-                            )
-                            action(copy)
-
-    for first in range(0, HEADS, GROUP):
-        for_copies(first, lambda copy: copy.start())
+    def tile_copy(source, kind, tile, j, slot, group):
+        lanes = pl.ds(group * GROUP * HD, GROUP * HD)
+        target = held.at[kind, tile, pl.ds(j * SPOT, SPOT), lanes]
+        return pltpu.make_async_copy(source.at[:, lanes], target, sems.at[kind, slot, group])
+
+    for f in range(2):
+        for a in range(2):
+            rows = pl.ds(a * SPOT, SPOT)
+            by_rows = (cross_first_ref, cross_last_ref)[a], (corner_first_ref, corner_last_ref)[a]
+            for j in range(NFAR):
+                slot = (f * 2 + a) * NFAR + j
+                wanted = far_ref[f, a, 0, j]
+                owner, place = wanted // 2, wanted % 2
+                inner = place != owner % 2
+                is_core, is_cross = owner == ta + 1 - 2 * parity, owner == members - 1 - ta
+                is_corner = jnp.logical_not(jnp.logical_or(is_core, is_cross))
+                sources = [
+                    (jnp.logical_and(is_core, place == 0), [core_ref.at[kind, 0, rows] for kind in range(2)]),
+                    (jnp.logical_and(is_core, place == 1), [core_ref.at[kind, 1, rows] for kind in range(2)]),
+                    (jnp.logical_and(is_cross, jnp.logical_not(inner)), [by_rows[0].at[kind] for kind in range(2)]),
+                    (jnp.logical_and(is_cross, inner), [ref.at[rows] for ref in last_refs]),
+                    (jnp.logical_and(is_corner, jnp.logical_not(inner)), [by_rows[1].at[kind] for kind in range(2)]),
+                    (jnp.logical_and(is_corner, inner), [ref.at[rows] for ref in corner_inner_refs]),
+                ]
+                for chosen, pair in sources:
+
+                    @pl.when(chosen)
+                    def _(pair=pair, f=f, a=a, j=j, slot=slot):
+                        for group in range(HEADS // GROUP):
+                            for kind, source in enumerate(pair):
+                                tile_copy(source, kind, f * 2 + a, j, slot, group).start()
 
     units = [(early, a) for early in range(2) for a in range(2)]
     frames = (1 - parity, parity)
     collected = [jnp.zeros((SPOT, HD), jnp.float32) for _ in units]
     for first in range(0, HEADS, GROUP):
-        for_copies(first, lambda copy: copy.wait())
+        for slot in range(4 * NFAR):
+            for kind in range(2):
+                tile_copy(cross_first_ref.at[kind], kind, slot // NFAR, slot % NFAR, slot, first // GROUP).wait()
         work = [(h, u) for h in range(first, first + GROUP) for u in range(len(units))]
         scores = []
         for h, u in work:
@@ -280,7 +285,7 @@
         out_specs=[in_vmem] * 2,
         scratch_shapes=[
             pltpu.VMEM((2, 4, NFAR * SPOT, features), jnp.bfloat16),
-            pltpu.SemaphoreType.DMA((4 * NFAR, HEADS // GROUP)),
+            pltpu.SemaphoreType.DMA((2, 4 * NFAR, HEADS // GROUP)),
         ],
         compiler_params=pltpu.CompilerParams(vmem_limit_bytes=VMEM_LIMIT),
         cost_estimate=kernel_cost(1),
@@ -362,44 +367,44 @@
         ways = [(right, left), (left, right)]
     tie = lax.optimization_barrier
 
-    visitors = [lax.ppermute(queries, "wa", there) for there, _ in ways]
     core = lax.ppermute(keyvals, "ta", core_pairs)
-    last_rows, first_rows, outer_last, outer_first, inner = cut(keyvals)
+    last_rows, first_rows, outer_last, outer_first, *inner = cut(keyvals)
     top = lax.ppermute(last_rows, "ha", up)
     bottom = lax.ppermute(first_rows, "ha", down)
     cross_last = lax.ppermute(outer_last, "ta", cross_pairs)
-    outer_first, core = tie((outer_first, core))
+    outer_first, core, sent = tie((outer_first, core, queries))
     cross_first = lax.ppermute(outer_first, "ta", cross_pairs)
-    top, bottom, visitors, cross_first, cross_last = tie((top, bottom, visitors, cross_first, cross_last))
+    visitors = [lax.ppermute(sent, "wa", there) for there, _ in ways]
+    top, bottom, cross_first, cross_last, inner = tie((top, bottom, cross_first, cross_last, inner))
     core_top = lax.ppermute(top, "ta", core_pairs)
     core_bottom = lax.ppermute(bottom, "ta", core_pairs)
-    inner, cross_first, cross_last, core_top, core_bottom = tie((inner, cross_first, cross_last, core_top, core_bottom))
     cross_top = lax.ppermute(cross_last, "ha", up)
     cross_bottom = lax.ppermute(cross_first, "ha", down)
-    last = lax.ppermute(inner, "ta", cross_pairs)
-
-    q_sides = visitors + [queries]
-    early = near_attention(
-        True, ha_size, keyvals, top, bottom, (core, core_top, core_bottom), q_sides, 1
-    )
-    early_parts = [lax.ppermute(early[s], "wa", back) for s, (_, back) in enumerate(ways)]
-    cross_top, cross_bottom, _ = tie((cross_top, cross_bottom, early[0]))
-    late = near_attention(
-        False, ha_size, keyvals, top, bottom, (cross_first, cross_last, cross_top, cross_bottom), q_sides, LATE_COST
-    )
-    late_results, early_parts, cross_first, cross_last, last = tie(
-        (late[: len(ways)], early_parts, cross_first, cross_last, last)
-    )
-    late_parts = [lax.ppermute(late_results[s], "wa", back) for s, (_, back) in enumerate(ways)]
+    last = [lax.ppermute(value, "ta", cross_pairs) for value in inner]
+
+    early_third = (core, core_top, core_bottom)
+    early = near_attention(True, False, ha_size, keyvals, top, bottom, early_third, visitors, 1)
+    early_parts = [lax.ppermute(result, "wa", back) for result, (_, back) in zip(early, ways)]
+    core_top, _ = tie((core_top, early[0]))
+    early_third = (core, core_top, core_bottom)
+    early_home = near_attention(True, True, ha_size, keyvals, top, bottom, early_third, [queries], 1)
+    cross_top, cross_bottom, _ = tie((cross_top, cross_bottom, early_home[1]))
+    late_third = (cross_first, cross_last, cross_top, cross_bottom)
+    late = near_attention(False, False, ha_size, keyvals, top, bottom, late_third, visitors, LATE_COST)
+    late_parts = [lax.ppermute(result, "wa", back) for result, (_, back) in zip(late, ways)]
+    cross_top, _ = tie((cross_top, late[0]))
+    late_third = (cross_first, cross_last, cross_top, cross_bottom)
+    late_home = near_attention(False, True, ha_size, keyvals, top, bottom, late_third, [queries], 1)
+    cross_first, cross_last, last, early_parts, _ = tie((cross_first, cross_last, last, early_parts, late_home[1]))
     corner_first = lax.ppermute(cross_first, "ta", core_pairs)
     corner_last = lax.ppermute(cross_last, "ta", core_pairs)
-    corner_inner = lax.ppermute(last, "ta", core_pairs)
+    corner_inner = [lax.ppermute(value, "ta", core_pairs) for value in last]
     own, own_sum = far_attention(
         ta_size,
         far_frames,
         queries,
-        (core, cross_first, cross_last, last, corner_first, corner_last, corner_inner),
-        (early[-2], late[-2], early[-1], late[-1]),
+        (core, cross_first, cross_last, *last, corner_first, corner_last, *corner_inner),
+        (early_home[0], late_home[0], early_home[1], late_home[1]),
     )
     out = finish(wa_size, own, own_sum, early_parts, None, FINISH_COST)
     out = finish(wa_size, own, own_sum, late_parts, out, 1)

time: 89.5 us -> 81.3 us (0.908)
  waiting for transfers between devices: 44.6 us -> 27 us
  Pallas kernels: 23.9 us -> 30.7 us
  starting transfers between devices: 19.1 us -> 21.6 us
    ppermute x5 -> x7, waiting for transfers between devices: 13.3 us -> 1.51 us  [the longest x2 1.5 us: per_device(): corner_inner = [lax.ppermute(value, 'ta', core_pairs) for value in last]]
    pallas_call x2 -> x4, Pallas kernels: 12 us -> 19.6 us  [near_attention(): pl.pallas_call(functools.partial(near_kernel, sides, early, home, has_row...]
    ppermute x1, waiting for transfers between devices: 4.18 us -> 7.74 us  [per_device(): top = lax.ppermute(last_rows, 'ha', up)]
    ppermute x5 -> x7, starting transfers between devices: 4.65 us -> 7.01 us  [the longest x2 3.17 us: per_device(): lax.ppermute(result, 'wa', back)]
    ppermute x1, waiting for transfers between devices: 2.15 us -> 0.01 us  [per_device(): core_top = lax.ppermute(top, 'ta', core_pairs)]
    ppermute x1, waiting for transfers between devices: 12.3 us -> 10.6 us  [per_device(): cross_last = lax.ppermute(outer_last, 'ta', cross_pairs)]
    ppermute x1, waiting for transfers between devices: 1.5 us -> 0.01 us  [per_device(): core_bottom = lax.ppermute(bottom, 'ta', core_pairs)]
    ppermute x1, waiting for transfers between devices: 2.7 us -> 1.33 us  [per_device(): cross_bottom = lax.ppermute(cross_first, 'ha', down)]
  transfers between devices with their start and end apart: 16 -> 18, of which waited for: 13 -> 8; matrix products, arithmetic and copies ran while one was open for 0% -> 0% of each run, Pallas kernels for 24% -> 35%
where the time goes in v6:
time: 81.3 us; the launch traced here: 81.1 us
  Pallas kernels  30.7 us (38%)
  waiting for transfers between devices  27 us (33%)
  starting transfers between devices  21.6 us (27%)
  local copies, waits for them, and re-layouts  1.6 us (2%)
    pallas_call x4, Pallas kernels, near_attention(): pl.pallas_call(functools.partial(near_kernel, sides, early, home, has_row...  19.6 us
    ppermute x1, waiting for transfers between devices, per_device(): cross_last = lax.ppermute(outer_last, 'ta', cross_pairs)  10.6 us
    ppermute x1, waiting for transfers between devices, per_device(): top = lax.ppermute(last_rows, 'ha', up)  7.74 us
    pallas_call x1, Pallas kernels, far_attention(): pl.pallas_call(functools.partial(far_kernel, members), out_shape=[jax.Sha...  7.04 us
    ppermute x1, starting transfers between devices, per_device(): top = lax.ppermute(last_rows, 'ha', up)  4.54 us
    ppermute x1, waiting for transfers between devices, per_device(): bottom = lax.ppermute(first_rows, 'ha', down)  4.18 us
    ppermute x1, starting transfers between devices, per_device(): cross_top = lax.ppermute(cross_last, 'ha', up)  4.07 us
    pallas_call x2, Pallas kernels, finish(): pl.pallas_call(functools.partial(finish_kernel, sides, columns, early), o...  3.74 us
  transfers between devices with their start and end apart: 18, of which 8 were waited for; matrix products, arithmetic and copies ran while one was open for 0% of the time, Pallas kernels for 35%

profile of v6, /device:TPU:0, one launch (start us, length us, event | category | flops | bytes accessed | tf_op | source)
XLA Modules:
  0.0 81.1 jit_solution(5730266381756572366)
XLA Ops:
  0.5 1.6 %copy-done = bf16[2,2,16,8,2048]{4,3,2,1,0:T(8,128)(2,1)S(1)} copy-done((bf16[2,2,16,8,2048]{4,3,2,1,0:T(8,128)(2,1)S(1)}, bf16[2,2,16,8,2048]{4,3,2,1,0:T(8,128)(2,1)}, u32[]{:S(2)}) %copy-start) | copy-done | bytes 2097176
  2.4 4.5 %collective-permute-start.1 = (bf16[2,2,64,2048]{3,2,1,0:T(8,128)(2,1)S(1)}, bf16[2,2,64,2048]{3,2,1,0:T(8,128)(2,1)S(1)}, u32[]{:S(2)}, u32[]{:S(2)}) collective-permute-start(bf16[2,2,64,2048]{3,2,1,0:T(8,128)(2,1)S(1)} %get-tuple-element.37), channel_id=1, source_target_pairs={{0,2},{2,4},{4,6},{1,3},{3,5},{5,7},{8,10},{10,12},{12,14},{9,11},... | collective-permute-start | bytes 3145736 | tf_op jit(solution)/shard_map/ppermute | solution.py:372
  7.0 1.3 %collective-permute-start.2 = (bf16[2,2,64,2048]{3,2,1,0:T(8,128)(2,1)S(1)}, bf16[2,2,64,2048]{3,2,1,0:T(8,128)(2,1)S(1)}, u32[]{:S(2)}, u32[]{:S(2)}) collective-permute-start(bf16[2,2,64,2048]{3,2,1,0:T(8,128)(2,1)S(1)} %get-tuple-element.38), channel_id=1, source_target_pairs={{2,0},{4,2},{6,4},{3,1},{5,3},{7,5},{10,8},{12,10},{14,12},{11,9},... | collective-permute-start | bytes 3145736 | tf_op jit(solution)/shard_map/ppermute | solution.py:373
  8.3 1.4 %collective-permute-start.4 = (bf16[2,64,2048]{2,1,0:T(8,128)(2,1)S(1)}, bf16[2,64,2048]{2,1,0:T(8,128)(2,1)S(1)}, u32[]{:S(2)}, u32[]{:S(2)}) collective-permute-start(bf16[2,64,2048]{2,1,0:T(8,128)(2,1)S(1)} %get-tuple-element.40), channel_id=1, source_target_pairs={{0,24},{8,16},{16,8},{24,0},{1,25},{9,17},{17,9},{25,1},{2,26},{10... | collective-permute-start | bytes 1572872 | tf_op jit(solution)/shard_map/ppermute | solution.py:374
  10.1 1.5 %collective-permute-start.9 = (bf16[2,128,2048]{2,1,0:T(8,128)(2,1)S(1)}, bf16[2,128,2048]{2,1,0:T(8,128)(2,1)S(1)}, u32[]{:S(2)}, u32[]{:S(2)}) collective-permute-start(bf16[2,128,2048]{2,1,0:T(8,128)(2,1)S(1)} %bitcast.9), channel_id=1, source_target_pairs={{0,1},{1,0},{2,3},{3,2},{4,5},{5,4},{6,7},{7,6},{8,9},{9,8},{10,11... | collective-permute-start | bytes 3145736 | tf_op jit(solution)/shard_map/ppermute | solution.py:377
  11.6 10.6 %collective-permute-done.4.refs_1_.cross_last_ref = bf16[2,64,2048]{2,1,0:T(8,128)(2,1)S(1)} collective-permute-done((bf16[2,64,2048]{2,1,0:T(8,128)(2,1)S(1)}, bf16[2,64,2048]{2,1,0:T(8,128)(2,1)S(1)}, u32[]{:S(2)}, u32[]{:S(2)}) %collective-permute-start.4) | collective-permute-done | bytes 524320 | tf_op jit(solution)/shard_map/ppermute | solution.py:374
  22.2 7.7 %collective-permute-done.1.top_ref = bf16[2,2,64,2048]{3,2,1,0:T(8,128)(2,1)S(1)} collective-permute-done((bf16[2,2,64,2048]{3,2,1,0:T(8,128)(2,1)S(1)}, bf16[2,2,64,2048]{3,2,1,0:T(8,128)(2,1)S(1)}, u32[]{:S(2)}, u32[]{:S(2)}) %collective-permute-start.1) | collective-permute-done | bytes 1048608 | tf_op jit(solution)/shard_map/ppermute | solution.py:372
  30.0 4.2 %collective-permute-done.2.bottom_ref = bf16[2,2,64,2048]{3,2,1,0:T(8,128)(2,1)S(1)} collective-permute-done((bf16[2,2,64,2048]{3,2,1,0:T(8,128)(2,1)S(1)}, bf16[2,2,64,2048]{3,2,1,0:T(8,128)(2,1)S(1)}, u32[]{:S(2)}, u32[]{:S(2)}) %collective-permute-start.2) | collective-permute-done | bytes 1048608 | tf_op jit(solution)/shard_map/ppermute | solution.py:373
  34.7 4.1 %collective-permute-start.11 = (bf16[2,64,2048]{2,1,0:T(8,128)(2,1)S(1)}, bf16[2,64,2048]{2,1,0:T(8,128)(2,1)S(1)}, u32[]{:S(2)}, u32[]{:S(2)}) collective-permute-start(bf16[2,64,2048]{2,1,0:T(8,128)(2,1)S(1)} %collective-permute-done.4.refs_1_.cross_last_ref), channel_id=1, source_target_pairs={{0,2},{2,4},{4,6},{1,3},{3,5},{5,7},{8,10},{10,12},{12,14},{9,11},... | collective-permute-start | bytes 1572872 | tf_op jit(solution)/shard_map/ppermute | solution.py:381
  38.7 1.3 %collective-permute-start.12 = (bf16[2,64,2048]{2,1,0:T(8,128)(2,1)S(1)}, bf16[2,64,2048]{2,1,0:T(8,128)(2,1)S(1)}, u32[]{:S(2)}, u32[]{:S(2)}) collective-permute-start(bf16[2,64,2048]{2,1,0:T(8,128)(2,1)S(1)} %collective-permute-done.3.refs_0_.cross_first_ref), channel_id=1, source_target_pairs={{2,0},{4,2},{6,4},{3,1},{5,3},{7,5},{10,8},{12,10},{14,12},{11,9},... | collective-permute-start | bytes 1572872 | tf_op jit(solution)/shard_map/ppermute | solution.py:382
  40.0 1.1 %collective-permute-start.5 = (bf16[128,2048]{1,0:T(8,128)(2,1)S(1)}, bf16[128,2048]{1,0:T(8,128)(2,1)S(1)}, u32[]{:S(2)}, u32[]{:S(2)}) collective-permute-start(bf16[128,2048]{1,0:T(8,128)(2,1)S(1)} %get-tuple-element.45), channel_id=1, source_target_pairs={{0,24},{8,16},{16,8},{24,0},{1,25},{9,17},{17,9},{25,1},{2,26},{10... | collective-permute-start | bytes 1572872 | tf_op jit(solution)/shard_map/ppermute | solution.py:383
  41.9 4.9 %shard_map.38 = bf16[128,2176]{1,0:T(8,128)(2,1)S(1)} custom-call(bf16[2,2,128,2048]{3,2,1,0:T(8,128)(2,1)S(1)} %bitcast.5, bf16[2,2,64,2048]{3,2,1,0:T(8,128)(2,1)S(1)} %collective-permute-done.1.top_ref, bf16[2,2,64,2048]{3,2,1,0:T(8,128)(2,1)S(1)} %collective-permute-done.2.bottom_ref, ...), custom_call_target="tpu_custom_call" | custom-call | flops 1 | bytes 1 | tf_op jit(solution)/shard_map/pallas_call | solution.py:186
  46.7 1.6 %collective-permute-start.10 = (bf16[128,2176]{1,0:T(8,128)(2,1)S(1)}, bf16[128,2176]{1,0:T(8,128)(2,1)S(1)}, u32[]{:S(2)}, u32[]{:S(2)}) collective-permute-start(bf16[128,2176]{1,0:T(8,128)(2,1)S(1)} %shard_map.38), channel_id=1, source_target_pairs={{0,1},{1,0},{2,3},{3,2},{4,5},{5,4},{6,7},{7,6},{8,9},{9,8},{10,11... | collective-permute-start | bytes 1671176 | tf_op jit(solution)/shard_map/ppermute | solution.py:387
  48.3 4.8 %shard_map.39 = (f32[128,2048]{1,0:T(8,128)S(1)}, f32[128,128]{1,0:T(8,128)S(1)}) custom-call(bf16[2,2,128,2048]{3,2,1,0:T(8,128)(2,1)S(1)} %bitcast.6, bf16[2,2,64,2048]{3,2,1,0:T(8,128)(2,1)S(1)} %collective-permute-done.1.top_ref, bf16[2,2,64,2048]{3,2,1,0:T(8,128)(2,1)S(1)} %collective-permute-done.2.bottom_ref, ...), custom_call_target="tpu_custom_call" | custom-call | flops 1 | bytes 1 | tf_op jit(solution)/shard_map/pallas_call | solution.py:186
  53.1 1.3 %collective-permute-done.12.refs_3_ = bf16[2,64,2048]{2,1,0:T(8,128)(2,1)S(1)} collective-permute-done((bf16[2,64,2048]{2,1,0:T(8,128)(2,1)S(1)}, bf16[2,64,2048]{2,1,0:T(8,128)(2,1)S(1)}, u32[]{:S(2)}, u32[]{:S(2)}) %collective-permute-start.12) | collective-permute-done | bytes 524320 | tf_op jit(solution)/shard_map/ppermute | solution.py:382
  54.4 5.0 %shard_map.40 = bf16[128,2176]{1,0:T(8,128)(2,1)S(1)} custom-call(bf16[2,2,128,2048]{3,2,1,0:T(8,128)(2,1)S(1)} %bitcast.7, bf16[2,2,64,2048]{3,2,1,0:T(8,128)(2,1)S(1)} %collective-permute-done.1.top_ref, bf16[2,2,64,2048]{3,2,1,0:T(8,128)(2,1)S(1)} %collective-permute-done.2.bottom_ref, ...), custom_call_target="tpu_custom_call" | custom-call | flops 8589934592 | bytes 1 | tf_op jit(solution)/shard_map/pallas_call | solution.py:186
  59.5 1.6 %collective-permute-start.17 = (bf16[128,2176]{1,0:T(8,128)(2,1)S(1)}, bf16[128,2176]{1,0:T(8,128)(2,1)S(1)}, u32[]{:S(2)}, u32[]{:S(2)}) collective-permute-start(bf16[128,2176]{1,0:T(8,128)(2,1)S(1)} %shard_map.40), channel_id=1, source_target_pairs={{0,1},{1,0},{2,3},{3,2},{4,5},{5,4},{6,7},{7,6},{8,9},{9,8},{10,11... | collective-permute-start | bytes 1671176 | tf_op jit(solution)/shard_map/ppermute | solution.py:394
  61.1 4.9 %shard_map.41 = (f32[128,2048]{1,0:T(8,128)S(1)}, f32[128,128]{1,0:T(8,128)S(1)}) custom-call(bf16[2,2,128,2048]{3,2,1,0:T(8,128)(2,1)S(1)} %bitcast.8, bf16[2,2,64,2048]{3,2,1,0:T(8,128)(2,1)S(1)} %collective-permute-done.1.top_ref, bf16[2,2,64,2048]{3,2,1,0:T(8,128)(2,1)S(1)} %collective-permute-done.2.bottom_ref, ...), custom_call_target="tpu_custom_call" | custom-call | flops 1 | bytes 1 | tf_op jit(solution)/shard_map/pallas_call | solution.py:186
  67.1 0.9 %collective-permute-done.13.refs_2_ = bf16[2,64,2048]{2,1,0:T(8,128)(2,1)S(1)} collective-permute-done((bf16[2,64,2048]{2,1,0:T(8,128)(2,1)S(1)}, bf16[2,64,2048]{2,1,0:T(8,128)(2,1)S(1)}, u32[]{:S(2)}, u32[]{:S(2)}) %collective-permute-start.13) | collective-permute-done | bytes 524320 | tf_op jit(solution)/shard_map/ppermute | solution.py:399
  68.0 0.7 collective-permute-done.14.refs_3_
  68.8 0.7 collective-permute-done.15.refs_4_
  70.3 7.0 %shard_map.42 = (f32[2,128,2048]{2,1,0:T(8,128)S(1)}, f32[2,128,128]{2,1,0:T(8,128)S(1)}) custom-call(s32[2,2,1,2]{3,2,1,0:T(1,128)S(1)} %copy-done.2, bf16[2,128,2048]{2,1,0:T(8,128)(2,1)S(1)} %bitcast.12, bf16[2,2,128,2048]{3,2,1,0:T(8,128)(2,1)S(1)} %collective-permute-done.refs_0_.core_ref, ...), custom_call_target="tpu_custom_call" | custom-call | flops 1 | bytes 1 | tf_op jit(solution)/shard_map/pallas_call | solution.py:278
  77.3 1.3 %shard_map.43.refs_1_ = bf16[128,2048]{1,0:T(8,128)(2,1)S(1)} custom-call(f32[2,128,2048]{2,1,0:T(8,128)S(1)} %get-tuple-element.62.own_ref, f32[2,128,128]{2,1,0:T(8,128)S(1)} %get-tuple-element.63.own_sum_ref, bf16[128,2176]{1,0:T(8,128)(2,1)S(1)} %collective-permute-done.10.refs_0_), custom_call_target="tpu_custom_call" | custom-call | flops 1 | bytes 1 | tf_op jit(solution)/shard_map/pallas_call | solution.py:339
  78.7 2.4 %shard_map.44 = bf16[2,128,2048]{2,1,0:T(8,128)(2,1)} custom-call(f32[2,128,2048]{2,1,0:T(8,128)S(1)} %get-tuple-element.62.own_ref, f32[2,128,128]{2,1,0:T(8,128)S(1)} %get-tuple-element.63.own_sum_ref, bf16[128,2176]{1,0:T(8,128)(2,1)S(1)} %collective-permute-done.17.refs_0_, bf16[128,2048]{1,0:T(8,128)(2,1)S(1)} %shard_map.43.refs_1_), custom_call_target="tpu_custom_call" | custom-call | flops 1 | bytes 1 | tf_op jit(solution)/shard_map/pallas_call | solution.py:339
  (26 shorter events, 4.3 us)
Async XLA Ops:
  0.0 9.6 %collective-permute-start = (bf16[2,2,128,2048]{3,2,1,0:T(8,128)(2,1)}, bf16[2,2,128,2048]{3,2,1,0:T(8,128)(2,1)S(1)}, u32[]{:S(2)}, u32[]{:S(2)}) collective-permute-start(bf16[2,2,128,2048]{3,2,1,0:T(8,128)(2,1)} %bitcast.3), channel_id=1, source_target_pairs={{0,8},{8,0},{16,24},{24,16},{1,9},{9,1},{17,25},{25,17},{2,10},{10... | collective-permute-start | bytes 6291464 | tf_op jit(solution)/shard_map/ppermute | solution.py:370
  0.5 1.6 %copy-start = (bf16[2,2,16,8,2048]{4,3,2,1,0:T(8,128)(2,1)S(1)}, bf16[2,2,16,8,2048]{4,3,2,1,0:T(8,128)(2,1)}, u32[]{:S(2)}) copy-start(bf16[2,2,16,8,2048]{4,3,2,1,0:T(8,128)(2,1)} %param.4) | copy-start | bytes 6291460
  2.0 8.0 %copy-start.1 = (bf16[2,16,8,2048]{3,2,1,0:T(8,128)(2,1)S(1)}, bf16[2,16,8,2048]{3,2,1,0:T(8,128)(2,1)}, u32[]{:S(2)}) copy-start(bf16[2,16,8,2048]{3,2,1,0:T(8,128)(2,1)} %param.3) | copy-start | bytes 3145732
  2.4 27.6 %collective-permute-start.1 = (bf16[2,2,64,2048]{3,2,1,0:T(8,128)(2,1)S(1)}, bf16[2,2,64,2048]{3,2,1,0:T(8,128)(2,1)S(1)}, u32[]{:S(2)}, u32[]{:S(2)}) collective-permute-start(bf16[2,2,64,2048]{3,2,1,0:T(8,128)(2,1)S(1)} %get-tuple-element.37), channel_id=1, source_target_pairs={{0,2},{2,4},{4,6},{1,3},{3,5},{5,7},{8,10},{10,12},{12,14},{9,11},... | collective-permute-start | bytes 3145736 | tf_op jit(solution)/shard_map/ppermute | solution.py:372
  7.0 27.2 %collective-permute-start.2 = (bf16[2,2,64,2048]{3,2,1,0:T(8,128)(2,1)S(1)}, bf16[2,2,64,2048]{3,2,1,0:T(8,128)(2,1)S(1)}, u32[]{:S(2)}, u32[]{:S(2)}) collective-permute-start(bf16[2,2,64,2048]{3,2,1,0:T(8,128)(2,1)S(1)} %get-tuple-element.38), channel_id=1, source_target_pairs={{2,0},{4,2},{6,4},{3,1},{5,3},{7,5},{10,8},{12,10},{14,12},{11,9},... | collective-permute-start | bytes 3145736 | tf_op jit(solution)/shard_map/ppermute | solution.py:373
  8.3 14.0 %collective-permute-start.4 = (bf16[2,64,2048]{2,1,0:T(8,128)(2,1)S(1)}, bf16[2,64,2048]{2,1,0:T(8,128)(2,1)S(1)}, u32[]{:S(2)}, u32[]{:S(2)}) collective-permute-start(bf16[2,64,2048]{2,1,0:T(8,128)(2,1)S(1)} %get-tuple-element.40), channel_id=1, source_target_pairs={{0,24},{8,16},{16,8},{24,0},{1,25},{9,17},{17,9},{25,1},{2,26},{10... | collective-permute-start | bytes 1572872 | tf_op jit(solution)/shard_map/ppermute | solution.py:374
  9.6 24.5 %collective-permute-start.3 = (bf16[2,64,2048]{2,1,0:T(8,128)(2,1)S(1)}, bf16[2,64,2048]{2,1,0:T(8,128)(2,1)S(1)}, u32[]{:S(2)}, u32[]{:S(2)}) collective-permute-start(bf16[2,64,2048]{2,1,0:T(8,128)(2,1)S(1)} %get-tuple-element.39), channel_id=1, source_target_pairs={{0,24},{8,16},{16,8},{24,0},{1,25},{9,17},{17,9},{25,1},{2,26},{10... | collective-permute-start | bytes 1572872 | tf_op jit(solution)/shard_map/ppermute | solution.py:376
  10.1 30.0 %collective-permute-start.9 = (bf16[2,128,2048]{2,1,0:T(8,128)(2,1)S(1)}, bf16[2,128,2048]{2,1,0:T(8,128)(2,1)S(1)}, u32[]{:S(2)}, u32[]{:S(2)}) collective-permute-start(bf16[2,128,2048]{2,1,0:T(8,128)(2,1)S(1)} %bitcast.9), channel_id=1, source_target_pairs={{0,1},{1,0},{2,3},{3,2},{4,5},{5,4},{6,7},{7,6},{8,9},{9,8},{10,11... | collective-permute-start | bytes 3145736 | tf_op jit(solution)/shard_map/ppermute | solution.py:377
  34.1 7.0 %collective-permute-start.7 = (bf16[2,2,64,2048]{3,2,1,0:T(8,128)(2,1)S(1)}, bf16[2,2,64,2048]{3,2,1,0:T(8,128)(2,1)S(1)}, u32[]{:S(2)}, u32[]{:S(2)}) collective-permute-start(bf16[2,2,64,2048]{3,2,1,0:T(8,128)(2,1)S(1)} %collective-permute-done.1.top_ref), channel_id=1, source_target_pairs={{0,8},{8,0},{16,24},{24,16},{1,9},{9,1},{17,25},{25,17},{2,10},{10... | collective-permute-start | bytes 3145736 | tf_op jit(solution)/shard_map/ppermute | solution.py:379
  34.1 7.7 %collective-permute-start.8 = (bf16[2,2,64,2048]{3,2,1,0:T(8,128)(2,1)S(1)}, bf16[2,2,64,2048]{3,2,1,0:T(8,128)(2,1)S(1)}, u32[]{:S(2)}, u32[]{:S(2)}) collective-permute-start(bf16[2,2,64,2048]{3,2,1,0:T(8,128)(2,1)S(1)} %collective-permute-done.2.bottom_ref), channel_id=1, source_target_pairs={{0,8},{8,0},{16,24},{24,16},{1,9},{9,1},{17,25},{25,17},{2,10},{10... | collective-permute-start | bytes 3145736 | tf_op jit(solution)/shard_map/ppermute | solution.py:380
  34.7 18.4 %collective-permute-start.11 = (bf16[2,64,2048]{2,1,0:T(8,128)(2,1)S(1)}, bf16[2,64,2048]{2,1,0:T(8,128)(2,1)S(1)}, u32[]{:S(2)}, u32[]{:S(2)}) collective-permute-start(bf16[2,64,2048]{2,1,0:T(8,128)(2,1)S(1)} %collective-permute-done.4.refs_1_.cross_last_ref), channel_id=1, source_target_pairs={{0,2},{2,4},{4,6},{1,3},{3,5},{5,7},{8,10},{10,12},{12,14},{9,11},... | collective-permute-start | bytes 1572872 | tf_op jit(solution)/shard_map/ppermute | solution.py:381
  38.7 15.7 %collective-permute-start.12 = (bf16[2,64,2048]{2,1,0:T(8,128)(2,1)S(1)}, bf16[2,64,2048]{2,1,0:T(8,128)(2,1)S(1)}, u32[]{:S(2)}, u32[]{:S(2)}) collective-permute-start(bf16[2,64,2048]{2,1,0:T(8,128)(2,1)S(1)} %collective-permute-done.3.refs_0_.cross_first_ref), channel_id=1, source_target_pairs={{2,0},{4,2},{6,4},{3,1},{5,3},{7,5},{10,8},{12,10},{14,12},{11,9},... | collective-permute-start | bytes 1572872 | tf_op jit(solution)/shard_map/ppermute | solution.py:382
  40.0 26.0 %collective-permute-start.5 = (bf16[128,2048]{1,0:T(8,128)(2,1)S(1)}, bf16[128,2048]{1,0:T(8,128)(2,1)S(1)}, u32[]{:S(2)}, u32[]{:S(2)}) collective-permute-start(bf16[128,2048]{1,0:T(8,128)(2,1)S(1)} %get-tuple-element.45), channel_id=1, source_target_pairs={{0,24},{8,16},{16,8},{24,0},{1,25},{9,17},{17,9},{25,1},{2,26},{10... | collective-permute-start | bytes 1572872 | tf_op jit(solution)/shard_map/ppermute | solution.py:383
  41.2 24.8 %collective-permute-start.6 = (bf16[128,2048]{1,0:T(8,128)(2,1)S(1)}, bf16[128,2048]{1,0:T(8,128)(2,1)S(1)}, u32[]{:S(2)}, u32[]{:S(2)}) collective-permute-start(bf16[128,2048]{1,0:T(8,128)(2,1)S(1)} %get-tuple-element.46), channel_id=1, source_target_pairs={{0,24},{8,16},{16,8},{24,0},{1,25},{9,17},{17,9},{25,1},{2,26},{10... | collective-permute-start | bytes 1572872 | tf_op jit(solution)/shard_map/ppermute | solution.py:383
  46.7 19.3 %collective-permute-start.10 = (bf16[128,2176]{1,0:T(8,128)(2,1)S(1)}, bf16[128,2176]{1,0:T(8,128)(2,1)S(1)}, u32[]{:S(2)}, u32[]{:S(2)}) collective-permute-start(bf16[128,2176]{1,0:T(8,128)(2,1)S(1)} %shard_map.38), channel_id=1, source_target_pairs={{0,1},{1,0},{2,3},{3,2},{4,5},{5,4},{6,7},{7,6},{8,9},{9,8},{10,11... | collective-permute-start | bytes 1671176 | tf_op jit(solution)/shard_map/ppermute | solution.py:387
  59.5 10.8 %copy-start.2 = (s32[2,2,1,2]{3,2,1,0:T(1,128)S(1)}, s32[2,2,1,2]{3,2,1,0:T(1,128)}, u32[]{:S(2)}) copy-start(s32[2,2,1,2]{3,2,1,0:T(1,128)} %far_ref.1) | copy-start | bytes 100
  59.5 19.2 %collective-permute-start.17 = (bf16[128,2176]{1,0:T(8,128)(2,1)S(1)}, bf16[128,2176]{1,0:T(8,128)(2,1)S(1)}, u32[]{:S(2)}, u32[]{:S(2)}) collective-permute-start(bf16[128,2176]{1,0:T(8,128)(2,1)S(1)} %shard_map.40), channel_id=1, source_target_pairs={{0,1},{1,0},{2,3},{3,2},{4,5},{5,4},{6,7},{7,6},{8,9},{9,8},{10,11... | collective-permute-start | bytes 1671176 | tf_op jit(solution)/shard_map/ppermute | solution.py:394
  66.0 2.0 %collective-permute-start.13 = (bf16[2,64,2048]{2,1,0:T(8,128)(2,1)S(1)}, bf16[2,64,2048]{2,1,0:T(8,128)(2,1)S(1)}, u32[]{:S(2)}, u32[]{:S(2)}) collective-permute-start(bf16[2,64,2048]{2,1,0:T(8,128)(2,1)S(1)} %collective-permute-done.3.refs_0_.cross_first_ref), channel_id=1, source_target_pairs={{0,8},{8,0},{16,24},{24,16},{1,9},{9,1},{17,25},{25,17},{2,10},{10... | collective-permute-start | bytes 1572872 | tf_op jit(solution)/shard_map/ppermute | solution.py:399
  66.1 2.6 %collective-permute-start.14 = (bf16[2,64,2048]{2,1,0:T(8,128)(2,1)S(1)}, bf16[2,64,2048]{2,1,0:T(8,128)(2,1)S(1)}, u32[]{:S(2)}, u32[]{:S(2)}) collective-permute-start(bf16[2,64,2048]{2,1,0:T(8,128)(2,1)S(1)} %collective-permute-done.4.refs_1_.cross_last_ref), channel_id=1, source_target_pairs={{0,8},{8,0},{16,24},{24,16},{1,9},{9,1},{17,25},{25,17},{2,10},{10... | collective-permute-start | bytes 1572872 | tf_op jit(solution)/shard_map/ppermute | solution.py:400
  66.6 2.9 %collective-permute-start.15 = (bf16[128,2048]{1,0:T(8,128)(2,1)S(1)}, bf16[128,2048]{1,0:T(8,128)(2,1)S(1)}, u32[]{:S(2)}, u32[]{:S(2)}) collective-permute-start(bf16[128,2048]{1,0:T(8,128)(2,1)S(1)} %collective-permute-done.5.refs_0_), channel_id=1, source_target_pairs={{0,8},{8,0},{16,24},{24,16},{1,9},{9,1},{17,25},{25,17},{2,10},{10... | collective-permute-start | bytes 1572872 | tf_op jit(solution)/shard_map/ppermute | solution.py:401
  66.7 3.6 %collective-permute-start.16 = (bf16[128,2048]{1,0:T(8,128)(2,1)S(1)}, bf16[128,2048]{1,0:T(8,128)(2,1)S(1)}, u32[]{:S(2)}, u32[]{:S(2)}) collective-permute-start(bf16[128,2048]{1,0:T(8,128)(2,1)S(1)} %collective-permute-done.6.refs_1_), channel_id=1, source_target_pairs={{0,8},{8,0},{16,24},{24,16},{1,9},{9,1},{17,25},{25,17},{2,10},{10... | collective-permute-start | bytes 1572872 | tf_op jit(solution)/shard_map/ppermute | solution.py:401

commit v7 on v6

v7 whole, which is shorter than its diff:
```python
import functools

import jax
import jax.numpy as jnp
from jax import lax
from jax.experimental import pallas as pl
from jax.experimental.pallas import tpu as pltpu
from jax.sharding import PartitionSpec as P

TILE = 8
HEADS = 16
HD = 128
NFAR = 2
SPOT = TILE * TILE
NEGATIVE = -1e30
EXP_SCALE = HD ** (-0.5) * 1.4426950408889634
VMEM_LIMIT = 16 * 1024 * 1024
GROUP = 4
FINISH_COST = 1
LATE_COST = 8 << 30


def contract_last(left, right):
    return lax.dot_general(left, right, (((1,), (1,)), ((), ())), preferred_element_type=jnp.float32)


def lane_index(rows):
    return lax.broadcasted_iota(jnp.int32, (rows, HD), 1)


def split_sums(value):
    high = value.astype(jnp.bfloat16).astype(jnp.float32)
    rest = value - high
    middle = rest.astype(jnp.bfloat16).astype(jnp.float32)
    low = rest - middle
    return (high + pltpu.roll(middle, HEADS, 1) + pltpu.roll(low, 2 * HEADS, 1)).astype(jnp.bfloat16)


def join_sums(value):
    terms = value.astype(jnp.float32)
    return terms + (pltpu.roll(terms, HD - HEADS, 1) + pltpu.roll(terms, HD - 2 * HEADS, 1))


def kernel_cost(flops):
    return pl.CostEstimate(flops=flops, bytes_accessed=1, transcendentals=0)


def cut_kernel(keyvals_ref, last_rows_ref, first_rows_ref, outer_last_ref, outer_first_ref, *refs):
    inner_last_ref, inner_first_ref, sems = refs
    outer = lax.axis_index("ta") % 2
    first, last = pl.ds(0, SPOT), pl.ds(SPOT, SPOT)
    pieces = [
        (keyvals_ref.at[:, :, last], last_rows_ref),
        (keyvals_ref.at[:, :, first], first_rows_ref),
        (keyvals_ref.at[:, outer, last], outer_last_ref),
        (keyvals_ref.at[:, outer, first], outer_first_ref),
        (keyvals_ref.at[:, 1 - outer, last], inner_last_ref),
        (keyvals_ref.at[:, 1 - outer, first], inner_first_ref),
    ]
    copies = [pltpu.make_async_copy(source, target, sems.at[i]) for i, (source, target) in enumerate(pieces)]
    for copy in copies:
        copy.start()
    for copy in copies:
        copy.wait()


def cut(keyvals):
    two, frames, tokens, features = keyvals.shape
    shapes = [(two, frames, SPOT, features)] * 2 + [(two, SPOT, features)] * 4
    return pl.pallas_call(
        cut_kernel,
        out_shape=[jax.ShapeDtypeStruct(shape, keyvals.dtype) for shape in shapes],
        in_specs=[pl.BlockSpec(memory_space=pl.ANY)],
        out_specs=[pl.BlockSpec(memory_space=pltpu.VMEM)] * 6,
        scratch_shapes=[pltpu.SemaphoreType.DMA((6,))],
        compiler_params=pltpu.CompilerParams(vmem_limit_bytes=VMEM_LIMIT),
        cost_estimate=kernel_cost(1),
    )(keyvals)


def near_kernel(sides, home, early, has_rows, own_ref, top_ref, bottom_ref, *refs):
    parity = lax.axis_index("ta") % 2
    ha = lax.axis_index("ha")
    valid = (ha > 0, ha < has_rows - 1)
    if early:
        ext_ref, ext_top_ref, ext_bottom_ref, refs = refs[0], refs[1], refs[2], refs[3:]
        frame = 1 - parity
    else:
        ext_first_ref, ext_last_ref, ext_top_ref, ext_bottom_ref, refs = refs[0], refs[1], refs[2], refs[3], refs[4:]
        frame = parity
    count = sides + home
    q_refs, out_refs, peak_ref, total_ref = refs[:count], refs[count:-2], refs[-2], refs[-1]
    group = pl.program_id(0)
    half = count * SPOT

    def middle(kind, lanes):
        parts = [own_ref[kind, 0, :, lanes], own_ref[kind, 1, :, lanes]]
        if early:
            parts.append(ext_ref[kind, parity, :, lanes])
        else:
            parts += [ext_first_ref[kind, :, lanes], ext_last_ref[kind, :, lanes]]
        return jnp.concatenate(parts, axis=0)

    def halo(a, kind, lanes):
        ref, ext = ((top_ref, ext_top_ref), (bottom_ref, ext_bottom_ref))[a]
        third = ext[kind, parity, :, lanes] if early else ext[kind, :, lanes]
        return jnp.concatenate([ref[kind, 0, :, lanes], ref[kind, 1, :, lanes], third], axis=0)

    members = [slice(i * HD, (i + 1) * HD) for i in range(GROUP)]
    scores = []
    for lanes in members:
        queries = [
            jnp.concatenate([ref[frame, a * SPOT : (a + 1) * SPOT, lanes] for ref in q_refs], axis=0) for a in range(2)
        ]
        near = contract_last(jnp.concatenate(queries, axis=0), middle(0, lanes))
        edges = [contract_last(queries[a], halo(a, 0, lanes)) for a in range(2)]
        scores.append([(near[a * half : (a + 1) * half], edges[a]) for a in range(2)])
    weights = []
    for pairs in scores:
        for a, (near, edge) in enumerate(pairs):
            best = functools.reduce(jnp.maximum, [near[:, i * HD : (i + 1) * HD] for i in range(3)])
            edge_best = jnp.maximum(edge[:, : 2 * SPOT], jnp.concatenate([edge[:, 2 * SPOT :]] * 2, axis=1))
            best = jnp.maximum(best, jnp.where(valid[a], edge_best, NEGATIVE))
            peak = jnp.max(best, axis=-1, keepdims=True)
            shift = jnp.where(valid[a], peak, -NEGATIVE)
            near = jnp.exp2((near - peak) * EXP_SCALE)
            edge = jnp.exp2((edge - shift) * EXP_SCALE)
            total = functools.reduce(jnp.add, [near[:, i * HD : (i + 1) * HD] for i in range(3)] + [edge[:, :HD]])
            total = jnp.sum(total, axis=-1, keepdims=True) + jnp.sum(edge[:, HD:], axis=-1, keepdims=True)
            weights.append((peak, total, near.astype(jnp.bfloat16), edge.astype(jnp.bfloat16)))
    peaks = [jnp.zeros((half, HD), jnp.float32) for _ in range(2)]
    totals = [jnp.zeros((half, HD), jnp.float32) for _ in range(2)]
    for i, lanes in enumerate(members):
        mask = lane_index(half) == group * GROUP + i
        at = pl.ds(pl.multiple_of((group * GROUP + i) * HD, HD), HD)
        middle_values = middle(1, lanes)
        for a in range(2):
            peak, total, near, edge = weights[2 * i + a]
            summed = jnp.dot(near, middle_values, preferred_element_type=jnp.float32)
            summed = summed + jnp.dot(edge, halo(a, 1, lanes), preferred_element_type=jnp.float32)
            peaks[a] = jnp.where(mask, peak, peaks[a])
            totals[a] = jnp.where(mask, total, totals[a])
            inverse = 1.0 / total
            for s in range(count):
                rows = slice(s * SPOT, (s + 1) * SPOT)
                result = summed[rows]
                if s < sides:
                    result = result * inverse[rows]
                out_refs[s][a * SPOT : (a + 1) * SPOT, at] = result.astype(out_refs[s].dtype)

    @pl.when(group == 0)
    def _():
        peak_ref[...] = jnp.zeros_like(peak_ref)
        total_ref[...] = jnp.zeros_like(total_ref)

    for a in range(2):
        for s in range(count):
            rows = slice(s * SPOT, (s + 1) * SPOT)
            peak_ref[s, a * SPOT : (a + 1) * SPOT, :] += peaks[a][rows] * EXP_SCALE
            total_ref[s, a * SPOT : (a + 1) * SPOT, :] += totals[a][rows]

    @pl.when(group == pl.num_programs(0) - 1)
    def _():
        for s in range(sides):
            heads = lane_index(2 * SPOT) < HEADS
            out_refs[s][:, HEADS * HD :] = split_sums(
                jnp.where(heads, peak_ref[s] + jnp.log2(jnp.where(heads, total_ref[s], 1.0)), 0.0)
            )
        if home:
            out_refs[sides + 1][...] = peak_ref[sides]
            out_refs[sides + 2][...] = total_ref[sides]


def near_attention(early, has_rows, own, top, bottom, third, visitors, queries, cost):
    home = len(queries)
    tokens, features = own.shape[2:]
    width = GROUP * HD
    operands = [own, top, bottom, *third, *visitors, *queries]
    outs = [jax.ShapeDtypeStruct((tokens, features + HD), jnp.bfloat16) for _ in visitors]
    for _ in queries:
        outs += [jax.ShapeDtypeStruct((tokens, lanes), jnp.float32) for lanes in (features, HD, HD)]

    def lanes_of_group(value):
        lead = value.ndim - 1
        return pl.BlockSpec(value.shape[:-1] + (width,), lambda g: (0,) * lead + (g,))

    return pl.pallas_call(
        functools.partial(near_kernel, len(visitors), home, early, has_rows),
        out_shape=outs,
        grid=(HEADS // GROUP,),
        in_specs=[lanes_of_group(value) for value in operands],
        out_specs=[pl.BlockSpec(out.shape, lambda g: (0, 0)) for out in outs],
        scratch_shapes=[pltpu.VMEM((len(visitors) + home, tokens, HD), jnp.float32)] * 2,
        compiler_params=pltpu.CompilerParams(vmem_limit_bytes=VMEM_LIMIT),
        cost_estimate=kernel_cost(cost),
    )(*operands)


def far_kernel(members, far_ref, q_ref, core_ref, *refs):
    cross, cross_inner, corner, corner_inner = refs[:2], refs[2:4], refs[4:6], refs[6:8]
    near_refs, (out_ref, peak_ref, total_ref, held, sems) = (refs[8:11], refs[11:14]), refs[14:]
    ta = lax.axis_index("ta")
    parity = ta % 2

    def tile_copy(source, tile, j, slot, group):
        lanes = pl.ds(group * GROUP * HD, GROUP * HD)
        target = held.at[:, tile, pl.ds(j * SPOT, SPOT), lanes]
        return pltpu.make_async_copy(source.at[:, :, lanes], target, sems.at[slot, group])

    for f in range(2):
        for a in range(2):
            rows = pl.ds(a * SPOT, SPOT)
            for j in range(NFAR):
                slot = (f * 2 + a) * NFAR + j
                wanted = far_ref[f, a, 0, j]
                owner, place = wanted // 2, wanted % 2
                inner = place != owner % 2
                is_core, is_cross = owner == ta + 1 - 2 * parity, owner == members - 1 - ta
                is_corner = jnp.logical_not(jnp.logical_or(is_core, is_cross))
                sources = [
                    (jnp.logical_and(is_core, place == 0), core_ref.at[:, 0, rows]),
                    (jnp.logical_and(is_core, place == 1), core_ref.at[:, 1, rows]),
                    (jnp.logical_and(is_cross, jnp.logical_not(inner)), cross[a]),
                    (jnp.logical_and(is_cross, inner), cross_inner[a]),
                    (jnp.logical_and(is_corner, jnp.logical_not(inner)), corner[a]),
                    (jnp.logical_and(is_corner, inner), corner_inner[a]),
                ]
                for chosen, source in sources:

                    @pl.when(chosen)
                    def _(source=source, f=f, a=a, j=j, slot=slot):
                        for group in range(HEADS // GROUP):
                            tile_copy(source, f * 2 + a, j, slot, group).start()

    units = [(early, a) for early in range(2) for a in range(2)]
    frames = (1 - parity, parity)
    collected = [(jnp.zeros((SPOT, HD), jnp.float32), jnp.zeros((SPOT, HD), jnp.float32)) for _ in units]
    for first in range(0, HEADS, GROUP):
        for slot in range(4 * NFAR):
            tile_copy(cross[0], slot // NFAR, slot % NFAR, slot, first // GROUP).wait()
        work = [(h, u) for h in range(first, first + GROUP) for u in range(len(units))]
        scores = []
        for h, u in work:
            early, a = units[u]
            frame, lanes = frames[early], slice(h * HD, (h + 1) * HD)
            queries = q_ref[frame, a * SPOT : (a + 1) * SPOT, lanes]
            scores.append(contract_last(queries, held[0, frame * 2 + a, :, lanes]))
        weights = []
        for (h, u), value in zip(work, scores):
            early, a = units[u]
            near_peak = near_refs[early][1][a * SPOT : (a + 1) * SPOT, h : h + 1]
            value = value * EXP_SCALE
            peak = jnp.maximum(jnp.max(value, axis=-1, keepdims=True), near_peak)
            value = jnp.exp2(value - peak)
            total = jnp.sum(value, axis=-1, keepdims=True)
            weights.append((peak, jnp.exp2(near_peak - peak), total, value.astype(jnp.bfloat16)))
        for (h, u), (peak, near_scale, total, weight) in zip(work, weights):
            early, a = units[u]
            frame, lanes, tokens = frames[early], slice(h * HD, (h + 1) * HD), slice(a * SPOT, (a + 1) * SPOT)
            summed = jnp.dot(weight, held[1, frame * 2 + a, :, lanes], preferred_element_type=jnp.float32)
            total = total + near_scale * near_refs[early][2][tokens, h : h + 1]
            out_ref[early, tokens, lanes] = summed + near_scale * near_refs[early][0][tokens, lanes]
            mask = lane_index(SPOT) == h
            collected[u] = jnp.where(mask, peak, collected[u][0]), jnp.where(mask, total, collected[u][1])
    for (early, a), (peak, total) in zip(units, collected):
        peak_ref[early, a * SPOT : (a + 1) * SPOT, :] = peak
        total_ref[early, a * SPOT : (a + 1) * SPOT, :] = total


def far_attention(members, far_frames, queries, buffers, near):
    tokens, features = queries.shape[1:]
    in_vmem = pl.BlockSpec(memory_space=pltpu.VMEM)
    in_specs = [pl.BlockSpec(memory_space=pltpu.SMEM), in_vmem]
    in_specs += [pl.BlockSpec(memory_space=pl.ANY)] * len(buffers) + [in_vmem] * len(near)
    return pl.pallas_call(
        functools.partial(far_kernel, members),
        out_shape=[jax.ShapeDtypeStruct((2, tokens, lanes), jnp.float32) for lanes in (features, HD, HD)],
        in_specs=in_specs,
        out_specs=[in_vmem] * 3,
        scratch_shapes=[
            pltpu.VMEM((2, 4, NFAR * SPOT, features), jnp.bfloat16),
            pltpu.SemaphoreType.DMA((4 * NFAR, HEADS // GROUP)),
        ],
        compiler_params=pltpu.CompilerParams(vmem_limit_bytes=VMEM_LIMIT),
        cost_estimate=kernel_cost(1),
    )(far_frames, queries, *buffers, *near)


def finish_kernel(sides, columns, early, own_ref, own_peak_ref, own_total_ref, *refs):
    parts, refs = refs[:sides], refs[sides:]
    wa = lax.axis_index("wa")
    logs = [own_peak_ref[0]]
    for s in range(sides):
        value = join_sums(parts[s][:, HEADS * HD :])
        if columns > 2:
            value = jnp.where(wa < columns - 1 if s == 0 else wa > 0, value, NEGATIVE)
        logs.append(value)
    top = functools.reduce(jnp.maximum, logs)
    scales = [jnp.exp2(value - top) for value in logs]
    total = functools.reduce(jnp.add, [scales[0] * own_total_ref[0]] + scales[1:])
    scales = [value / total for value in scales]
    if not early:
        parity = lax.axis_index("ta") % 2
        refs[1][1 - parity] = refs[0][...]
    for h in range(HEADS):
        lanes = slice(h * HD, (h + 1) * HD)
        joined = scales[0][:, h : h + 1] * own_ref[0, :, lanes]
        for s in range(sides):
            joined = joined + scales[1 + s][:, h : h + 1] * parts[s][:, lanes].astype(jnp.float32)
        if early:
            refs[0][:, lanes] = joined.astype(jnp.bfloat16)
        else:
            refs[1][parity, :, lanes] = joined.astype(jnp.bfloat16)


def finish(columns, own, parts, early_out, cost):
    sides, rows = len(parts), 32
    frames, tokens, features = own[0].shape
    early = early_out is None
    at = 0 if early else 1
    in_specs = [
        pl.BlockSpec((1, rows, features), lambda i: (at, i, 0)),
        pl.BlockSpec((1, rows, HD), lambda i: (at, i, 0)),
        pl.BlockSpec((1, rows, HD), lambda i: (at, i, 0)),
    ]
    in_specs += [pl.BlockSpec((rows, features + HD), lambda i: (i, 0)) for _ in parts]
    one_frame = pl.BlockSpec((rows, features), lambda i: (i, 0))
    if early:
        extra, out_spec, out_shape = (), one_frame, (tokens, features)
    else:
        extra, out_spec = (early_out,), pl.BlockSpec((frames, rows, features), lambda i: (0, i, 0))
        in_specs.append(one_frame)
        out_shape = own[0].shape
    return pl.pallas_call(
        functools.partial(finish_kernel, sides, columns, early),
        out_shape=jax.ShapeDtypeStruct(out_shape, jnp.bfloat16),
        grid=(tokens // rows,),
        in_specs=in_specs,
        out_specs=out_spec,
        compiler_params=pltpu.CompilerParams(vmem_limit_bytes=VMEM_LIMIT),
        cost_estimate=kernel_cost(cost),
    )(*own, *parts, *extra)


def per_device(queries, keyvals, far_frames):
    shape = queries.shape
    frames, rows, columns, features = shape
    tokens = rows * columns
    ta_size, ha_size, wa_size = lax.axis_size("ta"), lax.axis_size("ha"), lax.axis_size("wa")
    queries = queries.reshape(frames, tokens, features)
    keyvals = keyvals.reshape(2, frames, tokens, features)

    core_pairs = [(i, i ^ 1) for i in range(ta_size)]
    cross_pairs = [(i, ta_size - 1 - i) for i in range(ta_size)]
    up = [(i, i + 1) for i in range(ha_size - 1)]
    down = [(i + 1, i) for i in range(ha_size - 1)]
    if wa_size == 2:
        ways = [([(0, 1), (1, 0)], [(0, 1), (1, 0)])]
    else:
        right = [(i, i + 1) for i in range(wa_size - 1)]
        left = [(i + 1, i) for i in range(wa_size - 1)]
        ways = [(right, left), (left, right)]
    tie = lax.optimization_barrier

    core = lax.ppermute(keyvals, "ta", core_pairs)
    last_rows, first_rows, outer_last, outer_first, *inner = cut(keyvals)
    top = lax.ppermute(last_rows, "ha", up)
    bottom = lax.ppermute(first_rows, "ha", down)
    cross_last = lax.ppermute(outer_last, "ta", cross_pairs)
    outer_first, core, sent = tie((outer_first, core, queries))
    cross_first = lax.ppermute(outer_first, "ta", cross_pairs)
    visitors = [lax.ppermute(sent, "wa", there) for there, _ in ways]
    top, bottom, cross_first, cross_last, inner = tie((top, bottom, cross_first, cross_last, inner))
    core_top = lax.ppermute(top, "ta", core_pairs)
    core_bottom = lax.ppermute(bottom, "ta", core_pairs)
    cross_top = lax.ppermute(cross_last, "ha", up)
    cross_bottom = lax.ppermute(cross_first, "ha", down)
    inner_last, inner_first = [lax.ppermute(value, "ta", cross_pairs) for value in inner]

    early_third = (core, core_top, core_bottom)
    early = near_attention(True, ha_size, keyvals, top, bottom, early_third, visitors, [], 1)
    early_parts = [lax.ppermute(result, "wa", back) for result, (_, back) in zip(early, ways)]
    core_top, _ = tie((core_top, early[0]))
    early_third = (core, core_top, core_bottom)
    early_home = near_attention(True, ha_size, keyvals, top, bottom, early_third, [], [queries], 1)
    cross_top, cross_bottom, _ = tie((cross_top, cross_bottom, early_home[1]))
    late_third = (cross_first, cross_last, cross_top, cross_bottom)
    late = near_attention(False, ha_size, keyvals, top, bottom, late_third, visitors, [queries], LATE_COST)
    late_parts = [lax.ppermute(result, "wa", back) for result, (_, back) in zip(late, ways)]
    frames_here = (cross_first, cross_last, inner_first, inner_last)
    frames_here, early_parts, _ = tie((frames_here, early_parts, late[0]))
    corner = [lax.ppermute(value, "ta", core_pairs) for value in frames_here]
    buffers = (core, *frames_here, *corner)
    own = far_attention(ta_size, far_frames, queries, buffers, (*early_home, *late[-3:]))
    out = finish(wa_size, own, early_parts, None, FINISH_COST)
    out = finish(wa_size, own, late_parts, out, 1)
    return out.reshape(shape)


def solution(mesh):
    placed = (P("ta", "ha", "wa", None), P(None, "ta", "ha", "wa", None), P("ta", "ha", "wa", None))
    return jax.shard_map(
        per_device, mesh=mesh, in_specs=placed, out_specs=P("ta", "ha", "wa", None), check_vma=False
    )
```

time: 81.3 us -> 85 us (1.046)
  Pallas kernels: 30.7 us -> 35 us
    pallas_call x1, Pallas kernels: 7.04 us -> 11.4 us  [far_attention(): pl.pallas_call(functools.partial(far_kernel, members), out_shape=[jax.Sha...]
    ppermute x1, waiting for transfers between devices: 1.33 us -> 0.01 us  [per_device(): cross_bottom = lax.ppermute(cross_first, 'ha', down)]
    ppermute x6, waiting for transfers between devices: 3.14 us -> 4.32 us  [the longest x4 3.14 us: per_device(): corner = [lax.ppermute(value, 'ta', core_pairs) for value in frames_here]]
    pallas_call x4 -> x3, Pallas kernels: 19.6 us -> 19.5 us  [near_attention(): pl.pallas_call(functools.partial(near_kernel, len(visitors), home, early,...]
  transfers between devices with their start and end apart: 18 -> 18, of which waited for: 8 -> 8; matrix products, arithmetic and copies ran while one was open for 0% -> 0% of each run, Pallas kernels for 35% -> 38%
where the time goes in v7:
time: 85 us; the launch traced here: 84.7 us
  Pallas kernels  35 us (41%)
  waiting for transfers between devices  26.9 us (32%)
  starting transfers between devices  21.2 us (25%)
  local copies, waits for them, and re-layouts  1.6 us (2%)
    pallas_call x3, Pallas kernels, near_attention(): pl.pallas_call(functools.partial(near_kernel, len(visitors), home, early,...  19.5 us
    pallas_call x1, Pallas kernels, far_attention(): pl.pallas_call(functools.partial(far_kernel, members), out_shape=[jax.Sha...  11.4 us
    ppermute x1, waiting for transfers between devices, per_device(): cross_last = lax.ppermute(outer_last, 'ta', cross_pairs)  10.6 us
    ppermute x1, waiting for transfers between devices, per_device(): top = lax.ppermute(last_rows, 'ha', up)  7.74 us
    ppermute x1, starting transfers between devices, per_device(): top = lax.ppermute(last_rows, 'ha', up)  4.54 us
    ppermute x1, waiting for transfers between devices, per_device(): bottom = lax.ppermute(first_rows, 'ha', down)  4.18 us
    ppermute x1, starting transfers between devices, per_device(): cross_top = lax.ppermute(cross_last, 'ha', up)  4.07 us
    pallas_call x2, Pallas kernels, finish(): pl.pallas_call(functools.partial(finish_kernel, sides, columns, early), o...  3.74 us
  transfers between devices with their start and end apart: 18, of which 8 were waited for; matrix products, arithmetic and copies ran while one was open for 0% of the time, Pallas kernels for 38%

profile of v7, /device:TPU:0, one launch (start us, length us, event | category | flops | bytes accessed | tf_op | source)
XLA Modules:
  0.0 84.7 jit_solution(10492861718536262233)
XLA Ops:
  0.5 1.6 %copy-done = bf16[2,2,16,8,2048]{4,3,2,1,0:T(8,128)(2,1)S(1)} copy-done((bf16[2,2,16,8,2048]{4,3,2,1,0:T(8,128)(2,1)S(1)}, bf16[2,2,16,8,2048]{4,3,2,1,0:T(8,128)(2,1)}, u32[]{:S(2)}) %copy-start) | copy-done | bytes 2097176
  2.4 4.5 %collective-permute-start.1 = (bf16[2,2,64,2048]{3,2,1,0:T(8,128)(2,1)S(1)}, bf16[2,2,64,2048]{3,2,1,0:T(8,128)(2,1)S(1)}, u32[]{:S(2)}, u32[]{:S(2)}) collective-permute-start(bf16[2,2,64,2048]{3,2,1,0:T(8,128)(2,1)S(1)} %get-tuple-element.40), channel_id=1, source_target_pairs={{0,2},{2,4},{4,6},{1,3},{3,5},{5,7},{8,10},{10,12},{12,14},{9,11},... | collective-permute-start | bytes 3145736 | tf_op jit(solution)/shard_map/ppermute | solution.py:367
  7.0 1.3 %collective-permute-start.2 = (bf16[2,2,64,2048]{3,2,1,0:T(8,128)(2,1)S(1)}, bf16[2,2,64,2048]{3,2,1,0:T(8,128)(2,1)S(1)}, u32[]{:S(2)}, u32[]{:S(2)}) collective-permute-start(bf16[2,2,64,2048]{3,2,1,0:T(8,128)(2,1)S(1)} %get-tuple-element.41), channel_id=1, source_target_pairs={{2,0},{4,2},{6,4},{3,1},{5,3},{7,5},{10,8},{12,10},{14,12},{11,9},... | collective-permute-start | bytes 3145736 | tf_op jit(solution)/shard_map/ppermute | solution.py:368
  8.3 1.4 %collective-permute-start.4 = (bf16[2,64,2048]{2,1,0:T(8,128)(2,1)S(1)}, bf16[2,64,2048]{2,1,0:T(8,128)(2,1)S(1)}, u32[]{:S(2)}, u32[]{:S(2)}) collective-permute-start(bf16[2,64,2048]{2,1,0:T(8,128)(2,1)S(1)} %get-tuple-element.43), channel_id=1, source_target_pairs={{0,24},{8,16},{16,8},{24,0},{1,25},{9,17},{17,9},{25,1},{2,26},{10... | collective-permute-start | bytes 1572872 | tf_op jit(solution)/shard_map/ppermute | solution.py:369
  10.1 1.5 %collective-permute-start.9 = (bf16[2,128,2048]{2,1,0:T(8,128)(2,1)S(1)}, bf16[2,128,2048]{2,1,0:T(8,128)(2,1)S(1)}, u32[]{:S(2)}, u32[]{:S(2)}) collective-permute-start(bf16[2,128,2048]{2,1,0:T(8,128)(2,1)S(1)} %bitcast.8), channel_id=1, source_target_pairs={{0,1},{1,0},{2,3},{3,2},{4,5},{5,4},{6,7},{7,6},{8,9},{9,8},{10,11... | collective-permute-start | bytes 3145736 | tf_op jit(solution)/shard_map/ppermute | solution.py:372
  11.6 10.6 %collective-permute-done.4.refs_1_ = bf16[2,64,2048]{2,1,0:T(8,128)(2,1)S(1)} collective-permute-done((bf16[2,64,2048]{2,1,0:T(8,128)(2,1)S(1)}, bf16[2,64,2048]{2,1,0:T(8,128)(2,1)S(1)}, u32[]{:S(2)}, u32[]{:S(2)}) %collective-permute-start.4) | collective-permute-done | bytes 524320 | tf_op jit(solution)/shard_map/ppermute | solution.py:369
  22.2 7.7 %collective-permute-done.1.top_ref = bf16[2,2,64,2048]{3,2,1,0:T(8,128)(2,1)S(1)} collective-permute-done((bf16[2,2,64,2048]{3,2,1,0:T(8,128)(2,1)S(1)}, bf16[2,2,64,2048]{3,2,1,0:T(8,128)(2,1)S(1)}, u32[]{:S(2)}, u32[]{:S(2)}) %collective-permute-start.1) | collective-permute-done | bytes 1048608 | tf_op jit(solution)/shard_map/ppermute | solution.py:367
  30.0 4.2 %collective-permute-done.2.bottom_ref = bf16[2,2,64,2048]{3,2,1,0:T(8,128)(2,1)S(1)} collective-permute-done((bf16[2,2,64,2048]{3,2,1,0:T(8,128)(2,1)S(1)}, bf16[2,2,64,2048]{3,2,1,0:T(8,128)(2,1)S(1)}, u32[]{:S(2)}, u32[]{:S(2)}) %collective-permute-start.2) | collective-permute-done | bytes 1048608 | tf_op jit(solution)/shard_map/ppermute | solution.py:368
  34.7 4.1 %collective-permute-start.11 = (bf16[2,64,2048]{2,1,0:T(8,128)(2,1)S(1)}, bf16[2,64,2048]{2,1,0:T(8,128)(2,1)S(1)}, u32[]{:S(2)}, u32[]{:S(2)}) collective-permute-start(bf16[2,64,2048]{2,1,0:T(8,128)(2,1)S(1)} %collective-permute-done.4.refs_1_), channel_id=1, source_target_pairs={{0,2},{2,4},{4,6},{1,3},{3,5},{5,7},{8,10},{10,12},{12,14},{9,11},... | collective-permute-start | bytes 1572872 | tf_op jit(solution)/shard_map/ppermute | solution.py:376
  38.7 1.3 %collective-permute-start.12 = (bf16[2,64,2048]{2,1,0:T(8,128)(2,1)S(1)}, bf16[2,64,2048]{2,1,0:T(8,128)(2,1)S(1)}, u32[]{:S(2)}, u32[]{:S(2)}) collective-permute-start(bf16[2,64,2048]{2,1,0:T(8,128)(2,1)S(1)} %collective-permute-done.3.refs_0_), channel_id=1, source_target_pairs={{2,0},{4,2},{6,4},{3,1},{5,3},{7,5},{10,8},{12,10},{14,12},{11,9},... | collective-permute-start | bytes 1572872 | tf_op jit(solution)/shard_map/ppermute | solution.py:377
  40.0 1.1 %collective-permute-start.5 = (bf16[2,64,2048]{2,1,0:T(8,128)(2,1)S(1)}, bf16[2,64,2048]{2,1,0:T(8,128)(2,1)S(1)}, u32[]{:S(2)}, u32[]{:S(2)}) collective-permute-start(bf16[2,64,2048]{2,1,0:T(8,128)(2,1)S(1)} %get-tuple-element.48), channel_id=1, source_target_pairs={{0,24},{8,16},{16,8},{24,0},{1,25},{9,17},{17,9},{25,1},{2,26},{10... | collective-permute-start | bytes 1572872 | tf_op jit(solution)/shard_map/ppermute | solution.py:378
  41.9 5.7 %shard_map.38 = bf16[128,2176]{1,0:T(8,128)(2,1)S(1)} custom-call(bf16[2,2,128,2048]{3,2,1,0:T(8,128)(2,1)S(1)} %bitcast.5, bf16[2,2,64,2048]{3,2,1,0:T(8,128)(2,1)S(1)} %collective-permute-done.1.top_ref, bf16[2,2,64,2048]{3,2,1,0:T(8,128)(2,1)S(1)} %collective-permute-done.2.bottom_ref, ...), custom_call_target="tpu_custom_call" | custom-call | flops 1 | bytes 1 | tf_op jit(solution)/shard_map/pallas_call | solution.py:187
  47.6 1.6 %collective-permute-start.10 = (bf16[128,2176]{1,0:T(8,128)(2,1)S(1)}, bf16[128,2176]{1,0:T(8,128)(2,1)S(1)}, u32[]{:S(2)}, u32[]{:S(2)}) collective-permute-start(bf16[128,2176]{1,0:T(8,128)(2,1)S(1)} %shard_map.38), channel_id=1, source_target_pairs={{0,1},{1,0},{2,3},{3,2},{4,5},{5,4},{6,7},{7,6},{8,9},{9,8},{10,11... | collective-permute-start | bytes 1671176 | tf_op jit(solution)/shard_map/ppermute | solution.py:382
  49.1 5.6 %shard_map.39 = (f32[128,2048]{1,0:T(8,128)S(1)}, f32[128,128]{1,0:T(8,128)S(1)}, f32[128,128]{1,0:T(8,128)S(1)}) custom-call(bf16[2,2,128,2048]{3,2,1,0:T(8,128)(2,1)S(1)} %bitcast.6, bf16[2,2,64,2048]{3,2,1,0:T(8,128)(2,1)S(1)} %collective-permute-done.1.top_ref, bf16[2,2,64,2048]{3,2,1,0:T(8,128)(2,1)S(1)} %collective-permute-done.2.bottom_ref, ...), custom_call_target="tpu_custom_call" | custom-call | flops 1 | bytes 1 | tf_op jit(solution)/shard_map/pallas_call | solution.py:187
  54.7 8.2 %shard_map.40 = (bf16[128,2176]{1,0:T(8,128)(2,1)S(1)}, f32[128,2048]{1,0:T(8,128)S(1)}, f32[128,128]{1,0:T(8,128)S(1)}, f32[128,128]{1,0:T(8,128)S(1)}) custom-call(bf16[2,2,128,2048]{3,2,1,0:T(8,128)(2,1)S(1)} %bitcast.7, bf16[2,2,64,2048]{3,2,1,0:T(8,128)(2,1)S(1)} %collective-permute-done.1.top_ref, ...), custom_call_target="tpu_custom_call" | custom-call | flops 8589934592 | bytes 1 | tf_op jit(solution)/shard_map/pallas_call | solution.py:187
  63.0 1.3 %collective-permute-start.17 = (bf16[128,2176]{1,0:T(8,128)(2,1)S(1)}, bf16[128,2176]{1,0:T(8,128)(2,1)S(1)}, u32[]{:S(2)}, u32[]{:S(2)}) collective-permute-start(bf16[128,2176]{1,0:T(8,128)(2,1)S(1)} %get-tuple-element.57), channel_id=1, source_target_pairs={{0,1},{1,0},{2,3},{3,2},{4,5},{5,4},{6,7},{7,6},{8,9},{9,8},{10,11... | collective-permute-start | bytes 1671176 | tf_op jit(solution)/shard_map/ppermute | solution.py:389
  64.2 1.2 %collective-permute-done.6.refs_3_ = bf16[2,64,2048]{2,1,0:T(8,128)(2,1)S(1)} collective-permute-done((bf16[2,64,2048]{2,1,0:T(8,128)(2,1)S(1)}, bf16[2,64,2048]{2,1,0:T(8,128)(2,1)S(1)}, u32[]{:S(2)}, u32[]{:S(2)}) %collective-permute-start.6) | collective-permute-done | bytes 524320 | tf_op jit(solution)/shard_map/ppermute | solution.py:378
  66.4 0.9 %collective-permute-done.13.refs_4_ = bf16[2,64,2048]{2,1,0:T(8,128)(2,1)S(1)} collective-permute-done((bf16[2,64,2048]{2,1,0:T(8,128)(2,1)S(1)}, bf16[2,64,2048]{2,1,0:T(8,128)(2,1)S(1)}, u32[]{:S(2)}, u32[]{:S(2)}) %collective-permute-start.13) | collective-permute-done | bytes 524320 | tf_op jit(solution)/shard_map/ppermute | solution.py:392
  67.3 0.7 collective-permute-done.14.refs_5_
  68.1 0.7 collective-permute-done.15.refs_6_
  68.8 0.7 collective-permute-done.16.refs_7_
  69.6 11.4 %shard_map.41 = (f32[2,128,2048]{2,1,0:T(8,128)S(1)}, f32[2,128,128]{2,1,0:T(8,128)S(1)}, f32[2,128,128]{2,1,0:T(8,128)S(1)}) custom-call(s32[2,2,1,2]{3,2,1,0:T(1,128)S(1)} %copy-done.2, bf16[2,128,2048]{2,1,0:T(8,128)(2,1)S(1)} %bitcast.11, bf16[2,2,128,2048]{3,2,1,0:T(8,128)(2,1)S(1)} %collective-permute-done.refs_0_.core_ref, ...), custom_call_target="tpu_custom_call" | custom-call | flops 1 | bytes 1 | tf_op jit(solution)/shard_map/pallas_call | solution.py:275
  81.0 1.3 %shard_map.42.refs_1_ = bf16[128,2048]{1,0:T(8,128)(2,1)S(1)} custom-call(f32[2,128,2048]{2,1,0:T(8,128)S(1)} %get-tuple-element.67.own_ref, f32[2,128,128]{2,1,0:T(8,128)S(1)} %get-tuple-element.68.own_peak_ref, f32[2,128,128]{2,1,0:T(8,128)S(1)} %get-tuple-element.69.own_total_ref, bf16[128,2176]{1,0:T(8,128)(2,1)S(1)} %collective-permute-done.10.refs_0_), custom_call_target="tpu_custom_call" | custom-call | flops 1 | bytes 1 | tf_op jit(solution)/shard_map/pallas_call | solution.py:334
  82.3 2.4 %shard_map.43 = bf16[2,128,2048]{2,1,0:T(8,128)(2,1)} custom-call(f32[2,128,2048]{2,1,0:T(8,128)S(1)} %get-tuple-element.67.own_ref, f32[2,128,128]{2,1,0:T(8,128)S(1)} %get-tuple-element.68.own_peak_ref, f32[2,128,128]{2,1,0:T(8,128)S(1)} %get-tuple-element.69.own_total_ref, bf16[128,2176]{1,0:T(8,128)(2,1)S(1)} %collective-permute-done.17.refs_0_, ...), custom_call_target="tpu_custom_call" | custom-call | flops 1 | bytes 1 | tf_op jit(solution)/shard_map/pallas_call | solution.py:334
  (25 shorter events, 3.5 us)
Async XLA Ops:
  0.0 9.6 %collective-permute-start = (bf16[2,2,128,2048]{3,2,1,0:T(8,128)(2,1)}, bf16[2,2,128,2048]{3,2,1,0:T(8,128)(2,1)S(1)}, u32[]{:S(2)}, u32[]{:S(2)}) collective-permute-start(bf16[2,2,128,2048]{3,2,1,0:T(8,128)(2,1)} %bitcast.3), channel_id=1, source_target_pairs={{0,8},{8,0},{16,24},{24,16},{1,9},{9,1},{17,25},{25,17},{2,10},{10... | collective-permute-start | bytes 6291464 | tf_op jit(solution)/shard_map/ppermute | solution.py:365
  0.5 1.6 %copy-start = (bf16[2,2,16,8,2048]{4,3,2,1,0:T(8,128)(2,1)S(1)}, bf16[2,2,16,8,2048]{4,3,2,1,0:T(8,128)(2,1)}, u32[]{:S(2)}) copy-start(bf16[2,2,16,8,2048]{4,3,2,1,0:T(8,128)(2,1)} %param.4) | copy-start | bytes 6291460
  2.0 8.0 %copy-start.1 = (bf16[2,16,8,2048]{3,2,1,0:T(8,128)(2,1)S(1)}, bf16[2,16,8,2048]{3,2,1,0:T(8,128)(2,1)}, u32[]{:S(2)}) copy-start(bf16[2,16,8,2048]{3,2,1,0:T(8,128)(2,1)} %param.3) | copy-start | bytes 3145732
  2.4 27.6 %collective-permute-start.1 = (bf16[2,2,64,2048]{3,2,1,0:T(8,128)(2,1)S(1)}, bf16[2,2,64,2048]{3,2,1,0:T(8,128)(2,1)S(1)}, u32[]{:S(2)}, u32[]{:S(2)}) collective-permute-start(bf16[2,2,64,2048]{3,2,1,0:T(8,128)(2,1)S(1)} %get-tuple-element.40), channel_id=1, source_target_pairs={{0,2},{2,4},{4,6},{1,3},{3,5},{5,7},{8,10},{10,12},{12,14},{9,11},... | collective-permute-start | bytes 3145736 | tf_op jit(solution)/shard_map/ppermute | solution.py:367
  7.0 27.2 %collective-permute-start.2 = (bf16[2,2,64,2048]{3,2,1,0:T(8,128)(2,1)S(1)}, bf16[2,2,64,2048]{3,2,1,0:T(8,128)(2,1)S(1)}, u32[]{:S(2)}, u32[]{:S(2)}) collective-permute-start(bf16[2,2,64,2048]{3,2,1,0:T(8,128)(2,1)S(1)} %get-tuple-element.41), channel_id=1, source_target_pairs={{2,0},{4,2},{6,4},{3,1},{5,3},{7,5},{10,8},{12,10},{14,12},{11,9},... | collective-permute-start | bytes 3145736 | tf_op jit(solution)/shard_map/ppermute | solution.py:368
  8.3 14.0 %collective-permute-start.4 = (bf16[2,64,2048]{2,1,0:T(8,128)(2,1)S(1)}, bf16[2,64,2048]{2,1,0:T(8,128)(2,1)S(1)}, u32[]{:S(2)}, u32[]{:S(2)}) collective-permute-start(bf16[2,64,2048]{2,1,0:T(8,128)(2,1)S(1)} %get-tuple-element.43), channel_id=1, source_target_pairs={{0,24},{8,16},{16,8},{24,0},{1,25},{9,17},{17,9},{25,1},{2,26},{10... | collective-permute-start | bytes 1572872 | tf_op jit(solution)/shard_map/ppermute | solution.py:369
  9.6 24.5 %collective-permute-start.3 = (bf16[2,64,2048]{2,1,0:T(8,128)(2,1)S(1)}, bf16[2,64,2048]{2,1,0:T(8,128)(2,1)S(1)}, u32[]{:S(2)}, u32[]{:S(2)}) collective-permute-start(bf16[2,64,2048]{2,1,0:T(8,128)(2,1)S(1)} %get-tuple-element.42), channel_id=1, source_target_pairs={{0,24},{8,16},{16,8},{24,0},{1,25},{9,17},{17,9},{25,1},{2,26},{10... | collective-permute-start | bytes 1572872 | tf_op jit(solution)/shard_map/ppermute | solution.py:371
  10.1 30.0 %collective-permute-start.9 = (bf16[2,128,2048]{2,1,0:T(8,128)(2,1)S(1)}, bf16[2,128,2048]{2,1,0:T(8,128)(2,1)S(1)}, u32[]{:S(2)}, u32[]{:S(2)}) collective-permute-start(bf16[2,128,2048]{2,1,0:T(8,128)(2,1)S(1)} %bitcast.8), channel_id=1, source_target_pairs={{0,1},{1,0},{2,3},{3,2},{4,5},{5,4},{6,7},{7,6},{8,9},{9,8},{10,11... | collective-permute-start | bytes 3145736 | tf_op jit(solution)/shard_map/ppermute | solution.py:372
  34.1 7.0 %collective-permute-start.7 = (bf16[2,2,64,2048]{3,2,1,0:T(8,128)(2,1)S(1)}, bf16[2,2,64,2048]{3,2,1,0:T(8,128)(2,1)S(1)}, u32[]{:S(2)}, u32[]{:S(2)}) collective-permute-start(bf16[2,2,64,2048]{3,2,1,0:T(8,128)(2,1)S(1)} %collective-permute-done.1.top_ref), channel_id=1, source_target_pairs={{0,8},{8,0},{16,24},{24,16},{1,9},{9,1},{17,25},{25,17},{2,10},{10... | collective-permute-start | bytes 3145736 | tf_op jit(solution)/shard_map/ppermute | solution.py:374
  34.1 7.7 %collective-permute-start.8 = (bf16[2,2,64,2048]{3,2,1,0:T(8,128)(2,1)S(1)}, bf16[2,2,64,2048]{3,2,1,0:T(8,128)(2,1)S(1)}, u32[]{:S(2)}, u32[]{:S(2)}) collective-permute-start(bf16[2,2,64,2048]{3,2,1,0:T(8,128)(2,1)S(1)} %collective-permute-done.2.bottom_ref), channel_id=1, source_target_pairs={{0,8},{8,0},{16,24},{24,16},{1,9},{9,1},{17,25},{25,17},{2,10},{10... | collective-permute-start | bytes 3145736 | tf_op jit(solution)/shard_map/ppermute | solution.py:375
  34.7 20.1 %collective-permute-start.11 = (bf16[2,64,2048]{2,1,0:T(8,128)(2,1)S(1)}, bf16[2,64,2048]{2,1,0:T(8,128)(2,1)S(1)}, u32[]{:S(2)}, u32[]{:S(2)}) collective-permute-start(bf16[2,64,2048]{2,1,0:T(8,128)(2,1)S(1)} %collective-permute-done.4.refs_1_), channel_id=1, source_target_pairs={{0,2},{2,4},{4,6},{1,3},{3,5},{5,7},{8,10},{10,12},{12,14},{9,11},... | collective-permute-start | bytes 1572872 | tf_op jit(solution)/shard_map/ppermute | solution.py:376
  38.7 16.0 %collective-permute-start.12 = (bf16[2,64,2048]{2,1,0:T(8,128)(2,1)S(1)}, bf16[2,64,2048]{2,1,0:T(8,128)(2,1)S(1)}, u32[]{:S(2)}, u32[]{:S(2)}) collective-permute-start(bf16[2,64,2048]{2,1,0:T(8,128)(2,1)S(1)} %collective-permute-done.3.refs_0_), channel_id=1, source_target_pairs={{2,0},{4,2},{6,4},{3,1},{5,3},{7,5},{10,8},{12,10},{14,12},{11,9},... | collective-permute-start | bytes 1572872 | tf_op jit(solution)/shard_map/ppermute | solution.py:377
  40.0 24.2 %collective-permute-start.5 = (bf16[2,64,2048]{2,1,0:T(8,128)(2,1)S(1)}, bf16[2,64,2048]{2,1,0:T(8,128)(2,1)S(1)}, u32[]{:S(2)}, u32[]{:S(2)}) collective-permute-start(bf16[2,64,2048]{2,1,0:T(8,128)(2,1)S(1)} %get-tuple-element.48), channel_id=1, source_target_pairs={{0,24},{8,16},{16,8},{24,0},{1,25},{9,17},{17,9},{25,1},{2,26},{10... | collective-permute-start | bytes 1572872 | tf_op jit(solution)/shard_map/ppermute | solution.py:378
  41.2 24.2 %collective-permute-start.6 = (bf16[2,64,2048]{2,1,0:T(8,128)(2,1)S(1)}, bf16[2,64,2048]{2,1,0:T(8,128)(2,1)S(1)}, u32[]{:S(2)}, u32[]{:S(2)}) collective-permute-start(bf16[2,64,2048]{2,1,0:T(8,128)(2,1)S(1)} %get-tuple-element.49), channel_id=1, source_target_pairs={{0,24},{8,16},{16,8},{24,0},{1,25},{9,17},{17,9},{25,1},{2,26},{10... | collective-permute-start | bytes 1572872 | tf_op jit(solution)/shard_map/ppermute | solution.py:378
  47.6 17.9 %collective-permute-start.10 = (bf16[128,2176]{1,0:T(8,128)(2,1)S(1)}, bf16[128,2176]{1,0:T(8,128)(2,1)S(1)}, u32[]{:S(2)}, u32[]{:S(2)}) collective-permute-start(bf16[128,2176]{1,0:T(8,128)(2,1)S(1)} %shard_map.38), channel_id=1, source_target_pairs={{0,1},{1,0},{2,3},{3,2},{4,5},{5,4},{6,7},{7,6},{8,9},{9,8},{10,11... | collective-permute-start | bytes 1671176 | tf_op jit(solution)/shard_map/ppermute | solution.py:382
  54.7 14.9 %copy-start.2 = (s32[2,2,1,2]{3,2,1,0:T(1,128)S(1)}, s32[2,2,1,2]{3,2,1,0:T(1,128)}, u32[]{:S(2)}) copy-start(s32[2,2,1,2]{3,2,1,0:T(1,128)} %far_ref.1) | copy-start | bytes 100
  63.0 19.3 %collective-permute-start.17 = (bf16[128,2176]{1,0:T(8,128)(2,1)S(1)}, bf16[128,2176]{1,0:T(8,128)(2,1)S(1)}, u32[]{:S(2)}, u32[]{:S(2)}) collective-permute-start(bf16[128,2176]{1,0:T(8,128)(2,1)S(1)} %get-tuple-element.57), channel_id=1, source_target_pairs={{0,1},{1,0},{2,3},{3,2},{4,5},{5,4},{6,7},{7,6},{8,9},{9,8},{10,11... | collective-permute-start | bytes 1671176 | tf_op jit(solution)/shard_map/ppermute | solution.py:389
  65.4 1.9 %collective-permute-start.13 = (bf16[2,64,2048]{2,1,0:T(8,128)(2,1)S(1)}, bf16[2,64,2048]{2,1,0:T(8,128)(2,1)S(1)}, u32[]{:S(2)}, u32[]{:S(2)}) collective-permute-start(bf16[2,64,2048]{2,1,0:T(8,128)(2,1)S(1)} %collective-permute-done.3.refs_0_), channel_id=1, source_target_pairs={{0,8},{8,0},{16,24},{24,16},{1,9},{9,1},{17,25},{25,17},{2,10},{10... | collective-permute-start | bytes 1572872 | tf_op jit(solution)/shard_map/ppermute | solution.py:392
  65.5 2.5 %collective-permute-start.14 = (bf16[2,64,2048]{2,1,0:T(8,128)(2,1)S(1)}, bf16[2,64,2048]{2,1,0:T(8,128)(2,1)S(1)}, u32[]{:S(2)}, u32[]{:S(2)}) collective-permute-start(bf16[2,64,2048]{2,1,0:T(8,128)(2,1)S(1)} %collective-permute-done.4.refs_1_), channel_id=1, source_target_pairs={{0,8},{8,0},{16,24},{24,16},{1,9},{9,1},{17,25},{25,17},{2,10},{10... | collective-permute-start | bytes 1572872 | tf_op jit(solution)/shard_map/ppermute | solution.py:392
  65.9 2.9 %collective-permute-start.15 = (bf16[2,64,2048]{2,1,0:T(8,128)(2,1)S(1)}, bf16[2,64,2048]{2,1,0:T(8,128)(2,1)S(1)}, u32[]{:S(2)}, u32[]{:S(2)}) collective-permute-start(bf16[2,64,2048]{2,1,0:T(8,128)(2,1)S(1)} %collective-permute-done.5.refs_2_), channel_id=1, source_target_pairs={{0,8},{8,0},{16,24},{24,16},{1,9},{9,1},{17,25},{25,17},{2,10},{10... | collective-permute-start | bytes 1572872 | tf_op jit(solution)/shard_map/ppermute | solution.py:392
  66.1 3.5 %collective-permute-start.16 = (bf16[2,64,2048]{2,1,0:T(8,128)(2,1)S(1)}, bf16[2,64,2048]{2,1,0:T(8,128)(2,1)S(1)}, u32[]{:S(2)}, u32[]{:S(2)}) collective-permute-start(bf16[2,64,2048]{2,1,0:T(8,128)(2,1)S(1)} %collective-permute-done.6.refs_3_), channel_id=1, source_target_pairs={{0,8},{8,0},{16,24},{24,16},{1,9},{9,1},{17,25},{25,17},{2,10},{10... | collective-permute-start | bytes 1572872 | tf_op jit(solution)/shard_map/ppermute | solution.py:392

commit v8 on v7

--- a/solution.py
+++ b/solution.py
@@ -17,11 +17,15 @@
 VMEM_LIMIT = 16 * 1024 * 1024
 GROUP = 4
 FINISH_COST = 1
-LATE_COST = 8 << 30
+LATE_COST = 4 << 30
 
 
 def contract_last(left, right):
     return lax.dot_general(left, right, (((1,), (1,)), ((), ())), preferred_element_type=jnp.float32)
+
+
+def with_ones(values):
+    return jnp.concatenate([values, jnp.ones_like(values)], axis=1)
 
 
 def lane_index(rows):
@@ -45,8 +49,7 @@
     return pl.CostEstimate(flops=flops, bytes_accessed=1, transcendentals=0)
 
 
-def cut_kernel(keyvals_ref, last_rows_ref, first_rows_ref, outer_last_ref, outer_first_ref, *refs):
-    inner_last_ref, inner_first_ref, sems = refs
+def cut_kernel(keyvals_ref, last_rows_ref, first_rows_ref, outer_last_ref, outer_first_ref, inner_ref, sems):
     outer = lax.axis_index("ta") % 2
     first, last = pl.ds(0, SPOT), pl.ds(SPOT, SPOT)
     pieces = [
@@ -54,8 +57,7 @@
         (keyvals_ref.at[:, :, first], first_rows_ref),
         (keyvals_ref.at[:, outer, last], outer_last_ref),
         (keyvals_ref.at[:, outer, first], outer_first_ref),
-        (keyvals_ref.at[:, 1 - outer, last], inner_last_ref),
-        (keyvals_ref.at[:, 1 - outer, first], inner_first_ref),
+        (keyvals_ref.at[:, 1 - outer], inner_ref),
     ]
     copies = [pltpu.make_async_copy(source, target, sems.at[i]) for i, (source, target) in enumerate(pieces)]
     for copy in copies:
@@ -66,16 +68,40 @@
 
 def cut(keyvals):
     two, frames, tokens, features = keyvals.shape
-    shapes = [(two, frames, SPOT, features)] * 2 + [(two, SPOT, features)] * 4
+    shapes = [(two, frames, SPOT, features)] * 2 + [(two, SPOT, features)] * 2 + [(two, tokens, features)]
     return pl.pallas_call(
         cut_kernel,
         out_shape=[jax.ShapeDtypeStruct(shape, keyvals.dtype) for shape in shapes],
         in_specs=[pl.BlockSpec(memory_space=pl.ANY)],
-        out_specs=[pl.BlockSpec(memory_space=pltpu.VMEM)] * 6,
-        scratch_shapes=[pltpu.SemaphoreType.DMA((6,))],
+        out_specs=[pl.BlockSpec(memory_space=pltpu.VMEM)] * 5,
+        scratch_shapes=[pltpu.SemaphoreType.DMA((5,))],
         compiler_params=pltpu.CompilerParams(vmem_limit_bytes=VMEM_LIMIT),
         cost_estimate=kernel_cost(1),
     )(keyvals)
+
+
+def inner_rows_kernel(top_ref, bottom_ref, out_top_ref, out_bottom_ref, sems):
+    inner = 1 - lax.axis_index("ta") % 2
+    pairs = ((top_ref, out_top_ref), (bottom_ref, out_bottom_ref))
+    copies = [pltpu.make_async_copy(ref.at[:, inner], out, sems.at[i]) for i, (ref, out) in enumerate(pairs)]
+    for copy in copies:
+        copy.start()
+    for copy in copies:
+        copy.wait()
+
+
+def inner_rows(top, bottom):
+    shape = jax.ShapeDtypeStruct((top.shape[0],) + top.shape[2:], top.dtype)
+    in_vmem = pl.BlockSpec(memory_space=pltpu.VMEM)
+    return pl.pallas_call(
+        inner_rows_kernel,
+        out_shape=[shape] * 2,
+        in_specs=[in_vmem] * 2,
+        out_specs=[in_vmem] * 2,
+        scratch_shapes=[pltpu.SemaphoreType.DMA((2,))],
+        compiler_params=pltpu.CompilerParams(vmem_limit_bytes=VMEM_LIMIT),
+        cost_estimate=kernel_cost(1),
+    )(top, bottom)
 
 
 def near_kernel(sides, home, early, has_rows, own_ref, top_ref, bottom_ref, *refs):
@@ -89,8 +115,7 @@
         ext_first_ref, ext_last_ref, ext_top_ref, ext_bottom_ref, refs = refs[0], refs[1], refs[2], refs[3], refs[4:]
         frame = parity
     count = sides + home
-    q_refs, out_refs, peak_ref, total_ref = refs[:count], refs[count:-2], refs[-2], refs[-1]
-    group = pl.program_id(0)
+    q_refs, out_refs = refs[:count], refs[count:]
     half = count * SPOT
 
     def middle(kind, lanes):
@@ -103,102 +128,80 @@
 
     def halo(a, kind, lanes):
         ref, ext = ((top_ref, ext_top_ref), (bottom_ref, ext_bottom_ref))[a]
-        third = ext[kind, parity, :, lanes] if early else ext[kind, :, lanes]
-        return jnp.concatenate([ref[kind, 0, :, lanes], ref[kind, 1, :, lanes], third], axis=0)
-
-    members = [slice(i * HD, (i + 1) * HD) for i in range(GROUP)]
-    scores = []
-    for lanes in members:
-        queries = [
-            jnp.concatenate([ref[frame, a * SPOT : (a + 1) * SPOT, lanes] for ref in q_refs], axis=0) for a in range(2)
-        ]
-        near = contract_last(jnp.concatenate(queries, axis=0), middle(0, lanes))
-        edges = [contract_last(queries[a], halo(a, 0, lanes)) for a in range(2)]
-        scores.append([(near[a * half : (a + 1) * half], edges[a]) for a in range(2)])
-    weights = []
-    for pairs in scores:
-        for a, (near, edge) in enumerate(pairs):
-            best = functools.reduce(jnp.maximum, [near[:, i * HD : (i + 1) * HD] for i in range(3)])
-            edge_best = jnp.maximum(edge[:, : 2 * SPOT], jnp.concatenate([edge[:, 2 * SPOT :]] * 2, axis=1))
-            best = jnp.maximum(best, jnp.where(valid[a], edge_best, NEGATIVE))
-            peak = jnp.max(best, axis=-1, keepdims=True)
-            shift = jnp.where(valid[a], peak, -NEGATIVE)
-            near = jnp.exp2((near - peak) * EXP_SCALE)
-            edge = jnp.exp2((edge - shift) * EXP_SCALE)
-            total = functools.reduce(jnp.add, [near[:, i * HD : (i + 1) * HD] for i in range(3)] + [edge[:, :HD]])
-            total = jnp.sum(total, axis=-1, keepdims=True) + jnp.sum(edge[:, HD:], axis=-1, keepdims=True)
-            weights.append((peak, total, near.astype(jnp.bfloat16), edge.astype(jnp.bfloat16)))
+        return jnp.concatenate([ref[kind, 0, :, lanes], ref[kind, 1, :, lanes], ext[kind, :, lanes]], axis=0)
+
     peaks = [jnp.zeros((half, HD), jnp.float32) for _ in range(2)]
-    totals = [jnp.zeros((half, HD), jnp.float32) for _ in range(2)]
-    for i, lanes in enumerate(members):
-        mask = lane_index(half) == group * GROUP + i
-        at = pl.ds(pl.multiple_of((group * GROUP + i) * HD, HD), HD)
-        middle_values = middle(1, lanes)
-        for a in range(2):
-            peak, total, near, edge = weights[2 * i + a]
-            summed = jnp.dot(near, middle_values, preferred_element_type=jnp.float32)
-            summed = summed + jnp.dot(edge, halo(a, 1, lanes), preferred_element_type=jnp.float32)
-            peaks[a] = jnp.where(mask, peak, peaks[a])
-            totals[a] = jnp.where(mask, total, totals[a])
-            inverse = 1.0 / total
-            for s in range(count):
-                rows = slice(s * SPOT, (s + 1) * SPOT)
-                result = summed[rows]
-                if s < sides:
-                    result = result * inverse[rows]
-                out_refs[s][a * SPOT : (a + 1) * SPOT, at] = result.astype(out_refs[s].dtype)
-
-    @pl.when(group == 0)
-    def _():
-        peak_ref[...] = jnp.zeros_like(peak_ref)
-        total_ref[...] = jnp.zeros_like(total_ref)
-
+    totals = [jnp.ones((half, HD), jnp.float32) for _ in range(2)]
+    for first in range(0, HEADS, GROUP):
+        members = [slice(h * HD, (h + 1) * HD) for h in range(first, first + GROUP)]
+        scores = []
+        for lanes in members:
+            queries = [
+                jnp.concatenate([ref[frame, a * SPOT : (a + 1) * SPOT, lanes] for ref in q_refs], axis=0)
+                for a in range(2)
+            ]
+            near = contract_last(jnp.concatenate(queries, axis=0), middle(0, lanes))
+            edges = [contract_last(queries[a], halo(a, 0, lanes)) for a in range(2)]
+            scores.append([(near[a * half : (a + 1) * half], edges[a]) for a in range(2)])
+        weights = []
+        for pairs in scores:
+            for a, (near, edge) in enumerate(pairs):
+                best = functools.reduce(jnp.maximum, [near[:, i * HD : (i + 1) * HD] for i in range(3)])
+                edge_best = jnp.maximum(edge[:, : 2 * SPOT], jnp.concatenate([edge[:, 2 * SPOT :]] * 2, axis=1))
+                best = jnp.maximum(best, jnp.where(valid[a], edge_best, NEGATIVE))
+                peak = jnp.max(best, axis=-1, keepdims=True)
+                shift = jnp.where(valid[a], peak, -NEGATIVE)
+                near = jnp.exp2((near - peak) * EXP_SCALE).astype(jnp.bfloat16)
+                edge = jnp.exp2((edge - shift) * EXP_SCALE).astype(jnp.bfloat16)
+                weights.append((peak, near, edge))
+        for i, lanes in enumerate(members):
+            mask = lane_index(half) == first + i
+            middle_values = with_ones(middle(1, lanes))
+            for a in range(2):
+                peak, near, edge = weights[2 * i + a]
+                summed = jnp.dot(near, middle_values, preferred_element_type=jnp.float32)
+                summed = summed + jnp.dot(edge, with_ones(halo(a, 1, lanes)), preferred_element_type=jnp.float32)
+                total = summed[:, HD:]
+                peaks[a] = jnp.where(mask, peak, peaks[a])
+                totals[a] = jnp.where(mask, total, totals[a])
+                for s in range(count):
+                    rows = slice(s * SPOT, (s + 1) * SPOT)
+                    result = summed[rows, :HD]
+                    if s < sides:
+                        result = result / total[rows]
+                    out_refs[s][a * SPOT : (a + 1) * SPOT, lanes] = result.astype(out_refs[s].dtype)
     for a in range(2):
+        tokens = slice(a * SPOT, (a + 1) * SPOT)
         for s in range(count):
             rows = slice(s * SPOT, (s + 1) * SPOT)
-            peak_ref[s, a * SPOT : (a + 1) * SPOT, :] += peaks[a][rows] * EXP_SCALE
-            total_ref[s, a * SPOT : (a + 1) * SPOT, :] += totals[a][rows]
-
-    @pl.when(group == pl.num_programs(0) - 1)
-    def _():
-        for s in range(sides):
-            heads = lane_index(2 * SPOT) < HEADS
-            out_refs[s][:, HEADS * HD :] = split_sums(
-                jnp.where(heads, peak_ref[s] + jnp.log2(jnp.where(heads, total_ref[s], 1.0)), 0.0)
-            )
-        if home:
-            out_refs[sides + 1][...] = peak_ref[sides]
-            out_refs[sides + 2][...] = total_ref[sides]
+            if s < sides:
+                log_sum = peaks[a][rows] * EXP_SCALE + jnp.log2(totals[a][rows])
+                out_refs[s][tokens, HEADS * HD :] = split_sums(log_sum)
+            else:
+                out_refs[s + 1][tokens, :] = peaks[a][rows] * EXP_SCALE
+                out_refs[s + 2][tokens, :] = totals[a][rows]
 
 
 def near_attention(early, has_rows, own, top, bottom, third, visitors, queries, cost):
-    home = len(queries)
     tokens, features = own.shape[2:]
-    width = GROUP * HD
     operands = [own, top, bottom, *third, *visitors, *queries]
     outs = [jax.ShapeDtypeStruct((tokens, features + HD), jnp.bfloat16) for _ in visitors]
     for _ in queries:
         outs += [jax.ShapeDtypeStruct((tokens, lanes), jnp.float32) for lanes in (features, HD, HD)]
-
-    def lanes_of_group(value):
-        lead = value.ndim - 1
-        return pl.BlockSpec(value.shape[:-1] + (width,), lambda g: (0,) * lead + (g,))
-
+    in_vmem = pl.BlockSpec(memory_space=pltpu.VMEM)
     return pl.pallas_call(
-        functools.partial(near_kernel, len(visitors), home, early, has_rows),
+        functools.partial(near_kernel, len(visitors), len(queries), early, has_rows),
         out_shape=outs,
-        grid=(HEADS // GROUP,),
-        in_specs=[lanes_of_group(value) for value in operands],
-        out_specs=[pl.BlockSpec(out.shape, lambda g: (0, 0)) for out in outs],
-        scratch_shapes=[pltpu.VMEM((len(visitors) + home, tokens, HD), jnp.float32)] * 2,
+        in_specs=[in_vmem] * len(operands),
+        out_specs=[in_vmem] * len(outs),
         compiler_params=pltpu.CompilerParams(vmem_limit_bytes=VMEM_LIMIT),
         cost_estimate=kernel_cost(cost),
     )(*operands)
 
 
 def far_kernel(members, far_ref, q_ref, core_ref, *refs):
-    cross, cross_inner, corner, corner_inner = refs[:2], refs[2:4], refs[4:6], refs[6:8]
-    near_refs, (out_ref, peak_ref, total_ref, held, sems) = (refs[8:11], refs[11:14]), refs[14:]
+    cross, cross_inner, corner, corner_inner = refs[:2], refs[2], refs[3:5], refs[5]
+    near_refs, (out_ref, peak_ref, total_ref, held, sems) = (refs[6:9], refs[9:12]), refs[12:]
     ta = lax.axis_index("ta")
     parity = ta % 2
 
@@ -221,9 +224,9 @@
                     (jnp.logical_and(is_core, place == 0), core_ref.at[:, 0, rows]),
                     (jnp.logical_and(is_core, place == 1), core_ref.at[:, 1, rows]),
                     (jnp.logical_and(is_cross, jnp.logical_not(inner)), cross[a]),
-                    (jnp.logical_and(is_cross, inner), cross_inner[a]),
+                    (jnp.logical_and(is_cross, inner), cross_inner.at[:, rows]),
                     (jnp.logical_and(is_corner, jnp.logical_not(inner)), corner[a]),
-                    (jnp.logical_and(is_corner, inner), corner_inner[a]),
+                    (jnp.logical_and(is_corner, inner), corner_inner.at[:, rows]),
                 ]
                 for chosen, source in sources:
 
@@ -251,20 +254,21 @@
             near_peak = near_refs[early][1][a * SPOT : (a + 1) * SPOT, h : h + 1]
             value = value * EXP_SCALE
             peak = jnp.maximum(jnp.max(value, axis=-1, keepdims=True), near_peak)
-            value = jnp.exp2(value - peak)
-            total = jnp.sum(value, axis=-1, keepdims=True)
-            weights.append((peak, jnp.exp2(near_peak - peak), total, value.astype(jnp.bfloat16)))
-        for (h, u), (peak, near_scale, total, weight) in zip(work, weights):
+            weights.append((peak, jnp.exp2(near_peak - peak), jnp.exp2(value - peak).astype(jnp.bfloat16)))
+        for (h, u), (peak, near_scale, weight) in zip(work, weights):
             early, a = units[u]
             frame, lanes, tokens = frames[early], slice(h * HD, (h + 1) * HD), slice(a * SPOT, (a + 1) * SPOT)
-            summed = jnp.dot(weight, held[1, frame * 2 + a, :, lanes], preferred_element_type=jnp.float32)
-            total = total + near_scale * near_refs[early][2][tokens, h : h + 1]
-            out_ref[early, tokens, lanes] = summed + near_scale * near_refs[early][0][tokens, lanes]
+            values = with_ones(held[1, frame * 2 + a, :, lanes])
+            summed = jnp.dot(weight, values, preferred_element_type=jnp.float32)
+            total = summed[:, HD:]
+            out_ref[early, tokens, lanes] = summed[:, :HD] + near_scale * near_refs[early][0][tokens, lanes]
             mask = lane_index(SPOT) == h
             collected[u] = jnp.where(mask, peak, collected[u][0]), jnp.where(mask, total, collected[u][1])
     for (early, a), (peak, total) in zip(units, collected):
-        peak_ref[early, a * SPOT : (a + 1) * SPOT, :] = peak
-        total_ref[early, a * SPOT : (a + 1) * SPOT, :] = total
+        tokens = slice(a * SPOT, (a + 1) * SPOT)
+        near_scale = jnp.exp2(near_refs[early][1][tokens, :] - peak)
+        peak_ref[early, tokens, :] = peak
+        total_ref[early, tokens, :] = total + near_scale * near_refs[early][2][tokens, :]
 
 
 def far_attention(members, far_frames, queries, buffers, near):
@@ -363,19 +367,19 @@
     tie = lax.optimization_barrier
 
     core = lax.ppermute(keyvals, "ta", core_pairs)
-    last_rows, first_rows, outer_last, outer_first, *inner = cut(keyvals)
+    last_rows, first_rows, outer_last, outer_first, inner = cut(keyvals)
     top = lax.ppermute(last_rows, "ha", up)
     bottom = lax.ppermute(first_rows, "ha", down)
     cross_last = lax.ppermute(outer_last, "ta", cross_pairs)
     outer_first, core, sent = tie((outer_first, core, queries))
     cross_first = lax.ppermute(outer_first, "ta", cross_pairs)
     visitors = [lax.ppermute(sent, "wa", there) for there, _ in ways]
-    top, bottom, cross_first, cross_last, inner = tie((top, bottom, cross_first, cross_last, inner))
-    core_top = lax.ppermute(top, "ta", core_pairs)
-    core_bottom = lax.ppermute(bottom, "ta", core_pairs)
+    inner, cross_last = tie((inner, cross_last))
+    last = lax.ppermute(inner, "ta", cross_pairs)
+    top, bottom, cross_first, cross_last, visitors = tie((top, bottom, cross_first, cross_last, visitors))
+    core_top, core_bottom = [lax.ppermute(value, "ta", core_pairs) for value in inner_rows(top, bottom)]
     cross_top = lax.ppermute(cross_last, "ha", up)
     cross_bottom = lax.ppermute(cross_first, "ha", down)
-    inner_last, inner_first = [lax.ppermute(value, "ta", cross_pairs) for value in inner]
 
     early_third = (core, core_top, core_bottom)
     early = near_attention(True, ha_size, keyvals, top, bottom, early_third, visitors, [], 1)
@@ -383,11 +387,11 @@
     core_top, _ = tie((core_top, early[0]))
     early_third = (core, core_top, core_bottom)
     early_home = near_attention(True, ha_size, keyvals, top, bottom, early_third, [], [queries], 1)
-    cross_top, cross_bottom, _ = tie((cross_top, cross_bottom, early_home[1]))
+    cross_top, cross_bottom, last, _ = tie((cross_top, cross_bottom, last, early_home[1]))
     late_third = (cross_first, cross_last, cross_top, cross_bottom)
     late = near_attention(False, ha_size, keyvals, top, bottom, late_third, visitors, [queries], LATE_COST)
     late_parts = [lax.ppermute(result, "wa", back) for result, (_, back) in zip(late, ways)]
-    frames_here = (cross_first, cross_last, inner_first, inner_last)
+    frames_here = (cross_first, cross_last, last)
     frames_here, early_parts, _ = tie((frames_here, early_parts, late[0]))
     corner = [lax.ppermute(value, "ta", core_pairs) for value in frames_here]
     buffers = (core, *frames_here, *corner)

time: 85 us -> 80.2 us (0.944)
  Pallas kernels: 35 us -> 22.1 us
  waiting for transfers between devices: 26.9 us -> 35.9 us
  starting transfers between devices: 21.2 us -> 20.3 us
    pallas_call x3 -> x4, Pallas kernels: 19.5 us -> 11.8 us  [the longest x3 11.7 us: near_attention(): pl.pallas_call(functools.partial(near_kernel, len(visitors), len(queries)...]
    ppermute x4 -> x3, waiting for transfers between devices: 1.19 us -> 7.54 us  [the longest x1 7.54 us: per_device(): last = lax.ppermute(inner, 'ta', cross_pairs)]
    pallas_call x1, Pallas kernels: 11.4 us -> 6.23 us  [far_attention(): pl.pallas_call(functools.partial(far_kernel, members), out_shape=[jax.Sha...]
    ppermute x2, waiting for transfers between devices: 0.01 us -> 3.31 us  [per_device(): lax.ppermute(result, 'wa', back)]
    ppermute x1, waiting for transfers between devices: 7.74 us -> 4.55 us  [per_device(): top = lax.ppermute(last_rows, 'ha', up)]
    ppermute x2, starting transfers between devices: 2.84 us -> 1.07 us  [per_device(): lax.ppermute(result, 'wa', back)]
    ppermute x1, waiting for transfers between devices: 10.6 us -> 12.3 us  [per_device(): cross_last = lax.ppermute(outer_last, 'ta', cross_pairs)]
    ppermute x1, starting transfers between devices: 4.07 us -> 5.16 us  [per_device(): cross_top = lax.ppermute(cross_last, 'ha', up)]
  transfers between devices with their start and end apart: 18 -> 16, of which waited for: 8 -> 8; matrix products, arithmetic and copies ran while one was open for 0% -> 0% of each run, Pallas kernels for 38% -> 25%
where the time goes in v8:
time: 80.2 us; the launch traced here: 79.9 us
  waiting for transfers between devices  35.9 us (45%)
  Pallas kernels  22.1 us (28%)
  starting transfers between devices  20.3 us (25%)
  local copies, waits for them, and re-layouts  1.6 us (2%)
    ppermute x1, waiting for transfers between devices, per_device(): cross_last = lax.ppermute(outer_last, 'ta', cross_pairs)  12.3 us
    pallas_call x3, Pallas kernels, near_attention(): pl.pallas_call(functools.partial(near_kernel, len(visitors), len(queries)...  11.7 us
    ppermute x1, waiting for transfers between devices, per_device(): last = lax.ppermute(inner, 'ta', cross_pairs)  7.54 us
    pallas_call x1, Pallas kernels, far_attention(): pl.pallas_call(functools.partial(far_kernel, members), out_shape=[jax.Sha...  6.23 us
    ppermute x1, starting transfers between devices, per_device(): cross_top = lax.ppermute(cross_last, 'ha', up)  5.16 us
    ppermute x1, starting transfers between devices, per_device(): top = lax.ppermute(last_rows, 'ha', up)  4.68 us
    ppermute x1, waiting for transfers between devices, per_device(): top = lax.ppermute(last_rows, 'ha', up)  4.55 us
    ppermute x1, waiting for transfers between devices, per_device(): bottom = lax.ppermute(first_rows, 'ha', down)  4.18 us
  transfers between devices with their start and end apart: 16, of which 8 were waited for; matrix products, arithmetic and copies ran while one was open for 0% of the time, Pallas kernels for 25%

profile of v8, /device:TPU:0, one launch (start us, length us, event | category | flops | bytes accessed | tf_op | source)
XLA Modules:
  0.0 79.9 jit_solution(17837543112652954520)
XLA Ops:
  0.5 1.6 %copy-done = bf16[2,2,16,8,2048]{4,3,2,1,0:T(8,128)(2,1)S(1)} copy-done((bf16[2,2,16,8,2048]{4,3,2,1,0:T(8,128)(2,1)S(1)}, bf16[2,2,16,8,2048]{4,3,2,1,0:T(8,128)(2,1)}, u32[]{:S(2)}) %copy-start) | copy-done | bytes 2097176
  2.4 4.7 %collective-permute-start.1 = (bf16[2,2,64,2048]{3,2,1,0:T(8,128)(2,1)S(1)}, bf16[2,2,64,2048]{3,2,1,0:T(8,128)(2,1)S(1)}, u32[]{:S(2)}, u32[]{:S(2)}) collective-permute-start(bf16[2,2,64,2048]{3,2,1,0:T(8,128)(2,1)S(1)} %get-tuple-element.42), channel_id=1, source_target_pairs={{0,2},{2,4},{4,6},{1,3},{3,5},{5,7},{8,10},{10,12},{12,14},{9,11},... | collective-permute-start | bytes 3145736 | tf_op jit(solution)/shard_map/ppermute | solution.py:371
  7.1 1.3 %collective-permute-start.2 = (bf16[2,2,64,2048]{3,2,1,0:T(8,128)(2,1)S(1)}, bf16[2,2,64,2048]{3,2,1,0:T(8,128)(2,1)S(1)}, u32[]{:S(2)}, u32[]{:S(2)}) collective-permute-start(bf16[2,2,64,2048]{3,2,1,0:T(8,128)(2,1)S(1)} %get-tuple-element.43), channel_id=1, source_target_pairs={{2,0},{4,2},{6,4},{3,1},{5,3},{7,5},{10,8},{12,10},{14,12},{11,9},... | collective-permute-start | bytes 3145736 | tf_op jit(solution)/shard_map/ppermute | solution.py:372
  8.4 1.6 %collective-permute-start.5 = (bf16[2,128,2048]{2,1,0:T(8,128)(2,1)}, bf16[2,128,2048]{2,1,0:T(8,128)(2,1)S(1)}, u32[]{:S(2)}, u32[]{:S(2)}) collective-permute-start(bf16[2,128,2048]{2,1,0:T(8,128)(2,1)} %bitcast.8), channel_id=1, source_target_pairs={{0,1},{1,0},{2,3},{3,2},{4,5},{5,4},{6,7},{7,6},{8,9},{9,8},{10,11... | collective-permute-start | bytes 3145736 | tf_op jit(solution)/shard_map/ppermute | solution.py:376
  10.0 1.0 %collective-permute-start.4 = (bf16[2,64,2048]{2,1,0:T(8,128)(2,1)S(1)}, bf16[2,64,2048]{2,1,0:T(8,128)(2,1)S(1)}, u32[]{:S(2)}, u32[]{:S(2)}) collective-permute-start(bf16[2,64,2048]{2,1,0:T(8,128)(2,1)S(1)} %get-tuple-element.46), channel_id=1, source_target_pairs={{0,24},{8,16},{16,8},{24,0},{1,25},{9,17},{17,9},{25,1},{2,26},{10... | collective-permute-start | bytes 1572872 | tf_op jit(solution)/shard_map/ppermute | solution.py:373
  11.0 0.7 collective-permute-start.3
  11.7 12.3 %collective-permute-done.4.refs_1_ = bf16[2,64,2048]{2,1,0:T(8,128)(2,1)S(1)} collective-permute-done((bf16[2,64,2048]{2,1,0:T(8,128)(2,1)S(1)}, bf16[2,64,2048]{2,1,0:T(8,128)(2,1)S(1)}, u32[]{:S(2)}, u32[]{:S(2)}) %collective-permute-start.4) | collective-permute-done | bytes 524320 | tf_op jit(solution)/shard_map/ppermute | solution.py:373
  24.1 1.5 %collective-permute-start.8 = (bf16[2,128,2048]{2,1,0:T(8,128)(2,1)S(1)}, bf16[2,128,2048]{2,1,0:T(8,128)(2,1)S(1)}, u32[]{:S(2)}, u32[]{:S(2)}) collective-permute-start(bf16[2,128,2048]{2,1,0:T(8,128)(2,1)S(1)} %get-tuple-element.51), channel_id=1, source_target_pairs={{0,24},{8,16},{16,8},{24,0},{1,25},{9,17},{17,9},{25,1},{2,26},{10... | collective-permute-start | bytes 3145736 | tf_op jit(solution)/shard_map/ppermute | solution.py:378
  25.5 4.5 %collective-permute-done.1.top_ref = bf16[2,2,64,2048]{3,2,1,0:T(8,128)(2,1)S(1)} collective-permute-done((bf16[2,2,64,2048]{3,2,1,0:T(8,128)(2,1)S(1)}, bf16[2,2,64,2048]{3,2,1,0:T(8,128)(2,1)S(1)}, u32[]{:S(2)}, u32[]{:S(2)}) %collective-permute-start.1) | collective-permute-done | bytes 1048608 | tf_op jit(solution)/shard_map/ppermute | solution.py:371
  30.1 4.2 %collective-permute-done.2.bottom_ref = bf16[2,2,64,2048]{3,2,1,0:T(8,128)(2,1)S(1)} collective-permute-done((bf16[2,2,64,2048]{3,2,1,0:T(8,128)(2,1)S(1)}, bf16[2,2,64,2048]{3,2,1,0:T(8,128)(2,1)S(1)}, u32[]{:S(2)}, u32[]{:S(2)}) %collective-permute-start.2) | collective-permute-done | bytes 1048608 | tf_op jit(solution)/shard_map/ppermute | solution.py:372
  34.3 1.0 %collective-permute-done.3.refs_0_ = bf16[2,64,2048]{2,1,0:T(8,128)(2,1)S(1)} collective-permute-done((bf16[2,64,2048]{2,1,0:T(8,128)(2,1)S(1)}, bf16[2,64,2048]{2,1,0:T(8,128)(2,1)S(1)}, u32[]{:S(2)}, u32[]{:S(2)}) %collective-permute-start.3) | collective-permute-done | bytes 524320 | tf_op jit(solution)/shard_map/ppermute | solution.py:375
  36.0 1.4 %collective-permute-start.7 = (bf16[2,64,2048]{2,1,0:T(8,128)(2,1)S(1)}, bf16[2,64,2048]{2,1,0:T(8,128)(2,1)S(1)}, u32[]{:S(2)}, u32[]{:S(2)}) collective-permute-start(bf16[2,64,2048]{2,1,0:T(8,128)(2,1)S(1)} %collective-permute-done.3.refs_0_), channel_id=1, source_target_pairs={{2,0},{4,2},{6,4},{3,1},{5,3},{7,5},{10,8},{12,10},{14,12},{11,9},... | collective-permute-start | bytes 1572872 | tf_op jit(solution)/shard_map/ppermute | solution.py:382
  37.4 5.2 %collective-permute-start.6 = (bf16[2,64,2048]{2,1,0:T(8,128)(2,1)S(1)}, bf16[2,64,2048]{2,1,0:T(8,128)(2,1)S(1)}, u32[]{:S(2)}, u32[]{:S(2)}) collective-permute-start(bf16[2,64,2048]{2,1,0:T(8,128)(2,1)S(1)} %collective-permute-done.4.refs_1_), channel_id=1, source_target_pairs={{0,2},{2,4},{4,6},{1,3},{3,5},{5,7},{8,10},{10,12},{12,14},{9,11},... | collective-permute-start | bytes 1572872 | tf_op jit(solution)/shard_map/ppermute | solution.py:381
  42.6 3.6 %shard_map.39 = bf16[128,2176]{1,0:T(8,128)(2,1)S(1)} custom-call(bf16[2,2,128,2048]{3,2,1,0:T(8,128)(2,1)S(1)} %bitcast.5, bf16[2,2,64,2048]{3,2,1,0:T(8,128)(2,1)S(1)} %collective-permute-done.1.top_ref, bf16[2,2,64,2048]{3,2,1,0:T(8,128)(2,1)S(1)} %collective-permute-done.2.bottom_ref, ...), custom_call_target="tpu_custom_call" | custom-call | flops 1 | bytes 1 | tf_op jit(solution)/shard_map/pallas_call | solution.py:192
  46.2 0.6 collective-permute-start.11
  46.7 3.5 %shard_map.40 = (f32[128,2048]{1,0:T(8,128)S(1)}, f32[128,128]{1,0:T(8,128)S(1)}, f32[128,128]{1,0:T(8,128)S(1)}) custom-call(bf16[2,2,128,2048]{3,2,1,0:T(8,128)(2,1)S(1)} %bitcast.6, bf16[2,2,64,2048]{3,2,1,0:T(8,128)(2,1)S(1)} %collective-permute-done.1.top_ref, bf16[2,2,64,2048]{3,2,1,0:T(8,128)(2,1)S(1)} %collective-permute-done.2.bottom_ref, ...), custom_call_target="tpu_custom_call" | custom-call | flops 1 | bytes 1 | tf_op jit(solution)/shard_map/pallas_call | solution.py:192
  50.2 7.5 %collective-permute-done.8.refs_2_ = bf16[2,128,2048]{2,1,0:T(8,128)(2,1)S(1)} collective-permute-done((bf16[2,128,2048]{2,1,0:T(8,128)(2,1)S(1)}, bf16[2,128,2048]{2,1,0:T(8,128)(2,1)S(1)}, u32[]{:S(2)}, u32[]{:S(2)}) %collective-permute-start.8) | collective-permute-done | bytes 1048608 | tf_op jit(solution)/shard_map/ppermute | solution.py:378
  57.8 4.6 %shard_map.41 = (bf16[128,2176]{1,0:T(8,128)(2,1)S(1)}, f32[128,2048]{1,0:T(8,128)S(1)}, f32[128,128]{1,0:T(8,128)S(1)}, f32[128,128]{1,0:T(8,128)S(1)}) custom-call(bf16[2,2,128,2048]{3,2,1,0:T(8,128)(2,1)S(1)} %bitcast.7, bf16[2,2,64,2048]{3,2,1,0:T(8,128)(2,1)S(1)} %collective-permute-done.1.top_ref, ...), custom_call_target="tpu_custom_call" | custom-call | flops 4294967296 | bytes 1 | tf_op jit(solution)/shard_map/pallas_call | solution.py:192
  63.8 2.1 %collective-permute-done.12.refs_3_ = bf16[2,64,2048]{2,1,0:T(8,128)(2,1)S(1)} collective-permute-done((bf16[2,64,2048]{2,1,0:T(8,128)(2,1)S(1)}, bf16[2,64,2048]{2,1,0:T(8,128)(2,1)S(1)}, u32[]{:S(2)}, u32[]{:S(2)}) %collective-permute-start.12) | collective-permute-done | bytes 524320 | tf_op jit(solution)/shard_map/ppermute | solution.py:396
  65.9 0.7 collective-permute-done.13.refs_4_
  66.7 6.2 %shard_map.42 = (f32[2,128,2048]{2,1,0:T(8,128)S(1)}, f32[2,128,128]{2,1,0:T(8,128)S(1)}, f32[2,128,128]{2,1,0:T(8,128)S(1)}) custom-call(s32[2,2,1,2]{3,2,1,0:T(1,128)S(1)} %copy-done.3, bf16[2,128,2048]{2,1,0:T(8,128)(2,1)S(1)} %bitcast.11, bf16[2,2,128,2048]{3,2,1,0:T(8,128)(2,1)S(1)} %collective-permute-done.refs_0_.core_ref, ...), custom_call_target="tpu_custom_call" | custom-call | flops 1 | bytes 1 | tf_op jit(solution)/shard_map/pallas_call | solution.py:279
  72.9 1.3 %shard_map.43.refs_1_ = bf16[128,2048]{1,0:T(8,128)(2,1)S(1)} custom-call(f32[2,128,2048]{2,1,0:T(8,128)S(1)} %get-tuple-element.71.own_ref, f32[2,128,128]{2,1,0:T(8,128)S(1)} %get-tuple-element.72.own_peak_ref, f32[2,128,128]{2,1,0:T(8,128)S(1)} %get-tuple-element.73.own_total_ref, bf16[128,2176]{1,0:T(8,128)(2,1)S(1)} %collective-permute-done.11.refs_0_), custom_call_target="tpu_custom_call" | custom-call | flops 1 | bytes 1 | tf_op jit(solution)/shard_map/pallas_call | solution.py:338
  74.2 3.3 %collective-permute-done.15.refs_0_ = bf16[128,2176]{1,0:T(8,128)(2,1)S(1)} collective-permute-done((bf16[128,2176]{1,0:T(8,128)(2,1)S(1)}, bf16[128,2176]{1,0:T(8,128)(2,1)S(1)}, u32[]{:S(2)}, u32[]{:S(2)}) %collective-permute-start.15) | collective-permute-done | bytes 557088 | tf_op jit(solution)/shard_map/ppermute | solution.py:393
  77.5 2.4 %shard_map.44 = bf16[2,128,2048]{2,1,0:T(8,128)(2,1)} custom-call(f32[2,128,2048]{2,1,0:T(8,128)S(1)} %get-tuple-element.71.own_ref, f32[2,128,128]{2,1,0:T(8,128)S(1)} %get-tuple-element.72.own_peak_ref, f32[2,128,128]{2,1,0:T(8,128)S(1)} %get-tuple-element.73.own_total_ref, bf16[128,2176]{1,0:T(8,128)(2,1)S(1)} %collective-permute-done.15.refs_0_, ...), custom_call_target="tpu_custom_call" | custom-call | flops 1 | bytes 1 | tf_op jit(solution)/shard_map/pallas_call | solution.py:338
  (24 shorter events, 2.8 us)
Async XLA Ops:
  0.0 8.4 %collective-permute-start = (bf16[2,2,128,2048]{3,2,1,0:T(8,128)(2,1)}, bf16[2,2,128,2048]{3,2,1,0:T(8,128)(2,1)S(1)}, u32[]{:S(2)}, u32[]{:S(2)}) collective-permute-start(bf16[2,2,128,2048]{3,2,1,0:T(8,128)(2,1)} %bitcast.3), channel_id=1, source_target_pairs={{0,8},{8,0},{16,24},{24,16},{1,9},{9,1},{17,25},{25,17},{2,10},{10... | collective-permute-start | bytes 6291464 | tf_op jit(solution)/shard_map/ppermute | solution.py:369
  0.5 1.6 %copy-start = (bf16[2,2,16,8,2048]{4,3,2,1,0:T(8,128)(2,1)S(1)}, bf16[2,2,16,8,2048]{4,3,2,1,0:T(8,128)(2,1)}, u32[]{:S(2)}) copy-start(bf16[2,2,16,8,2048]{4,3,2,1,0:T(8,128)(2,1)} %param.4) | copy-start | bytes 6291460
  2.0 40.5 %copy-start.1 = (bf16[2,2,16,8,2048]{4,3,2,1,0:T(8,128)(2,1)S(1)}, bf16[2,2,16,8,2048]{4,3,2,1,0:T(8,128)(2,1)}, u32[]{:S(2)}) copy-start(bf16[2,2,16,8,2048]{4,3,2,1,0:T(8,128)(2,1)} %param.4) | copy-start | bytes 6291460
  2.4 27.7 %collective-permute-start.1 = (bf16[2,2,64,2048]{3,2,1,0:T(8,128)(2,1)S(1)}, bf16[2,2,64,2048]{3,2,1,0:T(8,128)(2,1)S(1)}, u32[]{:S(2)}, u32[]{:S(2)}) collective-permute-start(bf16[2,2,64,2048]{3,2,1,0:T(8,128)(2,1)S(1)} %get-tuple-element.42), channel_id=1, source_target_pairs={{0,2},{2,4},{4,6},{1,3},{3,5},{5,7},{8,10},{10,12},{12,14},{9,11},... | collective-permute-start | bytes 3145736 | tf_op jit(solution)/shard_map/ppermute | solution.py:371
  7.1 27.2 %collective-permute-start.2 = (bf16[2,2,64,2048]{3,2,1,0:T(8,128)(2,1)S(1)}, bf16[2,2,64,2048]{3,2,1,0:T(8,128)(2,1)S(1)}, u32[]{:S(2)}, u32[]{:S(2)}) collective-permute-start(bf16[2,2,64,2048]{3,2,1,0:T(8,128)(2,1)S(1)} %get-tuple-element.43), channel_id=1, source_target_pairs={{2,0},{4,2},{6,4},{3,1},{5,3},{7,5},{10,8},{12,10},{14,12},{11,9},... | collective-permute-start | bytes 3145736 | tf_op jit(solution)/shard_map/ppermute | solution.py:372
  8.4 26.9 %collective-permute-start.5 = (bf16[2,128,2048]{2,1,0:T(8,128)(2,1)}, bf16[2,128,2048]{2,1,0:T(8,128)(2,1)S(1)}, u32[]{:S(2)}, u32[]{:S(2)}) collective-permute-start(bf16[2,128,2048]{2,1,0:T(8,128)(2,1)} %bitcast.8), channel_id=1, source_target_pairs={{0,1},{1,0},{2,3},{3,2},{4,5},{5,4},{6,7},{7,6},{8,9},{9,8},{10,11... | collective-permute-start | bytes 3145736 | tf_op jit(solution)/shard_map/ppermute | solution.py:376
  10.0 14.1 %collective-permute-start.4 = (bf16[2,64,2048]{2,1,0:T(8,128)(2,1)S(1)}, bf16[2,64,2048]{2,1,0:T(8,128)(2,1)S(1)}, u32[]{:S(2)}, u32[]{:S(2)}) collective-permute-start(bf16[2,64,2048]{2,1,0:T(8,128)(2,1)S(1)} %get-tuple-element.46), channel_id=1, source_target_pairs={{0,24},{8,16},{16,8},{24,0},{1,25},{9,17},{17,9},{25,1},{2,26},{10... | collective-permute-start | bytes 1572872 | tf_op jit(solution)/shard_map/ppermute | solution.py:373
  11.0 24.3 %collective-permute-start.3 = (bf16[2,64,2048]{2,1,0:T(8,128)(2,1)S(1)}, bf16[2,64,2048]{2,1,0:T(8,128)(2,1)S(1)}, u32[]{:S(2)}, u32[]{:S(2)}) collective-permute-start(bf16[2,64,2048]{2,1,0:T(8,128)(2,1)S(1)} %get-tuple-element.44), channel_id=1, source_target_pairs={{0,24},{8,16},{16,8},{24,0},{1,25},{9,17},{17,9},{25,1},{2,26},{10... | collective-permute-start | bytes 1572872 | tf_op jit(solution)/shard_map/ppermute | solution.py:375
  24.1 33.7 %collective-permute-start.8 = (bf16[2,128,2048]{2,1,0:T(8,128)(2,1)S(1)}, bf16[2,128,2048]{2,1,0:T(8,128)(2,1)S(1)}, u32[]{:S(2)}, u32[]{:S(2)}) collective-permute-start(bf16[2,128,2048]{2,1,0:T(8,128)(2,1)S(1)} %get-tuple-element.51), channel_id=1, source_target_pairs={{0,24},{8,16},{16,8},{24,0},{1,25},{9,17},{17,9},{25,1},{2,26},{10... | collective-permute-start | bytes 3145736 | tf_op jit(solution)/shard_map/ppermute | solution.py:378
  35.4 7.2 %collective-permute-start.9 = (bf16[2,64,2048]{2,1,0:T(8,128)(2,1)S(1)}, bf16[2,64,2048]{2,1,0:T(8,128)(2,1)S(1)}, u32[]{:S(2)}, u32[]{:S(2)}) collective-permute-start(bf16[2,64,2048]{2,1,0:T(8,128)(2,1)S(1)} %get-tuple-element.54), channel_id=1, source_target_pairs={{0,8},{8,0},{16,24},{24,16},{1,9},{9,1},{17,25},{25,17},{2,10},{10... | collective-permute-start | bytes 1572872 | tf_op jit(solution)/shard_map/ppermute | solution.py:380
  35.8 10.9 %copy-start.2 = (bf16[2,16,8,2048]{3,2,1,0:T(8,128)(2,1)S(1)}, bf16[2,16,8,2048]{3,2,1,0:T(8,128)(2,1)}, u32[]{:S(2)}) copy-start(bf16[2,16,8,2048]{3,2,1,0:T(8,128)(2,1)} %param.3) | copy-start | bytes 3145732
  35.8 6.7 %collective-permute-start.10 = (bf16[2,64,2048]{2,1,0:T(8,128)(2,1)S(1)}, bf16[2,64,2048]{2,1,0:T(8,128)(2,1)S(1)}, u32[]{:S(2)}, u32[]{:S(2)}) collective-permute-start(bf16[2,64,2048]{2,1,0:T(8,128)(2,1)S(1)} %get-tuple-element.55), channel_id=1, source_target_pairs={{0,8},{8,0},{16,24},{24,16},{1,9},{9,1},{17,25},{25,17},{2,10},{10... | collective-permute-start | bytes 1572872 | tf_op jit(solution)/shard_map/ppermute | solution.py:380
  36.0 21.8 %collective-permute-start.7 = (bf16[2,64,2048]{2,1,0:T(8,128)(2,1)S(1)}, bf16[2,64,2048]{2,1,0:T(8,128)(2,1)S(1)}, u32[]{:S(2)}, u32[]{:S(2)}) collective-permute-start(bf16[2,64,2048]{2,1,0:T(8,128)(2,1)S(1)} %collective-permute-done.3.refs_0_), channel_id=1, source_target_pairs={{2,0},{4,2},{6,4},{3,1},{5,3},{7,5},{10,8},{12,10},{14,12},{11,9},... | collective-permute-start | bytes 1572872 | tf_op jit(solution)/shard_map/ppermute | solution.py:382
  37.4 20.4 %collective-permute-start.6 = (bf16[2,64,2048]{2,1,0:T(8,128)(2,1)S(1)}, bf16[2,64,2048]{2,1,0:T(8,128)(2,1)S(1)}, u32[]{:S(2)}, u32[]{:S(2)}) collective-permute-start(bf16[2,64,2048]{2,1,0:T(8,128)(2,1)S(1)} %collective-permute-done.4.refs_1_), channel_id=1, source_target_pairs={{0,2},{2,4},{4,6},{1,3},{3,5},{5,7},{8,10},{10,12},{12,14},{9,11},... | collective-permute-start | bytes 1572872 | tf_op jit(solution)/shard_map/ppermute | solution.py:381
  46.2 16.3 %collective-permute-start.11 = (bf16[128,2176]{1,0:T(8,128)(2,1)S(1)}, bf16[128,2176]{1,0:T(8,128)(2,1)S(1)}, u32[]{:S(2)}, u32[]{:S(2)}) collective-permute-start(bf16[128,2176]{1,0:T(8,128)(2,1)S(1)} %shard_map.39), channel_id=1, source_target_pairs={{0,1},{1,0},{2,3},{3,2},{4,5},{5,4},{6,7},{7,6},{8,9},{9,8},{10,11... | collective-permute-start | bytes 1671176 | tf_op jit(solution)/shard_map/ppermute | solution.py:386
  57.8 8.9 %copy-start.3 = (s32[2,2,1,2]{3,2,1,0:T(1,128)S(1)}, s32[2,2,1,2]{3,2,1,0:T(1,128)}, u32[]{:S(2)}) copy-start(s32[2,2,1,2]{3,2,1,0:T(1,128)} %far_ref.1) | copy-start | bytes 100
  62.4 4.2 %collective-permute-start.14 = (bf16[2,128,2048]{2,1,0:T(8,128)(2,1)S(1)}, bf16[2,128,2048]{2,1,0:T(8,128)(2,1)S(1)}, u32[]{:S(2)}, u32[]{:S(2)}) collective-permute-start(bf16[2,128,2048]{2,1,0:T(8,128)(2,1)S(1)} %collective-permute-done.8.refs_2_), channel_id=1, source_target_pairs={{0,8},{8,0},{16,24},{24,16},{1,9},{9,1},{17,25},{25,17},{2,10},{10... | collective-permute-start | bytes 3145736 | tf_op jit(solution)/shard_map/ppermute | solution.py:396
  62.8 14.8 %collective-permute-start.15 = (bf16[128,2176]{1,0:T(8,128)(2,1)S(1)}, bf16[128,2176]{1,0:T(8,128)(2,1)S(1)}, u32[]{:S(2)}, u32[]{:S(2)}) collective-permute-start(bf16[128,2176]{1,0:T(8,128)(2,1)S(1)} %get-tuple-element.62), channel_id=1, source_target_pairs={{0,1},{1,0},{2,3},{3,2},{4,5},{5,4},{6,7},{7,6},{8,9},{9,8},{10,11... | collective-permute-start | bytes 1671176 | tf_op jit(solution)/shard_map/ppermute | solution.py:393
  63.3 2.7 %collective-permute-start.12 = (bf16[2,64,2048]{2,1,0:T(8,128)(2,1)S(1)}, bf16[2,64,2048]{2,1,0:T(8,128)(2,1)S(1)}, u32[]{:S(2)}, u32[]{:S(2)}) collective-permute-start(bf16[2,64,2048]{2,1,0:T(8,128)(2,1)S(1)} %collective-permute-done.3.refs_0_), channel_id=1, source_target_pairs={{0,8},{8,0},{16,24},{24,16},{1,9},{9,1},{17,25},{25,17},{2,10},{10... | collective-permute-start | bytes 1572872 | tf_op jit(solution)/shard_map/ppermute | solution.py:396
  63.3 3.4 %collective-permute-start.13 = (bf16[2,64,2048]{2,1,0:T(8,128)(2,1)S(1)}, bf16[2,64,2048]{2,1,0:T(8,128)(2,1)S(1)}, u32[]{:S(2)}, u32[]{:S(2)}) collective-permute-start(bf16[2,64,2048]{2,1,0:T(8,128)(2,1)S(1)} %collective-permute-done.4.refs_1_), channel_id=1, source_target_pairs={{0,8},{8,0},{16,24},{24,16},{1,9},{9,1},{17,25},{25,17},{2,10},{10... | collective-permute-start | bytes 1572872 | tf_op jit(solution)/shard_map/ppermute | solution.py:396

commit v9 on v8

--- a/solution.py
+++ b/solution.py
@@ -17,7 +17,7 @@
 VMEM_LIMIT = 16 * 1024 * 1024
 GROUP = 4
 FINISH_COST = 1
-LATE_COST = 4 << 30
+LATE_COST = 8 << 30
 
 
 def contract_last(left, right):
@@ -78,6 +78,56 @@
         compiler_params=pltpu.CompilerParams(vmem_limit_bytes=VMEM_LIMIT),
         cost_estimate=kernel_cost(1),
     )(keyvals)
+
+
+def widen_kernel(rows_ref, out_ref, sems):
+    tokens = rows_ref.shape[1]
+    extra = out_ref.shape[1] - tokens
+    copies = [
+        pltpu.make_async_copy(rows_ref, out_ref.at[:, pl.ds(0, tokens)], sems.at[0]),
+        pltpu.make_async_copy(rows_ref.at[:, pl.ds(0, extra)], out_ref.at[:, pl.ds(tokens, extra)], sems.at[1]),
+    ]
+    for copy in copies:
+        copy.start()
+    for copy in copies:
+        copy.wait()
+
+
+def widen(rows):
+    two, tokens, features = rows.shape
+    in_vmem = pl.BlockSpec(memory_space=pltpu.VMEM)
+    return pl.pallas_call(
+        widen_kernel,
+        out_shape=jax.ShapeDtypeStruct((two, tokens + tokens // 2, features), rows.dtype),
+        in_specs=[in_vmem],
+        out_specs=in_vmem,
+        scratch_shapes=[pltpu.SemaphoreType.DMA((2,))],
+        compiler_params=pltpu.CompilerParams(vmem_limit_bytes=VMEM_LIMIT),
+        cost_estimate=kernel_cost(1),
+    )(rows)
+
+
+def by_rows_kernel(frame_ref, first_ref, last_ref, sems):
+    pairs = ((pl.ds(0, SPOT), first_ref), (pl.ds(SPOT, SPOT), last_ref))
+    copies = [pltpu.make_async_copy(frame_ref.at[:, rows], out, sems.at[i]) for i, (rows, out) in enumerate(pairs)]
+    for copy in copies:
+        copy.start()
+    for copy in copies:
+        copy.wait()
+
+
+def by_rows(frame):
+    two, _, features = frame.shape
+    in_vmem = pl.BlockSpec(memory_space=pltpu.VMEM)
+    return pl.pallas_call(
+        by_rows_kernel,
+        out_shape=[jax.ShapeDtypeStruct((two, SPOT, features), frame.dtype)] * 2,
+        in_specs=[in_vmem],
+        out_specs=[in_vmem] * 2,
+        scratch_shapes=[pltpu.SemaphoreType.DMA((2,))],
+        compiler_params=pltpu.CompilerParams(vmem_limit_bytes=VMEM_LIMIT),
+        cost_estimate=kernel_cost(1),
+    )(frame)
 
 
 def inner_rows_kernel(top_ref, bottom_ref, out_top_ref, out_bottom_ref, sems):
@@ -128,7 +178,7 @@
 
     def halo(a, kind, lanes):
         ref, ext = ((top_ref, ext_top_ref), (bottom_ref, ext_bottom_ref))[a]
-        return jnp.concatenate([ref[kind, 0, :, lanes], ref[kind, 1, :, lanes], ext[kind, :, lanes]], axis=0)
+        return jnp.concatenate([ref[kind, 0, :, lanes], ref[kind, 1, :, lanes], ext[kind, :SPOT, lanes]], axis=0)
 
     peaks = [jnp.zeros((half, HD), jnp.float32) for _ in range(2)]
     totals = [jnp.ones((half, HD), jnp.float32) for _ in range(2)]
@@ -169,6 +219,9 @@
                     result = summed[rows, :HD]
                     if s < sides:
                         result = result / total[rows]
+                    else:
+                        filled = jnp.broadcast_to(peak[rows] * EXP_SCALE, (SPOT, HD))
+                        out_refs[s + 3][a * SPOT : (a + 1) * SPOT, lanes] = filled
                     out_refs[s][a * SPOT : (a + 1) * SPOT, lanes] = result.astype(out_refs[s].dtype)
     for a in range(2):
         tokens = slice(a * SPOT, (a + 1) * SPOT)
@@ -187,7 +240,7 @@
     operands = [own, top, bottom, *third, *visitors, *queries]
     outs = [jax.ShapeDtypeStruct((tokens, features + HD), jnp.bfloat16) for _ in visitors]
     for _ in queries:
-        outs += [jax.ShapeDtypeStruct((tokens, lanes), jnp.float32) for lanes in (features, HD, HD)]
+        outs += [jax.ShapeDtypeStruct((tokens, lanes), jnp.float32) for lanes in (features, HD, HD, features)]
     in_vmem = pl.BlockSpec(memory_space=pltpu.VMEM)
     return pl.pallas_call(
         functools.partial(near_kernel, len(visitors), len(queries), early, has_rows),
@@ -200,8 +253,8 @@
 
 
 def far_kernel(members, far_ref, q_ref, core_ref, *refs):
-    cross, cross_inner, corner, corner_inner = refs[:2], refs[2], refs[3:5], refs[5]
-    near_refs, (out_ref, peak_ref, total_ref, held, sems) = (refs[6:9], refs[9:12]), refs[12:]
+    cross, cross_inner, corner, corner_inner = refs[:2], refs[2:4], refs[4:6], refs[6:8]
+    near_refs, (out_ref, peak_ref, total_ref, held, sems) = (refs[8:12], refs[12:16]), refs[16:]
     ta = lax.axis_index("ta")
     parity = ta % 2
 
@@ -224,9 +277,9 @@
                     (jnp.logical_and(is_core, place == 0), core_ref.at[:, 0, rows]),
                     (jnp.logical_and(is_core, place == 1), core_ref.at[:, 1, rows]),
                     (jnp.logical_and(is_cross, jnp.logical_not(inner)), cross[a]),
-                    (jnp.logical_and(is_cross, inner), cross_inner.at[:, rows]),
+                    (jnp.logical_and(is_cross, inner), cross_inner[a]),
                     (jnp.logical_and(is_corner, jnp.logical_not(inner)), corner[a]),
-                    (jnp.logical_and(is_corner, inner), corner_inner.at[:, rows]),
+                    (jnp.logical_and(is_corner, inner), corner_inner[a]),
                 ]
                 for chosen, source in sources:
 
@@ -251,7 +304,7 @@
         weights = []
         for (h, u), value in zip(work, scores):
             early, a = units[u]
-            near_peak = near_refs[early][1][a * SPOT : (a + 1) * SPOT, h : h + 1]
+            near_peak = near_refs[early][3][a * SPOT : (a + 1) * SPOT, h * HD : (h + 1) * HD]
             value = value * EXP_SCALE
             peak = jnp.maximum(jnp.max(value, axis=-1, keepdims=True), near_peak)
             weights.append((peak, jnp.exp2(near_peak - peak), jnp.exp2(value - peak).astype(jnp.bfloat16)))
@@ -376,9 +429,8 @@
     visitors = [lax.ppermute(sent, "wa", there) for there, _ in ways]
     inner, cross_last = tie((inner, cross_last))
     last = lax.ppermute(inner, "ta", cross_pairs)
-    top, bottom, cross_first, cross_last, visitors = tie((top, bottom, cross_first, cross_last, visitors))
     core_top, core_bottom = [lax.ppermute(value, "ta", core_pairs) for value in inner_rows(top, bottom)]
-    cross_top = lax.ppermute(cross_last, "ha", up)
+    cross_top = lax.ppermute(widen(cross_last), "ha", up)
     cross_bottom = lax.ppermute(cross_first, "ha", down)
 
     early_third = (core, core_top, core_bottom)
@@ -387,15 +439,16 @@
     core_top, _ = tie((core_top, early[0]))
     early_third = (core, core_top, core_bottom)
     early_home = near_attention(True, ha_size, keyvals, top, bottom, early_third, [], [queries], 1)
-    cross_top, cross_bottom, last, _ = tie((cross_top, cross_bottom, last, early_home[1]))
+    cross_top, cross_bottom, _ = tie((cross_top, cross_bottom, early_home[1]))
     late_third = (cross_first, cross_last, cross_top, cross_bottom)
     late = near_attention(False, ha_size, keyvals, top, bottom, late_third, visitors, [queries], LATE_COST)
     late_parts = [lax.ppermute(result, "wa", back) for result, (_, back) in zip(late, ways)]
-    frames_here = (cross_first, cross_last, last)
-    frames_here, early_parts, _ = tie((frames_here, early_parts, late[0]))
+    last, _ = tie((last, late[0]))
+    cross_first, cross_last, early_parts, _ = tie((cross_first, cross_last, early_parts, late[0]))
+    frames_here = (cross_first, cross_last, *by_rows(last))
     corner = [lax.ppermute(value, "ta", core_pairs) for value in frames_here]
     buffers = (core, *frames_here, *corner)
-    own = far_attention(ta_size, far_frames, queries, buffers, (*early_home, *late[-3:]))
+    own = far_attention(ta_size, far_frames, queries, buffers, (*early_home, *late[-4:]))
     out = finish(wa_size, own, early_parts, None, FINISH_COST)
     out = finish(wa_size, own, late_parts, out, 1)
     return out.reshape(shape)

time: 80.2 us -> 75.3 us (0.939)
  waiting for transfers between devices: 35.9 us -> 30 us
  starting transfers between devices: 20.3 us -> 21.6 us
    ppermute x1, waiting for transfers between devices: 0.01 us -> 3.8 us  [per_device(): cross_bottom = lax.ppermute(cross_first, 'ha', down)]
    ppermute x2, waiting for transfers between devices: 3.31 us -> 0.01 us  [per_device(): lax.ppermute(result, 'wa', back)]
    ppermute x1, waiting for transfers between devices: 7.54 us -> 4.39 us  [per_device(): last = lax.ppermute(inner, 'ta', cross_pairs)]
    ppermute x2, starting transfers between devices: 1.07 us -> 3.19 us  [per_device(): lax.ppermute(result, 'wa', back)]
    ppermute x1, waiting for transfers between devices: 12.3 us -> 10.9 us  [per_device(): cross_last = lax.ppermute(outer_last, 'ta', cross_pairs)]
    ppermute x1, waiting for transfers between devices: 4.55 us -> 3.23 us  [per_device(): top = lax.ppermute(last_rows, 'ha', up)]
    ppermute x1, waiting for transfers between devices: 1.04 us -> 0.01 us  [per_device(): cross_first = lax.ppermute(outer_first, 'ta', cross_pairs)]
    pallas_call x1, Pallas kernels: 6.23 us -> 5.29 us  [far_attention(): pl.pallas_call(functools.partial(far_kernel, members), out_shape=[jax.Sha...]
  transfers between devices with their start and end apart: 16 -> 17, of which waited for: 8 -> 11; matrix products, arithmetic and copies ran while one was open for 0% -> 0% of each run, Pallas kernels for 25% -> 26%
where the time goes in v9:
time: 75.3 us; the launch traced here: 74.9 us
  waiting for transfers between devices  30 us (40%)
  starting transfers between devices  21.6 us (29%)
  Pallas kernels  21.6 us (29%)
  local copies, waits for them, and re-layouts  1.6 us (2%)
    pallas_call x3, Pallas kernels, near_attention(): pl.pallas_call(functools.partial(near_kernel, len(visitors), len(queries)...  11.9 us
    ppermute x1, waiting for transfers between devices, per_device(): cross_last = lax.ppermute(outer_last, 'ta', cross_pairs)  10.9 us
    pallas_call x1, Pallas kernels, far_attention(): pl.pallas_call(functools.partial(far_kernel, members), out_shape=[jax.Sha...  5.29 us
    ppermute x1, starting transfers between devices, per_device(): cross_top = lax.ppermute(widen(cross_last), 'ha', up)  4.8 us
    ppermute x1, starting transfers between devices, per_device(): top = lax.ppermute(last_rows, 'ha', up)  4.68 us
    ppermute x1, waiting for transfers between devices, per_device(): last = lax.ppermute(inner, 'ta', cross_pairs)  4.39 us
    ppermute x1, waiting for transfers between devices, per_device(): cross_bottom = lax.ppermute(cross_first, 'ha', down)  3.8 us
    ppermute x1, waiting for transfers between devices, per_device(): bottom = lax.ppermute(first_rows, 'ha', down)  3.79 us
  transfers between devices with their start and end apart: 17, of which 11 were waited for; matrix products, arithmetic and copies ran while one was open for 0% of the time, Pallas kernels for 26%

profile of v9, /device:TPU:0, one launch (start us, length us, event | category | flops | bytes accessed | tf_op | source)
XLA Modules:
  0.0 74.9 jit_solution(18009138303063235752)
XLA Ops:
  0.5 1.6 %copy-done = bf16[2,2,16,8,2048]{4,3,2,1,0:T(8,128)(2,1)S(1)} copy-done((bf16[2,2,16,8,2048]{4,3,2,1,0:T(8,128)(2,1)S(1)}, bf16[2,2,16,8,2048]{4,3,2,1,0:T(8,128)(2,1)}, u32[]{:S(2)}) %copy-start) | copy-done | bytes 2097176
  2.4 4.7 %collective-permute-start.3 = (bf16[2,2,64,2048]{3,2,1,0:T(8,128)(2,1)S(1)}, bf16[2,2,64,2048]{3,2,1,0:T(8,128)(2,1)S(1)}, u32[]{:S(2)}, u32[]{:S(2)}) collective-permute-start(bf16[2,2,64,2048]{3,2,1,0:T(8,128)(2,1)S(1)} %get-tuple-element.44), channel_id=1, source_target_pairs={{0,2},{2,4},{4,6},{1,3},{3,5},{5,7},{8,10},{10,12},{12,14},{9,11},... | collective-permute-start | bytes 3145736 | tf_op jit(solution)/shard_map/ppermute | solution.py:424
  7.1 1.3 %collective-permute-start.4 = (bf16[2,2,64,2048]{3,2,1,0:T(8,128)(2,1)S(1)}, bf16[2,2,64,2048]{3,2,1,0:T(8,128)(2,1)S(1)}, u32[]{:S(2)}, u32[]{:S(2)}) collective-permute-start(bf16[2,2,64,2048]{3,2,1,0:T(8,128)(2,1)S(1)} %get-tuple-element.45), channel_id=1, source_target_pairs={{2,0},{4,2},{6,4},{3,1},{5,3},{7,5},{10,8},{12,10},{14,12},{11,9},... | collective-permute-start | bytes 3145736 | tf_op jit(solution)/shard_map/ppermute | solution.py:425
  8.4 1.4 %collective-permute-start.2 = (bf16[2,64,2048]{2,1,0:T(8,128)(2,1)S(1)}, bf16[2,64,2048]{2,1,0:T(8,128)(2,1)S(1)}, u32[]{:S(2)}, u32[]{:S(2)}) collective-permute-start(bf16[2,64,2048]{2,1,0:T(8,128)(2,1)S(1)} %get-tuple-element.42), channel_id=1, source_target_pairs={{0,24},{8,16},{16,8},{24,0},{1,25},{9,17},{17,9},{25,1},{2,26},{10... | collective-permute-start | bytes 1572872 | tf_op jit(solution)/shard_map/ppermute | solution.py:426
  9.8 1.5 %collective-permute-start.7 = (bf16[2,128,2048]{2,1,0:T(8,128)(2,1)S(1)}, bf16[2,128,2048]{2,1,0:T(8,128)(2,1)S(1)}, u32[]{:S(2)}, u32[]{:S(2)}) collective-permute-start(bf16[2,128,2048]{2,1,0:T(8,128)(2,1)S(1)} %bitcast.8), channel_id=1, source_target_pairs={{0,1},{1,0},{2,3},{3,2},{4,5},{5,4},{6,7},{7,6},{8,9},{9,8},{10,11... | collective-permute-start | bytes 3145736 | tf_op jit(solution)/shard_map/ppermute | solution.py:429
  11.4 10.9 %collective-permute-done.2.rows_ref.refs_1_ = bf16[2,64,2048]{2,1,0:T(8,128)(2,1)S(1)} collective-permute-done((bf16[2,64,2048]{2,1,0:T(8,128)(2,1)S(1)}, bf16[2,64,2048]{2,1,0:T(8,128)(2,1)S(1)}, u32[]{:S(2)}, u32[]{:S(2)}) %collective-permute-start.2) | collective-permute-done | bytes 524320 | tf_op jit(solution)/shard_map/ppermute | solution.py:426
  22.4 4.8 %collective-permute-start.9 = (bf16[2,96,2048]{2,1,0:T(8,128)(2,1)S(1)}, bf16[2,96,2048]{2,1,0:T(8,128)(2,1)S(1)}, u32[]{:S(2)}, u32[]{:S(2)}) collective-permute-start(bf16[2,96,2048]{2,1,0:T(8,128)(2,1)S(1)} %shard_map.40), channel_id=1, source_target_pairs={{0,2},{2,4},{4,6},{1,3},{3,5},{5,7},{8,10},{10,12},{12,14},{9,11},... | collective-permute-start | bytes 2359304 | tf_op jit(solution)/shard_map/ppermute | solution.py:433
  27.2 3.2 %collective-permute-done.3.top_ref = bf16[2,2,64,2048]{3,2,1,0:T(8,128)(2,1)S(1)} collective-permute-done((bf16[2,2,64,2048]{3,2,1,0:T(8,128)(2,1)S(1)}, bf16[2,2,64,2048]{3,2,1,0:T(8,128)(2,1)S(1)}, u32[]{:S(2)}, u32[]{:S(2)}) %collective-permute-start.3) | collective-permute-done | bytes 1048608 | tf_op jit(solution)/shard_map/ppermute | solution.py:424
  30.5 3.8 %collective-permute-done.4.bottom_ref = bf16[2,2,64,2048]{3,2,1,0:T(8,128)(2,1)S(1)} collective-permute-done((bf16[2,2,64,2048]{3,2,1,0:T(8,128)(2,1)S(1)}, bf16[2,2,64,2048]{3,2,1,0:T(8,128)(2,1)S(1)}, u32[]{:S(2)}, u32[]{:S(2)}) %collective-permute-start.4) | collective-permute-done | bytes 1048608 | tf_op jit(solution)/shard_map/ppermute | solution.py:425
  34.9 1.3 %collective-permute-start.10 = (bf16[2,64,2048]{2,1,0:T(8,128)(2,1)S(1)}, bf16[2,64,2048]{2,1,0:T(8,128)(2,1)S(1)}, u32[]{:S(2)}, u32[]{:S(2)}) collective-permute-start(bf16[2,64,2048]{2,1,0:T(8,128)(2,1)S(1)} %collective-permute-done.1.refs_0_), channel_id=1, source_target_pairs={{2,0},{4,2},{6,4},{3,1},{5,3},{7,5},{10,8},{12,10},{14,12},{11,9},... | collective-permute-start | bytes 1572872 | tf_op jit(solution)/shard_map/ppermute | solution.py:434
  36.3 1.2 %collective-permute-start.11 = (bf16[2,128,2048]{2,1,0:T(8,128)(2,1)S(1)}, bf16[2,128,2048]{2,1,0:T(8,128)(2,1)S(1)}, u32[]{:S(2)}, u32[]{:S(2)}) collective-permute-start(bf16[2,128,2048]{2,1,0:T(8,128)(2,1)S(1)} %get-tuple-element.56), channel_id=1, source_target_pairs={{0,24},{8,16},{16,8},{24,0},{1,25},{9,17},{17,9},{25,1},{2,26},{10... | collective-permute-start | bytes 3145736 | tf_op jit(solution)/shard_map/ppermute | solution.py:431
  37.6 3.6 %shard_map.39 = bf16[128,2176]{1,0:T(8,128)(2,1)S(1)} custom-call(bf16[2,2,128,2048]{3,2,1,0:T(8,128)(2,1)S(1)} %bitcast.5, bf16[2,2,64,2048]{3,2,1,0:T(8,128)(2,1)S(1)} %collective-permute-done.3.top_ref, bf16[2,2,64,2048]{3,2,1,0:T(8,128)(2,1)S(1)} %collective-permute-done.4.bottom_ref, ...), custom_call_target="tpu_custom_call" | custom-call | flops 1 | bytes 1 | tf_op jit(solution)/shard_map/pallas_call | solution.py:245
  41.2 1.6 %collective-permute-start.8 = (bf16[128,2176]{1,0:T(8,128)(2,1)S(1)}, bf16[128,2176]{1,0:T(8,128)(2,1)S(1)}, u32[]{:S(2)}, u32[]{:S(2)}) collective-permute-start(bf16[128,2176]{1,0:T(8,128)(2,1)S(1)} %shard_map.39), channel_id=1, source_target_pairs={{0,1},{1,0},{2,3},{3,2},{4,5},{5,4},{6,7},{7,6},{8,9},{9,8},{10,11... | collective-permute-start | bytes 1671176 | tf_op jit(solution)/shard_map/ppermute | solution.py:438
  42.8 3.6 %shard_map.41 = (f32[128,2048]{1,0:T(8,128)S(1)}, f32[128,128]{1,0:T(8,128)S(1)}, f32[128,128]{1,0:T(8,128)S(1)}, f32[128,2048]{1,0:T(8,128)S(1)}) custom-call(bf16[2,2,128,2048]{3,2,1,0:T(8,128)(2,1)S(1)} %bitcast.6, bf16[2,2,64,2048]{3,2,1,0:T(8,128)(2,1)S(1)} %collective-permute-done.3.top_ref, ...), custom_call_target="tpu_custom_call" | custom-call | flops 1 | bytes 1 | tf_op jit(solution)/shard_map/pallas_call | solution.py:245
  46.9 3.8 %collective-permute-done.10.refs_3_ = bf16[2,64,2048]{2,1,0:T(8,128)(2,1)S(1)} collective-permute-done((bf16[2,64,2048]{2,1,0:T(8,128)(2,1)S(1)}, bf16[2,64,2048]{2,1,0:T(8,128)(2,1)S(1)}, u32[]{:S(2)}, u32[]{:S(2)}) %collective-permute-start.10) | collective-permute-done | bytes 524320 | tf_op jit(solution)/shard_map/ppermute | solution.py:434
  50.7 4.8 %shard_map.42 = (bf16[128,2176]{1,0:T(8,128)(2,1)S(1)}, f32[128,2048]{1,0:T(8,128)S(1)}, f32[128,128]{1,0:T(8,128)S(1)}, f32[128,128]{1,0:T(8,128)S(1)}, f32[128,2048]{1,0:T(8,128)S(1)}) custom-call(bf16[2,2,128,2048]{3,2,1,0:T(8,128)(2,1)S(1)} %bitcast.7, bf16[2,2,64,2048]{3,2,1,0:T(8,128)(2,1)S(1)} %collective-permute-done.3.top_ref, ...), custom_call_target="tpu_custom_call" | custom-call | flops 8589934592 | bytes 1 | tf_op jit(solution)/shard_map/pallas_call | solution.py:245
  55.5 1.6 %collective-permute-start.16 = (bf16[128,2176]{1,0:T(8,128)(2,1)S(1)}, bf16[128,2176]{1,0:T(8,128)(2,1)S(1)}, u32[]{:S(2)}, u32[]{:S(2)}) collective-permute-start(bf16[128,2176]{1,0:T(8,128)(2,1)S(1)} %get-tuple-element.53), channel_id=1, source_target_pairs={{0,1},{1,0},{2,3},{3,2},{4,5},{5,4},{6,7},{7,6},{8,9},{9,8},{10,11... | collective-permute-start | bytes 1671176 | tf_op jit(solution)/shard_map/ppermute | solution.py:445
  57.1 4.4 %collective-permute-done.11.frame_ref = bf16[2,128,2048]{2,1,0:T(8,128)(2,1)S(1)} collective-permute-done((bf16[2,128,2048]{2,1,0:T(8,128)(2,1)S(1)}, bf16[2,128,2048]{2,1,0:T(8,128)(2,1)S(1)}, u32[]{:S(2)}, u32[]{:S(2)}) %collective-permute-start.11) | collective-permute-done | bytes 1048608 | tf_op jit(solution)/shard_map/ppermute | solution.py:431
  62.7 0.9 %collective-permute-done.14.refs_6_ = bf16[2,64,2048]{2,1,0:T(8,128)(2,1)S(1)} collective-permute-done((bf16[2,64,2048]{2,1,0:T(8,128)(2,1)S(1)}, bf16[2,64,2048]{2,1,0:T(8,128)(2,1)S(1)}, u32[]{:S(2)}, u32[]{:S(2)}) %collective-permute-start.14) | collective-permute-done | bytes 524320 | tf_op jit(solution)/shard_map/ppermute | solution.py:449
  63.6 0.7 %collective-permute-done.15.refs_7_ = bf16[2,64,2048]{2,1,0:T(8,128)(2,1)S(1)} collective-permute-done((bf16[2,64,2048]{2,1,0:T(8,128)(2,1)S(1)}, bf16[2,64,2048]{2,1,0:T(8,128)(2,1)S(1)}, u32[]{:S(2)}, u32[]{:S(2)}) %collective-permute-start.15) | collective-permute-done | bytes 524320 | tf_op jit(solution)/shard_map/ppermute | solution.py:449
  64.4 0.7 %collective-permute-done.12.refs_4_ = bf16[2,64,2048]{2,1,0:T(8,128)(2,1)S(1)} collective-permute-done((bf16[2,64,2048]{2,1,0:T(8,128)(2,1)S(1)}, bf16[2,64,2048]{2,1,0:T(8,128)(2,1)S(1)}, u32[]{:S(2)}, u32[]{:S(2)}) %collective-permute-start.12) | collective-permute-done | bytes 524320 | tf_op jit(solution)/shard_map/ppermute | solution.py:449
  65.9 5.3 %shard_map.44 = (f32[2,128,2048]{2,1,0:T(8,128)S(1)}, f32[2,128,128]{2,1,0:T(8,128)S(1)}, f32[2,128,128]{2,1,0:T(8,128)S(1)}) custom-call(s32[2,2,1,2]{3,2,1,0:T(1,128)S(1)} %copy-done.3, bf16[2,128,2048]{2,1,0:T(8,128)(2,1)S(1)} %bitcast.11, bf16[2,2,128,2048]{3,2,1,0:T(8,128)(2,1)S(1)} %collective-permute-done.refs_0_.core_ref, ...), custom_call_target="tpu_custom_call" | custom-call | flops 1 | bytes 1 | tf_op jit(solution)/shard_map/pallas_call | solution.py:332
  71.2 1.3 %shard_map.45.refs_1_ = bf16[128,2048]{1,0:T(8,128)(2,1)S(1)} custom-call(f32[2,128,2048]{2,1,0:T(8,128)S(1)} %get-tuple-element.67.own_ref, f32[2,128,128]{2,1,0:T(8,128)S(1)} %get-tuple-element.68.own_peak_ref, f32[2,128,128]{2,1,0:T(8,128)S(1)} %get-tuple-element.69.own_total_ref, bf16[128,2176]{1,0:T(8,128)(2,1)S(1)} %collective-permute-done.8.refs_0_), custom_call_target="tpu_custom_call" | custom-call | flops 1 | bytes 1 | tf_op jit(solution)/shard_map/pallas_call | solution.py:391
  72.5 2.4 %shard_map.46 = bf16[2,128,2048]{2,1,0:T(8,128)(2,1)} custom-call(f32[2,128,2048]{2,1,0:T(8,128)S(1)} %get-tuple-element.67.own_ref, f32[2,128,128]{2,1,0:T(8,128)S(1)} %get-tuple-element.68.own_peak_ref, f32[2,128,128]{2,1,0:T(8,128)S(1)} %get-tuple-element.69.own_total_ref, bf16[128,2176]{1,0:T(8,128)(2,1)S(1)} %collective-permute-done.16.refs_0_, ...), custom_call_target="tpu_custom_call" | custom-call | flops 1 | bytes 1 | tf_op jit(solution)/shard_map/pallas_call | solution.py:391
  (28 shorter events, 4.3 us)
Async XLA Ops:
  0.0 9.8 %collective-permute-start = (bf16[2,2,128,2048]{3,2,1,0:T(8,128)(2,1)}, bf16[2,2,128,2048]{3,2,1,0:T(8,128)(2,1)S(1)}, u32[]{:S(2)}, u32[]{:S(2)}) collective-permute-start(bf16[2,2,128,2048]{3,2,1,0:T(8,128)(2,1)} %bitcast.3), channel_id=1, source_target_pairs={{0,8},{8,0},{16,24},{24,16},{1,9},{9,1},{17,25},{25,17},{2,10},{10... | collective-permute-start | bytes 6291464 | tf_op jit(solution)/shard_map/ppermute | solution.py:422
  0.5 1.6 %copy-start = (bf16[2,2,16,8,2048]{4,3,2,1,0:T(8,128)(2,1)S(1)}, bf16[2,2,16,8,2048]{4,3,2,1,0:T(8,128)(2,1)}, u32[]{:S(2)}) copy-start(bf16[2,2,16,8,2048]{4,3,2,1,0:T(8,128)(2,1)} %param.4) | copy-start | bytes 6291460
  2.0 7.7 %copy-start.2 = (bf16[2,16,8,2048]{3,2,1,0:T(8,128)(2,1)S(1)}, bf16[2,16,8,2048]{3,2,1,0:T(8,128)(2,1)}, u32[]{:S(2)}) copy-start(bf16[2,16,8,2048]{3,2,1,0:T(8,128)(2,1)} %param.3) | copy-start | bytes 3145732
  2.4 35.2 %copy-start.1 = (bf16[2,2,16,8,2048]{4,3,2,1,0:T(8,128)(2,1)S(1)}, bf16[2,2,16,8,2048]{4,3,2,1,0:T(8,128)(2,1)}, u32[]{:S(2)}) copy-start(bf16[2,2,16,8,2048]{4,3,2,1,0:T(8,128)(2,1)} %param.4) | copy-start | bytes 6291460
  2.4 28.1 %collective-permute-start.3 = (bf16[2,2,64,2048]{3,2,1,0:T(8,128)(2,1)S(1)}, bf16[2,2,64,2048]{3,2,1,0:T(8,128)(2,1)S(1)}, u32[]{:S(2)}, u32[]{:S(2)}) collective-permute-start(bf16[2,2,64,2048]{3,2,1,0:T(8,128)(2,1)S(1)} %get-tuple-element.44), channel_id=1, source_target_pairs={{0,2},{2,4},{4,6},{1,3},{3,5},{5,7},{8,10},{10,12},{12,14},{9,11},... | collective-permute-start | bytes 3145736 | tf_op jit(solution)/shard_map/ppermute | solution.py:424
  7.1 27.2 %collective-permute-start.4 = (bf16[2,2,64,2048]{3,2,1,0:T(8,128)(2,1)S(1)}, bf16[2,2,64,2048]{3,2,1,0:T(8,128)(2,1)S(1)}, u32[]{:S(2)}, u32[]{:S(2)}) collective-permute-start(bf16[2,2,64,2048]{3,2,1,0:T(8,128)(2,1)S(1)} %get-tuple-element.45), channel_id=1, source_target_pairs={{2,0},{4,2},{6,4},{3,1},{5,3},{7,5},{10,8},{12,10},{14,12},{11,9},... | collective-permute-start | bytes 3145736 | tf_op jit(solution)/shard_map/ppermute | solution.py:425
  8.4 14.0 %collective-permute-start.2 = (bf16[2,64,2048]{2,1,0:T(8,128)(2,1)S(1)}, bf16[2,64,2048]{2,1,0:T(8,128)(2,1)S(1)}, u32[]{:S(2)}, u32[]{:S(2)}) collective-permute-start(bf16[2,64,2048]{2,1,0:T(8,128)(2,1)S(1)} %get-tuple-element.42), channel_id=1, source_target_pairs={{0,24},{8,16},{16,8},{24,0},{1,25},{9,17},{17,9},{25,1},{2,26},{10... | collective-permute-start | bytes 1572872 | tf_op jit(solution)/shard_map/ppermute | solution.py:426
  9.8 27.8 %collective-permute-start.7 = (bf16[2,128,2048]{2,1,0:T(8,128)(2,1)S(1)}, bf16[2,128,2048]{2,1,0:T(8,128)(2,1)S(1)}, u32[]{:S(2)}, u32[]{:S(2)}) collective-permute-start(bf16[2,128,2048]{2,1,0:T(8,128)(2,1)S(1)} %bitcast.8), channel_id=1, source_target_pairs={{0,1},{1,0},{2,3},{3,2},{4,5},{5,4},{6,7},{7,6},{8,9},{9,8},{10,11... | collective-permute-start | bytes 3145736 | tf_op jit(solution)/shard_map/ppermute | solution.py:429
  11.3 23.6 %collective-permute-start.1 = (bf16[2,64,2048]{2,1,0:T(8,128)(2,1)S(1)}, bf16[2,64,2048]{2,1,0:T(8,128)(2,1)S(1)}, u32[]{:S(2)}, u32[]{:S(2)}) collective-permute-start(bf16[2,64,2048]{2,1,0:T(8,128)(2,1)S(1)} %get-tuple-element.40), channel_id=1, source_target_pairs={{0,24},{8,16},{16,8},{24,0},{1,25},{9,17},{17,9},{25,1},{2,26},{10... | collective-permute-start | bytes 1572872 | tf_op jit(solution)/shard_map/ppermute | solution.py:428
  22.4 24.5 %collective-permute-start.9 = (bf16[2,96,2048]{2,1,0:T(8,128)(2,1)S(1)}, bf16[2,96,2048]{2,1,0:T(8,128)(2,1)S(1)}, u32[]{:S(2)}, u32[]{:S(2)}) collective-permute-start(bf16[2,96,2048]{2,1,0:T(8,128)(2,1)S(1)} %shard_map.40), channel_id=1, source_target_pairs={{0,2},{2,4},{4,6},{1,3},{3,5},{5,7},{8,10},{10,12},{12,14},{9,11},... | collective-permute-start | bytes 2359304 | tf_op jit(solution)/shard_map/ppermute | solution.py:433
  34.4 2.0 %collective-permute-start.5 = (bf16[2,64,2048]{2,1,0:T(8,128)(2,1)S(1)}, bf16[2,64,2048]{2,1,0:T(8,128)(2,1)S(1)}, u32[]{:S(2)}, u32[]{:S(2)}) collective-permute-start(bf16[2,64,2048]{2,1,0:T(8,128)(2,1)S(1)} %get-tuple-element.46), channel_id=1, source_target_pairs={{0,8},{8,0},{16,24},{24,16},{1,9},{9,1},{17,25},{25,17},{2,10},{10... | collective-permute-start | bytes 1572872 | tf_op jit(solution)/shard_map/ppermute | solution.py:432
  34.4 3.1 %collective-permute-start.6 = (bf16[2,64,2048]{2,1,0:T(8,128)(2,1)S(1)}, bf16[2,64,2048]{2,1,0:T(8,128)(2,1)S(1)}, u32[]{:S(2)}, u32[]{:S(2)}) collective-permute-start(bf16[2,64,2048]{2,1,0:T(8,128)(2,1)S(1)} %get-tuple-element.47), channel_id=1, source_target_pairs={{0,8},{8,0},{16,24},{24,16},{1,9},{9,1},{17,25},{25,17},{2,10},{10... | collective-permute-start | bytes 1572872 | tf_op jit(solution)/shard_map/ppermute | solution.py:432
  34.9 15.8 %collective-permute-start.10 = (bf16[2,64,2048]{2,1,0:T(8,128)(2,1)S(1)}, bf16[2,64,2048]{2,1,0:T(8,128)(2,1)S(1)}, u32[]{:S(2)}, u32[]{:S(2)}) collective-permute-start(bf16[2,64,2048]{2,1,0:T(8,128)(2,1)S(1)} %collective-permute-done.1.refs_0_), channel_id=1, source_target_pairs={{2,0},{4,2},{6,4},{3,1},{5,3},{7,5},{10,8},{12,10},{14,12},{11,9},... | collective-permute-start | bytes 1572872 | tf_op jit(solution)/shard_map/ppermute | solution.py:434
  36.3 25.1 %collective-permute-start.11 = (bf16[2,128,2048]{2,1,0:T(8,128)(2,1)S(1)}, bf16[2,128,2048]{2,1,0:T(8,128)(2,1)S(1)}, u32[]{:S(2)}, u32[]{:S(2)}) collective-permute-start(bf16[2,128,2048]{2,1,0:T(8,128)(2,1)S(1)} %get-tuple-element.56), channel_id=1, source_target_pairs={{0,24},{8,16},{16,8},{24,0},{1,25},{9,17},{17,9},{25,1},{2,26},{10... | collective-permute-start | bytes 3145736 | tf_op jit(solution)/shard_map/ppermute | solution.py:431
  41.2 21.0 %collective-permute-start.8 = (bf16[128,2176]{1,0:T(8,128)(2,1)S(1)}, bf16[128,2176]{1,0:T(8,128)(2,1)S(1)}, u32[]{:S(2)}, u32[]{:S(2)}) collective-permute-start(bf16[128,2176]{1,0:T(8,128)(2,1)S(1)} %shard_map.39), channel_id=1, source_target_pairs={{0,1},{1,0},{2,3},{3,2},{4,5},{5,4},{6,7},{7,6},{8,9},{9,8},{10,11... | collective-permute-start | bytes 1671176 | tf_op jit(solution)/shard_map/ppermute | solution.py:438
  50.7 15.1 %copy-start.3 = (s32[2,2,1,2]{3,2,1,0:T(1,128)S(1)}, s32[2,2,1,2]{3,2,1,0:T(1,128)}, u32[]{:S(2)}) copy-start(s32[2,2,1,2]{3,2,1,0:T(1,128)} %far_ref.1) | copy-start | bytes 100
  55.5 17.0 %collective-permute-start.16 = (bf16[128,2176]{1,0:T(8,128)(2,1)S(1)}, bf16[128,2176]{1,0:T(8,128)(2,1)S(1)}, u32[]{:S(2)}, u32[]{:S(2)}) collective-permute-start(bf16[128,2176]{1,0:T(8,128)(2,1)S(1)} %get-tuple-element.53), channel_id=1, source_target_pairs={{0,1},{1,0},{2,3},{3,2},{4,5},{5,4},{6,7},{7,6},{8,9},{9,8},{10,11... | collective-permute-start | bytes 1671176 | tf_op jit(solution)/shard_map/ppermute | solution.py:445
  61.6 2.0 %collective-permute-start.14 = (bf16[2,64,2048]{2,1,0:T(8,128)(2,1)S(1)}, bf16[2,64,2048]{2,1,0:T(8,128)(2,1)S(1)}, u32[]{:S(2)}, u32[]{:S(2)}) collective-permute-start(bf16[2,64,2048]{2,1,0:T(8,128)(2,1)S(1)} %get-tuple-element.58.refs_2_), channel_id=1, source_target_pairs={{0,8},{8,0},{16,24},{24,16},{1,9},{9,1},{17,25},{25,17},{2,10},{10... | collective-permute-start | bytes 1572872 | tf_op jit(solution)/shard_map/ppermute | solution.py:449
  62.1 2.3 %collective-permute-start.15 = (bf16[2,64,2048]{2,1,0:T(8,128)(2,1)S(1)}, bf16[2,64,2048]{2,1,0:T(8,128)(2,1)S(1)}, u32[]{:S(2)}, u32[]{:S(2)}) collective-permute-start(bf16[2,64,2048]{2,1,0:T(8,128)(2,1)S(1)} %get-tuple-element.59.refs_3_), channel_id=1, source_target_pairs={{0,8},{8,0},{16,24},{24,16},{1,9},{9,1},{17,25},{25,17},{2,10},{10... | collective-permute-start | bytes 1572872 | tf_op jit(solution)/shard_map/ppermute | solution.py:449
  62.2 3.0 %collective-permute-start.12 = (bf16[2,64,2048]{2,1,0:T(8,128)(2,1)S(1)}, bf16[2,64,2048]{2,1,0:T(8,128)(2,1)S(1)}, u32[]{:S(2)}, u32[]{:S(2)}) collective-permute-start(bf16[2,64,2048]{2,1,0:T(8,128)(2,1)S(1)} %collective-permute-done.1.refs_0_), channel_id=1, source_target_pairs={{0,8},{8,0},{16,24},{24,16},{1,9},{9,1},{17,25},{25,17},{2,10},{10... | collective-permute-start | bytes 1572872 | tf_op jit(solution)/shard_map/ppermute | solution.py:449
  62.6 3.3 %collective-permute-start.13 = (bf16[2,64,2048]{2,1,0:T(8,128)(2,1)S(1)}, bf16[2,64,2048]{2,1,0:T(8,128)(2,1)S(1)}, u32[]{:S(2)}, u32[]{:S(2)}) collective-permute-start(bf16[2,64,2048]{2,1,0:T(8,128)(2,1)S(1)} %collective-permute-done.2.rows_ref.refs_1_), channel_id=1, source_target_pairs={{0,8},{8,0},{16,24},{24,16},{1,9},{9,1},{17,25},{25,17},{2,10},{10... | collective-permute-start | bytes 1572872 | tf_op jit(solution)/shard_map/ppermute | solution.py:449

commit v10 on v8

--- a/solution.py
+++ b/solution.py
@@ -12,12 +12,13 @@
 HD = 128
 NFAR = 2
 SPOT = TILE * TILE
+ROWS = 32
 NEGATIVE = -1e30
 EXP_SCALE = HD ** (-0.5) * 1.4426950408889634
 VMEM_LIMIT = 16 * 1024 * 1024
 GROUP = 4
 FINISH_COST = 1
-LATE_COST = 4 << 30
+LATE_COST = 16 << 30
 
 
 def contract_last(left, right):
@@ -49,81 +50,99 @@
     return pl.CostEstimate(flops=flops, bytes_accessed=1, transcendentals=0)
 
 
-def cut_kernel(keyvals_ref, last_rows_ref, first_rows_ref, outer_last_ref, outer_first_ref, inner_ref, sems):
-    outer = lax.axis_index("ta") % 2
-    first, last = pl.ds(0, SPOT), pl.ds(SPOT, SPOT)
-    pieces = [
-        (keyvals_ref.at[:, :, last], last_rows_ref),
-        (keyvals_ref.at[:, :, first], first_rows_ref),
-        (keyvals_ref.at[:, outer, last], outer_last_ref),
-        (keyvals_ref.at[:, outer, first], outer_first_ref),
-        (keyvals_ref.at[:, 1 - outer], inner_ref),
-    ]
-    copies = [pltpu.make_async_copy(source, target, sems.at[i]) for i, (source, target) in enumerate(pieces)]
+def run_copies(pairs, sems):
+    copies = [pltpu.make_async_copy(source, target, sems.at[i]) for i, (source, target) in enumerate(pairs)]
     for copy in copies:
         copy.start()
     for copy in copies:
         copy.wait()
 
 
+def copying_call(kernel, shapes, copies, *operands):
+    in_vmem = pl.BlockSpec(memory_space=pltpu.VMEM)
+    return pl.pallas_call(
+        kernel,
+        out_shape=[jax.ShapeDtypeStruct(shape, operands[0].dtype) for shape in shapes],
+        in_specs=[in_vmem] * len(operands),
+        out_specs=[in_vmem] * len(shapes),
+        scratch_shapes=[pltpu.SemaphoreType.DMA((copies,))],
+        compiler_params=pltpu.CompilerParams(vmem_limit_bytes=VMEM_LIMIT),
+        cost_estimate=kernel_cost(1),
+    )(*operands)
+
+
+FIRST, LAST = pl.ds(0, SPOT), pl.ds(SPOT, SPOT)
+
+
+def cut_kernel(keyvals_ref, last_rows_ref, first_rows_ref, outer_ref, inner_ref, sems):
+    outer = lax.axis_index("ta") % 2
+    pairs = [
+        (keyvals_ref.at[:, :, LAST], last_rows_ref),
+        (keyvals_ref.at[:, :, FIRST], first_rows_ref),
+        (keyvals_ref.at[:, outer], outer_ref),
+        (keyvals_ref.at[:, 1 - outer], inner_ref),
+    ]
+    run_copies(pairs, sems)
+
+
 def cut(keyvals):
     two, frames, tokens, features = keyvals.shape
-    shapes = [(two, frames, SPOT, features)] * 2 + [(two, SPOT, features)] * 2 + [(two, tokens, features)]
-    return pl.pallas_call(
-        cut_kernel,
-        out_shape=[jax.ShapeDtypeStruct(shape, keyvals.dtype) for shape in shapes],
-        in_specs=[pl.BlockSpec(memory_space=pl.ANY)],
-        out_specs=[pl.BlockSpec(memory_space=pltpu.VMEM)] * 5,
-        scratch_shapes=[pltpu.SemaphoreType.DMA((5,))],
-        compiler_params=pltpu.CompilerParams(vmem_limit_bytes=VMEM_LIMIT),
-        cost_estimate=kernel_cost(1),
-    )(keyvals)
+    shapes = [(two, frames, SPOT, features)] * 2 + [(two, tokens, features)] * 2
+    return copying_call(cut_kernel, shapes, 4, keyvals)
+
+
+def by_rows_kernel(*refs):
+    frame_refs, out_refs, sems = refs[: len(refs) // 3], refs[len(refs) // 3 : -1], refs[-1]
+    pairs = []
+    for i, frame_ref in enumerate(frame_refs):
+        for rows, out_ref in zip((FIRST, LAST), out_refs[2 * i : 2 * i + 2]):
+            pairs.append((frame_ref.at[:, rows], out_ref))
+    run_copies(pairs, sems)
+
+
+def by_rows(*frames):
+    two, _, features = frames[0].shape
+    shapes = [(two, SPOT, features)] * (2 * len(frames))
+    return copying_call(by_rows_kernel, shapes, 2 * len(frames), *frames)
+
+
+def widened_rows_kernel(frame_ref, first_ref, last_ref, sems):
+    features = frame_ref.shape[2]
+    main, extra = pl.ds(0, features), pl.ds(features, HD)
+    pairs = []
+    for rows, out_ref in ((FIRST, first_ref), (LAST, last_ref)):
+        pairs.append((frame_ref.at[:, rows], out_ref.at[:, :, main]))
+        pairs.append((frame_ref.at[:, rows, pl.ds(0, HD)], out_ref.at[:, :, extra]))
+    run_copies(pairs, sems)
+
+
+def widened_rows(frame):
+    two, _, features = frame.shape
+    return copying_call(widened_rows_kernel, [(two, SPOT, features + HD)] * 2, 4, frame)
 
 
 def inner_rows_kernel(top_ref, bottom_ref, out_top_ref, out_bottom_ref, sems):
     inner = 1 - lax.axis_index("ta") % 2
-    pairs = ((top_ref, out_top_ref), (bottom_ref, out_bottom_ref))
-    copies = [pltpu.make_async_copy(ref.at[:, inner], out, sems.at[i]) for i, (ref, out) in enumerate(pairs)]
-    for copy in copies:
-        copy.start()
-    for copy in copies:
-        copy.wait()
+    run_copies([(top_ref.at[:, inner], out_top_ref), (bottom_ref.at[:, inner], out_bottom_ref)], sems)
 
 
 def inner_rows(top, bottom):
-    shape = jax.ShapeDtypeStruct((top.shape[0],) + top.shape[2:], top.dtype)
-    in_vmem = pl.BlockSpec(memory_space=pltpu.VMEM)
-    return pl.pallas_call(
-        inner_rows_kernel,
-        out_shape=[shape] * 2,
-        in_specs=[in_vmem] * 2,
-        out_specs=[in_vmem] * 2,
-        scratch_shapes=[pltpu.SemaphoreType.DMA((2,))],
-        compiler_params=pltpu.CompilerParams(vmem_limit_bytes=VMEM_LIMIT),
-        cost_estimate=kernel_cost(1),
-    )(top, bottom)
+    return copying_call(inner_rows_kernel, [top.shape[:1] + top.shape[2:]] * 2, 2, top, bottom)
 
 
 def near_kernel(sides, home, early, has_rows, own_ref, top_ref, bottom_ref, *refs):
     parity = lax.axis_index("ta") % 2
     ha = lax.axis_index("ha")
     valid = (ha > 0, ha < has_rows - 1)
-    if early:
-        ext_ref, ext_top_ref, ext_bottom_ref, refs = refs[0], refs[1], refs[2], refs[3:]
-        frame = 1 - parity
-    else:
-        ext_first_ref, ext_last_ref, ext_top_ref, ext_bottom_ref, refs = refs[0], refs[1], refs[2], refs[3], refs[4:]
-        frame = parity
+    ext_ref, ext_top_ref, ext_bottom_ref, refs = refs[0], refs[1], refs[2], refs[3:]
+    frame = 1 - parity if early else parity
     count = sides + home
     q_refs, out_refs = refs[:count], refs[count:]
     half = count * SPOT
 
     def middle(kind, lanes):
         parts = [own_ref[kind, 0, :, lanes], own_ref[kind, 1, :, lanes]]
-        if early:
-            parts.append(ext_ref[kind, parity, :, lanes])
-        else:
-            parts += [ext_first_ref[kind, :, lanes], ext_last_ref[kind, :, lanes]]
+        parts.append(ext_ref[kind, parity, :, lanes] if early else ext_ref[kind, :, lanes])
         return jnp.concatenate(parts, axis=0)
 
     def halo(a, kind, lanes):
@@ -169,6 +188,9 @@
                     result = summed[rows, :HD]
                     if s < sides:
                         result = result / total[rows]
+                    else:
+                        filled = jnp.broadcast_to(peak[rows] * EXP_SCALE, (SPOT, HD))
+                        out_refs[s + 3][a * SPOT : (a + 1) * SPOT, lanes] = filled
                     out_refs[s][a * SPOT : (a + 1) * SPOT, lanes] = result.astype(out_refs[s].dtype)
     for a in range(2):
         tokens = slice(a * SPOT, (a + 1) * SPOT)
@@ -187,7 +209,7 @@
     operands = [own, top, bottom, *third, *visitors, *queries]
     outs = [jax.ShapeDtypeStruct((tokens, features + HD), jnp.bfloat16) for _ in visitors]
     for _ in queries:
-        outs += [jax.ShapeDtypeStruct((tokens, lanes), jnp.float32) for lanes in (features, HD, HD)]
+        outs += [jax.ShapeDtypeStruct((tokens, lanes), jnp.float32) for lanes in (features, HD, HD, features)]
     in_vmem = pl.BlockSpec(memory_space=pltpu.VMEM)
     return pl.pallas_call(
         functools.partial(near_kernel, len(visitors), len(queries), early, has_rows),
@@ -200,8 +222,8 @@
 
 
 def far_kernel(members, far_ref, q_ref, core_ref, *refs):
-    cross, cross_inner, corner, corner_inner = refs[:2], refs[2], refs[3:5], refs[5]
-    near_refs, (out_ref, peak_ref, total_ref, held, sems) = (refs[6:9], refs[9:12]), refs[12:]
+    cross_ref, cross_inner_ref, corner, corner_inner = refs[0], refs[1], refs[2:4], refs[4:6]
+    near_refs, (out_ref, peak_ref, total_ref, held, sems) = (refs[6:10], refs[10:14]), refs[14:]
     ta = lax.axis_index("ta")
     parity = ta % 2
 
@@ -223,10 +245,10 @@
                 sources = [
                     (jnp.logical_and(is_core, place == 0), core_ref.at[:, 0, rows]),
                     (jnp.logical_and(is_core, place == 1), core_ref.at[:, 1, rows]),
-                    (jnp.logical_and(is_cross, jnp.logical_not(inner)), cross[a]),
-                    (jnp.logical_and(is_cross, inner), cross_inner.at[:, rows]),
+                    (jnp.logical_and(is_cross, jnp.logical_not(inner)), cross_ref.at[:, rows]),
+                    (jnp.logical_and(is_cross, inner), cross_inner_ref.at[:, rows]),
                     (jnp.logical_and(is_corner, jnp.logical_not(inner)), corner[a]),
-                    (jnp.logical_and(is_corner, inner), corner_inner.at[:, rows]),
+                    (jnp.logical_and(is_corner, inner), corner_inner[a]),
                 ]
                 for chosen, source in sources:
 
@@ -240,7 +262,7 @@
     collected = [(jnp.zeros((SPOT, HD), jnp.float32), jnp.zeros((SPOT, HD), jnp.float32)) for _ in units]
     for first in range(0, HEADS, GROUP):
         for slot in range(4 * NFAR):
-            tile_copy(cross[0], slot // NFAR, slot % NFAR, slot, first // GROUP).wait()
+            tile_copy(corner[0], slot // NFAR, slot % NFAR, slot, first // GROUP).wait()
         work = [(h, u) for h in range(first, first + GROUP) for u in range(len(units))]
         scores = []
         for h, u in work:
@@ -251,7 +273,7 @@
         weights = []
         for (h, u), value in zip(work, scores):
             early, a = units[u]
-            near_peak = near_refs[early][1][a * SPOT : (a + 1) * SPOT, h : h + 1]
+            near_peak = near_refs[early][3][a * SPOT : (a + 1) * SPOT, h * HD : (h + 1) * HD]
             value = value * EXP_SCALE
             peak = jnp.maximum(jnp.max(value, axis=-1, keepdims=True), near_peak)
             weights.append((peak, jnp.exp2(near_peak - peak), jnp.exp2(value - peak).astype(jnp.bfloat16)))
@@ -290,60 +312,77 @@
     )(far_frames, queries, *buffers, *near)
 
 
-def finish_kernel(sides, columns, early, own_ref, own_peak_ref, own_total_ref, *refs):
-    parts, refs = refs[:sides], refs[sides:]
+def joined_frame(sides, columns, at, own_refs, parts, rows, store):
+    own_ref, own_peak_ref, own_total_ref = own_refs
     wa = lax.axis_index("wa")
-    logs = [own_peak_ref[0]]
+    logs = [own_peak_ref[at, rows, :]]
     for s in range(sides):
-        value = join_sums(parts[s][:, HEADS * HD :])
+        value = join_sums(parts[s][rows, HEADS * HD :])
         if columns > 2:
             value = jnp.where(wa < columns - 1 if s == 0 else wa > 0, value, NEGATIVE)
         logs.append(value)
     top = functools.reduce(jnp.maximum, logs)
     scales = [jnp.exp2(value - top) for value in logs]
-    total = functools.reduce(jnp.add, [scales[0] * own_total_ref[0]] + scales[1:])
+    total = functools.reduce(jnp.add, [scales[0] * own_total_ref[at, rows, :]] + scales[1:])
     scales = [value / total for value in scales]
-    if not early:
-        parity = lax.axis_index("ta") % 2
-        refs[1][1 - parity] = refs[0][...]
     for h in range(HEADS):
         lanes = slice(h * HD, (h + 1) * HD)
-        joined = scales[0][:, h : h + 1] * own_ref[0, :, lanes]
+        joined = scales[0][:, h : h + 1] * own_ref[at, rows, lanes]
         for s in range(sides):
-            joined = joined + scales[1 + s][:, h : h + 1] * parts[s][:, lanes].astype(jnp.float32)
-        if early:
-            refs[0][:, lanes] = joined.astype(jnp.bfloat16)
-        else:
-            refs[1][parity, :, lanes] = joined.astype(jnp.bfloat16)
+            joined = joined + scales[1 + s][:, h : h + 1] * parts[s][rows, lanes].astype(jnp.float32)
+        store(lanes, joined.astype(jnp.bfloat16))
+
+
+def finish_early_kernel(sides, columns, *refs):
+    own_refs, parts, out_ref = refs[:3], refs[3 : 3 + sides], refs[-1]
+    for first in range(0, out_ref.shape[0], ROWS):
+        rows = slice(first, first + ROWS)
+
+        def store(lanes, value, rows=rows):
+            out_ref[rows, lanes] = value
+
+        joined_frame(sides, columns, 0, own_refs, parts, rows, store)
+
+
+def finish_late_kernel(sides, columns, *refs):
+    own_refs, parts, (early_ref, out_ref, held, sems) = refs[:3], refs[3 : 3 + sides], refs[3 + sides :]
+    parity = lax.axis_index("ta") % 2
+    copies = [pltpu.make_async_copy(early_ref, out_ref.at[1 - parity], sems.at[0])]
+    copies[0].start()
+    for i, first in enumerate(range(0, held.shape[0], ROWS)):
+        rows, span = slice(first, first + ROWS), pl.ds(first, ROWS)
+
+        def store(lanes, value, rows=rows):
+            held[rows, lanes] = value
+
+        joined_frame(sides, columns, 1, own_refs, parts, rows, store)
+        copies.append(pltpu.make_async_copy(held.at[span], out_ref.at[parity, span], sems.at[1 + i]))
+        copies[-1].start()
+    for copy in copies:
+        copy.wait()
 
 
 def finish(columns, own, parts, early_out, cost):
-    sides, rows = len(parts), 32
+    sides = len(parts)
     frames, tokens, features = own[0].shape
+    in_vmem = pl.BlockSpec(memory_space=pltpu.VMEM)
     early = early_out is None
-    at = 0 if early else 1
-    in_specs = [
-        pl.BlockSpec((1, rows, features), lambda i: (at, i, 0)),
-        pl.BlockSpec((1, rows, HD), lambda i: (at, i, 0)),
-        pl.BlockSpec((1, rows, HD), lambda i: (at, i, 0)),
-    ]
-    in_specs += [pl.BlockSpec((rows, features + HD), lambda i: (i, 0)) for _ in parts]
-    one_frame = pl.BlockSpec((rows, features), lambda i: (i, 0))
+    operands = [*own, *parts] + ([] if early else [early_out])
+    one_frame = (tokens, features)
     if early:
-        extra, out_spec, out_shape = (), one_frame, (tokens, features)
+        kernel, out_shape, out_spec, scratch = finish_early_kernel, one_frame, in_vmem, []
     else:
-        extra, out_spec = (early_out,), pl.BlockSpec((frames, rows, features), lambda i: (0, i, 0))
-        in_specs.append(one_frame)
-        out_shape = own[0].shape
+        kernel, out_shape, out_spec = finish_late_kernel, (frames, *one_frame), pl.BlockSpec(memory_space=pl.ANY)
+        scratch = [pltpu.VMEM(one_frame, jnp.bfloat16), pltpu.SemaphoreType.DMA((1 + tokens // ROWS,))]
     return pl.pallas_call(
-        functools.partial(finish_kernel, sides, columns, early),
+        functools.partial(kernel, sides, columns),
         out_shape=jax.ShapeDtypeStruct(out_shape, jnp.bfloat16),
-        grid=(tokens // rows,),
-        in_specs=in_specs,
+        in_specs=[in_vmem] * len(operands),
         out_specs=out_spec,
+        scratch_shapes=scratch,
         compiler_params=pltpu.CompilerParams(vmem_limit_bytes=VMEM_LIMIT),
         cost_estimate=kernel_cost(cost),
-    )(*own, *parts, *extra)
+    )(*operands)
 
 
 def per_device(queries, keyvals, far_frames):
@@ -367,19 +406,18 @@
     tie = lax.optimization_barrier
 
     core = lax.ppermute(keyvals, "ta", core_pairs)
-    last_rows, first_rows, outer_last, outer_first, inner = cut(keyvals)
+    last_rows, first_rows, outer, inner = cut(keyvals)
+    cross = lax.ppermute(outer, "ta", cross_pairs)
     top = lax.ppermute(last_rows, "ha", up)
     bottom = lax.ppermute(first_rows, "ha", down)
-    cross_last = lax.ppermute(outer_last, "ta", cross_pairs)
-    outer_first, core, sent = tie((outer_first, core, queries))
-    cross_first = lax.ppermute(outer_first, "ta", cross_pairs)
+    sent, core = tie((queries, core))
     visitors = [lax.ppermute(sent, "wa", there) for there, _ in ways]
-    inner, cross_last = tie((inner, cross_last))
-    last = lax.ppermute(inner, "ta", cross_pairs)
-    top, bottom, cross_first, cross_last, visitors = tie((top, bottom, cross_first, cross_last, visitors))
-    core_top, core_bottom = [lax.ppermute(value, "ta", core_pairs) for value in inner_rows(top, bottom)]
+    cross_first, cross_last = widened_rows(cross)
     cross_top = lax.ppermute(cross_last, "ha", up)
     cross_bottom = lax.ppermute(cross_first, "ha", down)
+    inner, cross = tie((inner, cross))
+    last = lax.ppermute(inner, "ta", cross_pairs)
+    core_top, core_bottom = [lax.ppermute(value, "ta", core_pairs) for value in inner_rows(top, bottom)]
 
     early_third = (core, core_top, core_bottom)
     early = near_attention(True, ha_size, keyvals, top, bottom, early_third, visitors, [], 1)
@@ -387,15 +425,16 @@
     core_top, _ = tie((core_top, early[0]))
     early_third = (core, core_top, core_bottom)
     early_home = near_attention(True, ha_size, keyvals, top, bottom, early_third, [], [queries], 1)
-    cross_top, cross_bottom, last, _ = tie((cross_top, cross_bottom, last, early_home[1]))
-    late_third = (cross_first, cross_last, cross_top, cross_bottom)
+    cross_top, cross_bottom, _ = tie((cross_top, cross_bottom, early_home[1]))
+    late_third = (cross, cross_top, cross_bottom)
     late = near_attention(False, ha_size, keyvals, top, bottom, late_third, visitors, [queries], LATE_COST)
     late_parts = [lax.ppermute(result, "wa", back) for result, (_, back) in zip(late, ways)]
-    frames_here = (cross_first, cross_last, last)
-    frames_here, early_parts, _ = tie((frames_here, early_parts, late[0]))
-    corner = [lax.ppermute(value, "ta", core_pairs) for value in frames_here]
-    buffers = (core, *frames_here, *corner)
-    own = far_attention(ta_size, far_frames, queries, buffers, (*early_home, *late[-3:]))
+    last, _ = tie((last, late[0]))
+    *cross_rows, inner_first, inner_last = by_rows(cross, last)
+    cross_rows, early_parts, _ = tie((cross_rows, early_parts, late[0]))
+    corner = [lax.ppermute(value, "ta", core_pairs) for value in (*cross_rows, inner_first, inner_last)]
+    buffers = (core, cross, last, *corner)
+    own = far_attention(ta_size, far_frames, queries, buffers, (*early_home, *late[-4:]))
     out = finish(wa_size, own, early_parts, None, FINISH_COST)
     out = finish(wa_size, own, late_parts, out, 1)
     return out.reshape(shape)

time: 80.2 us -> 76.1 us (0.949)
  waiting for transfers between devices: 35.9 us -> 33.4 us
  starting transfers between devices: 20.3 us -> 19.3 us
    ppermute x2 -> x6, waiting for transfers between devices: 0.01 us -> 4.93 us  [per_device(): lax.ppermute(value, 'ta', core_pairs)]
    ppermute x1, waiting for transfers between devices: 4.55 us -> 0.01 us  [per_device(): top = lax.ppermute(last_rows, 'ha', up)]
    ppermute x2, waiting for transfers between devices: 3.31 us -> 0.01 us  [per_device(): lax.ppermute(result, 'wa', back)]
    ppermute x1, waiting for transfers between devices: 4.18 us -> 2.04 us  [per_device(): bottom = lax.ppermute(first_rows, 'ha', down)]
    ppermute x2, starting transfers between devices: 1.07 us -> 3.18 us  [per_device(): lax.ppermute(result, 'wa', back)]
    ppermute x1, starting transfers between devices: 5.16 us -> 3.19 us  [per_device(): cross_top = lax.ppermute(cross_last, 'ha', up)]
    ppermute x1, waiting for transfers between devices: 0.01 us -> 1.95 us  [per_device(): cross_bottom = lax.ppermute(cross_first, 'ha', down)]
    ppermute x1, starting transfers between devices: 4.68 us -> 3.53 us  [per_device(): top = lax.ppermute(last_rows, 'ha', up)]
  transfers between devices with their start and end apart: 16 -> 16, of which waited for: 8 -> 10; matrix products, arithmetic and copies ran while one was open for 0% -> 0% of each run, Pallas kernels for 25% -> 25%
where the time goes in v10:
time: 76.1 us; the launch traced here: 75.9 us
  waiting for transfers between devices  33.4 us (44%)
  Pallas kernels  21.3 us (28%)
  starting transfers between devices  19.3 us (25%)
  local copies, waits for them, and re-layouts  1.61 us (2%)
    ppermute x1, waiting for transfers between devices, per_device(): cross = lax.ppermute(outer, 'ta', cross_pairs)  17.1 us
    pallas_call x3, Pallas kernels, near_attention(): pl.pallas_call(functools.partial(near_kernel, len(visitors), len(queries)...  11.8 us
    ppermute x1, waiting for transfers between devices, per_device(): last = lax.ppermute(inner, 'ta', cross_pairs)  7.38 us
    pallas_call x1, Pallas kernels, far_attention(): pl.pallas_call(functools.partial(far_kernel, members), out_shape=[jax.Sha...  5.19 us
    ppermute x6, waiting for transfers between devices, per_device(): lax.ppermute(value, 'ta', core_pairs)  4.93 us
    pallas_call x2, Pallas kernels, finish(): pl.pallas_call(functools.partial(kernel, sides, columns), out_shape=jax.S...  3.56 us
    ppermute x1, starting transfers between devices, per_device(): top = lax.ppermute(last_rows, 'ha', up)  3.53 us
    ppermute x1, starting transfers between devices, per_device(): cross_top = lax.ppermute(cross_last, 'ha', up)  3.19 us
  transfers between devices with their start and end apart: 16, of which 10 were waited for; matrix products, arithmetic and copies ran while one was open for 0% of the time, Pallas kernels for 25%

profile of v10, /device:TPU:0, one launch (start us, length us, event | category | flops | bytes accessed | tf_op | source)
XLA Modules:
  0.0 75.9 jit_solution(3257839299477528551)
XLA Ops:
  0.5 1.6 %copy-done = bf16[2,2,16,8,2048]{4,3,2,1,0:T(8,128)(2,1)S(1)} copy-done((bf16[2,2,16,8,2048]{4,3,2,1,0:T(8,128)(2,1)S(1)}, bf16[2,2,16,8,2048]{4,3,2,1,0:T(8,128)(2,1)}, u32[]{:S(2)}) %copy-start) | copy-done | bytes 2097176
  2.4 2.7 %collective-permute-start.1 = (bf16[2,128,2048]{2,1,0:T(8,128)(2,1)S(1)}, bf16[2,128,2048]{2,1,0:T(8,128)(2,1)S(1)}, u32[]{:S(2)}, u32[]{:S(2)}) collective-permute-start(bf16[2,128,2048]{2,1,0:T(8,128)(2,1)S(1)} %get-tuple-element.42), channel_id=1, source_target_pairs={{0,24},{8,16},{16,8},{24,0},{1,25},{9,17},{17,9},{25,1},{2,26},{10... | collective-permute-start | bytes 3145736 | tf_op jit(solution)/shard_map/ppermute | solution.py:410
  5.1 3.5 %collective-permute-start.3 = (bf16[2,2,64,2048]{3,2,1,0:T(8,128)(2,1)S(1)}, bf16[2,2,64,2048]{3,2,1,0:T(8,128)(2,1)S(1)}, u32[]{:S(2)}, u32[]{:S(2)}) collective-permute-start(bf16[2,2,64,2048]{3,2,1,0:T(8,128)(2,1)S(1)} %get-tuple-element.45), channel_id=1, source_target_pairs={{0,2},{2,4},{4,6},{1,3},{3,5},{5,7},{8,10},{10,12},{12,14},{9,11},... | collective-permute-start | bytes 3145736 | tf_op jit(solution)/shard_map/ppermute | solution.py:411
  8.6 1.3 %collective-permute-start.4 = (bf16[2,2,64,2048]{3,2,1,0:T(8,128)(2,1)S(1)}, bf16[2,2,64,2048]{3,2,1,0:T(8,128)(2,1)S(1)}, u32[]{:S(2)}, u32[]{:S(2)}) collective-permute-start(bf16[2,2,64,2048]{3,2,1,0:T(8,128)(2,1)S(1)} %get-tuple-element.46), channel_id=1, source_target_pairs={{2,0},{4,2},{6,4},{3,1},{5,3},{7,5},{10,8},{12,10},{14,12},{11,9},... | collective-permute-start | bytes 3145736 | tf_op jit(solution)/shard_map/ppermute | solution.py:412
  9.9 1.6 %collective-permute-start.9 = (bf16[2,128,2048]{2,1,0:T(8,128)(2,1)S(1)}, bf16[2,128,2048]{2,1,0:T(8,128)(2,1)S(1)}, u32[]{:S(2)}, u32[]{:S(2)}) collective-permute-start(bf16[2,128,2048]{2,1,0:T(8,128)(2,1)S(1)} %bitcast.8), channel_id=1, source_target_pairs={{0,1},{1,0},{2,3},{3,2},{4,5},{5,4},{6,7},{7,6},{8,9},{9,8},{10,11... | collective-permute-start | bytes 3145736 | tf_op jit(solution)/shard_map/ppermute | solution.py:414
  11.5 17.1 %collective-permute-done.1.frame_ref.refs_0_ = bf16[2,128,2048]{2,1,0:T(8,128)(2,1)S(1)} collective-permute-done((bf16[2,128,2048]{2,1,0:T(8,128)(2,1)S(1)}, bf16[2,128,2048]{2,1,0:T(8,128)(2,1)S(1)}, u32[]{:S(2)}, u32[]{:S(2)}) %collective-permute-start.1) | collective-permute-done | bytes 1048608 | tf_op jit(solution)/shard_map/ppermute | solution.py:410
  28.7 3.2 %collective-permute-start.5 = (bf16[2,64,2176]{2,1,0:T(8,128)(2,1)S(1)}, bf16[2,64,2176]{2,1,0:T(8,128)(2,1)S(1)}, u32[]{:S(2)}, u32[]{:S(2)}) collective-permute-start(bf16[2,64,2176]{2,1,0:T(8,128)(2,1)S(1)} %get-tuple-element.47), channel_id=1, source_target_pairs={{0,2},{2,4},{4,6},{1,3},{3,5},{5,7},{8,10},{10,12},{12,14},{9,11},... | collective-permute-start | bytes 1671176 | tf_op jit(solution)/shard_map/ppermute | solution.py:416
  31.9 1.3 %collective-permute-start.6 = (bf16[2,64,2176]{2,1,0:T(8,128)(2,1)S(1)}, bf16[2,64,2176]{2,1,0:T(8,128)(2,1)S(1)}, u32[]{:S(2)}, u32[]{:S(2)}) collective-permute-start(bf16[2,64,2176]{2,1,0:T(8,128)(2,1)S(1)} %get-tuple-element.48), channel_id=1, source_target_pairs={{2,0},{4,2},{6,4},{3,1},{5,3},{7,5},{10,8},{12,10},{14,12},{11,9},... | collective-permute-start | bytes 1671176 | tf_op jit(solution)/shard_map/ppermute | solution.py:417
  33.2 2.0 %collective-permute-done.4.bottom_ref = bf16[2,2,64,2048]{3,2,1,0:T(8,128)(2,1)S(1)} collective-permute-done((bf16[2,2,64,2048]{3,2,1,0:T(8,128)(2,1)S(1)}, bf16[2,2,64,2048]{3,2,1,0:T(8,128)(2,1)S(1)}, u32[]{:S(2)}, u32[]{:S(2)}) %collective-permute-start.4) | collective-permute-done | bytes 1048608 | tf_op jit(solution)/shard_map/ppermute | solution.py:412
  36.0 1.4 %collective-permute-done.7.refs_1_ = bf16[2,64,2048]{2,1,0:T(8,128)(2,1)S(1)} collective-permute-done((bf16[2,64,2048]{2,1,0:T(8,128)(2,1)S(1)}, bf16[2,64,2048]{2,1,0:T(8,128)(2,1)S(1)}, u32[]{:S(2)}, u32[]{:S(2)}) %collective-permute-start.7) | collective-permute-done | bytes 524320 | tf_op jit(solution)/shard_map/ppermute | solution.py:420
  38.1 3.6 %shard_map.40 = bf16[128,2176]{1,0:T(8,128)(2,1)S(1)} custom-call(bf16[2,2,128,2048]{3,2,1,0:T(8,128)(2,1)S(1)} %bitcast.5, bf16[2,2,64,2048]{3,2,1,0:T(8,128)(2,1)S(1)} %collective-permute-done.3.top_ref, bf16[2,2,64,2048]{3,2,1,0:T(8,128)(2,1)S(1)} %collective-permute-done.4.bottom_ref, ...), custom_call_target="tpu_custom_call" | custom-call | flops 1 | bytes 1 | tf_op jit(solution)/shard_map/pallas_call | solution.py:214
  41.7 1.6 %collective-permute-start.10 = (bf16[128,2176]{1,0:T(8,128)(2,1)S(1)}, bf16[128,2176]{1,0:T(8,128)(2,1)S(1)}, u32[]{:S(2)}, u32[]{:S(2)}) collective-permute-start(bf16[128,2176]{1,0:T(8,128)(2,1)S(1)} %shard_map.40), channel_id=1, source_target_pairs={{0,1},{1,0},{2,3},{3,2},{4,5},{5,4},{6,7},{7,6},{8,9},{9,8},{10,11... | collective-permute-start | bytes 1671176 | tf_op jit(solution)/shard_map/ppermute | solution.py:424
  43.3 3.6 %shard_map.41 = (f32[128,2048]{1,0:T(8,128)S(1)}, f32[128,128]{1,0:T(8,128)S(1)}, f32[128,128]{1,0:T(8,128)S(1)}, f32[128,2048]{1,0:T(8,128)S(1)}) custom-call(bf16[2,2,128,2048]{3,2,1,0:T(8,128)(2,1)S(1)} %bitcast.6, bf16[2,2,64,2048]{3,2,1,0:T(8,128)(2,1)S(1)} %collective-permute-done.3.top_ref, ...), custom_call_target="tpu_custom_call" | custom-call | flops 1 | bytes 1 | tf_op jit(solution)/shard_map/pallas_call | solution.py:214
  46.9 2.0 %collective-permute-done.6.refs_2_ = bf16[2,64,2176]{2,1,0:T(8,128)(2,1)S(1)} collective-permute-done((bf16[2,64,2176]{2,1,0:T(8,128)(2,1)S(1)}, bf16[2,64,2176]{2,1,0:T(8,128)(2,1)S(1)}, u32[]{:S(2)}, u32[]{:S(2)}) %collective-permute-start.6) | collective-permute-done | bytes 557088 | tf_op jit(solution)/shard_map/ppermute | solution.py:417
  48.8 4.7 %shard_map.42 = (bf16[128,2176]{1,0:T(8,128)(2,1)S(1)}, f32[128,2048]{1,0:T(8,128)S(1)}, f32[128,128]{1,0:T(8,128)S(1)}, f32[128,128]{1,0:T(8,128)S(1)}, f32[128,2048]{1,0:T(8,128)S(1)}) custom-call(bf16[2,2,128,2048]{3,2,1,0:T(8,128)(2,1)S(1)} %bitcast.7, bf16[2,2,64,2048]{3,2,1,0:T(8,128)(2,1)S(1)} %collective-permute-done.3.top_ref, ...), custom_call_target="tpu_custom_call" | custom-call | flops 17179869184 | bytes 1 | tf_op jit(solution)/shard_map/pallas_call | solution.py:214
  53.5 1.6 %collective-permute-start.15 = (bf16[128,2176]{1,0:T(8,128)(2,1)S(1)}, bf16[128,2176]{1,0:T(8,128)(2,1)S(1)}, u32[]{:S(2)}, u32[]{:S(2)}) collective-permute-start(bf16[128,2176]{1,0:T(8,128)(2,1)S(1)} %get-tuple-element.56), channel_id=1, source_target_pairs={{0,1},{1,0},{2,3},{3,2},{4,5},{5,4},{6,7},{7,6},{8,9},{9,8},{10,11... | collective-permute-start | bytes 1671176 | tf_op jit(solution)/shard_map/ppermute | solution.py:431
  55.1 7.4 %collective-permute-done.2.refs_1_ = bf16[2,128,2048]{2,1,0:T(8,128)(2,1)S(1)} collective-permute-done((bf16[2,128,2048]{2,1,0:T(8,128)(2,1)S(1)}, bf16[2,128,2048]{2,1,0:T(8,128)(2,1)S(1)}, u32[]{:S(2)}, u32[]{:S(2)}) %collective-permute-start.2) | collective-permute-done | bytes 1048608 | tf_op jit(solution)/shard_map/ppermute | solution.py:419
  63.8 0.9 %collective-permute-done.13.refs_4_ = bf16[2,64,2048]{2,1,0:T(8,128)(2,1)S(1)} collective-permute-done((bf16[2,64,2048]{2,1,0:T(8,128)(2,1)S(1)}, bf16[2,64,2048]{2,1,0:T(8,128)(2,1)S(1)}, u32[]{:S(2)}, u32[]{:S(2)}) %collective-permute-start.13) | collective-permute-done | bytes 524320 | tf_op jit(solution)/shard_map/ppermute | solution.py:435
  64.7 0.7 collective-permute-done.14.refs_5_
  65.5 0.7 collective-permute-done.11.refs_2_
  66.2 0.7 collective-permute-done.12.refs_3_
  67.0 5.2 %shard_map.44 = (f32[2,128,2048]{2,1,0:T(8,128)S(1)}, f32[2,128,128]{2,1,0:T(8,128)S(1)}, f32[2,128,128]{2,1,0:T(8,128)S(1)}) custom-call(s32[2,2,1,2]{3,2,1,0:T(1,128)S(1)} %copy-done.3, bf16[2,128,2048]{2,1,0:T(8,128)(2,1)S(1)} %bitcast.11, bf16[2,2,128,2048]{3,2,1,0:T(8,128)(2,1)S(1)} %collective-permute-done.refs_0_.core_ref, ...), custom_call_target="tpu_custom_call" | custom-call | flops 1 | bytes 1 | tf_op jit(solution)/shard_map/pallas_call | solution.py:301
  72.2 1.3 %shard_map.45.refs_4_ = bf16[128,2048]{1,0:T(8,128)(2,1)S(1)} custom-call(f32[2,128,2048]{2,1,0:T(8,128)S(1)} %get-tuple-element.71.refs_0_, f32[2,128,128]{2,1,0:T(8,128)S(1)} %get-tuple-element.72.refs_1_, f32[2,128,128]{2,1,0:T(8,128)S(1)} %get-tuple-element.73.refs_2_, bf16[128,2176]{1,0:T(8,128)(2,1)S(1)} %collective-permute-done.10.refs_3_), custom_call_target="tpu_custom_call" | custom-call | flops 1 | bytes 1 | tf_op jit(solution)/shard_map/pallas_call | solution.py:377
  73.5 2.2 %shard_map.46 = bf16[2,128,2048]{2,1,0:T(8,128)(2,1)} custom-call(f32[2,128,2048]{2,1,0:T(8,128)S(1)} %get-tuple-element.71.refs_0_, f32[2,128,128]{2,1,0:T(8,128)S(1)} %get-tuple-element.72.refs_1_, f32[2,128,128]{2,1,0:T(8,128)S(1)} %get-tuple-element.73.refs_2_, bf16[128,2176]{1,0:T(8,128)(2,1)S(1)} %collective-permute-done.15.refs_3_, ...), custom_call_target="tpu_custom_call" | custom-call | flops 1 | bytes 1 | tf_op jit(solution)/shard_map/pallas_call | solution.py:377
  (26 shorter events, 3.6 us)
Async XLA Ops:
  0.0 9.9 %collective-permute-start = (bf16[2,2,128,2048]{3,2,1,0:T(8,128)(2,1)}, bf16[2,2,128,2048]{3,2,1,0:T(8,128)(2,1)S(1)}, u32[]{:S(2)}, u32[]{:S(2)}) collective-permute-start(bf16[2,2,128,2048]{3,2,1,0:T(8,128)(2,1)} %bitcast.3), channel_id=1, source_target_pairs={{0,8},{8,0},{16,24},{24,16},{1,9},{9,1},{17,25},{25,17},{2,10},{10... | collective-permute-start | bytes 6291464 | tf_op jit(solution)/shard_map/ppermute | solution.py:408
  0.5 1.6 %copy-start = (bf16[2,2,16,8,2048]{4,3,2,1,0:T(8,128)(2,1)S(1)}, bf16[2,2,16,8,2048]{4,3,2,1,0:T(8,128)(2,1)}, u32[]{:S(2)}) copy-start(bf16[2,2,16,8,2048]{4,3,2,1,0:T(8,128)(2,1)} %param.4) | copy-start | bytes 6291460
  2.0 7.9 %copy-start.2 = (bf16[2,16,8,2048]{3,2,1,0:T(8,128)(2,1)S(1)}, bf16[2,16,8,2048]{3,2,1,0:T(8,128)(2,1)}, u32[]{:S(2)}) copy-start(bf16[2,16,8,2048]{3,2,1,0:T(8,128)(2,1)} %param.3) | copy-start | bytes 3145732
  2.4 35.7 %copy-start.1 = (bf16[2,2,16,8,2048]{4,3,2,1,0:T(8,128)(2,1)S(1)}, bf16[2,2,16,8,2048]{4,3,2,1,0:T(8,128)(2,1)}, u32[]{:S(2)}) copy-start(bf16[2,2,16,8,2048]{4,3,2,1,0:T(8,128)(2,1)} %param.4) | copy-start | bytes 6291460
  2.4 26.2 %collective-permute-start.1 = (bf16[2,128,2048]{2,1,0:T(8,128)(2,1)S(1)}, bf16[2,128,2048]{2,1,0:T(8,128)(2,1)S(1)}, u32[]{:S(2)}, u32[]{:S(2)}) collective-permute-start(bf16[2,128,2048]{2,1,0:T(8,128)(2,1)S(1)} %get-tuple-element.42), channel_id=1, source_target_pairs={{0,24},{8,16},{16,8},{24,0},{1,25},{9,17},{17,9},{25,1},{2,26},{10... | collective-permute-start | bytes 3145736 | tf_op jit(solution)/shard_map/ppermute | solution.py:410
  5.1 28.2 %collective-permute-start.3 = (bf16[2,2,64,2048]{3,2,1,0:T(8,128)(2,1)S(1)}, bf16[2,2,64,2048]{3,2,1,0:T(8,128)(2,1)S(1)}, u32[]{:S(2)}, u32[]{:S(2)}) collective-permute-start(bf16[2,2,64,2048]{3,2,1,0:T(8,128)(2,1)S(1)} %get-tuple-element.45), channel_id=1, source_target_pairs={{0,2},{2,4},{4,6},{1,3},{3,5},{5,7},{8,10},{10,12},{12,14},{9,11},... | collective-permute-start | bytes 3145736 | tf_op jit(solution)/shard_map/ppermute | solution.py:411
  8.6 26.7 %collective-permute-start.4 = (bf16[2,2,64,2048]{3,2,1,0:T(8,128)(2,1)S(1)}, bf16[2,2,64,2048]{3,2,1,0:T(8,128)(2,1)S(1)}, u32[]{:S(2)}, u32[]{:S(2)}) collective-permute-start(bf16[2,2,64,2048]{3,2,1,0:T(8,128)(2,1)S(1)} %get-tuple-element.46), channel_id=1, source_target_pairs={{2,0},{4,2},{6,4},{3,1},{5,3},{7,5},{10,8},{12,10},{14,12},{11,9},... | collective-permute-start | bytes 3145736 | tf_op jit(solution)/shard_map/ppermute | solution.py:412
  9.9 28.2 %collective-permute-start.9 = (bf16[2,128,2048]{2,1,0:T(8,128)(2,1)S(1)}, bf16[2,128,2048]{2,1,0:T(8,128)(2,1)S(1)}, u32[]{:S(2)}, u32[]{:S(2)}) collective-permute-start(bf16[2,128,2048]{2,1,0:T(8,128)(2,1)S(1)} %bitcast.8), channel_id=1, source_target_pairs={{0,1},{1,0},{2,3},{3,2},{4,5},{5,4},{6,7},{7,6},{8,9},{9,8},{10,11... | collective-permute-start | bytes 3145736 | tf_op jit(solution)/shard_map/ppermute | solution.py:414
  28.7 18.1 %collective-permute-start.5 = (bf16[2,64,2176]{2,1,0:T(8,128)(2,1)S(1)}, bf16[2,64,2176]{2,1,0:T(8,128)(2,1)S(1)}, u32[]{:S(2)}, u32[]{:S(2)}) collective-permute-start(bf16[2,64,2176]{2,1,0:T(8,128)(2,1)S(1)} %get-tuple-element.47), channel_id=1, source_target_pairs={{0,2},{2,4},{4,6},{1,3},{3,5},{5,7},{8,10},{10,12},{12,14},{9,11},... | collective-permute-start | bytes 1671176 | tf_op jit(solution)/shard_map/ppermute | solution.py:416
  31.9 16.9 %collective-permute-start.6 = (bf16[2,64,2176]{2,1,0:T(8,128)(2,1)S(1)}, bf16[2,64,2176]{2,1,0:T(8,128)(2,1)S(1)}, u32[]{:S(2)}, u32[]{:S(2)}) collective-permute-start(bf16[2,64,2176]{2,1,0:T(8,128)(2,1)S(1)} %get-tuple-element.48), channel_id=1, source_target_pairs={{2,0},{4,2},{6,4},{3,1},{5,3},{7,5},{10,8},{12,10},{14,12},{11,9},... | collective-permute-start | bytes 1671176 | tf_op jit(solution)/shard_map/ppermute | solution.py:417
  35.4 2.0 %collective-permute-start.7 = (bf16[2,64,2048]{2,1,0:T(8,128)(2,1)S(1)}, bf16[2,64,2048]{2,1,0:T(8,128)(2,1)S(1)}, u32[]{:S(2)}, u32[]{:S(2)}) collective-permute-start(bf16[2,64,2048]{2,1,0:T(8,128)(2,1)S(1)} %get-tuple-element.49), channel_id=1, source_target_pairs={{0,8},{8,0},{16,24},{24,16},{1,9},{9,1},{17,25},{25,17},{2,10},{10... | collective-permute-start | bytes 1572872 | tf_op jit(solution)/shard_map/ppermute | solution.py:420
  35.5 2.6 %collective-permute-start.8 = (bf16[2,64,2048]{2,1,0:T(8,128)(2,1)S(1)}, bf16[2,64,2048]{2,1,0:T(8,128)(2,1)S(1)}, u32[]{:S(2)}, u32[]{:S(2)}) collective-permute-start(bf16[2,64,2048]{2,1,0:T(8,128)(2,1)S(1)} %get-tuple-element.50), channel_id=1, source_target_pairs={{0,8},{8,0},{16,24},{24,16},{1,9},{9,1},{17,25},{25,17},{2,10},{10... | collective-permute-start | bytes 1572872 | tf_op jit(solution)/shard_map/ppermute | solution.py:420
  37.4 25.1 %collective-permute-start.2 = (bf16[2,128,2048]{2,1,0:T(8,128)(2,1)S(1)}, bf16[2,128,2048]{2,1,0:T(8,128)(2,1)S(1)}, u32[]{:S(2)}, u32[]{:S(2)}) collective-permute-start(bf16[2,128,2048]{2,1,0:T(8,128)(2,1)S(1)} %get-tuple-element.44), channel_id=1, source_target_pairs={{0,24},{8,16},{16,8},{24,0},{1,25},{9,17},{17,9},{25,1},{2,26},{10... | collective-permute-start | bytes 3145736 | tf_op jit(solution)/shard_map/ppermute | solution.py:419
  41.7 21.6 %collective-permute-start.10 = (bf16[128,2176]{1,0:T(8,128)(2,1)S(1)}, bf16[128,2176]{1,0:T(8,128)(2,1)S(1)}, u32[]{:S(2)}, u32[]{:S(2)}) collective-permute-start(bf16[128,2176]{1,0:T(8,128)(2,1)S(1)} %shard_map.40), channel_id=1, source_target_pairs={{0,1},{1,0},{2,3},{3,2},{4,5},{5,4},{6,7},{7,6},{8,9},{9,8},{10,11... | collective-permute-start | bytes 1671176 | tf_op jit(solution)/shard_map/ppermute | solution.py:424
  53.5 13.5 %copy-start.3 = (s32[2,2,1,2]{3,2,1,0:T(1,128)S(1)}, s32[2,2,1,2]{3,2,1,0:T(1,128)}, u32[]{:S(2)}) copy-start(s32[2,2,1,2]{3,2,1,0:T(1,128)} %far_ref.1) | copy-start | bytes 100
  53.5 20.0 %collective-permute-start.15 = (bf16[128,2176]{1,0:T(8,128)(2,1)S(1)}, bf16[128,2176]{1,0:T(8,128)(2,1)S(1)}, u32[]{:S(2)}, u32[]{:S(2)}) collective-permute-start(bf16[128,2176]{1,0:T(8,128)(2,1)S(1)} %get-tuple-element.56), channel_id=1, source_target_pairs={{0,1},{1,0},{2,3},{3,2},{4,5},{5,4},{6,7},{7,6},{8,9},{9,8},{10,11... | collective-permute-start | bytes 1671176 | tf_op jit(solution)/shard_map/ppermute | solution.py:431
  62.7 2.0 %collective-permute-start.13 = (bf16[2,64,2048]{2,1,0:T(8,128)(2,1)S(1)}, bf16[2,64,2048]{2,1,0:T(8,128)(2,1)S(1)}, u32[]{:S(2)}, u32[]{:S(2)}) collective-permute-start(bf16[2,64,2048]{2,1,0:T(8,128)(2,1)S(1)} %get-tuple-element.62), channel_id=1, source_target_pairs={{0,8},{8,0},{16,24},{24,16},{1,9},{9,1},{17,25},{25,17},{2,10},{10... | collective-permute-start | bytes 1572872 | tf_op jit(solution)/shard_map/ppermute | solution.py:435
  63.2 2.3 %collective-permute-start.14 = (bf16[2,64,2048]{2,1,0:T(8,128)(2,1)S(1)}, bf16[2,64,2048]{2,1,0:T(8,128)(2,1)S(1)}, u32[]{:S(2)}, u32[]{:S(2)}) collective-permute-start(bf16[2,64,2048]{2,1,0:T(8,128)(2,1)S(1)} %get-tuple-element.63), channel_id=1, source_target_pairs={{0,8},{8,0},{16,24},{24,16},{1,9},{9,1},{17,25},{25,17},{2,10},{10... | collective-permute-start | bytes 1572872 | tf_op jit(solution)/shard_map/ppermute | solution.py:435
  63.3 3.0 %collective-permute-start.11 = (bf16[2,64,2048]{2,1,0:T(8,128)(2,1)S(1)}, bf16[2,64,2048]{2,1,0:T(8,128)(2,1)S(1)}, u32[]{:S(2)}, u32[]{:S(2)}) collective-permute-start(bf16[2,64,2048]{2,1,0:T(8,128)(2,1)S(1)} %get-tuple-element.60), channel_id=1, source_target_pairs={{0,8},{8,0},{16,24},{24,16},{1,9},{9,1},{17,25},{25,17},{2,10},{10... | collective-permute-start | bytes 1572872 | tf_op jit(solution)/shard_map/ppermute | solution.py:435
  63.7 3.3 %collective-permute-start.12 = (bf16[2,64,2048]{2,1,0:T(8,128)(2,1)S(1)}, bf16[2,64,2048]{2,1,0:T(8,128)(2,1)S(1)}, u32[]{:S(2)}, u32[]{:S(2)}) collective-permute-start(bf16[2,64,2048]{2,1,0:T(8,128)(2,1)S(1)} %get-tuple-element.61), channel_id=1, source_target_pairs={{0,8},{8,0},{16,24},{24,16},{1,9},{9,1},{17,25},{25,17},{2,10},{10... | collective-permute-start | bytes 1572872 | tf_op jit(solution)/shard_map/ppermute | solution.py:435

commit v11 on v10

--- a/solution.py
+++ b/solution.py
@@ -12,13 +12,12 @@
 HD = 128
 NFAR = 2
 SPOT = TILE * TILE
-ROWS = 32
 NEGATIVE = -1e30
 EXP_SCALE = HD ** (-0.5) * 1.4426950408889634
 VMEM_LIMIT = 16 * 1024 * 1024
 GROUP = 4
 FINISH_COST = 1
-LATE_COST = 16 << 30
+LATE_COST = 28 << 30
 
 
 def contract_last(left, right):
@@ -312,36 +311,38 @@
     )(far_frames, queries, *buffers, *near)
 
 
-def joined_frame(sides, columns, at, own_refs, parts, rows, store):
-    own_ref, own_peak_ref, own_total_ref = own_refs
+def frame_scales(sides, columns, at, own_refs, parts):
+    _, own_peak_ref, own_total_ref = own_refs
     wa = lax.axis_index("wa")
-    logs = [own_peak_ref[at, rows, :]]
+    logs = [own_peak_ref[at]]
     for s in range(sides):
-        value = join_sums(parts[s][rows, HEADS * HD :])
+        value = join_sums(parts[s][:, HEADS * HD :])
         if columns > 2:
             value = jnp.where(wa < columns - 1 if s == 0 else wa > 0, value, NEGATIVE)
         logs.append(value)
     top = functools.reduce(jnp.maximum, logs)
     scales = [jnp.exp2(value - top) for value in logs]
-    total = functools.reduce(jnp.add, [scales[0] * own_total_ref[at, rows, :]] + scales[1:])
-    scales = [value / total for value in scales]
-    for h in range(HEADS):
-        lanes = slice(h * HD, (h + 1) * HD)
-        joined = scales[0][:, h : h + 1] * own_ref[at, rows, lanes]
-        for s in range(sides):
-            joined = joined + scales[1 + s][:, h : h + 1] * parts[s][rows, lanes].astype(jnp.float32)
-        store(lanes, joined.astype(jnp.bfloat16))
+    total = functools.reduce(jnp.add, [scales[0] * own_total_ref[at]] + scales[1:])
+    heads = lane_index(top.shape[0]) < HEADS
+    return [split_sums(jnp.where(heads, value / total, 0.0)) for value in scales]
+
+
+def joined_head(h, at, own_ref, parts, scales):
+    row = lax.broadcasted_iota(jnp.int32, (HD, HD), 0)
+    spread = jnp.where(jnp.logical_and(row % HEADS == h, row < 3 * HEADS), 1.0, 0.0).astype(jnp.bfloat16)
+    lanes = slice(h * HD, (h + 1) * HD)
+    factors = [jnp.dot(value, spread, preferred_element_type=jnp.float32) for value in scales]
+    joined = factors[0] * own_ref[at, :, lanes]
+    for factor, part in zip(factors[1:], parts):
+        joined = joined + factor * part[:, lanes].astype(jnp.float32)
+    return joined.astype(jnp.bfloat16)
 
 
 def finish_early_kernel(sides, columns, *refs):
     own_refs, parts, out_ref = refs[:3], refs[3 : 3 + sides], refs[-1]
-    for first in range(0, out_ref.shape[0], ROWS):
-        rows = slice(first, first + ROWS)
-
-        def store(lanes, value, rows=rows):
-            out_ref[rows, lanes] = value
-
-        joined_frame(sides, columns, 0, own_refs, parts, rows, store)
+    scales = frame_scales(sides, columns, 0, own_refs, parts)
+    for h in range(HEADS):
+        out_ref[:, h * HD : (h + 1) * HD] = joined_head(h, 0, own_refs[0], parts, scales)
 
 
 def finish_late_kernel(sides, columns, *refs):
@@ -349,15 +350,14 @@
     parity = lax.axis_index("ta") % 2
     copies = [pltpu.make_async_copy(early_ref, out_ref.at[1 - parity], sems.at[0])]
     copies[0].start()
-    for i, first in enumerate(range(0, held.shape[0], ROWS)):
-        rows, span = slice(first, first + ROWS), pl.ds(first, ROWS)
-
-        def store(lanes, value, rows=rows):
-            held[rows, lanes] = value
-
-        joined_frame(sides, columns, 1, own_refs, parts, rows, store)
-        copies.append(pltpu.make_async_copy(held.at[span], out_ref.at[parity, span], sems.at[1 + i]))
-        copies[-1].start()
+    scales = frame_scales(sides, columns, 1, own_refs, parts)
+    for first in range(0, HEADS, GROUP):
+        for h in range(first, first + GROUP):
+            held[:, h * HD : (h + 1) * HD] = joined_head(h, 1, own_refs[0], parts, scales)
+        lanes = pl.ds(first * HD, GROUP * HD)
+        copy = pltpu.make_async_copy(held.at[:, lanes], out_ref.at[parity, :, lanes], sems.at[1 + first // GROUP])
+        copy.start()
+        copies.append(copy)
     for copy in copies:
         copy.wait()
 
@@ -373,7 +373,7 @@
         kernel, out_shape, out_spec, scratch = finish_early_kernel, one_frame, in_vmem, []
     else:
         kernel, out_shape, out_spec = finish_late_kernel, (frames, *one_frame), pl.BlockSpec(memory_space=pl.ANY)
-        scratch = [pltpu.VMEM(one_frame, jnp.bfloat16), pltpu.SemaphoreType.DMA((1 + tokens // ROWS,))]
+        scratch = [pltpu.VMEM(one_frame, jnp.bfloat16), pltpu.SemaphoreType.DMA((1 + HEADS // GROUP,))]
     return pl.pallas_call(
         functools.partial(kernel, sides, columns),
         out_shape=jax.ShapeDtypeStruct(out_shape, jnp.bfloat16),
@@ -417,6 +417,7 @@
     cross_bottom = lax.ppermute(cross_first, "ha", down)
     inner, cross = tie((inner, cross))
     last = lax.ppermute(inner, "ta", cross_pairs)
+    top, bottom, visitors = tie((top, bottom, visitors))
     core_top, core_bottom = [lax.ppermute(value, "ta", core_pairs) for value in inner_rows(top, bottom)]
 
     early_third = (core, core_top, core_bottom)
@@ -427,14 +428,17 @@
     early_home = near_attention(True, ha_size, keyvals, top, bottom, early_third, [], [queries], 1)
     cross_top, cross_bottom, _ = tie((cross_top, cross_bottom, early_home[1]))
     late_third = (cross, cross_top, cross_bottom)
-    late = near_attention(False, ha_size, keyvals, top, bottom, late_third, visitors, [queries], LATE_COST)
+    late = near_attention(False, ha_size, keyvals, top, bottom, late_third, visitors, [], 1)
     late_parts = [lax.ppermute(result, "wa", back) for result, (_, back) in zip(late, ways)]
-    last, _ = tie((last, late[0]))
-    *cross_rows, inner_first, inner_last = by_rows(cross, last)
-    cross_rows, early_parts, _ = tie((cross_rows, early_parts, late[0]))
-    corner = [lax.ppermute(value, "ta", core_pairs) for value in (*cross_rows, inner_first, inner_last)]
-    buffers = (core, cross, last, *corner)
-    own = far_attention(ta_size, far_frames, queries, buffers, (*early_home, *late[-4:]))
+    cross_top, last, _ = tie((cross_top, last, late[0]))
+    late_third = (cross, cross_top, cross_bottom)
+    late_home = near_attention(False, ha_size, keyvals, top, bottom, late_third, [], [queries], LATE_COST)
+    inner_corner = [lax.ppermute(value, "ta", core_pairs) for value in widened_rows(last)]
+    sent, early_parts, _ = tie((cross, early_parts, late_home[1]))
+    cross_rows = by_rows(sent)
+    corner = [lax.ppermute(value, "ta", core_pairs) for value in cross_rows]
+    buffers = (core, cross, last, *corner, *inner_corner)
+    own = far_attention(ta_size, far_frames, queries, buffers, (*early_home, *late_home))
     out = finish(wa_size, own, early_parts, None, FINISH_COST)
     out = finish(wa_size, own, late_parts, out, 1)
     return out.reshape(shape)

time: 76.1 us -> 70.3 us (0.924)
  waiting for transfers between devices: 33.4 us -> 24.4 us
  Pallas kernels: 21.3 us -> 23 us
  starting transfers between devices: 19.3 us -> 20.7 us
    ppermute x1, waiting for transfers between devices: 7.38 us -> 0.01 us  [per_device(): last = lax.ppermute(inner, 'ta', cross_pairs)]
    pallas_call x3 -> x4, Pallas kernels: 11.8 us -> 15.1 us  [near_attention(): pl.pallas_call(functools.partial(near_kernel, len(visitors), len(queries)...]
    ppermute x6 -> x4, waiting for transfers between devices: 4.93 us -> 2.15 us  [per_device(): lax.ppermute(value, 'ta', core_pairs)]
    ppermute x0 -> x2, waiting for transfers between devices: none -> 2.14 us  [per_device(): corner = [lax.ppermute(value, 'ta', core_pairs) for value in cross_rows]]
    ppermute x1, waiting for transfers between devices: 2.04 us -> 0.18 us  [per_device(): bottom = lax.ppermute(first_rows, 'ha', down)]
    pallas_call x2, Pallas kernels: 3.56 us -> 1.94 us  [finish(): pl.pallas_call(functools.partial(kernel, sides, columns), out_shape=jax.S...]
    ppermute x1, starting transfers between devices: 0.41 us -> 1.53 us  [per_device(): last = lax.ppermute(inner, 'ta', cross_pairs)]
    ppermute x1, waiting for transfers between devices: 1.95 us -> 2.82 us  [per_device(): cross_bottom = lax.ppermute(cross_first, 'ha', down)]
  transfers between devices with their start and end apart: 16 -> 16, of which waited for: 10 -> 7; matrix products, arithmetic and copies ran while one was open for 0% -> 0% of each run, Pallas kernels for 25% -> 31%
where the time goes in v11:
time: 70.3 us; the launch traced here: 70.1 us
  waiting for transfers between devices  24.4 us (35%)
  Pallas kernels  23 us (33%)
  starting transfers between devices  20.7 us (29%)
  local copies, waits for them, and re-layouts  1.61 us (2%)
    ppermute x1, waiting for transfers between devices, per_device(): cross = lax.ppermute(outer, 'ta', cross_pairs)  17.1 us
    pallas_call x4, Pallas kernels, near_attention(): pl.pallas_call(functools.partial(near_kernel, len(visitors), len(queries)...  15.1 us
    pallas_call x1, Pallas kernels, far_attention(): pl.pallas_call(functools.partial(far_kernel, members), out_shape=[jax.Sha...  5.02 us
    ppermute x1, starting transfers between devices, per_device(): top = lax.ppermute(last_rows, 'ha', up)  3.53 us
    ppermute x1, starting transfers between devices, per_device(): cross_top = lax.ppermute(cross_last, 'ha', up)  3.52 us
    ppermute x2, starting transfers between devices, per_device(): lax.ppermute(result, 'wa', back)  3.17 us
    ppermute x1, waiting for transfers between devices, per_device(): cross_bottom = lax.ppermute(cross_first, 'ha', down)  2.82 us
    ppermute x1, starting transfers between devices, per_device(): cross = lax.ppermute(outer, 'ta', cross_pairs)  2.67 us
  transfers between devices with their start and end apart: 16, of which 7 were waited for; matrix products, arithmetic and copies ran while one was open for 0% of the time, Pallas kernels for 31%

profile of v11, /device:TPU:0, one launch (start us, length us, event | category | flops | bytes accessed | tf_op | source)
XLA Modules:
  0.0 70.1 jit_solution(7266615769658493145)
XLA Ops:
  0.5 1.6 %copy-done = bf16[2,2,16,8,2048]{4,3,2,1,0:T(8,128)(2,1)S(1)} copy-done((bf16[2,2,16,8,2048]{4,3,2,1,0:T(8,128)(2,1)S(1)}, bf16[2,2,16,8,2048]{4,3,2,1,0:T(8,128)(2,1)}, u32[]{:S(2)}) %copy-start) | copy-done | bytes 2097176
  2.4 2.7 %collective-permute-start.1 = (bf16[2,128,2048]{2,1,0:T(8,128)(2,1)S(1)}, bf16[2,128,2048]{2,1,0:T(8,128)(2,1)S(1)}, u32[]{:S(2)}, u32[]{:S(2)}) collective-permute-start(bf16[2,128,2048]{2,1,0:T(8,128)(2,1)S(1)} %get-tuple-element.44), channel_id=1, source_target_pairs={{0,24},{8,16},{16,8},{24,0},{1,25},{9,17},{17,9},{25,1},{2,26},{10... | collective-permute-start | bytes 3145736 | tf_op jit(solution)/shard_map/ppermute | solution.py:410
  5.1 3.5 %collective-permute-start.4 = (bf16[2,2,64,2048]{3,2,1,0:T(8,128)(2,1)S(1)}, bf16[2,2,64,2048]{3,2,1,0:T(8,128)(2,1)S(1)}, u32[]{:S(2)}, u32[]{:S(2)}) collective-permute-start(bf16[2,2,64,2048]{3,2,1,0:T(8,128)(2,1)S(1)} %get-tuple-element.48), channel_id=1, source_target_pairs={{0,2},{2,4},{4,6},{1,3},{3,5},{5,7},{8,10},{10,12},{12,14},{9,11},... | collective-permute-start | bytes 3145736 | tf_op jit(solution)/shard_map/ppermute | solution.py:411
  8.6 1.3 %collective-permute-start.5 = (bf16[2,2,64,2048]{3,2,1,0:T(8,128)(2,1)S(1)}, bf16[2,2,64,2048]{3,2,1,0:T(8,128)(2,1)S(1)}, u32[]{:S(2)}, u32[]{:S(2)}) collective-permute-start(bf16[2,2,64,2048]{3,2,1,0:T(8,128)(2,1)S(1)} %get-tuple-element.49), channel_id=1, source_target_pairs={{2,0},{4,2},{6,4},{3,1},{5,3},{7,5},{10,8},{12,10},{14,12},{11,9},... | collective-permute-start | bytes 3145736 | tf_op jit(solution)/shard_map/ppermute | solution.py:412
  9.9 1.6 %collective-permute-start.6 = (bf16[2,128,2048]{2,1,0:T(8,128)(2,1)S(1)}, bf16[2,128,2048]{2,1,0:T(8,128)(2,1)S(1)}, u32[]{:S(2)}, u32[]{:S(2)}) collective-permute-start(bf16[2,128,2048]{2,1,0:T(8,128)(2,1)S(1)} %bitcast.9), channel_id=1, source_target_pairs={{0,1},{1,0},{2,3},{3,2},{4,5},{5,4},{6,7},{7,6},{8,9},{9,8},{10,11... | collective-permute-start | bytes 3145736 | tf_op jit(solution)/shard_map/ppermute | solution.py:414
  11.5 17.1 %collective-permute-done.1.frame_ref.refs_0_ = bf16[2,128,2048]{2,1,0:T(8,128)(2,1)S(1)} collective-permute-done((bf16[2,128,2048]{2,1,0:T(8,128)(2,1)S(1)}, bf16[2,128,2048]{2,1,0:T(8,128)(2,1)S(1)}, u32[]{:S(2)}, u32[]{:S(2)}) %collective-permute-start.1) | collective-permute-done | bytes 1048608 | tf_op jit(solution)/shard_map/ppermute | solution.py:410
  28.6 1.5 %collective-permute-start.9 = (bf16[2,128,2048]{2,1,0:T(8,128)(2,1)S(1)}, bf16[2,128,2048]{2,1,0:T(8,128)(2,1)S(1)}, u32[]{:S(2)}, u32[]{:S(2)}) collective-permute-start(bf16[2,128,2048]{2,1,0:T(8,128)(2,1)S(1)} %get-tuple-element.59), channel_id=1, source_target_pairs={{0,24},{8,16},{16,8},{24,0},{1,25},{9,17},{17,9},{25,1},{2,26},{10... | collective-permute-start | bytes 3145736 | tf_op jit(solution)/shard_map/ppermute | solution.py:419
  30.3 3.5 %collective-permute-start.2 = (bf16[2,64,2176]{2,1,0:T(8,128)(2,1)S(1)}, bf16[2,64,2176]{2,1,0:T(8,128)(2,1)S(1)}, u32[]{:S(2)}, u32[]{:S(2)}) collective-permute-start(bf16[2,64,2176]{2,1,0:T(8,128)(2,1)S(1)} %get-tuple-element.46), channel_id=1, source_target_pairs={{0,2},{2,4},{4,6},{1,3},{3,5},{5,7},{8,10},{10,12},{12,14},{9,11},... | collective-permute-start | bytes 1671176 | tf_op jit(solution)/shard_map/ppermute | solution.py:416
  33.8 1.3 %collective-permute-start.3 = (bf16[2,64,2176]{2,1,0:T(8,128)(2,1)S(1)}, bf16[2,64,2176]{2,1,0:T(8,128)(2,1)S(1)}, u32[]{:S(2)}, u32[]{:S(2)}) collective-permute-start(bf16[2,64,2176]{2,1,0:T(8,128)(2,1)S(1)} %get-tuple-element.47), channel_id=1, source_target_pairs={{2,0},{4,2},{6,4},{3,1},{5,3},{7,5},{10,8},{12,10},{14,12},{11,9},... | collective-permute-start | bytes 1671176 | tf_op jit(solution)/shard_map/ppermute | solution.py:417
  35.5 0.5 collective-permute-start.8
  36.0 1.4 %collective-permute-done.7.refs_1_ = bf16[2,64,2048]{2,1,0:T(8,128)(2,1)S(1)} collective-permute-done((bf16[2,64,2048]{2,1,0:T(8,128)(2,1)S(1)}, bf16[2,64,2048]{2,1,0:T(8,128)(2,1)S(1)}, u32[]{:S(2)}, u32[]{:S(2)}) %collective-permute-start.7) | collective-permute-done | bytes 524320 | tf_op jit(solution)/shard_map/ppermute | solution.py:421
  37.4 0.7 %collective-permute-done.8.refs_2_ = bf16[2,64,2048]{2,1,0:T(8,128)(2,1)S(1)} collective-permute-done((bf16[2,64,2048]{2,1,0:T(8,128)(2,1)S(1)}, bf16[2,64,2048]{2,1,0:T(8,128)(2,1)S(1)}, u32[]{:S(2)}, u32[]{:S(2)}) %collective-permute-start.8) | collective-permute-done | bytes 524320 | tf_op jit(solution)/shard_map/ppermute | solution.py:421
  38.1 3.6 %shard_map.40 = bf16[128,2176]{1,0:T(8,128)(2,1)S(1)} custom-call(bf16[2,2,128,2048]{3,2,1,0:T(8,128)(2,1)S(1)} %bitcast.5, bf16[2,2,64,2048]{3,2,1,0:T(8,128)(2,1)S(1)} %collective-permute-done.4.top_ref, bf16[2,2,64,2048]{3,2,1,0:T(8,128)(2,1)S(1)} %collective-permute-done.5.bottom_ref, ...), custom_call_target="tpu_custom_call" | custom-call | flops 1 | bytes 1 | tf_op jit(solution)/shard_map/pallas_call | solution.py:213
  41.7 1.6 %collective-permute-start.10 = (bf16[128,2176]{1,0:T(8,128)(2,1)S(1)}, bf16[128,2176]{1,0:T(8,128)(2,1)S(1)}, u32[]{:S(2)}, u32[]{:S(2)}) collective-permute-start(bf16[128,2176]{1,0:T(8,128)(2,1)S(1)} %shard_map.40), channel_id=1, source_target_pairs={{0,1},{1,0},{2,3},{3,2},{4,5},{5,4},{6,7},{7,6},{8,9},{9,8},{10,11... | collective-permute-start | bytes 1671176 | tf_op jit(solution)/shard_map/ppermute | solution.py:425
  43.3 3.6 %shard_map.41 = (f32[128,2048]{1,0:T(8,128)S(1)}, f32[128,128]{1,0:T(8,128)S(1)}, f32[128,128]{1,0:T(8,128)S(1)}, f32[128,2048]{1,0:T(8,128)S(1)}) custom-call(bf16[2,2,128,2048]{3,2,1,0:T(8,128)(2,1)S(1)} %bitcast.6, bf16[2,2,64,2048]{3,2,1,0:T(8,128)(2,1)S(1)} %collective-permute-done.4.top_ref, ...), custom_call_target="tpu_custom_call" | custom-call | flops 1 | bytes 1 | tf_op jit(solution)/shard_map/pallas_call | solution.py:213
  46.9 2.8 %collective-permute-done.3.refs_2_ = bf16[2,64,2176]{2,1,0:T(8,128)(2,1)S(1)} collective-permute-done((bf16[2,64,2176]{2,1,0:T(8,128)(2,1)S(1)}, bf16[2,64,2176]{2,1,0:T(8,128)(2,1)S(1)}, u32[]{:S(2)}, u32[]{:S(2)}) %collective-permute-start.3) | collective-permute-done | bytes 557088 | tf_op jit(solution)/shard_map/ppermute | solution.py:417
  49.7 4.0 %shard_map.42 = bf16[128,2176]{1,0:T(8,128)(2,1)S(1)} custom-call(bf16[2,2,128,2048]{3,2,1,0:T(8,128)(2,1)S(1)} %bitcast.7, bf16[2,2,64,2048]{3,2,1,0:T(8,128)(2,1)S(1)} %collective-permute-done.4.top_ref, bf16[2,2,64,2048]{3,2,1,0:T(8,128)(2,1)S(1)} %collective-permute-done.5.bottom_ref, bf16[2,128,2048]{2,1,0:T(8,128)(2,1)S(1)} %collective-permute-done.1.frame_ref.refs_0_, ...), custom_call_target="tpu_custom_call" | custom-call | flops 1 | bytes 1 | tf_op jit(solution)/shard_map/pallas_call | solution.py:213
  53.7 1.6 %collective-permute-start.15 = (bf16[128,2176]{1,0:T(8,128)(2,1)S(1)}, bf16[128,2176]{1,0:T(8,128)(2,1)S(1)}, u32[]{:S(2)}, u32[]{:S(2)}) collective-permute-start(bf16[128,2176]{1,0:T(8,128)(2,1)S(1)} %shard_map.42), channel_id=1, source_target_pairs={{0,1},{1,0},{2,3},{3,2},{4,5},{5,4},{6,7},{7,6},{8,9},{9,8},{10,11... | collective-permute-start | bytes 1671176 | tf_op jit(solution)/shard_map/ppermute | solution.py:432
  56.2 3.9 %shard_map.43 = (f32[128,2048]{1,0:T(8,128)S(1)}, f32[128,128]{1,0:T(8,128)S(1)}, f32[128,128]{1,0:T(8,128)S(1)}, f32[128,2048]{1,0:T(8,128)S(1)}) custom-call(bf16[2,2,128,2048]{3,2,1,0:T(8,128)(2,1)S(1)} %bitcast.8, bf16[2,2,64,2048]{3,2,1,0:T(8,128)(2,1)S(1)} %collective-permute-done.4.top_ref, ...), custom_call_target="tpu_custom_call" | custom-call | flops 30064771072 | bytes 1 | tf_op jit(solution)/shard_map/pallas_call | solution.py:213
  60.8 1.4 %collective-permute-done.11.refs_2_ = bf16[2,64,2048]{2,1,0:T(8,128)(2,1)S(1)} collective-permute-done((bf16[2,64,2048]{2,1,0:T(8,128)(2,1)S(1)}, bf16[2,64,2048]{2,1,0:T(8,128)(2,1)S(1)}, u32[]{:S(2)}, u32[]{:S(2)}) %collective-permute-start.11) | collective-permute-done | bytes 524320 | tf_op jit(solution)/shard_map/ppermute | solution.py:439
  62.2 0.7 %collective-permute-done.12.refs_3_ = bf16[2,64,2048]{2,1,0:T(8,128)(2,1)S(1)} collective-permute-done((bf16[2,64,2048]{2,1,0:T(8,128)(2,1)S(1)}, bf16[2,64,2048]{2,1,0:T(8,128)(2,1)S(1)}, u32[]{:S(2)}, u32[]{:S(2)}) %collective-permute-start.12) | collective-permute-done | bytes 524320 | tf_op jit(solution)/shard_map/ppermute | solution.py:439
  63.0 5.0 %shard_map.46 = (f32[2,128,2048]{2,1,0:T(8,128)S(1)}, f32[2,128,128]{2,1,0:T(8,128)S(1)}, f32[2,128,128]{2,1,0:T(8,128)S(1)}) custom-call(s32[2,2,1,2]{3,2,1,0:T(1,128)S(1)} %copy-done.3, bf16[2,128,2048]{2,1,0:T(8,128)(2,1)S(1)} %bitcast.12, bf16[2,2,128,2048]{3,2,1,0:T(8,128)(2,1)S(1)} %collective-permute-done.refs_0_.core_ref, ...), custom_call_target="tpu_custom_call" | custom-call | flops 1 | bytes 1 | tf_op jit(solution)/shard_map/pallas_call | solution.py:300
  68.0 0.6 shard_map.47.refs_4_
  68.6 1.3 %shard_map.48 = bf16[2,128,2048]{2,1,0:T(8,128)(2,1)} custom-call(f32[2,128,2048]{2,1,0:T(8,128)S(1)} %get-tuple-element.75.refs_0_, f32[2,128,128]{2,1,0:T(8,128)S(1)} %get-tuple-element.76.refs_1_, f32[2,128,128]{2,1,0:T(8,128)S(1)} %get-tuple-element.77.refs_2_, bf16[128,2176]{1,0:T(8,128)(2,1)S(1)} %collective-permute-done.15.refs_3_, ...), custom_call_target="tpu_custom_call" | custom-call | flops 1 | bytes 1 | tf_op jit(solution)/shard_map/pallas_call | solution.py:377
  (28 shorter events, 2.8 us)
Async XLA Ops:
  0.0 9.9 %collective-permute-start = (bf16[2,2,128,2048]{3,2,1,0:T(8,128)(2,1)}, bf16[2,2,128,2048]{3,2,1,0:T(8,128)(2,1)S(1)}, u32[]{:S(2)}, u32[]{:S(2)}) collective-permute-start(bf16[2,2,128,2048]{3,2,1,0:T(8,128)(2,1)} %bitcast.3), channel_id=1, source_target_pairs={{0,8},{8,0},{16,24},{24,16},{1,9},{9,1},{17,25},{25,17},{2,10},{10... | collective-permute-start | bytes 6291464 | tf_op jit(solution)/shard_map/ppermute | solution.py:408
  0.5 1.6 %copy-start = (bf16[2,2,16,8,2048]{4,3,2,1,0:T(8,128)(2,1)S(1)}, bf16[2,2,16,8,2048]{4,3,2,1,0:T(8,128)(2,1)}, u32[]{:S(2)}) copy-start(bf16[2,2,16,8,2048]{4,3,2,1,0:T(8,128)(2,1)} %param.4) | copy-start | bytes 6291460
  2.0 7.9 %copy-start.2 = (bf16[2,16,8,2048]{3,2,1,0:T(8,128)(2,1)S(1)}, bf16[2,16,8,2048]{3,2,1,0:T(8,128)(2,1)}, u32[]{:S(2)}) copy-start(bf16[2,16,8,2048]{3,2,1,0:T(8,128)(2,1)} %param.3) | copy-start | bytes 3145732
  2.4 35.7 %copy-start.1 = (bf16[2,2,16,8,2048]{4,3,2,1,0:T(8,128)(2,1)S(1)}, bf16[2,2,16,8,2048]{4,3,2,1,0:T(8,128)(2,1)}, u32[]{:S(2)}) copy-start(bf16[2,2,16,8,2048]{4,3,2,1,0:T(8,128)(2,1)} %param.4) | copy-start | bytes 6291460
  2.4 26.2 %collective-permute-start.1 = (bf16[2,128,2048]{2,1,0:T(8,128)(2,1)S(1)}, bf16[2,128,2048]{2,1,0:T(8,128)(2,1)S(1)}, u32[]{:S(2)}, u32[]{:S(2)}) collective-permute-start(bf16[2,128,2048]{2,1,0:T(8,128)(2,1)S(1)} %get-tuple-element.44), channel_id=1, source_target_pairs={{0,24},{8,16},{16,8},{24,0},{1,25},{9,17},{17,9},{25,1},{2,26},{10... | collective-permute-start | bytes 3145736 | tf_op jit(solution)/shard_map/ppermute | solution.py:410
  5.1 28.7 %collective-permute-start.4 = (bf16[2,2,64,2048]{3,2,1,0:T(8,128)(2,1)S(1)}, bf16[2,2,64,2048]{3,2,1,0:T(8,128)(2,1)S(1)}, u32[]{:S(2)}, u32[]{:S(2)}) collective-permute-start(bf16[2,2,64,2048]{3,2,1,0:T(8,128)(2,1)S(1)} %get-tuple-element.48), channel_id=1, source_target_pairs={{0,2},{2,4},{4,6},{1,3},{3,5},{5,7},{8,10},{10,12},{12,14},{9,11},... | collective-permute-start | bytes 3145736 | tf_op jit(solution)/shard_map/ppermute | solution.py:411
  8.6 26.7 %collective-permute-start.5 = (bf16[2,2,64,2048]{3,2,1,0:T(8,128)(2,1)S(1)}, bf16[2,2,64,2048]{3,2,1,0:T(8,128)(2,1)S(1)}, u32[]{:S(2)}, u32[]{:S(2)}) collective-permute-start(bf16[2,2,64,2048]{3,2,1,0:T(8,128)(2,1)S(1)} %get-tuple-element.49), channel_id=1, source_target_pairs={{2,0},{4,2},{6,4},{3,1},{5,3},{7,5},{10,8},{12,10},{14,12},{11,9},... | collective-permute-start | bytes 3145736 | tf_op jit(solution)/shard_map/ppermute | solution.py:412
  9.9 25.4 %collective-permute-start.6 = (bf16[2,128,2048]{2,1,0:T(8,128)(2,1)S(1)}, bf16[2,128,2048]{2,1,0:T(8,128)(2,1)S(1)}, u32[]{:S(2)}, u32[]{:S(2)}) collective-permute-start(bf16[2,128,2048]{2,1,0:T(8,128)(2,1)S(1)} %bitcast.9), channel_id=1, source_target_pairs={{0,1},{1,0},{2,3},{3,2},{4,5},{5,4},{6,7},{7,6},{8,9},{9,8},{10,11... | collective-permute-start | bytes 3145736 | tf_op jit(solution)/shard_map/ppermute | solution.py:414
  28.6 26.7 %collective-permute-start.9 = (bf16[2,128,2048]{2,1,0:T(8,128)(2,1)S(1)}, bf16[2,128,2048]{2,1,0:T(8,128)(2,1)S(1)}, u32[]{:S(2)}, u32[]{:S(2)}) collective-permute-start(bf16[2,128,2048]{2,1,0:T(8,128)(2,1)S(1)} %get-tuple-element.59), channel_id=1, source_target_pairs={{0,24},{8,16},{16,8},{24,0},{1,25},{9,17},{17,9},{25,1},{2,26},{10... | collective-permute-start | bytes 3145736 | tf_op jit(solution)/shard_map/ppermute | solution.py:419
  30.3 16.6 %collective-permute-start.2 = (bf16[2,64,2176]{2,1,0:T(8,128)(2,1)S(1)}, bf16[2,64,2176]{2,1,0:T(8,128)(2,1)S(1)}, u32[]{:S(2)}, u32[]{:S(2)}) collective-permute-start(bf16[2,64,2176]{2,1,0:T(8,128)(2,1)S(1)} %get-tuple-element.46), channel_id=1, source_target_pairs={{0,2},{2,4},{4,6},{1,3},{3,5},{5,7},{8,10},{10,12},{12,14},{9,11},... | collective-permute-start | bytes 1671176 | tf_op jit(solution)/shard_map/ppermute | solution.py:416
  33.8 15.9 %collective-permute-start.3 = (bf16[2,64,2176]{2,1,0:T(8,128)(2,1)S(1)}, bf16[2,64,2176]{2,1,0:T(8,128)(2,1)S(1)}, u32[]{:S(2)}, u32[]{:S(2)}) collective-permute-start(bf16[2,64,2176]{2,1,0:T(8,128)(2,1)S(1)} %get-tuple-element.47), channel_id=1, source_target_pairs={{2,0},{4,2},{6,4},{3,1},{5,3},{7,5},{10,8},{12,10},{14,12},{11,9},... | collective-permute-start | bytes 1671176 | tf_op jit(solution)/shard_map/ppermute | solution.py:417
  35.4 2.0 %collective-permute-start.7 = (bf16[2,64,2048]{2,1,0:T(8,128)(2,1)S(1)}, bf16[2,64,2048]{2,1,0:T(8,128)(2,1)S(1)}, u32[]{:S(2)}, u32[]{:S(2)}) collective-permute-start(bf16[2,64,2048]{2,1,0:T(8,128)(2,1)S(1)} %get-tuple-element.53), channel_id=1, source_target_pairs={{0,8},{8,0},{16,24},{24,16},{1,9},{9,1},{17,25},{25,17},{2,10},{10... | collective-permute-start | bytes 1572872 | tf_op jit(solution)/shard_map/ppermute | solution.py:421
  35.5 2.6 %collective-permute-start.8 = (bf16[2,64,2048]{2,1,0:T(8,128)(2,1)S(1)}, bf16[2,64,2048]{2,1,0:T(8,128)(2,1)S(1)}, u32[]{:S(2)}, u32[]{:S(2)}) collective-permute-start(bf16[2,64,2048]{2,1,0:T(8,128)(2,1)S(1)} %get-tuple-element.54), channel_id=1, source_target_pairs={{0,8},{8,0},{16,24},{24,16},{1,9},{9,1},{17,25},{25,17},{2,10},{10... | collective-permute-start | bytes 1572872 | tf_op jit(solution)/shard_map/ppermute | solution.py:421
  41.7 18.4 %collective-permute-start.10 = (bf16[128,2176]{1,0:T(8,128)(2,1)S(1)}, bf16[128,2176]{1,0:T(8,128)(2,1)S(1)}, u32[]{:S(2)}, u32[]{:S(2)}) collective-permute-start(bf16[128,2176]{1,0:T(8,128)(2,1)S(1)} %shard_map.40), channel_id=1, source_target_pairs={{0,1},{1,0},{2,3},{3,2},{4,5},{5,4},{6,7},{7,6},{8,9},{9,8},{10,11... | collective-permute-start | bytes 1671176 | tf_op jit(solution)/shard_map/ppermute | solution.py:425
  53.7 14.9 %collective-permute-start.15 = (bf16[128,2176]{1,0:T(8,128)(2,1)S(1)}, bf16[128,2176]{1,0:T(8,128)(2,1)S(1)}, u32[]{:S(2)}, u32[]{:S(2)}) collective-permute-start(bf16[128,2176]{1,0:T(8,128)(2,1)S(1)} %shard_map.42), channel_id=1, source_target_pairs={{0,1},{1,0},{2,3},{3,2},{4,5},{5,4},{6,7},{7,6},{8,9},{9,8},{10,11... | collective-permute-start | bytes 1671176 | tf_op jit(solution)/shard_map/ppermute | solution.py:432
  55.6 5.2 %collective-permute-start.13 = (bf16[2,64,2176]{2,1,0:T(8,128)(2,1)S(1)}, bf16[2,64,2176]{2,1,0:T(8,128)(2,1)S(1)}, u32[]{:S(2)}, u32[]{:S(2)}) collective-permute-start(bf16[2,64,2176]{2,1,0:T(8,128)(2,1)S(1)} %get-tuple-element.67), channel_id=1, source_target_pairs={{0,8},{8,0},{16,24},{24,16},{1,9},{9,1},{17,25},{25,17},{2,10},{10... | collective-permute-start | bytes 1671176 | tf_op jit(solution)/shard_map/ppermute | solution.py:436
  55.7 7.3 %copy-start.3 = (s32[2,2,1,2]{3,2,1,0:T(1,128)S(1)}, s32[2,2,1,2]{3,2,1,0:T(1,128)}, u32[]{:S(2)}) copy-start(s32[2,2,1,2]{3,2,1,0:T(1,128)} %far_ref.1) | copy-start | bytes 100
  55.7 5.1 %collective-permute-start.14 = (bf16[2,64,2176]{2,1,0:T(8,128)(2,1)S(1)}, bf16[2,64,2176]{2,1,0:T(8,128)(2,1)S(1)}, u32[]{:S(2)}, u32[]{:S(2)}) collective-permute-start(bf16[2,64,2176]{2,1,0:T(8,128)(2,1)S(1)} %get-tuple-element.68), channel_id=1, source_target_pairs={{0,8},{8,0},{16,24},{24,16},{1,9},{9,1},{17,25},{25,17},{2,10},{10... | collective-permute-start | bytes 1671176 | tf_op jit(solution)/shard_map/ppermute | solution.py:436
  60.3 2.0 %collective-permute-start.11 = (bf16[2,64,2048]{2,1,0:T(8,128)(2,1)S(1)}, bf16[2,64,2048]{2,1,0:T(8,128)(2,1)S(1)}, u32[]{:S(2)}, u32[]{:S(2)}) collective-permute-start(bf16[2,64,2048]{2,1,0:T(8,128)(2,1)S(1)} %get-tuple-element.65), channel_id=1, source_target_pairs={{0,8},{8,0},{16,24},{24,16},{1,9},{9,1},{17,25},{25,17},{2,10},{10... | collective-permute-start | bytes 1572872 | tf_op jit(solution)/shard_map/ppermute | solution.py:439
  60.4 2.6 %collective-permute-start.12 = (bf16[2,64,2048]{2,1,0:T(8,128)(2,1)S(1)}, bf16[2,64,2048]{2,1,0:T(8,128)(2,1)S(1)}, u32[]{:S(2)}, u32[]{:S(2)}) collective-permute-start(bf16[2,64,2048]{2,1,0:T(8,128)(2,1)S(1)} %get-tuple-element.66), channel_id=1, source_target_pairs={{0,8},{8,0},{16,24},{24,16},{1,9},{9,1},{17,25},{25,17},{2,10},{10... | collective-permute-start | bytes 1572872 | tf_op jit(solution)/shard_map/ppermute | solution.py:439

commit v12 on v11

--- a/solution.py
+++ b/solution.py
@@ -174,11 +174,12 @@
                 weights.append((peak, near, edge))
         for i, lanes in enumerate(members):
             mask = lane_index(half) == first + i
-            middle_values = with_ones(middle(1, lanes))
-            for a in range(2):
-                peak, near, edge = weights[2 * i + a]
-                summed = jnp.dot(near, middle_values, preferred_element_type=jnp.float32)
-                summed = summed + jnp.dot(edge, with_ones(halo(a, 1, lanes)), preferred_element_type=jnp.float32)
+            pair = weights[2 * i : 2 * i + 2]
+            middle_weights = jnp.concatenate([near for _, near, _ in pair], axis=0)
+            middle_sums = jnp.dot(middle_weights, with_ones(middle(1, lanes)), preferred_element_type=jnp.float32)
+            for a, (peak, _, edge) in enumerate(pair):
+                summed = jnp.dot(edge, with_ones(halo(a, 1, lanes)), preferred_element_type=jnp.float32)
+                summed = summed + middle_sums[a * half : (a + 1) * half]
                 total = summed[:, HD:]
                 peaks[a] = jnp.where(mask, peak, peaks[a])
                 totals[a] = jnp.where(mask, total, totals[a])

time: 70.3 us -> 70.4 us (level)
  transfers between devices with their start and end apart: 16 -> 16, of which waited for: 7 -> 8; matrix products, arithmetic and copies ran while one was open for 0% -> 0% of each run, Pallas kernels for 31% -> 31%
where the time goes in v12:
time: 70.4 us; the launch traced here: 70.2 us
  waiting for transfers between devices  24.2 us (34%)
  Pallas kernels  23.3 us (33%)
  starting transfers between devices  20.7 us (29%)
  local copies, waits for them, and re-layouts  1.61 us (2%)
    ppermute x1, waiting for transfers between devices, per_device(): cross = lax.ppermute(outer, 'ta', cross_pairs)  17.1 us
    pallas_call x4, Pallas kernels, near_attention(): pl.pallas_call(functools.partial(near_kernel, len(visitors), len(queries)...  15.4 us
    pallas_call x1, Pallas kernels, far_attention(): pl.pallas_call(functools.partial(far_kernel, members), out_shape=[jax.Sha...  5.03 us
    ppermute x1, starting transfers between devices, per_device(): top = lax.ppermute(last_rows, 'ha', up)  3.53 us
    ppermute x1, starting transfers between devices, per_device(): cross_top = lax.ppermute(cross_last, 'ha', up)  3.52 us
    ppermute x2, starting transfers between devices, per_device(): lax.ppermute(result, 'wa', back)  3.17 us
    ppermute x1, starting transfers between devices, per_device(): cross = lax.ppermute(outer, 'ta', cross_pairs)  2.67 us
    ppermute x1, waiting for transfers between devices, per_device(): cross_bottom = lax.ppermute(cross_first, 'ha', down)  2.24 us
  transfers between devices with their start and end apart: 16, of which 8 were waited for; matrix products, arithmetic and copies ran while one was open for 0% of the time, Pallas kernels for 31%

profile of v12, /device:TPU:0, one launch (start us, length us, event | category | flops | bytes accessed | tf_op | source)
XLA Modules:
  0.0 70.2 jit_solution(2095207815630681148)
XLA Ops:
  0.5 1.6 %copy-done = bf16[2,2,16,8,2048]{4,3,2,1,0:T(8,128)(2,1)S(1)} copy-done((bf16[2,2,16,8,2048]{4,3,2,1,0:T(8,128)(2,1)S(1)}, bf16[2,2,16,8,2048]{4,3,2,1,0:T(8,128)(2,1)}, u32[]{:S(2)}) %copy-start) | copy-done | bytes 2097176
  2.4 2.7 %collective-permute-start.1 = (bf16[2,128,2048]{2,1,0:T(8,128)(2,1)S(1)}, bf16[2,128,2048]{2,1,0:T(8,128)(2,1)S(1)}, u32[]{:S(2)}, u32[]{:S(2)}) collective-permute-start(bf16[2,128,2048]{2,1,0:T(8,128)(2,1)S(1)} %get-tuple-element.44), channel_id=1, source_target_pairs={{0,24},{8,16},{16,8},{24,0},{1,25},{9,17},{17,9},{25,1},{2,26},{10... | collective-permute-start | bytes 3145736 | tf_op jit(solution)/shard_map/ppermute | solution.py:411
  5.1 3.5 %collective-permute-start.4 = (bf16[2,2,64,2048]{3,2,1,0:T(8,128)(2,1)S(1)}, bf16[2,2,64,2048]{3,2,1,0:T(8,128)(2,1)S(1)}, u32[]{:S(2)}, u32[]{:S(2)}) collective-permute-start(bf16[2,2,64,2048]{3,2,1,0:T(8,128)(2,1)S(1)} %get-tuple-element.48), channel_id=1, source_target_pairs={{0,2},{2,4},{4,6},{1,3},{3,5},{5,7},{8,10},{10,12},{12,14},{9,11},... | collective-permute-start | bytes 3145736 | tf_op jit(solution)/shard_map/ppermute | solution.py:412
  8.6 1.3 %collective-permute-start.5 = (bf16[2,2,64,2048]{3,2,1,0:T(8,128)(2,1)S(1)}, bf16[2,2,64,2048]{3,2,1,0:T(8,128)(2,1)S(1)}, u32[]{:S(2)}, u32[]{:S(2)}) collective-permute-start(bf16[2,2,64,2048]{3,2,1,0:T(8,128)(2,1)S(1)} %get-tuple-element.49), channel_id=1, source_target_pairs={{2,0},{4,2},{6,4},{3,1},{5,3},{7,5},{10,8},{12,10},{14,12},{11,9},... | collective-permute-start | bytes 3145736 | tf_op jit(solution)/shard_map/ppermute | solution.py:413
  9.9 1.6 %collective-permute-start.6 = (bf16[2,128,2048]{2,1,0:T(8,128)(2,1)S(1)}, bf16[2,128,2048]{2,1,0:T(8,128)(2,1)S(1)}, u32[]{:S(2)}, u32[]{:S(2)}) collective-permute-start(bf16[2,128,2048]{2,1,0:T(8,128)(2,1)S(1)} %bitcast.9), channel_id=1, source_target_pairs={{0,1},{1,0},{2,3},{3,2},{4,5},{5,4},{6,7},{7,6},{8,9},{9,8},{10,11... | collective-permute-start | bytes 3145736 | tf_op jit(solution)/shard_map/ppermute | solution.py:415
  11.5 17.1 %collective-permute-done.1.frame_ref.refs_0_ = bf16[2,128,2048]{2,1,0:T(8,128)(2,1)S(1)} collective-permute-done((bf16[2,128,2048]{2,1,0:T(8,128)(2,1)S(1)}, bf16[2,128,2048]{2,1,0:T(8,128)(2,1)S(1)}, u32[]{:S(2)}, u32[]{:S(2)}) %collective-permute-start.1) | collective-permute-done | bytes 1048608 | tf_op jit(solution)/shard_map/ppermute | solution.py:411
  28.6 1.5 %collective-permute-start.9 = (bf16[2,128,2048]{2,1,0:T(8,128)(2,1)S(1)}, bf16[2,128,2048]{2,1,0:T(8,128)(2,1)S(1)}, u32[]{:S(2)}, u32[]{:S(2)}) collective-permute-start(bf16[2,128,2048]{2,1,0:T(8,128)(2,1)S(1)} %get-tuple-element.59), channel_id=1, source_target_pairs={{0,24},{8,16},{16,8},{24,0},{1,25},{9,17},{17,9},{25,1},{2,26},{10... | collective-permute-start | bytes 3145736 | tf_op jit(solution)/shard_map/ppermute | solution.py:420
  30.3 3.5 %collective-permute-start.2 = (bf16[2,64,2176]{2,1,0:T(8,128)(2,1)S(1)}, bf16[2,64,2176]{2,1,0:T(8,128)(2,1)S(1)}, u32[]{:S(2)}, u32[]{:S(2)}) collective-permute-start(bf16[2,64,2176]{2,1,0:T(8,128)(2,1)S(1)} %get-tuple-element.46), channel_id=1, source_target_pairs={{0,2},{2,4},{4,6},{1,3},{3,5},{5,7},{8,10},{10,12},{12,14},{9,11},... | collective-permute-start | bytes 1671176 | tf_op jit(solution)/shard_map/ppermute | solution.py:417
  33.8 1.3 %collective-permute-start.3 = (bf16[2,64,2176]{2,1,0:T(8,128)(2,1)S(1)}, bf16[2,64,2176]{2,1,0:T(8,128)(2,1)S(1)}, u32[]{:S(2)}, u32[]{:S(2)}) collective-permute-start(bf16[2,64,2176]{2,1,0:T(8,128)(2,1)S(1)} %get-tuple-element.47), channel_id=1, source_target_pairs={{2,0},{4,2},{6,4},{3,1},{5,3},{7,5},{10,8},{12,10},{14,12},{11,9},... | collective-permute-start | bytes 1671176 | tf_op jit(solution)/shard_map/ppermute | solution.py:418
  35.5 0.5 collective-permute-start.8
  36.0 1.4 %collective-permute-done.7.refs_1_ = bf16[2,64,2048]{2,1,0:T(8,128)(2,1)S(1)} collective-permute-done((bf16[2,64,2048]{2,1,0:T(8,128)(2,1)S(1)}, bf16[2,64,2048]{2,1,0:T(8,128)(2,1)S(1)}, u32[]{:S(2)}, u32[]{:S(2)}) %collective-permute-start.7) | collective-permute-done | bytes 524320 | tf_op jit(solution)/shard_map/ppermute | solution.py:422
  37.4 0.7 %collective-permute-done.8.refs_2_ = bf16[2,64,2048]{2,1,0:T(8,128)(2,1)S(1)} collective-permute-done((bf16[2,64,2048]{2,1,0:T(8,128)(2,1)S(1)}, bf16[2,64,2048]{2,1,0:T(8,128)(2,1)S(1)}, u32[]{:S(2)}, u32[]{:S(2)}) %collective-permute-start.8) | collective-permute-done | bytes 524320 | tf_op jit(solution)/shard_map/ppermute | solution.py:422
  38.1 3.9 %shard_map.40 = bf16[128,2176]{1,0:T(8,128)(2,1)S(1)} custom-call(bf16[2,2,128,2048]{3,2,1,0:T(8,128)(2,1)S(1)} %bitcast.5, bf16[2,2,64,2048]{3,2,1,0:T(8,128)(2,1)S(1)} %collective-permute-done.4.top_ref, bf16[2,2,64,2048]{3,2,1,0:T(8,128)(2,1)S(1)} %collective-permute-done.5.bottom_ref, ...), custom_call_target="tpu_custom_call" | custom-call | flops 1 | bytes 1 | tf_op jit(solution)/shard_map/pallas_call | solution.py:214
  42.0 1.6 %collective-permute-start.10 = (bf16[128,2176]{1,0:T(8,128)(2,1)S(1)}, bf16[128,2176]{1,0:T(8,128)(2,1)S(1)}, u32[]{:S(2)}, u32[]{:S(2)}) collective-permute-start(bf16[128,2176]{1,0:T(8,128)(2,1)S(1)} %shard_map.40), channel_id=1, source_target_pairs={{0,1},{1,0},{2,3},{3,2},{4,5},{5,4},{6,7},{7,6},{8,9},{9,8},{10,11... | collective-permute-start | bytes 1671176 | tf_op jit(solution)/shard_map/ppermute | solution.py:426
  43.6 3.8 %shard_map.41 = (f32[128,2048]{1,0:T(8,128)S(1)}, f32[128,128]{1,0:T(8,128)S(1)}, f32[128,128]{1,0:T(8,128)S(1)}, f32[128,2048]{1,0:T(8,128)S(1)}) custom-call(bf16[2,2,128,2048]{3,2,1,0:T(8,128)(2,1)S(1)} %bitcast.6, bf16[2,2,64,2048]{3,2,1,0:T(8,128)(2,1)S(1)} %collective-permute-done.4.top_ref, ...), custom_call_target="tpu_custom_call" | custom-call | flops 1 | bytes 1 | tf_op jit(solution)/shard_map/pallas_call | solution.py:214
  47.5 2.2 %collective-permute-done.3.refs_2_ = bf16[2,64,2176]{2,1,0:T(8,128)(2,1)S(1)} collective-permute-done((bf16[2,64,2176]{2,1,0:T(8,128)(2,1)S(1)}, bf16[2,64,2176]{2,1,0:T(8,128)(2,1)S(1)}, u32[]{:S(2)}, u32[]{:S(2)}) %collective-permute-start.3) | collective-permute-done | bytes 557088 | tf_op jit(solution)/shard_map/ppermute | solution.py:418
  49.7 3.9 %shard_map.42 = bf16[128,2176]{1,0:T(8,128)(2,1)S(1)} custom-call(bf16[2,2,128,2048]{3,2,1,0:T(8,128)(2,1)S(1)} %bitcast.7, bf16[2,2,64,2048]{3,2,1,0:T(8,128)(2,1)S(1)} %collective-permute-done.4.top_ref, bf16[2,2,64,2048]{3,2,1,0:T(8,128)(2,1)S(1)} %collective-permute-done.5.bottom_ref, bf16[2,128,2048]{2,1,0:T(8,128)(2,1)S(1)} %collective-permute-done.1.frame_ref.refs_0_, ...), custom_call_target="tpu_custom_call" | custom-call | flops 1 | bytes 1 | tf_op jit(solution)/shard_map/pallas_call | solution.py:214
  53.6 1.6 %collective-permute-start.15 = (bf16[128,2176]{1,0:T(8,128)(2,1)S(1)}, bf16[128,2176]{1,0:T(8,128)(2,1)S(1)}, u32[]{:S(2)}, u32[]{:S(2)}) collective-permute-start(bf16[128,2176]{1,0:T(8,128)(2,1)S(1)} %shard_map.42), channel_id=1, source_target_pairs={{0,1},{1,0},{2,3},{3,2},{4,5},{5,4},{6,7},{7,6},{8,9},{9,8},{10,11... | collective-permute-start | bytes 1671176 | tf_op jit(solution)/shard_map/ppermute | solution.py:433
  56.1 3.8 %shard_map.43 = (f32[128,2048]{1,0:T(8,128)S(1)}, f32[128,128]{1,0:T(8,128)S(1)}, f32[128,128]{1,0:T(8,128)S(1)}, f32[128,2048]{1,0:T(8,128)S(1)}) custom-call(bf16[2,2,128,2048]{3,2,1,0:T(8,128)(2,1)S(1)} %bitcast.8, bf16[2,2,64,2048]{3,2,1,0:T(8,128)(2,1)S(1)} %collective-permute-done.4.top_ref, ...), custom_call_target="tpu_custom_call" | custom-call | flops 30064771072 | bytes 1 | tf_op jit(solution)/shard_map/pallas_call | solution.py:214
  60.6 1.4 %collective-permute-done.11.refs_2_ = bf16[2,64,2048]{2,1,0:T(8,128)(2,1)S(1)} collective-permute-done((bf16[2,64,2048]{2,1,0:T(8,128)(2,1)S(1)}, bf16[2,64,2048]{2,1,0:T(8,128)(2,1)S(1)}, u32[]{:S(2)}, u32[]{:S(2)}) %collective-permute-start.11) | collective-permute-done | bytes 524320 | tf_op jit(solution)/shard_map/ppermute | solution.py:440
  61.9 0.7 %collective-permute-done.12.refs_3_ = bf16[2,64,2048]{2,1,0:T(8,128)(2,1)S(1)} collective-permute-done((bf16[2,64,2048]{2,1,0:T(8,128)(2,1)S(1)}, bf16[2,64,2048]{2,1,0:T(8,128)(2,1)S(1)}, u32[]{:S(2)}, u32[]{:S(2)}) %collective-permute-start.12) | collective-permute-done | bytes 524320 | tf_op jit(solution)/shard_map/ppermute | solution.py:440
  62.7 5.0 %shard_map.46 = (f32[2,128,2048]{2,1,0:T(8,128)S(1)}, f32[2,128,128]{2,1,0:T(8,128)S(1)}, f32[2,128,128]{2,1,0:T(8,128)S(1)}) custom-call(s32[2,2,1,2]{3,2,1,0:T(1,128)S(1)} %copy-done.3, bf16[2,128,2048]{2,1,0:T(8,128)(2,1)S(1)} %bitcast.12, bf16[2,2,128,2048]{3,2,1,0:T(8,128)(2,1)S(1)} %collective-permute-done.refs_0_.core_ref, ...), custom_call_target="tpu_custom_call" | custom-call | flops 1 | bytes 1 | tf_op jit(solution)/shard_map/pallas_call | solution.py:301
  67.7 0.6 shard_map.47.refs_4_
  68.7 1.3 %shard_map.48 = bf16[2,128,2048]{2,1,0:T(8,128)(2,1)} custom-call(f32[2,128,2048]{2,1,0:T(8,128)S(1)} %get-tuple-element.75.refs_0_, f32[2,128,128]{2,1,0:T(8,128)S(1)} %get-tuple-element.76.refs_1_, f32[2,128,128]{2,1,0:T(8,128)S(1)} %get-tuple-element.77.refs_2_, bf16[128,2176]{1,0:T(8,128)(2,1)S(1)} %collective-permute-done.15.refs_3_, ...), custom_call_target="tpu_custom_call" | custom-call | flops 1 | bytes 1 | tf_op jit(solution)/shard_map/pallas_call | solution.py:378
  (28 shorter events, 3.2 us)
Async XLA Ops:
  0.0 9.9 %collective-permute-start = (bf16[2,2,128,2048]{3,2,1,0:T(8,128)(2,1)}, bf16[2,2,128,2048]{3,2,1,0:T(8,128)(2,1)S(1)}, u32[]{:S(2)}, u32[]{:S(2)}) collective-permute-start(bf16[2,2,128,2048]{3,2,1,0:T(8,128)(2,1)} %bitcast.3), channel_id=1, source_target_pairs={{0,8},{8,0},{16,24},{24,16},{1,9},{9,1},{17,25},{25,17},{2,10},{10... | collective-permute-start | bytes 6291464 | tf_op jit(solution)/shard_map/ppermute | solution.py:409
  0.5 1.6 %copy-start = (bf16[2,2,16,8,2048]{4,3,2,1,0:T(8,128)(2,1)S(1)}, bf16[2,2,16,8,2048]{4,3,2,1,0:T(8,128)(2,1)}, u32[]{:S(2)}) copy-start(bf16[2,2,16,8,2048]{4,3,2,1,0:T(8,128)(2,1)} %param.4) | copy-start | bytes 6291460
  2.0 7.9 %copy-start.2 = (bf16[2,16,8,2048]{3,2,1,0:T(8,128)(2,1)S(1)}, bf16[2,16,8,2048]{3,2,1,0:T(8,128)(2,1)}, u32[]{:S(2)}) copy-start(bf16[2,16,8,2048]{3,2,1,0:T(8,128)(2,1)} %param.3) | copy-start | bytes 3145732
  2.4 35.7 %copy-start.1 = (bf16[2,2,16,8,2048]{4,3,2,1,0:T(8,128)(2,1)S(1)}, bf16[2,2,16,8,2048]{4,3,2,1,0:T(8,128)(2,1)}, u32[]{:S(2)}) copy-start(bf16[2,2,16,8,2048]{4,3,2,1,0:T(8,128)(2,1)} %param.4) | copy-start | bytes 6291460
  2.4 26.2 %collective-permute-start.1 = (bf16[2,128,2048]{2,1,0:T(8,128)(2,1)S(1)}, bf16[2,128,2048]{2,1,0:T(8,128)(2,1)S(1)}, u32[]{:S(2)}, u32[]{:S(2)}) collective-permute-start(bf16[2,128,2048]{2,1,0:T(8,128)(2,1)S(1)} %get-tuple-element.44), channel_id=1, source_target_pairs={{0,24},{8,16},{16,8},{24,0},{1,25},{9,17},{17,9},{25,1},{2,26},{10... | collective-permute-start | bytes 3145736 | tf_op jit(solution)/shard_map/ppermute | solution.py:411
  5.1 28.7 %collective-permute-start.4 = (bf16[2,2,64,2048]{3,2,1,0:T(8,128)(2,1)S(1)}, bf16[2,2,64,2048]{3,2,1,0:T(8,128)(2,1)S(1)}, u32[]{:S(2)}, u32[]{:S(2)}) collective-permute-start(bf16[2,2,64,2048]{3,2,1,0:T(8,128)(2,1)S(1)} %get-tuple-element.48), channel_id=1, source_target_pairs={{0,2},{2,4},{4,6},{1,3},{3,5},{5,7},{8,10},{10,12},{12,14},{9,11},... | collective-permute-start | bytes 3145736 | tf_op jit(solution)/shard_map/ppermute | solution.py:412
  8.6 26.7 %collective-permute-start.5 = (bf16[2,2,64,2048]{3,2,1,0:T(8,128)(2,1)S(1)}, bf16[2,2,64,2048]{3,2,1,0:T(8,128)(2,1)S(1)}, u32[]{:S(2)}, u32[]{:S(2)}) collective-permute-start(bf16[2,2,64,2048]{3,2,1,0:T(8,128)(2,1)S(1)} %get-tuple-element.49), channel_id=1, source_target_pairs={{2,0},{4,2},{6,4},{3,1},{5,3},{7,5},{10,8},{12,10},{14,12},{11,9},... | collective-permute-start | bytes 3145736 | tf_op jit(solution)/shard_map/ppermute | solution.py:413
  9.9 25.4 %collective-permute-start.6 = (bf16[2,128,2048]{2,1,0:T(8,128)(2,1)S(1)}, bf16[2,128,2048]{2,1,0:T(8,128)(2,1)S(1)}, u32[]{:S(2)}, u32[]{:S(2)}) collective-permute-start(bf16[2,128,2048]{2,1,0:T(8,128)(2,1)S(1)} %bitcast.9), channel_id=1, source_target_pairs={{0,1},{1,0},{2,3},{3,2},{4,5},{5,4},{6,7},{7,6},{8,9},{9,8},{10,11... | collective-permute-start | bytes 3145736 | tf_op jit(solution)/shard_map/ppermute | solution.py:415
  28.6 26.6 %collective-permute-start.9 = (bf16[2,128,2048]{2,1,0:T(8,128)(2,1)S(1)}, bf16[2,128,2048]{2,1,0:T(8,128)(2,1)S(1)}, u32[]{:S(2)}, u32[]{:S(2)}) collective-permute-start(bf16[2,128,2048]{2,1,0:T(8,128)(2,1)S(1)} %get-tuple-element.59), channel_id=1, source_target_pairs={{0,24},{8,16},{16,8},{24,0},{1,25},{9,17},{17,9},{25,1},{2,26},{10... | collective-permute-start | bytes 3145736 | tf_op jit(solution)/shard_map/ppermute | solution.py:420
  30.3 17.2 %collective-permute-start.2 = (bf16[2,64,2176]{2,1,0:T(8,128)(2,1)S(1)}, bf16[2,64,2176]{2,1,0:T(8,128)(2,1)S(1)}, u32[]{:S(2)}, u32[]{:S(2)}) collective-permute-start(bf16[2,64,2176]{2,1,0:T(8,128)(2,1)S(1)} %get-tuple-element.46), channel_id=1, source_target_pairs={{0,2},{2,4},{4,6},{1,3},{3,5},{5,7},{8,10},{10,12},{12,14},{9,11},... | collective-permute-start | bytes 1671176 | tf_op jit(solution)/shard_map/ppermute | solution.py:417
  33.8 15.9 %collective-permute-start.3 = (bf16[2,64,2176]{2,1,0:T(8,128)(2,1)S(1)}, bf16[2,64,2176]{2,1,0:T(8,128)(2,1)S(1)}, u32[]{:S(2)}, u32[]{:S(2)}) collective-permute-start(bf16[2,64,2176]{2,1,0:T(8,128)(2,1)S(1)} %get-tuple-element.47), channel_id=1, source_target_pairs={{2,0},{4,2},{6,4},{3,1},{5,3},{7,5},{10,8},{12,10},{14,12},{11,9},... | collective-permute-start | bytes 1671176 | tf_op jit(solution)/shard_map/ppermute | solution.py:418
  35.4 2.0 %collective-permute-start.7 = (bf16[2,64,2048]{2,1,0:T(8,128)(2,1)S(1)}, bf16[2,64,2048]{2,1,0:T(8,128)(2,1)S(1)}, u32[]{:S(2)}, u32[]{:S(2)}) collective-permute-start(bf16[2,64,2048]{2,1,0:T(8,128)(2,1)S(1)} %get-tuple-element.53), channel_id=1, source_target_pairs={{0,8},{8,0},{16,24},{24,16},{1,9},{9,1},{17,25},{25,17},{2,10},{10... | collective-permute-start | bytes 1572872 | tf_op jit(solution)/shard_map/ppermute | solution.py:422
  35.5 2.6 %collective-permute-start.8 = (bf16[2,64,2048]{2,1,0:T(8,128)(2,1)S(1)}, bf16[2,64,2048]{2,1,0:T(8,128)(2,1)S(1)}, u32[]{:S(2)}, u32[]{:S(2)}) collective-permute-start(bf16[2,64,2048]{2,1,0:T(8,128)(2,1)S(1)} %get-tuple-element.54), channel_id=1, source_target_pairs={{0,8},{8,0},{16,24},{24,16},{1,9},{9,1},{17,25},{25,17},{2,10},{10... | collective-permute-start | bytes 1572872 | tf_op jit(solution)/shard_map/ppermute | solution.py:422
  42.0 17.8 %collective-permute-start.10 = (bf16[128,2176]{1,0:T(8,128)(2,1)S(1)}, bf16[128,2176]{1,0:T(8,128)(2,1)S(1)}, u32[]{:S(2)}, u32[]{:S(2)}) collective-permute-start(bf16[128,2176]{1,0:T(8,128)(2,1)S(1)} %shard_map.40), channel_id=1, source_target_pairs={{0,1},{1,0},{2,3},{3,2},{4,5},{5,4},{6,7},{7,6},{8,9},{9,8},{10,11... | collective-permute-start | bytes 1671176 | tf_op jit(solution)/shard_map/ppermute | solution.py:426
  53.6 15.1 %collective-permute-start.15 = (bf16[128,2176]{1,0:T(8,128)(2,1)S(1)}, bf16[128,2176]{1,0:T(8,128)(2,1)S(1)}, u32[]{:S(2)}, u32[]{:S(2)}) collective-permute-start(bf16[128,2176]{1,0:T(8,128)(2,1)S(1)} %shard_map.42), channel_id=1, source_target_pairs={{0,1},{1,0},{2,3},{3,2},{4,5},{5,4},{6,7},{7,6},{8,9},{9,8},{10,11... | collective-permute-start | bytes 1671176 | tf_op jit(solution)/shard_map/ppermute | solution.py:433
  55.5 5.0 %collective-permute-start.13 = (bf16[2,64,2176]{2,1,0:T(8,128)(2,1)S(1)}, bf16[2,64,2176]{2,1,0:T(8,128)(2,1)S(1)}, u32[]{:S(2)}, u32[]{:S(2)}) collective-permute-start(bf16[2,64,2176]{2,1,0:T(8,128)(2,1)S(1)} %get-tuple-element.67), channel_id=1, source_target_pairs={{0,8},{8,0},{16,24},{24,16},{1,9},{9,1},{17,25},{25,17},{2,10},{10... | collective-permute-start | bytes 1671176 | tf_op jit(solution)/shard_map/ppermute | solution.py:437
  55.6 7.1 %copy-start.3 = (s32[2,2,1,2]{3,2,1,0:T(1,128)S(1)}, s32[2,2,1,2]{3,2,1,0:T(1,128)}, u32[]{:S(2)}) copy-start(s32[2,2,1,2]{3,2,1,0:T(1,128)} %far_ref.1) | copy-start | bytes 100
  55.6 5.0 %collective-permute-start.14 = (bf16[2,64,2176]{2,1,0:T(8,128)(2,1)S(1)}, bf16[2,64,2176]{2,1,0:T(8,128)(2,1)S(1)}, u32[]{:S(2)}, u32[]{:S(2)}) collective-permute-start(bf16[2,64,2176]{2,1,0:T(8,128)(2,1)S(1)} %get-tuple-element.68), channel_id=1, source_target_pairs={{0,8},{8,0},{16,24},{24,16},{1,9},{9,1},{17,25},{25,17},{2,10},{10... | collective-permute-start | bytes 1671176 | tf_op jit(solution)/shard_map/ppermute | solution.py:437
  60.0 2.0 %collective-permute-start.11 = (bf16[2,64,2048]{2,1,0:T(8,128)(2,1)S(1)}, bf16[2,64,2048]{2,1,0:T(8,128)(2,1)S(1)}, u32[]{:S(2)}, u32[]{:S(2)}) collective-permute-start(bf16[2,64,2048]{2,1,0:T(8,128)(2,1)S(1)} %get-tuple-element.65), channel_id=1, source_target_pairs={{0,8},{8,0},{16,24},{24,16},{1,9},{9,1},{17,25},{25,17},{2,10},{10... | collective-permute-start | bytes 1572872 | tf_op jit(solution)/shard_map/ppermute | solution.py:440
  60.1 2.6 %collective-permute-start.12 = (bf16[2,64,2048]{2,1,0:T(8,128)(2,1)S(1)}, bf16[2,64,2048]{2,1,0:T(8,128)(2,1)S(1)}, u32[]{:S(2)}, u32[]{:S(2)}) collective-permute-start(bf16[2,64,2048]{2,1,0:T(8,128)(2,1)S(1)} %get-tuple-element.66), channel_id=1, source_target_pairs={{0,8},{8,0},{16,24},{24,16},{1,9},{9,1},{17,25},{25,17},{2,10},{10... | collective-permute-start | bytes 1572872 | tf_op jit(solution)/shard_map/ppermute | solution.py:440

commit v13 on v12

--- a/solution.py
+++ b/solution.py
@@ -144,9 +144,10 @@
         parts.append(ext_ref[kind, parity, :, lanes] if early else ext_ref[kind, :, lanes])
         return jnp.concatenate(parts, axis=0)
 
-    def halo(a, kind, lanes):
+    def halo(a, kind, lanes, copies):
         ref, ext = ((top_ref, ext_top_ref), (bottom_ref, ext_bottom_ref))[a]
-        return jnp.concatenate([ref[kind, 0, :, lanes], ref[kind, 1, :, lanes], ext[kind, :, lanes]], axis=0)
+        blocks = [ref[kind, 0, :, lanes], ref[kind, 1, :, lanes]] + [ext[kind, :, lanes]] * copies
+        return jnp.concatenate(blocks, axis=0)
 
     peaks = [jnp.zeros((half, HD), jnp.float32) for _ in range(2)]
     totals = [jnp.ones((half, HD), jnp.float32) for _ in range(2)]
@@ -159,18 +160,18 @@
                 for a in range(2)
             ]
             near = contract_last(jnp.concatenate(queries, axis=0), middle(0, lanes))
-            edges = [contract_last(queries[a], halo(a, 0, lanes)) for a in range(2)]
+            edges = [contract_last(queries[a], halo(a, 0, lanes, 2)) for a in range(2)]
             scores.append([(near[a * half : (a + 1) * half], edges[a]) for a in range(2)])
         weights = []
         for pairs in scores:
             for a, (near, edge) in enumerate(pairs):
                 best = functools.reduce(jnp.maximum, [near[:, i * HD : (i + 1) * HD] for i in range(3)])
-                edge_best = jnp.maximum(edge[:, : 2 * SPOT], jnp.concatenate([edge[:, 2 * SPOT :]] * 2, axis=1))
+                edge_best = jnp.maximum(edge[:, : 2 * SPOT], edge[:, 2 * SPOT :])
                 best = jnp.maximum(best, jnp.where(valid[a], edge_best, NEGATIVE))
                 peak = jnp.max(best, axis=-1, keepdims=True)
                 shift = jnp.where(valid[a], peak, -NEGATIVE)
                 near = jnp.exp2((near - peak) * EXP_SCALE).astype(jnp.bfloat16)
-                edge = jnp.exp2((edge - shift) * EXP_SCALE).astype(jnp.bfloat16)
+                edge = jnp.exp2((edge[:, : 3 * SPOT] - shift) * EXP_SCALE).astype(jnp.bfloat16)
                 weights.append((peak, near, edge))
         for i, lanes in enumerate(members):
             mask = lane_index(half) == first + i
@@ -178,7 +179,7 @@
             middle_weights = jnp.concatenate([near for _, near, _ in pair], axis=0)
             middle_sums = jnp.dot(middle_weights, with_ones(middle(1, lanes)), preferred_element_type=jnp.float32)
             for a, (peak, _, edge) in enumerate(pair):
-                summed = jnp.dot(edge, with_ones(halo(a, 1, lanes)), preferred_element_type=jnp.float32)
+                summed = jnp.dot(edge, with_ones(halo(a, 1, lanes, 1)), preferred_element_type=jnp.float32)
                 summed = summed + middle_sums[a * half : (a + 1) * half]
                 total = summed[:, HD:]
                 peaks[a] = jnp.where(mask, peak, peaks[a])
@@ -416,7 +417,6 @@
     cross_first, cross_last = widened_rows(cross)
     cross_top = lax.ppermute(cross_last, "ha", up)
     cross_bottom = lax.ppermute(cross_first, "ha", down)
-    inner, cross = tie((inner, cross))
     last = lax.ppermute(inner, "ta", cross_pairs)
     top, bottom, visitors = tie((top, bottom, visitors))
     core_top, core_bottom = [lax.ppermute(value, "ta", core_pairs) for value in inner_rows(top, bottom)]

time: 70.4 us -> 69.6 us (0.989)
  waiting for transfers between devices: 24.2 us -> 27.9 us
  Pallas kernels: 23.3 us -> 20.3 us
  starting transfers between devices: 20.7 us -> 19.2 us
    pallas_call x4, Pallas kernels: 15.4 us -> 12.4 us  [near_attention(): pl.pallas_call(functools.partial(near_kernel, len(visitors), len(queries)...]
    ppermute x1, waiting for transfers between devices: 0.18 us -> 1.74 us  [per_device(): bottom = lax.ppermute(first_rows, 'ha', down)]
    ppermute x1, starting transfers between devices: 1.53 us -> 0.01 us  [per_device(): last = lax.ppermute(inner, 'ta', cross_pairs)]
    ppermute x1, waiting for transfers between devices: 2.24 us -> 3.64 us  [per_device(): cross_bottom = lax.ppermute(cross_first, 'ha', down)]
    ppermute x2, waiting for transfers between devices: 0.35 us -> 1.11 us  [per_device(): lax.ppermute(result, 'wa', back)]
  transfers between devices with their start and end apart: 16 -> 16, of which waited for: 8 -> 8; matrix products, arithmetic and copies ran while one was open for 0% -> 0% of each run, Pallas kernels for 31% -> 27%
where the time goes in v13:
time: 69.6 us; the launch traced here: 69.4 us
  waiting for transfers between devices  27.9 us (40%)
  Pallas kernels  20.3 us (29%)
  starting transfers between devices  19.2 us (28%)
  local copies, waits for them, and re-layouts  1.61 us (2%)
    ppermute x1, waiting for transfers between devices, per_device(): cross = lax.ppermute(outer, 'ta', cross_pairs)  17.1 us
    pallas_call x4, Pallas kernels, near_attention(): pl.pallas_call(functools.partial(near_kernel, len(visitors), len(queries)...  12.4 us
    pallas_call x1, Pallas kernels, far_attention(): pl.pallas_call(functools.partial(far_kernel, members), out_shape=[jax.Sha...  5.23 us
    ppermute x1, waiting for transfers between devices, per_device(): cross_bottom = lax.ppermute(cross_first, 'ha', down)  3.64 us
    ppermute x1, starting transfers between devices, per_device(): top = lax.ppermute(last_rows, 'ha', up)  3.53 us
    ppermute x1, starting transfers between devices, per_device(): cross_top = lax.ppermute(cross_last, 'ha', up)  3.49 us
    ppermute x2, starting transfers between devices, per_device(): lax.ppermute(result, 'wa', back)  3.17 us
    ppermute x1, starting transfers between devices, per_device(): cross = lax.ppermute(outer, 'ta', cross_pairs)  2.67 us
  transfers between devices with their start and end apart: 16, of which 8 were waited for; matrix products, arithmetic and copies ran while one was open for 0% of the time, Pallas kernels for 27%

profile of v13, /device:TPU:0, one launch (start us, length us, event | category | flops | bytes accessed | tf_op | source)
XLA Modules:
  0.0 69.4 jit_solution(9625911477439999504)
XLA Ops:
  0.5 1.6 %copy-done = bf16[2,2,16,8,2048]{4,3,2,1,0:T(8,128)(2,1)S(1)} copy-done((bf16[2,2,16,8,2048]{4,3,2,1,0:T(8,128)(2,1)S(1)}, bf16[2,2,16,8,2048]{4,3,2,1,0:T(8,128)(2,1)}, u32[]{:S(2)}) %copy-start) | copy-done | bytes 2097176
  2.4 2.7 %collective-permute-start.1 = (bf16[2,128,2048]{2,1,0:T(8,128)(2,1)S(1)}, bf16[2,128,2048]{2,1,0:T(8,128)(2,1)S(1)}, u32[]{:S(2)}, u32[]{:S(2)}) collective-permute-start(bf16[2,128,2048]{2,1,0:T(8,128)(2,1)S(1)} %get-tuple-element.41), channel_id=1, source_target_pairs={{0,24},{8,16},{16,8},{24,0},{1,25},{9,17},{17,9},{25,1},{2,26},{10... | collective-permute-start | bytes 3145736 | tf_op jit(solution)/shard_map/ppermute | solution.py:412
  5.1 3.5 %collective-permute-start.4 = (bf16[2,2,64,2048]{3,2,1,0:T(8,128)(2,1)S(1)}, bf16[2,2,64,2048]{3,2,1,0:T(8,128)(2,1)S(1)}, u32[]{:S(2)}, u32[]{:S(2)}) collective-permute-start(bf16[2,2,64,2048]{3,2,1,0:T(8,128)(2,1)S(1)} %get-tuple-element.44), channel_id=1, source_target_pairs={{0,2},{2,4},{4,6},{1,3},{3,5},{5,7},{8,10},{10,12},{12,14},{9,11},... | collective-permute-start | bytes 3145736 | tf_op jit(solution)/shard_map/ppermute | solution.py:413
  8.6 1.3 %collective-permute-start.5 = (bf16[2,2,64,2048]{3,2,1,0:T(8,128)(2,1)S(1)}, bf16[2,2,64,2048]{3,2,1,0:T(8,128)(2,1)S(1)}, u32[]{:S(2)}, u32[]{:S(2)}) collective-permute-start(bf16[2,2,64,2048]{3,2,1,0:T(8,128)(2,1)S(1)} %get-tuple-element.45), channel_id=1, source_target_pairs={{2,0},{4,2},{6,4},{3,1},{5,3},{7,5},{10,8},{12,10},{14,12},{11,9},... | collective-permute-start | bytes 3145736 | tf_op jit(solution)/shard_map/ppermute | solution.py:414
  9.9 1.6 %collective-permute-start.6 = (bf16[2,128,2048]{2,1,0:T(8,128)(2,1)S(1)}, bf16[2,128,2048]{2,1,0:T(8,128)(2,1)S(1)}, u32[]{:S(2)}, u32[]{:S(2)}) collective-permute-start(bf16[2,128,2048]{2,1,0:T(8,128)(2,1)S(1)} %bitcast.9), channel_id=1, source_target_pairs={{0,1},{1,0},{2,3},{3,2},{4,5},{5,4},{6,7},{7,6},{8,9},{9,8},{10,11... | collective-permute-start | bytes 3145736 | tf_op jit(solution)/shard_map/ppermute | solution.py:416
  11.5 17.1 %collective-permute-done.1.frame_ref.refs_0_ = bf16[2,128,2048]{2,1,0:T(8,128)(2,1)S(1)} collective-permute-done((bf16[2,128,2048]{2,1,0:T(8,128)(2,1)S(1)}, bf16[2,128,2048]{2,1,0:T(8,128)(2,1)S(1)}, u32[]{:S(2)}, u32[]{:S(2)}) %collective-permute-start.1) | collective-permute-done | bytes 1048608 | tf_op jit(solution)/shard_map/ppermute | solution.py:412
  28.7 3.5 %collective-permute-start.2 = (bf16[2,64,2176]{2,1,0:T(8,128)(2,1)S(1)}, bf16[2,64,2176]{2,1,0:T(8,128)(2,1)S(1)}, u32[]{:S(2)}, u32[]{:S(2)}) collective-permute-start(bf16[2,64,2176]{2,1,0:T(8,128)(2,1)S(1)} %get-tuple-element.42), channel_id=1, source_target_pairs={{0,2},{2,4},{4,6},{1,3},{3,5},{5,7},{8,10},{10,12},{12,14},{9,11},... | collective-permute-start | bytes 1671176 | tf_op jit(solution)/shard_map/ppermute | solution.py:418
  32.2 1.3 %collective-permute-start.3 = (bf16[2,64,2176]{2,1,0:T(8,128)(2,1)S(1)}, bf16[2,64,2176]{2,1,0:T(8,128)(2,1)S(1)}, u32[]{:S(2)}, u32[]{:S(2)}) collective-permute-start(bf16[2,64,2176]{2,1,0:T(8,128)(2,1)S(1)} %get-tuple-element.43), channel_id=1, source_target_pairs={{2,0},{4,2},{6,4},{3,1},{5,3},{7,5},{10,8},{12,10},{14,12},{11,9},... | collective-permute-start | bytes 1671176 | tf_op jit(solution)/shard_map/ppermute | solution.py:419
  33.5 1.7 %collective-permute-done.5.bottom_ref = bf16[2,2,64,2048]{3,2,1,0:T(8,128)(2,1)S(1)} collective-permute-done((bf16[2,2,64,2048]{3,2,1,0:T(8,128)(2,1)S(1)}, bf16[2,2,64,2048]{3,2,1,0:T(8,128)(2,1)S(1)}, u32[]{:S(2)}, u32[]{:S(2)}) %collective-permute-start.5) | collective-permute-done | bytes 1048608 | tf_op jit(solution)/shard_map/ppermute | solution.py:414
  36.0 1.4 %collective-permute-done.7.refs_1_ = bf16[2,64,2048]{2,1,0:T(8,128)(2,1)S(1)} collective-permute-done((bf16[2,64,2048]{2,1,0:T(8,128)(2,1)S(1)}, bf16[2,64,2048]{2,1,0:T(8,128)(2,1)S(1)}, u32[]{:S(2)}, u32[]{:S(2)}) %collective-permute-start.7) | collective-permute-done | bytes 524320 | tf_op jit(solution)/shard_map/ppermute | solution.py:422
  37.4 0.7 %collective-permute-done.8.refs_2_ = bf16[2,64,2048]{2,1,0:T(8,128)(2,1)S(1)} collective-permute-done((bf16[2,64,2048]{2,1,0:T(8,128)(2,1)S(1)}, bf16[2,64,2048]{2,1,0:T(8,128)(2,1)S(1)}, u32[]{:S(2)}, u32[]{:S(2)}) %collective-permute-start.8) | collective-permute-done | bytes 524320 | tf_op jit(solution)/shard_map/ppermute | solution.py:422
  38.1 3.1 %shard_map.40 = bf16[128,2176]{1,0:T(8,128)(2,1)S(1)} custom-call(bf16[2,2,128,2048]{3,2,1,0:T(8,128)(2,1)S(1)} %bitcast.5, bf16[2,2,64,2048]{3,2,1,0:T(8,128)(2,1)S(1)} %collective-permute-done.4.top_ref, bf16[2,2,64,2048]{3,2,1,0:T(8,128)(2,1)S(1)} %collective-permute-done.5.bottom_ref, ...), custom_call_target="tpu_custom_call" | custom-call | flops 1 | bytes 1 | tf_op jit(solution)/shard_map/pallas_call | solution.py:215
  41.2 1.6 %collective-permute-start.10 = (bf16[128,2176]{1,0:T(8,128)(2,1)S(1)}, bf16[128,2176]{1,0:T(8,128)(2,1)S(1)}, u32[]{:S(2)}, u32[]{:S(2)}) collective-permute-start(bf16[128,2176]{1,0:T(8,128)(2,1)S(1)} %shard_map.40), channel_id=1, source_target_pairs={{0,1},{1,0},{2,3},{3,2},{4,5},{5,4},{6,7},{7,6},{8,9},{9,8},{10,11... | collective-permute-start | bytes 1671176 | tf_op jit(solution)/shard_map/ppermute | solution.py:426
  42.8 3.0 %shard_map.41 = (f32[128,2048]{1,0:T(8,128)S(1)}, f32[128,128]{1,0:T(8,128)S(1)}, f32[128,128]{1,0:T(8,128)S(1)}, f32[128,2048]{1,0:T(8,128)S(1)}) custom-call(bf16[2,2,128,2048]{3,2,1,0:T(8,128)(2,1)S(1)} %bitcast.6, bf16[2,2,64,2048]{3,2,1,0:T(8,128)(2,1)S(1)} %collective-permute-done.4.top_ref, ...), custom_call_target="tpu_custom_call" | custom-call | flops 1 | bytes 1 | tf_op jit(solution)/shard_map/pallas_call | solution.py:215
  45.8 3.6 %collective-permute-done.3.refs_2_ = bf16[2,64,2176]{2,1,0:T(8,128)(2,1)S(1)} collective-permute-done((bf16[2,64,2176]{2,1,0:T(8,128)(2,1)S(1)}, bf16[2,64,2176]{2,1,0:T(8,128)(2,1)S(1)}, u32[]{:S(2)}, u32[]{:S(2)}) %collective-permute-start.3) | collective-permute-done | bytes 557088 | tf_op jit(solution)/shard_map/ppermute | solution.py:419
  49.5 3.1 %shard_map.42 = bf16[128,2176]{1,0:T(8,128)(2,1)S(1)} custom-call(bf16[2,2,128,2048]{3,2,1,0:T(8,128)(2,1)S(1)} %bitcast.7, bf16[2,2,64,2048]{3,2,1,0:T(8,128)(2,1)S(1)} %collective-permute-done.4.top_ref, bf16[2,2,64,2048]{3,2,1,0:T(8,128)(2,1)S(1)} %collective-permute-done.5.bottom_ref, bf16[2,128,2048]{2,1,0:T(8,128)(2,1)S(1)} %collective-permute-done.1.frame_ref.refs_0_, ...), custom_call_target="tpu_custom_call" | custom-call | flops 1 | bytes 1 | tf_op jit(solution)/shard_map/pallas_call | solution.py:215
  52.6 1.6 %collective-permute-start.15 = (bf16[128,2176]{1,0:T(8,128)(2,1)S(1)}, bf16[128,2176]{1,0:T(8,128)(2,1)S(1)}, u32[]{:S(2)}, u32[]{:S(2)}) collective-permute-start(bf16[128,2176]{1,0:T(8,128)(2,1)S(1)} %shard_map.42), channel_id=1, source_target_pairs={{0,1},{1,0},{2,3},{3,2},{4,5},{5,4},{6,7},{7,6},{8,9},{9,8},{10,11... | collective-permute-start | bytes 1671176 | tf_op jit(solution)/shard_map/ppermute | solution.py:433
  54.9 3.1 %shard_map.43 = (f32[128,2048]{1,0:T(8,128)S(1)}, f32[128,128]{1,0:T(8,128)S(1)}, f32[128,128]{1,0:T(8,128)S(1)}, f32[128,2048]{1,0:T(8,128)S(1)}) custom-call(bf16[2,2,128,2048]{3,2,1,0:T(8,128)(2,1)S(1)} %bitcast.8, bf16[2,2,64,2048]{3,2,1,0:T(8,128)(2,1)S(1)} %collective-permute-done.4.top_ref, ...), custom_call_target="tpu_custom_call" | custom-call | flops 30064771072 | bytes 1 | tf_op jit(solution)/shard_map/pallas_call | solution.py:215
  58.8 1.4 %collective-permute-done.11.refs_2_ = bf16[2,64,2048]{2,1,0:T(8,128)(2,1)S(1)} collective-permute-done((bf16[2,64,2048]{2,1,0:T(8,128)(2,1)S(1)}, bf16[2,64,2048]{2,1,0:T(8,128)(2,1)S(1)}, u32[]{:S(2)}, u32[]{:S(2)}) %collective-permute-start.11) | collective-permute-done | bytes 524320 | tf_op jit(solution)/shard_map/ppermute | solution.py:440
  60.1 0.7 %collective-permute-done.12.refs_3_ = bf16[2,64,2048]{2,1,0:T(8,128)(2,1)S(1)} collective-permute-done((bf16[2,64,2048]{2,1,0:T(8,128)(2,1)S(1)}, bf16[2,64,2048]{2,1,0:T(8,128)(2,1)S(1)}, u32[]{:S(2)}, u32[]{:S(2)}) %collective-permute-start.12) | collective-permute-done | bytes 524320 | tf_op jit(solution)/shard_map/ppermute | solution.py:440
  60.9 5.2 %shard_map.46 = (f32[2,128,2048]{2,1,0:T(8,128)S(1)}, f32[2,128,128]{2,1,0:T(8,128)S(1)}, f32[2,128,128]{2,1,0:T(8,128)S(1)}) custom-call(s32[2,2,1,2]{3,2,1,0:T(1,128)S(1)} %copy-done.3, bf16[2,128,2048]{2,1,0:T(8,128)(2,1)S(1)} %bitcast.12, bf16[2,2,128,2048]{3,2,1,0:T(8,128)(2,1)S(1)} %collective-permute-done.refs_0_.core_ref, ...), custom_call_target="tpu_custom_call" | custom-call | flops 1 | bytes 1 | tf_op jit(solution)/shard_map/pallas_call | solution.py:302
  66.1 0.6 shard_map.47.refs_4_
  66.8 1.1 %collective-permute-done.15.refs_3_ = bf16[128,2176]{1,0:T(8,128)(2,1)S(1)} collective-permute-done((bf16[128,2176]{1,0:T(8,128)(2,1)S(1)}, bf16[128,2176]{1,0:T(8,128)(2,1)S(1)}, u32[]{:S(2)}, u32[]{:S(2)}) %collective-permute-start.15) | collective-permute-done | bytes 557088 | tf_op jit(solution)/shard_map/ppermute | solution.py:433
  67.9 1.3 %shard_map.48 = bf16[2,128,2048]{2,1,0:T(8,128)(2,1)} custom-call(f32[2,128,2048]{2,1,0:T(8,128)S(1)} %get-tuple-element.71.refs_0_, f32[2,128,128]{2,1,0:T(8,128)S(1)} %get-tuple-element.72.refs_1_, f32[2,128,128]{2,1,0:T(8,128)S(1)} %get-tuple-element.73.refs_2_, bf16[128,2176]{1,0:T(8,128)(2,1)S(1)} %collective-permute-done.15.refs_3_, ...), custom_call_target="tpu_custom_call" | custom-call | flops 1 | bytes 1 | tf_op jit(solution)/shard_map/pallas_call | solution.py:379
  (28 shorter events, 3.0 us)
Async XLA Ops:
  0.0 9.9 %collective-permute-start = (bf16[2,2,128,2048]{3,2,1,0:T(8,128)(2,1)}, bf16[2,2,128,2048]{3,2,1,0:T(8,128)(2,1)S(1)}, u32[]{:S(2)}, u32[]{:S(2)}) collective-permute-start(bf16[2,2,128,2048]{3,2,1,0:T(8,128)(2,1)} %bitcast.3), channel_id=1, source_target_pairs={{0,8},{8,0},{16,24},{24,16},{1,9},{9,1},{17,25},{25,17},{2,10},{10... | collective-permute-start | bytes 6291464 | tf_op jit(solution)/shard_map/ppermute | solution.py:410
  0.5 1.6 %copy-start = (bf16[2,2,16,8,2048]{4,3,2,1,0:T(8,128)(2,1)S(1)}, bf16[2,2,16,8,2048]{4,3,2,1,0:T(8,128)(2,1)}, u32[]{:S(2)}) copy-start(bf16[2,2,16,8,2048]{4,3,2,1,0:T(8,128)(2,1)} %param.4) | copy-start | bytes 6291460
  2.0 7.9 %copy-start.2 = (bf16[2,16,8,2048]{3,2,1,0:T(8,128)(2,1)S(1)}, bf16[2,16,8,2048]{3,2,1,0:T(8,128)(2,1)}, u32[]{:S(2)}) copy-start(bf16[2,16,8,2048]{3,2,1,0:T(8,128)(2,1)} %param.3) | copy-start | bytes 3145732
  2.4 35.7 %copy-start.1 = (bf16[2,2,16,8,2048]{4,3,2,1,0:T(8,128)(2,1)S(1)}, bf16[2,2,16,8,2048]{4,3,2,1,0:T(8,128)(2,1)}, u32[]{:S(2)}) copy-start(bf16[2,2,16,8,2048]{4,3,2,1,0:T(8,128)(2,1)} %param.4) | copy-start | bytes 6291460
  2.4 26.2 %collective-permute-start.1 = (bf16[2,128,2048]{2,1,0:T(8,128)(2,1)S(1)}, bf16[2,128,2048]{2,1,0:T(8,128)(2,1)S(1)}, u32[]{:S(2)}, u32[]{:S(2)}) collective-permute-start(bf16[2,128,2048]{2,1,0:T(8,128)(2,1)S(1)} %get-tuple-element.41), channel_id=1, source_target_pairs={{0,24},{8,16},{16,8},{24,0},{1,25},{9,17},{17,9},{25,1},{2,26},{10... | collective-permute-start | bytes 3145736 | tf_op jit(solution)/shard_map/ppermute | solution.py:412
  5.1 27.2 %collective-permute-start.4 = (bf16[2,2,64,2048]{3,2,1,0:T(8,128)(2,1)S(1)}, bf16[2,2,64,2048]{3,2,1,0:T(8,128)(2,1)S(1)}, u32[]{:S(2)}, u32[]{:S(2)}) collective-permute-start(bf16[2,2,64,2048]{3,2,1,0:T(8,128)(2,1)S(1)} %get-tuple-element.44), channel_id=1, source_target_pairs={{0,2},{2,4},{4,6},{1,3},{3,5},{5,7},{8,10},{10,12},{12,14},{9,11},... | collective-permute-start | bytes 3145736 | tf_op jit(solution)/shard_map/ppermute | solution.py:413
  8.6 26.7 %collective-permute-start.5 = (bf16[2,2,64,2048]{3,2,1,0:T(8,128)(2,1)S(1)}, bf16[2,2,64,2048]{3,2,1,0:T(8,128)(2,1)S(1)}, u32[]{:S(2)}, u32[]{:S(2)}) collective-permute-start(bf16[2,2,64,2048]{3,2,1,0:T(8,128)(2,1)S(1)} %get-tuple-element.45), channel_id=1, source_target_pairs={{2,0},{4,2},{6,4},{3,1},{5,3},{7,5},{10,8},{12,10},{14,12},{11,9},... | collective-permute-start | bytes 3145736 | tf_op jit(solution)/shard_map/ppermute | solution.py:414
  9.9 25.4 %collective-permute-start.6 = (bf16[2,128,2048]{2,1,0:T(8,128)(2,1)S(1)}, bf16[2,128,2048]{2,1,0:T(8,128)(2,1)S(1)}, u32[]{:S(2)}, u32[]{:S(2)}) collective-permute-start(bf16[2,128,2048]{2,1,0:T(8,128)(2,1)S(1)} %bitcast.9), channel_id=1, source_target_pairs={{0,1},{1,0},{2,3},{3,2},{4,5},{5,4},{6,7},{7,6},{8,9},{9,8},{10,11... | collective-permute-start | bytes 3145736 | tf_op jit(solution)/shard_map/ppermute | solution.py:416
  11.5 42.7 %collective-permute-start.9 = (bf16[2,128,2048]{2,1,0:T(8,128)(2,1)S(1)}, bf16[2,128,2048]{2,1,0:T(8,128)(2,1)S(1)}, u32[]{:S(2)}, u32[]{:S(2)}) collective-permute-start(bf16[2,128,2048]{2,1,0:T(8,128)(2,1)S(1)} %get-tuple-element.55), channel_id=1, source_target_pairs={{0,24},{8,16},{16,8},{24,0},{1,25},{9,17},{17,9},{25,1},{2,26},{10... | collective-permute-start | bytes 3145736 | tf_op jit(solution)/shard_map/ppermute | solution.py:420
  28.7 17.1 %collective-permute-start.2 = (bf16[2,64,2176]{2,1,0:T(8,128)(2,1)S(1)}, bf16[2,64,2176]{2,1,0:T(8,128)(2,1)S(1)}, u32[]{:S(2)}, u32[]{:S(2)}) collective-permute-start(bf16[2,64,2176]{2,1,0:T(8,128)(2,1)S(1)} %get-tuple-element.42), channel_id=1, source_target_pairs={{0,2},{2,4},{4,6},{1,3},{3,5},{5,7},{8,10},{10,12},{12,14},{9,11},... | collective-permute-start | bytes 1671176 | tf_op jit(solution)/shard_map/ppermute | solution.py:418
  32.2 17.3 %collective-permute-start.3 = (bf16[2,64,2176]{2,1,0:T(8,128)(2,1)S(1)}, bf16[2,64,2176]{2,1,0:T(8,128)(2,1)S(1)}, u32[]{:S(2)}, u32[]{:S(2)}) collective-permute-start(bf16[2,64,2176]{2,1,0:T(8,128)(2,1)S(1)} %get-tuple-element.43), channel_id=1, source_target_pairs={{2,0},{4,2},{6,4},{3,1},{5,3},{7,5},{10,8},{12,10},{14,12},{11,9},... | collective-permute-start | bytes 1671176 | tf_op jit(solution)/shard_map/ppermute | solution.py:419
  35.4 2.0 %collective-permute-start.7 = (bf16[2,64,2048]{2,1,0:T(8,128)(2,1)S(1)}, bf16[2,64,2048]{2,1,0:T(8,128)(2,1)S(1)}, u32[]{:S(2)}, u32[]{:S(2)}) collective-permute-start(bf16[2,64,2048]{2,1,0:T(8,128)(2,1)S(1)} %get-tuple-element.49), channel_id=1, source_target_pairs={{0,8},{8,0},{16,24},{24,16},{1,9},{9,1},{17,25},{25,17},{2,10},{10... | collective-permute-start | bytes 1572872 | tf_op jit(solution)/shard_map/ppermute | solution.py:422
  35.5 2.6 %collective-permute-start.8 = (bf16[2,64,2048]{2,1,0:T(8,128)(2,1)S(1)}, bf16[2,64,2048]{2,1,0:T(8,128)(2,1)S(1)}, u32[]{:S(2)}, u32[]{:S(2)}) collective-permute-start(bf16[2,64,2048]{2,1,0:T(8,128)(2,1)S(1)} %get-tuple-element.50), channel_id=1, source_target_pairs={{0,8},{8,0},{16,24},{24,16},{1,9},{9,1},{17,25},{25,17},{2,10},{10... | collective-permute-start | bytes 1572872 | tf_op jit(solution)/shard_map/ppermute | solution.py:422
  41.2 16.9 %collective-permute-start.10 = (bf16[128,2176]{1,0:T(8,128)(2,1)S(1)}, bf16[128,2176]{1,0:T(8,128)(2,1)S(1)}, u32[]{:S(2)}, u32[]{:S(2)}) collective-permute-start(bf16[128,2176]{1,0:T(8,128)(2,1)S(1)} %shard_map.40), channel_id=1, source_target_pairs={{0,1},{1,0},{2,3},{3,2},{4,5},{5,4},{6,7},{7,6},{8,9},{9,8},{10,11... | collective-permute-start | bytes 1671176 | tf_op jit(solution)/shard_map/ppermute | solution.py:426
  52.6 15.2 %collective-permute-start.15 = (bf16[128,2176]{1,0:T(8,128)(2,1)S(1)}, bf16[128,2176]{1,0:T(8,128)(2,1)S(1)}, u32[]{:S(2)}, u32[]{:S(2)}) collective-permute-start(bf16[128,2176]{1,0:T(8,128)(2,1)S(1)} %shard_map.42), channel_id=1, source_target_pairs={{0,1},{1,0},{2,3},{3,2},{4,5},{5,4},{6,7},{7,6},{8,9},{9,8},{10,11... | collective-permute-start | bytes 1671176 | tf_op jit(solution)/shard_map/ppermute | solution.py:433
  54.4 4.4 %collective-permute-start.13 = (bf16[2,64,2176]{2,1,0:T(8,128)(2,1)S(1)}, bf16[2,64,2176]{2,1,0:T(8,128)(2,1)S(1)}, u32[]{:S(2)}, u32[]{:S(2)}) collective-permute-start(bf16[2,64,2176]{2,1,0:T(8,128)(2,1)S(1)} %get-tuple-element.63), channel_id=1, source_target_pairs={{0,8},{8,0},{16,24},{24,16},{1,9},{9,1},{17,25},{25,17},{2,10},{10... | collective-permute-start | bytes 1671176 | tf_op jit(solution)/shard_map/ppermute | solution.py:437
  54.4 6.5 %copy-start.3 = (s32[2,2,1,2]{3,2,1,0:T(1,128)S(1)}, s32[2,2,1,2]{3,2,1,0:T(1,128)}, u32[]{:S(2)}) copy-start(s32[2,2,1,2]{3,2,1,0:T(1,128)} %far_ref.1) | copy-start | bytes 100
  54.5 4.3 %collective-permute-start.14 = (bf16[2,64,2176]{2,1,0:T(8,128)(2,1)S(1)}, bf16[2,64,2176]{2,1,0:T(8,128)(2,1)S(1)}, u32[]{:S(2)}, u32[]{:S(2)}) collective-permute-start(bf16[2,64,2176]{2,1,0:T(8,128)(2,1)S(1)} %get-tuple-element.64), channel_id=1, source_target_pairs={{0,8},{8,0},{16,24},{24,16},{1,9},{9,1},{17,25},{25,17},{2,10},{10... | collective-permute-start | bytes 1671176 | tf_op jit(solution)/shard_map/ppermute | solution.py:437
  58.2 2.0 %collective-permute-start.11 = (bf16[2,64,2048]{2,1,0:T(8,128)(2,1)S(1)}, bf16[2,64,2048]{2,1,0:T(8,128)(2,1)S(1)}, u32[]{:S(2)}, u32[]{:S(2)}) collective-permute-start(bf16[2,64,2048]{2,1,0:T(8,128)(2,1)S(1)} %get-tuple-element.61), channel_id=1, source_target_pairs={{0,8},{8,0},{16,24},{24,16},{1,9},{9,1},{17,25},{25,17},{2,10},{10... | collective-permute-start | bytes 1572872 | tf_op jit(solution)/shard_map/ppermute | solution.py:440
  58.3 2.6 %collective-permute-start.12 = (bf16[2,64,2048]{2,1,0:T(8,128)(2,1)S(1)}, bf16[2,64,2048]{2,1,0:T(8,128)(2,1)S(1)}, u32[]{:S(2)}, u32[]{:S(2)}) collective-permute-start(bf16[2,64,2048]{2,1,0:T(8,128)(2,1)S(1)} %get-tuple-element.62), channel_id=1, source_target_pairs={{0,8},{8,0},{16,24},{24,16},{1,9},{9,1},{17,25},{25,17},{2,10},{10... | collective-permute-start | bytes 1572872 | tf_op jit(solution)/shard_map/ppermute | solution.py:440

commit v14 on v13

--- a/solution.py
+++ b/solution.py
@@ -32,17 +32,30 @@
     return lax.broadcasted_iota(jnp.int32, (rows, HD), 1)
 
 
-def split_sums(value):
+def three_terms(value):
     high = value.astype(jnp.bfloat16).astype(jnp.float32)
     rest = value - high
     middle = rest.astype(jnp.bfloat16).astype(jnp.float32)
-    low = rest - middle
+    return high, middle, rest - middle
+
+
+def split_sums(value):
+    high, middle, low = three_terms(value)
     return (high + pltpu.roll(middle, HEADS, 1) + pltpu.roll(low, 2 * HEADS, 1)).astype(jnp.bfloat16)
 
 
-def join_sums(value):
-    terms = value.astype(jnp.float32)
-    return terms + (pltpu.roll(terms, HD - HEADS, 1) + pltpu.roll(terms, HD - 2 * HEADS, 1))
+def store_sums(ref, value):
+    turned = value.T[:HEADS]
+    for i, term in enumerate(three_terms(turned)):
+        start = HEADS * 2 * SPOT + i * HEADS
+        ref[start : start + HEADS, :] = term.astype(jnp.bfloat16)
+
+
+def load_sums(ref):
+    start = HEADS * 2 * SPOT
+    terms = [ref[start + i * HEADS : start + (i + 1) * HEADS, :].astype(jnp.float32) for i in range(3)]
+    turned = terms[0] + (terms[1] + terms[2])
+    return jnp.concatenate([turned, jnp.zeros((HD - HEADS, turned.shape[1]), jnp.float32)], axis=0).T
 
 
 def kernel_cost(flops):
@@ -73,11 +86,11 @@
 FIRST, LAST = pl.ds(0, SPOT), pl.ds(SPOT, SPOT)
 
 
-def cut_kernel(keyvals_ref, last_rows_ref, first_rows_ref, outer_ref, inner_ref, sems):
+def cut_kernel(keyvals_ref, first_rows_ref, last_rows_ref, outer_ref, inner_ref, sems):
     outer = lax.axis_index("ta") % 2
     pairs = [
+        (keyvals_ref.at[:, :, FIRST], first_rows_ref),
         (keyvals_ref.at[:, :, LAST], last_rows_ref),
-        (keyvals_ref.at[:, :, FIRST], first_rows_ref),
         (keyvals_ref.at[:, outer], outer_ref),
         (keyvals_ref.at[:, 1 - outer], inner_ref),
     ]
@@ -105,11 +118,11 @@
     return copying_call(by_rows_kernel, shapes, 2 * len(frames), *frames)
 
 
-def widened_rows_kernel(frame_ref, first_ref, last_ref, sems):
+def widened_rows_kernel(frame_ref, last_ref, first_ref, sems):
     features = frame_ref.shape[2]
     main, extra = pl.ds(0, features), pl.ds(features, HD)
     pairs = []
-    for rows, out_ref in ((FIRST, first_ref), (LAST, last_ref)):
+    for rows, out_ref in ((LAST, last_ref), (FIRST, first_ref)):
         pairs.append((frame_ref.at[:, rows], out_ref.at[:, :, main]))
         pairs.append((frame_ref.at[:, rows, pl.ds(0, HD)], out_ref.at[:, :, extra]))
     run_copies(pairs, sems)
@@ -120,13 +133,13 @@
     return copying_call(widened_rows_kernel, [(two, SPOT, features + HD)] * 2, 4, frame)
 
 
-def inner_rows_kernel(top_ref, bottom_ref, out_top_ref, out_bottom_ref, sems):
+def inner_rows_kernel(bottom_ref, top_ref, out_bottom_ref, out_top_ref, sems):
     inner = 1 - lax.axis_index("ta") % 2
-    run_copies([(top_ref.at[:, inner], out_top_ref), (bottom_ref.at[:, inner], out_bottom_ref)], sems)
-
-
-def inner_rows(top, bottom):
-    return copying_call(inner_rows_kernel, [top.shape[:1] + top.shape[2:]] * 2, 2, top, bottom)
+    run_copies([(bottom_ref.at[:, inner], out_bottom_ref), (top_ref.at[:, inner], out_top_ref)], sems)
+
+
+def inner_rows(bottom, top):
+    return copying_call(inner_rows_kernel, [top.shape[:1] + top.shape[2:]] * 2, 2, bottom, top)
 
 
 def near_kernel(sides, home, early, has_rows, own_ref, top_ref, bottom_ref, *refs):
@@ -192,23 +205,26 @@
                     else:
                         filled = jnp.broadcast_to(peak[rows] * EXP_SCALE, (SPOT, HD))
                         out_refs[s + 3][a * SPOT : (a + 1) * SPOT, lanes] = filled
-                    out_refs[s][a * SPOT : (a + 1) * SPOT, lanes] = result.astype(out_refs[s].dtype)
-    for a in range(2):
-        tokens = slice(a * SPOT, (a + 1) * SPOT)
-        for s in range(count):
-            rows = slice(s * SPOT, (s + 1) * SPOT)
-            if s < sides:
-                log_sum = peaks[a][rows] * EXP_SCALE + jnp.log2(totals[a][rows])
-                out_refs[s][tokens, HEADS * HD :] = split_sums(log_sum)
-            else:
-                out_refs[s + 1][tokens, :] = peaks[a][rows] * EXP_SCALE
-                out_refs[s + 2][tokens, :] = totals[a][rows]
+                        out_refs[s][a * SPOT : (a + 1) * SPOT, lanes] = result
+                    if s < sides:
+                        start = (first + i) * 2 * SPOT + a * SPOT
+                        out_refs[s][start : start + SPOT, :] = result.astype(jnp.bfloat16)
+    for s in range(count):
+        rows = slice(s * SPOT, (s + 1) * SPOT)
+        peak = jnp.concatenate([value[rows] for value in peaks], axis=0) * EXP_SCALE
+        total = jnp.concatenate([value[rows] for value in totals], axis=0)
+        if s < sides:
+            store_sums(out_refs[s], peak + jnp.log2(total))
+        else:
+            out_refs[s + 1][...] = peak
+            out_refs[s + 2][...] = total
 
 
 def near_attention(early, has_rows, own, top, bottom, third, visitors, queries, cost):
     tokens, features = own.shape[2:]
     operands = [own, top, bottom, *third, *visitors, *queries]
-    outs = [jax.ShapeDtypeStruct((tokens, features + HD), jnp.bfloat16) for _ in visitors]
+    payload = jax.ShapeDtypeStruct((HEADS * (tokens + 3), HD), jnp.bfloat16)
+    outs = [payload for _ in visitors]
     for _ in queries:
         outs += [jax.ShapeDtypeStruct((tokens, lanes), jnp.float32) for lanes in (features, HD, HD, features)]
     in_vmem = pl.BlockSpec(memory_space=pltpu.VMEM)
@@ -318,7 +334,7 @@
     wa = lax.axis_index("wa")
     logs = [own_peak_ref[at]]
     for s in range(sides):
-        value = join_sums(parts[s][:, HEADS * HD :])
+        value = load_sums(parts[s])
         if columns > 2:
             value = jnp.where(wa < columns - 1 if s == 0 else wa > 0, value, NEGATIVE)
         logs.append(value)
@@ -336,7 +352,7 @@
     factors = [jnp.dot(value, spread, preferred_element_type=jnp.float32) for value in scales]
     joined = factors[0] * own_ref[at, :, lanes]
     for factor, part in zip(factors[1:], parts):
-        joined = joined + factor * part[:, lanes].astype(jnp.float32)
+        joined = joined + factor * part[h * 2 * SPOT : (h + 1) * 2 * SPOT, :].astype(jnp.float32)
     return joined.astype(jnp.bfloat16)
 
 
@@ -408,18 +424,18 @@
     tie = lax.optimization_barrier
 
     core = lax.ppermute(keyvals, "ta", core_pairs)
-    last_rows, first_rows, outer, inner = cut(keyvals)
+    first_rows, last_rows, outer, inner = cut(keyvals)
     cross = lax.ppermute(outer, "ta", cross_pairs)
+    bottom = lax.ppermute(first_rows, "ha", down)
     top = lax.ppermute(last_rows, "ha", up)
-    bottom = lax.ppermute(first_rows, "ha", down)
     sent, core = tie((queries, core))
     visitors = [lax.ppermute(sent, "wa", there) for there, _ in ways]
-    cross_first, cross_last = widened_rows(cross)
+    cross_last, cross_first = widened_rows(cross)
     cross_top = lax.ppermute(cross_last, "ha", up)
     cross_bottom = lax.ppermute(cross_first, "ha", down)
     last = lax.ppermute(inner, "ta", cross_pairs)
-    top, bottom, visitors = tie((top, bottom, visitors))
-    core_top, core_bottom = [lax.ppermute(value, "ta", core_pairs) for value in inner_rows(top, bottom)]
+    bottom, top, visitors = tie((bottom, top, visitors))
+    core_bottom, core_top = [lax.ppermute(value, "ta", core_pairs) for value in inner_rows(bottom, top)]
 
     early_third = (core, core_top, core_bottom)
     early = near_attention(True, ha_size, keyvals, top, bottom, early_third, visitors, [], 1)
@@ -434,7 +450,7 @@
     cross_top, last, _ = tie((cross_top, last, late[0]))
     late_third = (cross, cross_top, cross_bottom)
     late_home = near_attention(False, ha_size, keyvals, top, bottom, late_third, [], [queries], LATE_COST)
-    inner_corner = [lax.ppermute(value, "ta", core_pairs) for value in widened_rows(last)]
+    inner_corner = [lax.ppermute(value, "ta", core_pairs) for value in reversed(widened_rows(last))]
     sent, early_parts, _ = tie((cross, early_parts, late_home[1]))
     cross_rows = by_rows(sent)
     corner = [lax.ppermute(value, "ta", core_pairs) for value in cross_rows]

time: 69.6 us -> 68.9 us (0.990)
  waiting for transfers between devices: 27.9 us -> 26.3 us
  starting transfers between devices: 19.2 us -> 20.2 us
    ppermute x1, waiting for transfers between devices: 0.01 us -> 2.01 us  [per_device(): visitors = [lax.ppermute(sent, 'wa', there) for there, _ in ways]]
    ppermute x1, waiting for transfers between devices: 1.74 us -> 0.01 us  [per_device(): bottom = lax.ppermute(first_rows, 'ha', down)]
    ppermute x1, starting transfers between devices: 3.53 us -> 4.61 us  [per_device(): top = lax.ppermute(last_rows, 'ha', up)]
    ppermute x1, waiting for transfers between devices: 17.1 us -> 16 us  [per_device(): cross = lax.ppermute(outer, 'ta', cross_pairs)]
where the time goes in v14:
time: 68.9 us; the launch traced here: 68.7 us
  waiting for transfers between devices  26.3 us (38%)
  starting transfers between devices  20.2 us (29%)
  Pallas kernels  20.2 us (29%)
  local copies, waits for them, and re-layouts  1.61 us (2%)
    ppermute x1, waiting for transfers between devices, per_device(): cross = lax.ppermute(outer, 'ta', cross_pairs)  16 us
    pallas_call x4, Pallas kernels, near_attention(): pl.pallas_call(functools.partial(near_kernel, len(visitors), len(queries)...  12.3 us
    pallas_call x1, Pallas kernels, far_attention(): pl.pallas_call(functools.partial(far_kernel, members), out_shape=[jax.Sha...  5.16 us
    ppermute x1, starting transfers between devices, per_device(): top = lax.ppermute(last_rows, 'ha', up)  4.61 us
    ppermute x1, starting transfers between devices, per_device(): cross_top = lax.ppermute(cross_last, 'ha', up)  3.49 us
    ppermute x1, waiting for transfers between devices, per_device(): cross_bottom = lax.ppermute(cross_first, 'ha', down)  3.41 us
    ppermute x2, starting transfers between devices, per_device(): lax.ppermute(result, 'wa', back)  3.11 us
    ppermute x1, starting transfers between devices, per_device(): cross = lax.ppermute(outer, 'ta', cross_pairs)  2.67 us
  transfers between devices with their start and end apart: 16, of which 8 were waited for; matrix products, arithmetic and copies ran while one was open for 0% of the time, Pallas kernels for 27%

profile of v14, /device:TPU:0, one launch (start us, length us, event | category | flops | bytes accessed | tf_op | source)
XLA Modules:
  0.0 68.7 jit_solution(12590170232735362035)
XLA Ops:
  0.5 1.6 %copy-done = bf16[2,2,16,8,2048]{4,3,2,1,0:T(8,128)(2,1)S(1)} copy-done((bf16[2,2,16,8,2048]{4,3,2,1,0:T(8,128)(2,1)S(1)}, bf16[2,2,16,8,2048]{4,3,2,1,0:T(8,128)(2,1)}, u32[]{:S(2)}) %copy-start) | copy-done | bytes 2097176
  2.4 2.7 %collective-permute-start.1 = (bf16[2,128,2048]{2,1,0:T(8,128)(2,1)S(1)}, bf16[2,128,2048]{2,1,0:T(8,128)(2,1)S(1)}, u32[]{:S(2)}, u32[]{:S(2)}) collective-permute-start(bf16[2,128,2048]{2,1,0:T(8,128)(2,1)S(1)} %get-tuple-element.41), channel_id=1, source_target_pairs={{0,24},{8,16},{16,8},{24,0},{1,25},{9,17},{17,9},{25,1},{2,26},{10... | collective-permute-start | bytes 3145736 | tf_op jit(solution)/shard_map/ppermute | solution.py:428
  5.1 1.3 %collective-permute-start.4 = (bf16[2,2,64,2048]{3,2,1,0:T(8,128)(2,1)S(1)}, bf16[2,2,64,2048]{3,2,1,0:T(8,128)(2,1)S(1)}, u32[]{:S(2)}, u32[]{:S(2)}) collective-permute-start(bf16[2,2,64,2048]{3,2,1,0:T(8,128)(2,1)S(1)} %get-tuple-element.44), channel_id=1, source_target_pairs={{2,0},{4,2},{6,4},{3,1},{5,3},{7,5},{10,8},{12,10},{14,12},{11,9},... | collective-permute-start | bytes 3145736 | tf_op jit(solution)/shard_map/ppermute | solution.py:429
  6.3 4.6 %collective-permute-start.5 = (bf16[2,2,64,2048]{3,2,1,0:T(8,128)(2,1)S(1)}, bf16[2,2,64,2048]{3,2,1,0:T(8,128)(2,1)S(1)}, u32[]{:S(2)}, u32[]{:S(2)}) collective-permute-start(bf16[2,2,64,2048]{3,2,1,0:T(8,128)(2,1)S(1)} %get-tuple-element.45), channel_id=1, source_target_pairs={{0,2},{2,4},{4,6},{1,3},{3,5},{5,7},{8,10},{10,12},{12,14},{9,11},... | collective-permute-start | bytes 3145736 | tf_op jit(solution)/shard_map/ppermute | solution.py:430
  11.0 1.6 %collective-permute-start.6 = (bf16[2,128,2048]{2,1,0:T(8,128)(2,1)S(1)}, bf16[2,128,2048]{2,1,0:T(8,128)(2,1)S(1)}, u32[]{:S(2)}, u32[]{:S(2)}) collective-permute-start(bf16[2,128,2048]{2,1,0:T(8,128)(2,1)S(1)} %bitcast.9), channel_id=1, source_target_pairs={{0,1},{1,0},{2,3},{3,2},{4,5},{5,4},{6,7},{7,6},{8,9},{9,8},{10,11... | collective-permute-start | bytes 3145736 | tf_op jit(solution)/shard_map/ppermute | solution.py:432
  12.6 16.0 %collective-permute-done.1.frame_ref.refs_0_ = bf16[2,128,2048]{2,1,0:T(8,128)(2,1)S(1)} collective-permute-done((bf16[2,128,2048]{2,1,0:T(8,128)(2,1)S(1)}, bf16[2,128,2048]{2,1,0:T(8,128)(2,1)S(1)}, u32[]{:S(2)}, u32[]{:S(2)}) %collective-permute-start.1) | collective-permute-done | bytes 1048608 | tf_op jit(solution)/shard_map/ppermute | solution.py:428
  28.7 3.5 %collective-permute-start.2 = (bf16[2,64,2176]{2,1,0:T(8,128)(2,1)S(1)}, bf16[2,64,2176]{2,1,0:T(8,128)(2,1)S(1)}, u32[]{:S(2)}, u32[]{:S(2)}) collective-permute-start(bf16[2,64,2176]{2,1,0:T(8,128)(2,1)S(1)} %get-tuple-element.42), channel_id=1, source_target_pairs={{0,2},{2,4},{4,6},{1,3},{3,5},{5,7},{8,10},{10,12},{12,14},{9,11},... | collective-permute-start | bytes 1671176 | tf_op jit(solution)/shard_map/ppermute | solution.py:434
  32.2 1.3 %collective-permute-start.3 = (bf16[2,64,2176]{2,1,0:T(8,128)(2,1)S(1)}, bf16[2,64,2176]{2,1,0:T(8,128)(2,1)S(1)}, u32[]{:S(2)}, u32[]{:S(2)}) collective-permute-start(bf16[2,64,2176]{2,1,0:T(8,128)(2,1)S(1)} %get-tuple-element.43), channel_id=1, source_target_pairs={{2,0},{4,2},{6,4},{3,1},{5,3},{7,5},{10,8},{12,10},{14,12},{11,9},... | collective-permute-start | bytes 1671176 | tf_op jit(solution)/shard_map/ppermute | solution.py:435
  33.5 2.0 %collective-permute-done.6.refs_3_ = bf16[2,128,2048]{2,1,0:T(8,128)(2,1)S(1)} collective-permute-done((bf16[2,128,2048]{2,1,0:T(8,128)(2,1)S(1)}, bf16[2,128,2048]{2,1,0:T(8,128)(2,1)S(1)}, u32[]{:S(2)}, u32[]{:S(2)}) %collective-permute-start.6) | collective-permute-done | bytes 1048608 | tf_op jit(solution)/shard_map/ppermute | solution.py:432
  36.2 1.4 %collective-permute-done.7.refs_1_ = bf16[2,64,2048]{2,1,0:T(8,128)(2,1)S(1)} collective-permute-done((bf16[2,64,2048]{2,1,0:T(8,128)(2,1)S(1)}, bf16[2,64,2048]{2,1,0:T(8,128)(2,1)S(1)}, u32[]{:S(2)}, u32[]{:S(2)}) %collective-permute-start.7) | collective-permute-done | bytes 524320 | tf_op jit(solution)/shard_map/ppermute | solution.py:438
  37.6 0.7 %collective-permute-done.8.refs_2_ = bf16[2,64,2048]{2,1,0:T(8,128)(2,1)S(1)} collective-permute-done((bf16[2,64,2048]{2,1,0:T(8,128)(2,1)S(1)}, bf16[2,64,2048]{2,1,0:T(8,128)(2,1)S(1)}, u32[]{:S(2)}, u32[]{:S(2)}) %collective-permute-start.8) | collective-permute-done | bytes 524320 | tf_op jit(solution)/shard_map/ppermute | solution.py:438
  38.4 3.1 %shard_map.40 = bf16[2096,128]{1,0:T(8,128)(2,1)S(1)} custom-call(bf16[2,2,128,2048]{3,2,1,0:T(8,128)(2,1)S(1)} %bitcast.5, bf16[2,2,64,2048]{3,2,1,0:T(8,128)(2,1)S(1)} %collective-permute-done.5.top_ref, bf16[2,2,64,2048]{3,2,1,0:T(8,128)(2,1)S(1)} %collective-permute-done.4.bottom_ref, ...), custom_call_target="tpu_custom_call" | custom-call | flops 1 | bytes 1 | tf_op jit(solution)/shard_map/pallas_call | solution.py:231
  41.4 1.6 %collective-permute-start.10 = (bf16[2096,128]{1,0:T(8,128)(2,1)S(1)}, bf16[2096,128]{1,0:T(8,128)(2,1)S(1)}, u32[]{:S(2)}, u32[]{:S(2)}) collective-permute-start(bf16[2096,128]{1,0:T(8,128)(2,1)S(1)} %shard_map.40), channel_id=1, source_target_pairs={{0,1},{1,0},{2,3},{3,2},{4,5},{5,4},{6,7},{7,6},{8,9},{9,8},{10,11... | collective-permute-start | bytes 1609736 | tf_op jit(solution)/shard_map/ppermute | solution.py:442
  43.0 3.0 %shard_map.41 = (f32[128,2048]{1,0:T(8,128)S(1)}, f32[128,128]{1,0:T(8,128)S(1)}, f32[128,128]{1,0:T(8,128)S(1)}, f32[128,2048]{1,0:T(8,128)S(1)}) custom-call(bf16[2,2,128,2048]{3,2,1,0:T(8,128)(2,1)S(1)} %bitcast.6, bf16[2,2,64,2048]{3,2,1,0:T(8,128)(2,1)S(1)} %collective-permute-done.5.top_ref, ...), custom_call_target="tpu_custom_call" | custom-call | flops 1 | bytes 1 | tf_op jit(solution)/shard_map/pallas_call | solution.py:231
  46.1 3.4 %collective-permute-done.3.refs_2_ = bf16[2,64,2176]{2,1,0:T(8,128)(2,1)S(1)} collective-permute-done((bf16[2,64,2176]{2,1,0:T(8,128)(2,1)S(1)}, bf16[2,64,2176]{2,1,0:T(8,128)(2,1)S(1)}, u32[]{:S(2)}, u32[]{:S(2)}) %collective-permute-start.3) | collective-permute-done | bytes 557088 | tf_op jit(solution)/shard_map/ppermute | solution.py:435
  49.5 3.1 %shard_map.42 = bf16[2096,128]{1,0:T(8,128)(2,1)S(1)} custom-call(bf16[2,2,128,2048]{3,2,1,0:T(8,128)(2,1)S(1)} %bitcast.7, bf16[2,2,64,2048]{3,2,1,0:T(8,128)(2,1)S(1)} %collective-permute-done.5.top_ref, bf16[2,2,64,2048]{3,2,1,0:T(8,128)(2,1)S(1)} %collective-permute-done.4.bottom_ref, bf16[2,128,2048]{2,1,0:T(8,128)(2,1)S(1)} %collective-permute-done.1.frame_ref.refs_0_, ...), custom_call_target="tpu_custom_call" | custom-call | flops 1 | bytes 1 | tf_op jit(solution)/shard_map/pallas_call | solution.py:231
  52.6 1.6 %collective-permute-start.15 = (bf16[2096,128]{1,0:T(8,128)(2,1)S(1)}, bf16[2096,128]{1,0:T(8,128)(2,1)S(1)}, u32[]{:S(2)}, u32[]{:S(2)}) collective-permute-start(bf16[2096,128]{1,0:T(8,128)(2,1)S(1)} %shard_map.42), channel_id=1, source_target_pairs={{0,1},{1,0},{2,3},{3,2},{4,5},{5,4},{6,7},{7,6},{8,9},{9,8},{10,11... | collective-permute-start | bytes 1609736 | tf_op jit(solution)/shard_map/ppermute | solution.py:449
  54.9 3.1 %shard_map.43 = (f32[128,2048]{1,0:T(8,128)S(1)}, f32[128,128]{1,0:T(8,128)S(1)}, f32[128,128]{1,0:T(8,128)S(1)}, f32[128,2048]{1,0:T(8,128)S(1)}) custom-call(bf16[2,2,128,2048]{3,2,1,0:T(8,128)(2,1)S(1)} %bitcast.8, bf16[2,2,64,2048]{3,2,1,0:T(8,128)(2,1)S(1)} %collective-permute-done.5.top_ref, ...), custom_call_target="tpu_custom_call" | custom-call | flops 30064771072 | bytes 1 | tf_op jit(solution)/shard_map/pallas_call | solution.py:231
  58.7 1.4 %collective-permute-done.11.refs_2_ = bf16[2,64,2048]{2,1,0:T(8,128)(2,1)S(1)} collective-permute-done((bf16[2,64,2048]{2,1,0:T(8,128)(2,1)S(1)}, bf16[2,64,2048]{2,1,0:T(8,128)(2,1)S(1)}, u32[]{:S(2)}, u32[]{:S(2)}) %collective-permute-start.11) | collective-permute-done | bytes 524320 | tf_op jit(solution)/shard_map/ppermute | solution.py:456
  60.1 0.7 %collective-permute-done.12.refs_3_ = bf16[2,64,2048]{2,1,0:T(8,128)(2,1)S(1)} collective-permute-done((bf16[2,64,2048]{2,1,0:T(8,128)(2,1)S(1)}, bf16[2,64,2048]{2,1,0:T(8,128)(2,1)S(1)}, u32[]{:S(2)}, u32[]{:S(2)}) %collective-permute-start.12) | collective-permute-done | bytes 524320 | tf_op jit(solution)/shard_map/ppermute | solution.py:456
  60.8 5.2 %shard_map.46 = (f32[2,128,2048]{2,1,0:T(8,128)S(1)}, f32[2,128,128]{2,1,0:T(8,128)S(1)}, f32[2,128,128]{2,1,0:T(8,128)S(1)}) custom-call(s32[2,2,1,2]{3,2,1,0:T(1,128)S(1)} %copy-done.3, bf16[2,128,2048]{2,1,0:T(8,128)(2,1)S(1)} %bitcast.12, bf16[2,2,128,2048]{3,2,1,0:T(8,128)(2,1)S(1)} %collective-permute-done.refs_0_.core_ref, ...), custom_call_target="tpu_custom_call" | custom-call | flops 1 | bytes 1 | tf_op jit(solution)/shard_map/pallas_call | solution.py:318
  66.0 0.6 shard_map.47.refs_4_
  66.6 0.6 collective-permute-done.15.refs_3_
  67.2 1.3 %shard_map.48 = bf16[2,128,2048]{2,1,0:T(8,128)(2,1)} custom-call(f32[2,128,2048]{2,1,0:T(8,128)S(1)} %get-tuple-element.71.refs_0_, f32[2,128,128]{2,1,0:T(8,128)S(1)} %get-tuple-element.72.refs_1_, f32[2,128,128]{2,1,0:T(8,128)S(1)} %get-tuple-element.73.refs_2_, bf16[2096,128]{1,0:T(8,128)(2,1)S(1)} %collective-permute-done.15.refs_3_, ...), custom_call_target="tpu_custom_call" | custom-call | flops 1 | bytes 1 | tf_op jit(solution)/shard_map/pallas_call | solution.py:395
  (28 shorter events, 3.0 us)
Async XLA Ops:
  0.0 11.0 %collective-permute-start = (bf16[2,2,128,2048]{3,2,1,0:T(8,128)(2,1)}, bf16[2,2,128,2048]{3,2,1,0:T(8,128)(2,1)S(1)}, u32[]{:S(2)}, u32[]{:S(2)}) collective-permute-start(bf16[2,2,128,2048]{3,2,1,0:T(8,128)(2,1)} %bitcast.3), channel_id=1, source_target_pairs={{0,8},{8,0},{16,24},{24,16},{1,9},{9,1},{17,25},{25,17},{2,10},{10... | collective-permute-start | bytes 6291464 | tf_op jit(solution)/shard_map/ppermute | solution.py:426
  0.5 1.6 %copy-start = (bf16[2,2,16,8,2048]{4,3,2,1,0:T(8,128)(2,1)S(1)}, bf16[2,2,16,8,2048]{4,3,2,1,0:T(8,128)(2,1)}, u32[]{:S(2)}) copy-start(bf16[2,2,16,8,2048]{4,3,2,1,0:T(8,128)(2,1)} %param.4) | copy-start | bytes 6291460
  2.0 8.9 %copy-start.2 = (bf16[2,16,8,2048]{3,2,1,0:T(8,128)(2,1)S(1)}, bf16[2,16,8,2048]{3,2,1,0:T(8,128)(2,1)}, u32[]{:S(2)}) copy-start(bf16[2,16,8,2048]{3,2,1,0:T(8,128)(2,1)} %param.3) | copy-start | bytes 3145732
  2.4 36.0 %copy-start.1 = (bf16[2,2,16,8,2048]{4,3,2,1,0:T(8,128)(2,1)S(1)}, bf16[2,2,16,8,2048]{4,3,2,1,0:T(8,128)(2,1)}, u32[]{:S(2)}) copy-start(bf16[2,2,16,8,2048]{4,3,2,1,0:T(8,128)(2,1)} %param.4) | copy-start | bytes 6291460
  2.4 26.2 %collective-permute-start.1 = (bf16[2,128,2048]{2,1,0:T(8,128)(2,1)S(1)}, bf16[2,128,2048]{2,1,0:T(8,128)(2,1)S(1)}, u32[]{:S(2)}, u32[]{:S(2)}) collective-permute-start(bf16[2,128,2048]{2,1,0:T(8,128)(2,1)S(1)} %get-tuple-element.41), channel_id=1, source_target_pairs={{0,24},{8,16},{16,8},{24,0},{1,25},{9,17},{17,9},{25,1},{2,26},{10... | collective-permute-start | bytes 3145736 | tf_op jit(solution)/shard_map/ppermute | solution.py:428
  5.1 27.2 %collective-permute-start.4 = (bf16[2,2,64,2048]{3,2,1,0:T(8,128)(2,1)S(1)}, bf16[2,2,64,2048]{3,2,1,0:T(8,128)(2,1)S(1)}, u32[]{:S(2)}, u32[]{:S(2)}) collective-permute-start(bf16[2,2,64,2048]{3,2,1,0:T(8,128)(2,1)S(1)} %get-tuple-element.44), channel_id=1, source_target_pairs={{2,0},{4,2},{6,4},{3,1},{5,3},{7,5},{10,8},{12,10},{14,12},{11,9},... | collective-permute-start | bytes 3145736 | tf_op jit(solution)/shard_map/ppermute | solution.py:429
  6.3 27.2 %collective-permute-start.5 = (bf16[2,2,64,2048]{3,2,1,0:T(8,128)(2,1)S(1)}, bf16[2,2,64,2048]{3,2,1,0:T(8,128)(2,1)S(1)}, u32[]{:S(2)}, u32[]{:S(2)}) collective-permute-start(bf16[2,2,64,2048]{3,2,1,0:T(8,128)(2,1)S(1)} %get-tuple-element.45), channel_id=1, source_target_pairs={{0,2},{2,4},{4,6},{1,3},{3,5},{5,7},{8,10},{10,12},{12,14},{9,11},... | collective-permute-start | bytes 3145736 | tf_op jit(solution)/shard_map/ppermute | solution.py:430
  11.0 24.6 %collective-permute-start.6 = (bf16[2,128,2048]{2,1,0:T(8,128)(2,1)S(1)}, bf16[2,128,2048]{2,1,0:T(8,128)(2,1)S(1)}, u32[]{:S(2)}, u32[]{:S(2)}) collective-permute-start(bf16[2,128,2048]{2,1,0:T(8,128)(2,1)S(1)} %bitcast.9), channel_id=1, source_target_pairs={{0,1},{1,0},{2,3},{3,2},{4,5},{5,4},{6,7},{7,6},{8,9},{9,8},{10,11... | collective-permute-start | bytes 3145736 | tf_op jit(solution)/shard_map/ppermute | solution.py:432
  12.6 41.6 %collective-permute-start.9 = (bf16[2,128,2048]{2,1,0:T(8,128)(2,1)S(1)}, bf16[2,128,2048]{2,1,0:T(8,128)(2,1)S(1)}, u32[]{:S(2)}, u32[]{:S(2)}) collective-permute-start(bf16[2,128,2048]{2,1,0:T(8,128)(2,1)S(1)} %get-tuple-element.55), channel_id=1, source_target_pairs={{0,24},{8,16},{16,8},{24,0},{1,25},{9,17},{17,9},{25,1},{2,26},{10... | collective-permute-start | bytes 3145736 | tf_op jit(solution)/shard_map/ppermute | solution.py:436
  28.7 17.3 %collective-permute-start.2 = (bf16[2,64,2176]{2,1,0:T(8,128)(2,1)S(1)}, bf16[2,64,2176]{2,1,0:T(8,128)(2,1)S(1)}, u32[]{:S(2)}, u32[]{:S(2)}) collective-permute-start(bf16[2,64,2176]{2,1,0:T(8,128)(2,1)S(1)} %get-tuple-element.42), channel_id=1, source_target_pairs={{0,2},{2,4},{4,6},{1,3},{3,5},{5,7},{8,10},{10,12},{12,14},{9,11},... | collective-permute-start | bytes 1671176 | tf_op jit(solution)/shard_map/ppermute | solution.py:434
  32.2 17.3 %collective-permute-start.3 = (bf16[2,64,2176]{2,1,0:T(8,128)(2,1)S(1)}, bf16[2,64,2176]{2,1,0:T(8,128)(2,1)S(1)}, u32[]{:S(2)}, u32[]{:S(2)}) collective-permute-start(bf16[2,64,2176]{2,1,0:T(8,128)(2,1)S(1)} %get-tuple-element.43), channel_id=1, source_target_pairs={{2,0},{4,2},{6,4},{3,1},{5,3},{7,5},{10,8},{12,10},{14,12},{11,9},... | collective-permute-start | bytes 1671176 | tf_op jit(solution)/shard_map/ppermute | solution.py:435
  35.7 2.0 %collective-permute-start.7 = (bf16[2,64,2048]{2,1,0:T(8,128)(2,1)S(1)}, bf16[2,64,2048]{2,1,0:T(8,128)(2,1)S(1)}, u32[]{:S(2)}, u32[]{:S(2)}) collective-permute-start(bf16[2,64,2048]{2,1,0:T(8,128)(2,1)S(1)} %get-tuple-element.49), channel_id=1, source_target_pairs={{0,8},{8,0},{16,24},{24,16},{1,9},{9,1},{17,25},{25,17},{2,10},{10... | collective-permute-start | bytes 1572872 | tf_op jit(solution)/shard_map/ppermute | solution.py:438
  35.7 2.6 %collective-permute-start.8 = (bf16[2,64,2048]{2,1,0:T(8,128)(2,1)S(1)}, bf16[2,64,2048]{2,1,0:T(8,128)(2,1)S(1)}, u32[]{:S(2)}, u32[]{:S(2)}) collective-permute-start(bf16[2,64,2048]{2,1,0:T(8,128)(2,1)S(1)} %get-tuple-element.50), channel_id=1, source_target_pairs={{0,8},{8,0},{16,24},{24,16},{1,9},{9,1},{17,25},{25,17},{2,10},{10... | collective-permute-start | bytes 1572872 | tf_op jit(solution)/shard_map/ppermute | solution.py:438
  41.4 16.5 %collective-permute-start.10 = (bf16[2096,128]{1,0:T(8,128)(2,1)S(1)}, bf16[2096,128]{1,0:T(8,128)(2,1)S(1)}, u32[]{:S(2)}, u32[]{:S(2)}) collective-permute-start(bf16[2096,128]{1,0:T(8,128)(2,1)S(1)} %shard_map.40), channel_id=1, source_target_pairs={{0,1},{1,0},{2,3},{3,2},{4,5},{5,4},{6,7},{7,6},{8,9},{9,8},{10,11... | collective-permute-start | bytes 1609736 | tf_op jit(solution)/shard_map/ppermute | solution.py:442
  52.6 14.6 %collective-permute-start.15 = (bf16[2096,128]{1,0:T(8,128)(2,1)S(1)}, bf16[2096,128]{1,0:T(8,128)(2,1)S(1)}, u32[]{:S(2)}, u32[]{:S(2)}) collective-permute-start(bf16[2096,128]{1,0:T(8,128)(2,1)S(1)} %shard_map.42), channel_id=1, source_target_pairs={{0,1},{1,0},{2,3},{3,2},{4,5},{5,4},{6,7},{7,6},{8,9},{9,8},{10,11... | collective-permute-start | bytes 1609736 | tf_op jit(solution)/shard_map/ppermute | solution.py:449
  54.3 4.4 %collective-permute-start.13 = (bf16[2,64,2176]{2,1,0:T(8,128)(2,1)S(1)}, bf16[2,64,2176]{2,1,0:T(8,128)(2,1)S(1)}, u32[]{:S(2)}, u32[]{:S(2)}) collective-permute-start(bf16[2,64,2176]{2,1,0:T(8,128)(2,1)S(1)} %get-tuple-element.63), channel_id=1, source_target_pairs={{0,8},{8,0},{16,24},{24,16},{1,9},{9,1},{17,25},{25,17},{2,10},{10... | collective-permute-start | bytes 1671176 | tf_op jit(solution)/shard_map/ppermute | solution.py:453
  54.4 6.5 %copy-start.3 = (s32[2,2,1,2]{3,2,1,0:T(1,128)S(1)}, s32[2,2,1,2]{3,2,1,0:T(1,128)}, u32[]{:S(2)}) copy-start(s32[2,2,1,2]{3,2,1,0:T(1,128)} %far_ref.1) | copy-start | bytes 100
  54.4 4.3 %collective-permute-start.14 = (bf16[2,64,2176]{2,1,0:T(8,128)(2,1)S(1)}, bf16[2,64,2176]{2,1,0:T(8,128)(2,1)S(1)}, u32[]{:S(2)}, u32[]{:S(2)}) collective-permute-start(bf16[2,64,2176]{2,1,0:T(8,128)(2,1)S(1)} %get-tuple-element.64), channel_id=1, source_target_pairs={{0,8},{8,0},{16,24},{24,16},{1,9},{9,1},{17,25},{25,17},{2,10},{10... | collective-permute-start | bytes 1671176 | tf_op jit(solution)/shard_map/ppermute | solution.py:453
  58.1 2.0 %collective-permute-start.11 = (bf16[2,64,2048]{2,1,0:T(8,128)(2,1)S(1)}, bf16[2,64,2048]{2,1,0:T(8,128)(2,1)S(1)}, u32[]{:S(2)}, u32[]{:S(2)}) collective-permute-start(bf16[2,64,2048]{2,1,0:T(8,128)(2,1)S(1)} %get-tuple-element.61), channel_id=1, source_target_pairs={{0,8},{8,0},{16,24},{24,16},{1,9},{9,1},{17,25},{25,17},{2,10},{10... | collective-permute-start | bytes 1572872 | tf_op jit(solution)/shard_map/ppermute | solution.py:456
  58.3 2.6 %collective-permute-start.12 = (bf16[2,64,2048]{2,1,0:T(8,128)(2,1)S(1)}, bf16[2,64,2048]{2,1,0:T(8,128)(2,1)S(1)}, u32[]{:S(2)}, u32[]{:S(2)}) collective-permute-start(bf16[2,64,2048]{2,1,0:T(8,128)(2,1)S(1)} %get-tuple-element.62), channel_id=1, source_target_pairs={{0,8},{8,0},{16,24},{24,16},{1,9},{9,1},{17,25},{25,17},{2,10},{10... | collective-permute-start | bytes 1572872 | tf_op jit(solution)/shard_map/ppermute | solution.py:456

commit v15 on v14

--- a/solution.py
+++ b/solution.py
@@ -103,19 +103,13 @@
     return copying_call(cut_kernel, shapes, 4, keyvals)
 
 
-def by_rows_kernel(*refs):
-    frame_refs, out_refs, sems = refs[: len(refs) // 3], refs[len(refs) // 3 : -1], refs[-1]
-    pairs = []
-    for i, frame_ref in enumerate(frame_refs):
-        for rows, out_ref in zip((FIRST, LAST), out_refs[2 * i : 2 * i + 2]):
-            pairs.append((frame_ref.at[:, rows], out_ref))
-    run_copies(pairs, sems)
-
-
-def by_rows(*frames):
-    two, _, features = frames[0].shape
-    shapes = [(two, SPOT, features)] * (2 * len(frames))
-    return copying_call(by_rows_kernel, shapes, 2 * len(frames), *frames)
+def first_rows_kernel(frame_ref, out_ref, sems):
+    run_copies([(frame_ref.at[:, FIRST], out_ref)], sems)
+
+
+def first_rows_of(frame):
+    two, _, features = frame.shape
+    return copying_call(first_rows_kernel, [(two, SPOT, features)], 1, frame)[0]
 
 
 def widened_rows_kernel(frame_ref, last_ref, first_ref, sems):
@@ -434,8 +428,11 @@
     cross_top = lax.ppermute(cross_last, "ha", up)
     cross_bottom = lax.ppermute(cross_first, "ha", down)
     last = lax.ppermute(inner, "ta", cross_pairs)
-    bottom, top, visitors = tie((bottom, top, visitors))
-    core_bottom, core_top = [lax.ppermute(value, "ta", core_pairs) for value in inner_rows(bottom, top)]
+    bottom, top = tie((bottom, top))
+    inner_bottom, inner_top = inner_rows(bottom, top)
+    core_bottom = lax.ppermute(inner_bottom, "ta", core_pairs)
+    inner_top, visitors = tie((inner_top, visitors))
+    core_top = lax.ppermute(inner_top, "ta", core_pairs)
 
     early_third = (core, core_top, core_bottom)
     early = near_attention(True, ha_size, keyvals, top, bottom, early_third, visitors, [], 1)
@@ -451,10 +448,11 @@
     late_third = (cross, cross_top, cross_bottom)
     late_home = near_attention(False, ha_size, keyvals, top, bottom, late_third, [], [queries], LATE_COST)
     inner_corner = [lax.ppermute(value, "ta", core_pairs) for value in reversed(widened_rows(last))]
+    cross_last, _ = tie((cross_last, late[0]))
+    corner_last = lax.ppermute(cross_last, "ta", core_pairs)
     sent, early_parts, _ = tie((cross, early_parts, late_home[1]))
-    cross_rows = by_rows(sent)
-    corner = [lax.ppermute(value, "ta", core_pairs) for value in cross_rows]
-    buffers = (core, cross, last, *corner, *inner_corner)
+    corner_first = lax.ppermute(first_rows_of(sent), "ta", core_pairs)
+    buffers = (core, cross, last, corner_first, corner_last, *inner_corner)
     own = far_attention(ta_size, far_frames, queries, buffers, (*early_home, *late_home))
     out = finish(wa_size, own, early_parts, None, FINISH_COST)
     out = finish(wa_size, own, late_parts, out, 1)

time: 68.9 us -> 68.9 us (level)
    ppermute x1, waiting for transfers between devices: 3.41 us -> 0.03 us  [per_device(): cross_bottom = lax.ppermute(cross_first, 'ha', down)]
    ppermute x2, waiting for transfers between devices: 0.59 us -> 3.33 us  [per_device(): lax.ppermute(result, 'wa', back)]
    ppermute x4 -> x2, waiting for transfers between devices: 2.15 us -> 0.01 us  [per_device(): lax.ppermute(value, 'ta', core_pairs)]
    ppermute x1, waiting for transfers between devices: 2.01 us -> 0.01 us  [per_device(): visitors = [lax.ppermute(sent, 'wa', there) for there, _ in ways]]
    ppermute x1, waiting for transfers between devices: 0.01 us -> 1.98 us  [per_device(): bottom = lax.ppermute(first_rows, 'ha', down)]
    ppermute x2 -> x4, waiting for transfers between devices: 2.14 us -> 4.01 us  [the longest x1 1.87 us: per_device(): corner_first = lax.ppermute(first_rows_of(sent), 'ta', core_pairs)]
    ppermute x1, waiting for transfers between devices: 0.01 us -> 1.19 us  [per_device(): cross_top = lax.ppermute(cross_last, 'ha', up)]
where the time goes in v15:
time: 68.9 us; the launch traced here: 68.7 us
  waiting for transfers between devices  26.6 us (39%)
  Pallas kernels  20.2 us (29%)
  starting transfers between devices  20 us (29%)
  local copies, waits for them, and re-layouts  1.6 us (2%)
    ppermute x1, waiting for transfers between devices, per_device(): cross = lax.ppermute(outer, 'ta', cross_pairs)  16 us
    pallas_call x4, Pallas kernels, near_attention(): pl.pallas_call(functools.partial(near_kernel, len(visitors), len(queries)...  12.3 us
    pallas_call x1, Pallas kernels, far_attention(): pl.pallas_call(functools.partial(far_kernel, members), out_shape=[jax.Sha...  5.18 us
    ppermute x1, starting transfers between devices, per_device(): top = lax.ppermute(last_rows, 'ha', up)  4.61 us
    ppermute x1, starting transfers between devices, per_device(): cross_top = lax.ppermute(cross_last, 'ha', up)  3.5 us
    ppermute x2, waiting for transfers between devices, per_device(): lax.ppermute(result, 'wa', back)  3.33 us
    ppermute x2, starting transfers between devices, per_device(): lax.ppermute(result, 'wa', back)  3.26 us
    ppermute x1, starting transfers between devices, per_device(): cross = lax.ppermute(outer, 'ta', cross_pairs)  2.67 us
  transfers between devices with their start and end apart: 16, of which 8 were waited for; matrix products, arithmetic and copies ran while one was open for 0% of the time, Pallas kernels for 27%

profile of v15, /device:TPU:0, one launch (start us, length us, event | category | flops | bytes accessed | tf_op | source)
XLA Modules:
  0.0 68.7 jit_solution(6289388943467402851)
XLA Ops:
  0.5 1.6 %copy-done = bf16[2,2,16,8,2048]{4,3,2,1,0:T(8,128)(2,1)S(1)} copy-done((bf16[2,2,16,8,2048]{4,3,2,1,0:T(8,128)(2,1)S(1)}, bf16[2,2,16,8,2048]{4,3,2,1,0:T(8,128)(2,1)}, u32[]{:S(2)}) %copy-start) | copy-done | bytes 2097176
  2.4 2.7 %collective-permute-start.1 = (bf16[2,128,2048]{2,1,0:T(8,128)(2,1)S(1)}, bf16[2,128,2048]{2,1,0:T(8,128)(2,1)S(1)}, u32[]{:S(2)}, u32[]{:S(2)}) collective-permute-start(bf16[2,128,2048]{2,1,0:T(8,128)(2,1)S(1)} %get-tuple-element.41), channel_id=1, source_target_pairs={{0,24},{8,16},{16,8},{24,0},{1,25},{9,17},{17,9},{25,1},{2,26},{10... | collective-permute-start | bytes 3145736 | tf_op jit(solution)/shard_map/ppermute | solution.py:422
  5.1 1.3 %collective-permute-start.4 = (bf16[2,2,64,2048]{3,2,1,0:T(8,128)(2,1)S(1)}, bf16[2,2,64,2048]{3,2,1,0:T(8,128)(2,1)S(1)}, u32[]{:S(2)}, u32[]{:S(2)}) collective-permute-start(bf16[2,2,64,2048]{3,2,1,0:T(8,128)(2,1)S(1)} %get-tuple-element.44), channel_id=1, source_target_pairs={{2,0},{4,2},{6,4},{3,1},{5,3},{7,5},{10,8},{12,10},{14,12},{11,9},... | collective-permute-start | bytes 3145736 | tf_op jit(solution)/shard_map/ppermute | solution.py:423
  6.3 4.6 %collective-permute-start.5 = (bf16[2,2,64,2048]{3,2,1,0:T(8,128)(2,1)S(1)}, bf16[2,2,64,2048]{3,2,1,0:T(8,128)(2,1)S(1)}, u32[]{:S(2)}, u32[]{:S(2)}) collective-permute-start(bf16[2,2,64,2048]{3,2,1,0:T(8,128)(2,1)S(1)} %get-tuple-element.45), channel_id=1, source_target_pairs={{0,2},{2,4},{4,6},{1,3},{3,5},{5,7},{8,10},{10,12},{12,14},{9,11},... | collective-permute-start | bytes 3145736 | tf_op jit(solution)/shard_map/ppermute | solution.py:424
  11.0 1.6 %collective-permute-start.6 = (bf16[2,128,2048]{2,1,0:T(8,128)(2,1)S(1)}, bf16[2,128,2048]{2,1,0:T(8,128)(2,1)S(1)}, u32[]{:S(2)}, u32[]{:S(2)}) collective-permute-start(bf16[2,128,2048]{2,1,0:T(8,128)(2,1)S(1)} %bitcast.9), channel_id=1, source_target_pairs={{0,1},{1,0},{2,3},{3,2},{4,5},{5,4},{6,7},{7,6},{8,9},{9,8},{10,11... | collective-permute-start | bytes 3145736 | tf_op jit(solution)/shard_map/ppermute | solution.py:426
  12.6 16.0 %collective-permute-done.1.frame_ref.refs_0_ = bf16[2,128,2048]{2,1,0:T(8,128)(2,1)S(1)} collective-permute-done((bf16[2,128,2048]{2,1,0:T(8,128)(2,1)S(1)}, bf16[2,128,2048]{2,1,0:T(8,128)(2,1)S(1)}, u32[]{:S(2)}, u32[]{:S(2)}) %collective-permute-start.1) | collective-permute-done | bytes 1048608 | tf_op jit(solution)/shard_map/ppermute | solution.py:422
  28.7 1.3 %collective-permute-start.3 = (bf16[2,64,2176]{2,1,0:T(8,128)(2,1)S(1)}, bf16[2,64,2176]{2,1,0:T(8,128)(2,1)S(1)}, u32[]{:S(2)}, u32[]{:S(2)}) collective-permute-start(bf16[2,64,2176]{2,1,0:T(8,128)(2,1)S(1)} %get-tuple-element.43), channel_id=1, source_target_pairs={{2,0},{4,2},{6,4},{3,1},{5,3},{7,5},{10,8},{12,10},{14,12},{11,9},... | collective-permute-start | bytes 1671176 | tf_op jit(solution)/shard_map/ppermute | solution.py:429
  30.0 2.0 %collective-permute-done.4.bottom_ref = bf16[2,2,64,2048]{3,2,1,0:T(8,128)(2,1)S(1)} collective-permute-done((bf16[2,2,64,2048]{3,2,1,0:T(8,128)(2,1)S(1)}, bf16[2,2,64,2048]{3,2,1,0:T(8,128)(2,1)S(1)}, u32[]{:S(2)}, u32[]{:S(2)}) %collective-permute-start.4) | collective-permute-done | bytes 1048608 | tf_op jit(solution)/shard_map/ppermute | solution.py:423
  32.0 3.5 %collective-permute-start.2 = (bf16[2,64,2176]{2,1,0:T(8,128)(2,1)S(1)}, bf16[2,64,2176]{2,1,0:T(8,128)(2,1)S(1)}, u32[]{:S(2)}, u32[]{:S(2)}) collective-permute-start(bf16[2,64,2176]{2,1,0:T(8,128)(2,1)S(1)} %get-tuple-element.62), channel_id=1, source_target_pairs={{0,2},{2,4},{4,6},{1,3},{3,5},{5,7},{8,10},{10,12},{12,14},{9,11},... | collective-permute-start | bytes 1671176 | tf_op jit(solution)/shard_map/ppermute | solution.py:428
  36.2 1.4 %collective-permute-done.8.refs_2_ = bf16[2,64,2048]{2,1,0:T(8,128)(2,1)S(1)} collective-permute-done((bf16[2,64,2048]{2,1,0:T(8,128)(2,1)S(1)}, bf16[2,64,2048]{2,1,0:T(8,128)(2,1)S(1)}, u32[]{:S(2)}, u32[]{:S(2)}) %collective-permute-start.8) | collective-permute-done | bytes 524320 | tf_op jit(solution)/shard_map/ppermute | solution.py:433
  37.6 0.7 %collective-permute-done.7.refs_1_ = bf16[2,64,2048]{2,1,0:T(8,128)(2,1)S(1)} collective-permute-done((bf16[2,64,2048]{2,1,0:T(8,128)(2,1)S(1)}, bf16[2,64,2048]{2,1,0:T(8,128)(2,1)S(1)}, u32[]{:S(2)}, u32[]{:S(2)}) %collective-permute-start.7) | collective-permute-done | bytes 524320 | tf_op jit(solution)/shard_map/ppermute | solution.py:435
  38.4 3.1 %shard_map.40 = bf16[2096,128]{1,0:T(8,128)(2,1)S(1)} custom-call(bf16[2,2,128,2048]{3,2,1,0:T(8,128)(2,1)S(1)} %bitcast.5, bf16[2,2,64,2048]{3,2,1,0:T(8,128)(2,1)S(1)} %collective-permute-done.5.top_ref, bf16[2,2,64,2048]{3,2,1,0:T(8,128)(2,1)S(1)} %collective-permute-done.4.bottom_ref, ...), custom_call_target="tpu_custom_call" | custom-call | flops 1 | bytes 1 | tf_op jit(solution)/shard_map/pallas_call | solution.py:225
  41.4 1.6 %collective-permute-start.10 = (bf16[2096,128]{1,0:T(8,128)(2,1)S(1)}, bf16[2096,128]{1,0:T(8,128)(2,1)S(1)}, u32[]{:S(2)}, u32[]{:S(2)}) collective-permute-start(bf16[2096,128]{1,0:T(8,128)(2,1)S(1)} %shard_map.40), channel_id=1, source_target_pairs={{0,1},{1,0},{2,3},{3,2},{4,5},{5,4},{6,7},{7,6},{8,9},{9,8},{10,11... | collective-permute-start | bytes 1609736 | tf_op jit(solution)/shard_map/ppermute | solution.py:439
  43.0 3.0 %shard_map.41 = (f32[128,2048]{1,0:T(8,128)S(1)}, f32[128,128]{1,0:T(8,128)S(1)}, f32[128,128]{1,0:T(8,128)S(1)}, f32[128,2048]{1,0:T(8,128)S(1)}) custom-call(bf16[2,2,128,2048]{3,2,1,0:T(8,128)(2,1)S(1)} %bitcast.6, bf16[2,2,64,2048]{3,2,1,0:T(8,128)(2,1)S(1)} %collective-permute-done.5.top_ref, ...), custom_call_target="tpu_custom_call" | custom-call | flops 1 | bytes 1 | tf_op jit(solution)/shard_map/pallas_call | solution.py:225
  46.1 1.2 %collective-permute-done.2.refs_1_ = bf16[2,64,2176]{2,1,0:T(8,128)(2,1)S(1)} collective-permute-done((bf16[2,64,2176]{2,1,0:T(8,128)(2,1)S(1)}, bf16[2,64,2176]{2,1,0:T(8,128)(2,1)S(1)}, u32[]{:S(2)}, u32[]{:S(2)}) %collective-permute-start.2) | collective-permute-done | bytes 557088 | tf_op jit(solution)/shard_map/ppermute | solution.py:428
  47.3 3.1 %shard_map.42 = bf16[2096,128]{1,0:T(8,128)(2,1)S(1)} custom-call(bf16[2,2,128,2048]{3,2,1,0:T(8,128)(2,1)S(1)} %bitcast.7, bf16[2,2,64,2048]{3,2,1,0:T(8,128)(2,1)S(1)} %collective-permute-done.5.top_ref, bf16[2,2,64,2048]{3,2,1,0:T(8,128)(2,1)S(1)} %collective-permute-done.4.bottom_ref, bf16[2,128,2048]{2,1,0:T(8,128)(2,1)S(1)} %collective-permute-done.1.frame_ref.refs_0_, ...), custom_call_target="tpu_custom_call" | custom-call | flops 1 | bytes 1 | tf_op jit(solution)/shard_map/pallas_call | solution.py:225
  50.4 1.7 %collective-permute-start.15 = (bf16[2096,128]{1,0:T(8,128)(2,1)S(1)}, bf16[2096,128]{1,0:T(8,128)(2,1)S(1)}, u32[]{:S(2)}, u32[]{:S(2)}) collective-permute-start(bf16[2096,128]{1,0:T(8,128)(2,1)S(1)} %shard_map.42), channel_id=1, source_target_pairs={{0,1},{1,0},{2,3},{3,2},{4,5},{5,4},{6,7},{7,6},{8,9},{9,8},{10,11... | collective-permute-start | bytes 1609736 | tf_op jit(solution)/shard_map/ppermute | solution.py:446
  52.2 0.6 collective-permute-start.13
  52.9 3.1 %shard_map.43 = (f32[128,2048]{1,0:T(8,128)S(1)}, f32[128,128]{1,0:T(8,128)S(1)}, f32[128,128]{1,0:T(8,128)S(1)}, f32[128,2048]{1,0:T(8,128)S(1)}) custom-call(bf16[2,2,128,2048]{3,2,1,0:T(8,128)(2,1)S(1)} %bitcast.8, bf16[2,2,64,2048]{3,2,1,0:T(8,128)(2,1)S(1)} %collective-permute-done.5.top_ref, ...), custom_call_target="tpu_custom_call" | custom-call | flops 30064771072 | bytes 1 | tf_op jit(solution)/shard_map/pallas_call | solution.py:225
  56.7 1.9 %collective-permute-done.11.refs_2_ = bf16[2,64,2048]{2,1,0:T(8,128)(2,1)S(1)} collective-permute-done((bf16[2,64,2048]{2,1,0:T(8,128)(2,1)S(1)}, bf16[2,64,2048]{2,1,0:T(8,128)(2,1)S(1)}, u32[]{:S(2)}, u32[]{:S(2)}) %collective-permute-start.11) | collective-permute-done | bytes 524320 | tf_op jit(solution)/shard_map/ppermute | solution.py:454
  58.5 5.2 %shard_map.46 = (f32[2,128,2048]{2,1,0:T(8,128)S(1)}, f32[2,128,128]{2,1,0:T(8,128)S(1)}, f32[2,128,128]{2,1,0:T(8,128)S(1)}) custom-call(s32[2,2,1,2]{3,2,1,0:T(1,128)S(1)} %copy-done.3, bf16[2,128,2048]{2,1,0:T(8,128)(2,1)S(1)} %bitcast.12, bf16[2,2,128,2048]{3,2,1,0:T(8,128)(2,1)S(1)} %collective-permute-done.refs_0_.core_ref, ...), custom_call_target="tpu_custom_call" | custom-call | flops 1 | bytes 1 | tf_op jit(solution)/shard_map/pallas_call | solution.py:312
  63.7 0.6 shard_map.47.refs_4_
  64.4 2.8 %collective-permute-done.15.refs_3_ = bf16[2096,128]{1,0:T(8,128)(2,1)S(1)} collective-permute-done((bf16[2096,128]{1,0:T(8,128)(2,1)S(1)}, bf16[2096,128]{1,0:T(8,128)(2,1)S(1)}, u32[]{:S(2)}, u32[]{:S(2)}) %collective-permute-start.15) | collective-permute-done | bytes 536608 | tf_op jit(solution)/shard_map/ppermute | solution.py:446
  67.2 1.3 %shard_map.48 = bf16[2,128,2048]{2,1,0:T(8,128)(2,1)} custom-call(f32[2,128,2048]{2,1,0:T(8,128)S(1)} %get-tuple-element.71.refs_0_, f32[2,128,128]{2,1,0:T(8,128)S(1)} %get-tuple-element.72.refs_1_, f32[2,128,128]{2,1,0:T(8,128)S(1)} %get-tuple-element.73.refs_2_, bf16[2096,128]{1,0:T(8,128)(2,1)S(1)} %collective-permute-done.15.refs_3_, ...), custom_call_target="tpu_custom_call" | custom-call | flops 1 | bytes 1 | tf_op jit(solution)/shard_map/pallas_call | solution.py:389
  (28 shorter events, 2.5 us)
Async XLA Ops:
  0.0 11.0 %collective-permute-start = (bf16[2,2,128,2048]{3,2,1,0:T(8,128)(2,1)}, bf16[2,2,128,2048]{3,2,1,0:T(8,128)(2,1)S(1)}, u32[]{:S(2)}, u32[]{:S(2)}) collective-permute-start(bf16[2,2,128,2048]{3,2,1,0:T(8,128)(2,1)} %bitcast.3), channel_id=1, source_target_pairs={{0,8},{8,0},{16,24},{24,16},{1,9},{9,1},{17,25},{25,17},{2,10},{10... | collective-permute-start | bytes 6291464 | tf_op jit(solution)/shard_map/ppermute | solution.py:420
  0.5 1.6 %copy-start = (bf16[2,2,16,8,2048]{4,3,2,1,0:T(8,128)(2,1)S(1)}, bf16[2,2,16,8,2048]{4,3,2,1,0:T(8,128)(2,1)}, u32[]{:S(2)}) copy-start(bf16[2,2,16,8,2048]{4,3,2,1,0:T(8,128)(2,1)} %param.4) | copy-start | bytes 6291460
  2.0 8.9 %copy-start.2 = (bf16[2,16,8,2048]{3,2,1,0:T(8,128)(2,1)S(1)}, bf16[2,16,8,2048]{3,2,1,0:T(8,128)(2,1)}, u32[]{:S(2)}) copy-start(bf16[2,16,8,2048]{3,2,1,0:T(8,128)(2,1)} %param.3) | copy-start | bytes 3145732
  2.4 36.0 %copy-start.1 = (bf16[2,2,16,8,2048]{4,3,2,1,0:T(8,128)(2,1)S(1)}, bf16[2,2,16,8,2048]{4,3,2,1,0:T(8,128)(2,1)}, u32[]{:S(2)}) copy-start(bf16[2,2,16,8,2048]{4,3,2,1,0:T(8,128)(2,1)} %param.4) | copy-start | bytes 6291460
  2.4 26.2 %collective-permute-start.1 = (bf16[2,128,2048]{2,1,0:T(8,128)(2,1)S(1)}, bf16[2,128,2048]{2,1,0:T(8,128)(2,1)S(1)}, u32[]{:S(2)}, u32[]{:S(2)}) collective-permute-start(bf16[2,128,2048]{2,1,0:T(8,128)(2,1)S(1)} %get-tuple-element.41), channel_id=1, source_target_pairs={{0,24},{8,16},{16,8},{24,0},{1,25},{9,17},{17,9},{25,1},{2,26},{10... | collective-permute-start | bytes 3145736 | tf_op jit(solution)/shard_map/ppermute | solution.py:422
  5.1 26.9 %collective-permute-start.4 = (bf16[2,2,64,2048]{3,2,1,0:T(8,128)(2,1)S(1)}, bf16[2,2,64,2048]{3,2,1,0:T(8,128)(2,1)S(1)}, u32[]{:S(2)}, u32[]{:S(2)}) collective-permute-start(bf16[2,2,64,2048]{3,2,1,0:T(8,128)(2,1)S(1)} %get-tuple-element.44), channel_id=1, source_target_pairs={{2,0},{4,2},{6,4},{3,1},{5,3},{7,5},{10,8},{12,10},{14,12},{11,9},... | collective-permute-start | bytes 3145736 | tf_op jit(solution)/shard_map/ppermute | solution.py:423
  6.3 29.2 %collective-permute-start.5 = (bf16[2,2,64,2048]{3,2,1,0:T(8,128)(2,1)S(1)}, bf16[2,2,64,2048]{3,2,1,0:T(8,128)(2,1)S(1)}, u32[]{:S(2)}, u32[]{:S(2)}) collective-permute-start(bf16[2,2,64,2048]{3,2,1,0:T(8,128)(2,1)S(1)} %get-tuple-element.45), channel_id=1, source_target_pairs={{0,2},{2,4},{4,6},{1,3},{3,5},{5,7},{8,10},{10,12},{12,14},{9,11},... | collective-permute-start | bytes 3145736 | tf_op jit(solution)/shard_map/ppermute | solution.py:424
  11.0 24.7 %collective-permute-start.6 = (bf16[2,128,2048]{2,1,0:T(8,128)(2,1)S(1)}, bf16[2,128,2048]{2,1,0:T(8,128)(2,1)S(1)}, u32[]{:S(2)}, u32[]{:S(2)}) collective-permute-start(bf16[2,128,2048]{2,1,0:T(8,128)(2,1)S(1)} %bitcast.9), channel_id=1, source_target_pairs={{0,1},{1,0},{2,3},{3,2},{4,5},{5,4},{6,7},{7,6},{8,9},{9,8},{10,11... | collective-permute-start | bytes 3145736 | tf_op jit(solution)/shard_map/ppermute | solution.py:426
  12.6 39.5 %collective-permute-start.9 = (bf16[2,128,2048]{2,1,0:T(8,128)(2,1)S(1)}, bf16[2,128,2048]{2,1,0:T(8,128)(2,1)S(1)}, u32[]{:S(2)}, u32[]{:S(2)}) collective-permute-start(bf16[2,128,2048]{2,1,0:T(8,128)(2,1)S(1)} %get-tuple-element.56), channel_id=1, source_target_pairs={{0,24},{8,16},{16,8},{24,0},{1,25},{9,17},{17,9},{25,1},{2,26},{10... | collective-permute-start | bytes 3145736 | tf_op jit(solution)/shard_map/ppermute | solution.py:430
  28.7 17.3 %collective-permute-start.3 = (bf16[2,64,2176]{2,1,0:T(8,128)(2,1)S(1)}, bf16[2,64,2176]{2,1,0:T(8,128)(2,1)S(1)}, u32[]{:S(2)}, u32[]{:S(2)}) collective-permute-start(bf16[2,64,2176]{2,1,0:T(8,128)(2,1)S(1)} %get-tuple-element.43), channel_id=1, source_target_pairs={{2,0},{4,2},{6,4},{3,1},{5,3},{7,5},{10,8},{12,10},{14,12},{11,9},... | collective-permute-start | bytes 1671176 | tf_op jit(solution)/shard_map/ppermute | solution.py:429
  32.0 15.3 %collective-permute-start.2 = (bf16[2,64,2176]{2,1,0:T(8,128)(2,1)S(1)}, bf16[2,64,2176]{2,1,0:T(8,128)(2,1)S(1)}, u32[]{:S(2)}, u32[]{:S(2)}) collective-permute-start(bf16[2,64,2176]{2,1,0:T(8,128)(2,1)S(1)} %get-tuple-element.62), channel_id=1, source_target_pairs={{0,2},{2,4},{4,6},{1,3},{3,5},{5,7},{8,10},{10,12},{12,14},{9,11},... | collective-permute-start | bytes 1671176 | tf_op jit(solution)/shard_map/ppermute | solution.py:428
  35.6 2.0 %collective-permute-start.8 = (bf16[2,64,2048]{2,1,0:T(8,128)(2,1)S(1)}, bf16[2,64,2048]{2,1,0:T(8,128)(2,1)S(1)}, u32[]{:S(2)}, u32[]{:S(2)}) collective-permute-start(bf16[2,64,2048]{2,1,0:T(8,128)(2,1)S(1)} %get-tuple-element.51), channel_id=1, source_target_pairs={{0,8},{8,0},{16,24},{24,16},{1,9},{9,1},{17,25},{25,17},{2,10},{10... | collective-permute-start | bytes 1572872 | tf_op jit(solution)/shard_map/ppermute | solution.py:433
  35.7 2.6 %collective-permute-start.7 = (bf16[2,64,2048]{2,1,0:T(8,128)(2,1)S(1)}, bf16[2,64,2048]{2,1,0:T(8,128)(2,1)S(1)}, u32[]{:S(2)}, u32[]{:S(2)}) collective-permute-start(bf16[2,64,2048]{2,1,0:T(8,128)(2,1)S(1)} %get-tuple-element.50), channel_id=1, source_target_pairs={{0,8},{8,0},{16,24},{24,16},{1,9},{9,1},{17,25},{25,17},{2,10},{10... | collective-permute-start | bytes 1572872 | tf_op jit(solution)/shard_map/ppermute | solution.py:435
  41.4 15.1 %collective-permute-start.10 = (bf16[2096,128]{1,0:T(8,128)(2,1)S(1)}, bf16[2096,128]{1,0:T(8,128)(2,1)S(1)}, u32[]{:S(2)}, u32[]{:S(2)}) collective-permute-start(bf16[2096,128]{1,0:T(8,128)(2,1)S(1)} %shard_map.40), channel_id=1, source_target_pairs={{0,1},{1,0},{2,3},{3,2},{4,5},{5,4},{6,7},{7,6},{8,9},{9,8},{10,11... | collective-permute-start | bytes 1609736 | tf_op jit(solution)/shard_map/ppermute | solution.py:439
  50.4 16.8 %collective-permute-start.15 = (bf16[2096,128]{1,0:T(8,128)(2,1)S(1)}, bf16[2096,128]{1,0:T(8,128)(2,1)S(1)}, u32[]{:S(2)}, u32[]{:S(2)}) collective-permute-start(bf16[2096,128]{1,0:T(8,128)(2,1)S(1)} %shard_map.42), channel_id=1, source_target_pairs={{0,1},{1,0},{2,3},{3,2},{4,5},{5,4},{6,7},{7,6},{8,9},{9,8},{10,11... | collective-permute-start | bytes 1609736 | tf_op jit(solution)/shard_map/ppermute | solution.py:446
  52.1 4.5 %collective-permute-start.12 = (bf16[2,64,2176]{2,1,0:T(8,128)(2,1)S(1)}, bf16[2,64,2176]{2,1,0:T(8,128)(2,1)S(1)}, u32[]{:S(2)}, u32[]{:S(2)}) collective-permute-start(bf16[2,64,2176]{2,1,0:T(8,128)(2,1)S(1)} %get-tuple-element.62), channel_id=1, source_target_pairs={{0,8},{8,0},{16,24},{24,16},{1,9},{9,1},{17,25},{25,17},{2,10},{10... | collective-permute-start | bytes 1671176 | tf_op jit(solution)/shard_map/ppermute | solution.py:452
  52.2 4.4 %collective-permute-start.13 = (bf16[2,64,2176]{2,1,0:T(8,128)(2,1)S(1)}, bf16[2,64,2176]{2,1,0:T(8,128)(2,1)S(1)}, u32[]{:S(2)}, u32[]{:S(2)}) collective-permute-start(bf16[2,64,2176]{2,1,0:T(8,128)(2,1)S(1)} %get-tuple-element.63), channel_id=1, source_target_pairs={{0,8},{8,0},{16,24},{24,16},{1,9},{9,1},{17,25},{25,17},{2,10},{10... | collective-permute-start | bytes 1671176 | tf_op jit(solution)/shard_map/ppermute | solution.py:450
  52.8 5.7 %copy-start.3 = (s32[2,2,1,2]{3,2,1,0:T(1,128)S(1)}, s32[2,2,1,2]{3,2,1,0:T(1,128)}, u32[]{:S(2)}) copy-start(s32[2,2,1,2]{3,2,1,0:T(1,128)} %far_ref.1) | copy-start | bytes 100
  52.8 3.8 %collective-permute-start.14 = (bf16[2,64,2176]{2,1,0:T(8,128)(2,1)S(1)}, bf16[2,64,2176]{2,1,0:T(8,128)(2,1)S(1)}, u32[]{:S(2)}, u32[]{:S(2)}) collective-permute-start(bf16[2,64,2176]{2,1,0:T(8,128)(2,1)S(1)} %get-tuple-element.64), channel_id=1, source_target_pairs={{0,8},{8,0},{16,24},{24,16},{1,9},{9,1},{17,25},{25,17},{2,10},{10... | collective-permute-start | bytes 1671176 | tf_op jit(solution)/shard_map/ppermute | solution.py:450
  56.6 2.0 %collective-permute-start.11 = (bf16[2,64,2048]{2,1,0:T(8,128)(2,1)S(1)}, bf16[2,64,2048]{2,1,0:T(8,128)(2,1)S(1)}, u32[]{:S(2)}, u32[]{:S(2)}) collective-permute-start(bf16[2,64,2048]{2,1,0:T(8,128)(2,1)S(1)} %shard_map.44), channel_id=1, source_target_pairs={{0,8},{8,0},{16,24},{24,16},{1,9},{9,1},{17,25},{25,17},{2,10},{10... | collective-permute-start | bytes 1572872 | tf_op jit(solution)/shard_map/ppermute | solution.py:454

commit v16 on v15

--- a/solution.py
+++ b/solution.py
@@ -103,13 +103,13 @@
     return copying_call(cut_kernel, shapes, 4, keyvals)
 
 
-def first_rows_kernel(frame_ref, out_ref, sems):
-    run_copies([(frame_ref.at[:, FIRST], out_ref)], sems)
-
-
-def first_rows_of(frame):
+def last_rows_kernel(frame_ref, out_ref, sems):
+    run_copies([(frame_ref.at[:, LAST], out_ref)], sems)
+
+
+def last_rows_of(frame):
     two, _, features = frame.shape
-    return copying_call(first_rows_kernel, [(two, SPOT, features)], 1, frame)[0]
+    return copying_call(last_rows_kernel, [(two, SPOT, features)], 1, frame)[0]
 
 
 def widened_rows_kernel(frame_ref, last_ref, first_ref, sems):
@@ -273,7 +273,7 @@
     collected = [(jnp.zeros((SPOT, HD), jnp.float32), jnp.zeros((SPOT, HD), jnp.float32)) for _ in units]
     for first in range(0, HEADS, GROUP):
         for slot in range(4 * NFAR):
-            tile_copy(corner[0], slot // NFAR, slot % NFAR, slot, first // GROUP).wait()
+            tile_copy(corner[1], slot // NFAR, slot % NFAR, slot, first // GROUP).wait()
         work = [(h, u) for h in range(first, first + GROUP) for u in range(len(units))]
         scores = []
         for h, u in work:
@@ -448,10 +448,10 @@
     late_third = (cross, cross_top, cross_bottom)
     late_home = near_attention(False, ha_size, keyvals, top, bottom, late_third, [], [queries], LATE_COST)
     inner_corner = [lax.ppermute(value, "ta", core_pairs) for value in reversed(widened_rows(last))]
-    cross_last, _ = tie((cross_last, late[0]))
-    corner_last = lax.ppermute(cross_last, "ta", core_pairs)
+    cross_first, _ = tie((cross_first, late[0]))
+    corner_first = lax.ppermute(cross_first, "ta", core_pairs)
     sent, early_parts, _ = tie((cross, early_parts, late_home[1]))
-    corner_first = lax.ppermute(first_rows_of(sent), "ta", core_pairs)
+    corner_last = lax.ppermute(last_rows_of(sent), "ta", core_pairs)
     buffers = (core, cross, last, corner_first, corner_last, *inner_corner)
     own = far_attention(ta_size, far_frames, queries, buffers, (*early_home, *late_home))
     out = finish(wa_size, own, early_parts, None, FINISH_COST)

time: 68.9 us -> 68.4 us (level)
  waiting for transfers between devices: 26.6 us -> 25.5 us
    ppermute x1, waiting for transfers between devices: 0.03 us -> 4.34 us  [per_device(): cross_bottom = lax.ppermute(cross_first, 'ha', down)]
    ppermute x2, waiting for transfers between devices: 3.33 us -> 0.71 us  [per_device(): lax.ppermute(result, 'wa', back)]
    ppermute x1, waiting for transfers between devices: 1.98 us -> 0.01 us  [per_device(): bottom = lax.ppermute(first_rows, 'ha', down)]
    ppermute x1, waiting for transfers between devices: 1.19 us -> 0.01 us  [per_device(): cross_top = lax.ppermute(cross_last, 'ha', up)]
    ppermute x1, waiting for transfers between devices: 0.01 us -> 1 us  [per_device(): visitors = [lax.ppermute(sent, 'wa', there) for there, _ in ways]]
    ppermute x1, waiting for transfers between devices: 1.4 us -> 0.53 us  [per_device(): core_bottom = lax.ppermute(inner_bottom, 'ta', core_pairs)]
    ppermute x1, starting transfers between devices: 0.07 us -> 0.89 us  [per_device(): core_bottom = lax.ppermute(inner_bottom, 'ta', core_pairs)]
  transfers between devices with their start and end apart: 16 -> 16, of which waited for: 8 -> 7; matrix products, arithmetic and copies ran while one was open for 0% -> 0% of each run, Pallas kernels for 27% -> 28%
where the time goes in v16:
time: 68.4 us; the launch traced here: 68.2 us
  waiting for transfers between devices  25.5 us (37%)
  starting transfers between devices  20.5 us (30%)
  Pallas kernels  20.2 us (30%)
  local copies, waits for them, and re-layouts  1.6 us (2%)
    ppermute x1, waiting for transfers between devices, per_device(): cross = lax.ppermute(outer, 'ta', cross_pairs)  16 us
    pallas_call x4, Pallas kernels, near_attention(): pl.pallas_call(functools.partial(near_kernel, len(visitors), len(queries)...  12.4 us
    pallas_call x1, Pallas kernels, far_attention(): pl.pallas_call(functools.partial(far_kernel, members), out_shape=[jax.Sha...  5.16 us
    ppermute x1, starting transfers between devices, per_device(): top = lax.ppermute(last_rows, 'ha', up)  4.61 us
    ppermute x1, waiting for transfers between devices, per_device(): cross_bottom = lax.ppermute(cross_first, 'ha', down)  4.34 us
    ppermute x1, starting transfers between devices, per_device(): cross_top = lax.ppermute(cross_last, 'ha', up)  3.49 us
    ppermute x2, starting transfers between devices, per_device(): lax.ppermute(result, 'wa', back)  3.1 us
    ppermute x1, starting transfers between devices, per_device(): cross = lax.ppermute(outer, 'ta', cross_pairs)  2.67 us
  transfers between devices with their start and end apart: 16, of which 7 were waited for; matrix products, arithmetic and copies ran while one was open for 0% of the time, Pallas kernels for 28%

profile of v16, /device:TPU:0, one launch (start us, length us, event | category | flops | bytes accessed | tf_op | source)
XLA Modules:
  0.0 68.2 jit_solution(13630724418634946920)
XLA Ops:
  0.5 1.6 %copy-done = bf16[2,2,16,8,2048]{4,3,2,1,0:T(8,128)(2,1)S(1)} copy-done((bf16[2,2,16,8,2048]{4,3,2,1,0:T(8,128)(2,1)S(1)}, bf16[2,2,16,8,2048]{4,3,2,1,0:T(8,128)(2,1)}, u32[]{:S(2)}) %copy-start) | copy-done | bytes 2097176
  2.4 2.7 %collective-permute-start.1 = (bf16[2,128,2048]{2,1,0:T(8,128)(2,1)S(1)}, bf16[2,128,2048]{2,1,0:T(8,128)(2,1)S(1)}, u32[]{:S(2)}, u32[]{:S(2)}) collective-permute-start(bf16[2,128,2048]{2,1,0:T(8,128)(2,1)S(1)} %get-tuple-element.41), channel_id=1, source_target_pairs={{0,24},{8,16},{16,8},{24,0},{1,25},{9,17},{17,9},{25,1},{2,26},{10... | collective-permute-start | bytes 3145736 | tf_op jit(solution)/shard_map/ppermute | solution.py:422
  5.1 1.3 %collective-permute-start.4 = (bf16[2,2,64,2048]{3,2,1,0:T(8,128)(2,1)S(1)}, bf16[2,2,64,2048]{3,2,1,0:T(8,128)(2,1)S(1)}, u32[]{:S(2)}, u32[]{:S(2)}) collective-permute-start(bf16[2,2,64,2048]{3,2,1,0:T(8,128)(2,1)S(1)} %get-tuple-element.44), channel_id=1, source_target_pairs={{2,0},{4,2},{6,4},{3,1},{5,3},{7,5},{10,8},{12,10},{14,12},{11,9},... | collective-permute-start | bytes 3145736 | tf_op jit(solution)/shard_map/ppermute | solution.py:423
  6.3 4.6 %collective-permute-start.5 = (bf16[2,2,64,2048]{3,2,1,0:T(8,128)(2,1)S(1)}, bf16[2,2,64,2048]{3,2,1,0:T(8,128)(2,1)S(1)}, u32[]{:S(2)}, u32[]{:S(2)}) collective-permute-start(bf16[2,2,64,2048]{3,2,1,0:T(8,128)(2,1)S(1)} %get-tuple-element.45), channel_id=1, source_target_pairs={{0,2},{2,4},{4,6},{1,3},{3,5},{5,7},{8,10},{10,12},{12,14},{9,11},... | collective-permute-start | bytes 3145736 | tf_op jit(solution)/shard_map/ppermute | solution.py:424
  11.0 1.6 %collective-permute-start.6 = (bf16[2,128,2048]{2,1,0:T(8,128)(2,1)S(1)}, bf16[2,128,2048]{2,1,0:T(8,128)(2,1)S(1)}, u32[]{:S(2)}, u32[]{:S(2)}) collective-permute-start(bf16[2,128,2048]{2,1,0:T(8,128)(2,1)S(1)} %bitcast.9), channel_id=1, source_target_pairs={{0,1},{1,0},{2,3},{3,2},{4,5},{5,4},{6,7},{7,6},{8,9},{9,8},{10,11... | collective-permute-start | bytes 3145736 | tf_op jit(solution)/shard_map/ppermute | solution.py:426
  12.6 16.0 %collective-permute-done.1.frame_ref.refs_0_ = bf16[2,128,2048]{2,1,0:T(8,128)(2,1)S(1)} collective-permute-done((bf16[2,128,2048]{2,1,0:T(8,128)(2,1)S(1)}, bf16[2,128,2048]{2,1,0:T(8,128)(2,1)S(1)}, u32[]{:S(2)}, u32[]{:S(2)}) %collective-permute-start.1) | collective-permute-done | bytes 1048608 | tf_op jit(solution)/shard_map/ppermute | solution.py:422
  28.7 3.5 %collective-permute-start.2 = (bf16[2,64,2176]{2,1,0:T(8,128)(2,1)S(1)}, bf16[2,64,2176]{2,1,0:T(8,128)(2,1)S(1)}, u32[]{:S(2)}, u32[]{:S(2)}) collective-permute-start(bf16[2,64,2176]{2,1,0:T(8,128)(2,1)S(1)} %get-tuple-element.42), channel_id=1, source_target_pairs={{0,2},{2,4},{4,6},{1,3},{3,5},{5,7},{8,10},{10,12},{12,14},{9,11},... | collective-permute-start | bytes 1671176 | tf_op jit(solution)/shard_map/ppermute | solution.py:428
  32.2 1.3 %collective-permute-start.3 = (bf16[2,64,2176]{2,1,0:T(8,128)(2,1)S(1)}, bf16[2,64,2176]{2,1,0:T(8,128)(2,1)S(1)}, u32[]{:S(2)}, u32[]{:S(2)}) collective-permute-start(bf16[2,64,2176]{2,1,0:T(8,128)(2,1)S(1)} %get-tuple-element.59), channel_id=1, source_target_pairs={{2,0},{4,2},{6,4},{3,1},{5,3},{7,5},{10,8},{12,10},{14,12},{11,9},... | collective-permute-start | bytes 1671176 | tf_op jit(solution)/shard_map/ppermute | solution.py:429
  33.7 0.9 %collective-permute-start.8 = (bf16[2,64,2048]{2,1,0:T(8,128)(2,1)S(1)}, bf16[2,64,2048]{2,1,0:T(8,128)(2,1)S(1)}, u32[]{:S(2)}, u32[]{:S(2)}) collective-permute-start(bf16[2,64,2048]{2,1,0:T(8,128)(2,1)S(1)} %get-tuple-element.51), channel_id=1, source_target_pairs={{0,8},{8,0},{16,24},{24,16},{1,9},{9,1},{17,25},{25,17},{2,10},{10... | collective-permute-start | bytes 1572872 | tf_op jit(solution)/shard_map/ppermute | solution.py:433
  34.6 1.0 %collective-permute-done.6.refs_3_ = bf16[2,128,2048]{2,1,0:T(8,128)(2,1)S(1)} collective-permute-done((bf16[2,128,2048]{2,1,0:T(8,128)(2,1)S(1)}, bf16[2,128,2048]{2,1,0:T(8,128)(2,1)S(1)}, u32[]{:S(2)}, u32[]{:S(2)}) %collective-permute-start.6) | collective-permute-done | bytes 1048608 | tf_op jit(solution)/shard_map/ppermute | solution.py:426
  36.1 1.4 %collective-permute-done.7.refs_1_ = bf16[2,64,2048]{2,1,0:T(8,128)(2,1)S(1)} collective-permute-done((bf16[2,64,2048]{2,1,0:T(8,128)(2,1)S(1)}, bf16[2,64,2048]{2,1,0:T(8,128)(2,1)S(1)}, u32[]{:S(2)}, u32[]{:S(2)}) %collective-permute-start.7) | collective-permute-done | bytes 524320 | tf_op jit(solution)/shard_map/ppermute | solution.py:435
  37.5 3.1 %shard_map.40 = bf16[2096,128]{1,0:T(8,128)(2,1)S(1)} custom-call(bf16[2,2,128,2048]{3,2,1,0:T(8,128)(2,1)S(1)} %bitcast.5, bf16[2,2,64,2048]{3,2,1,0:T(8,128)(2,1)S(1)} %collective-permute-done.5.top_ref, bf16[2,2,64,2048]{3,2,1,0:T(8,128)(2,1)S(1)} %collective-permute-done.4.bottom_ref, ...), custom_call_target="tpu_custom_call" | custom-call | flops 1 | bytes 1 | tf_op jit(solution)/shard_map/pallas_call | solution.py:225
  40.5 1.5 %collective-permute-start.11 = (bf16[2096,128]{1,0:T(8,128)(2,1)S(1)}, bf16[2096,128]{1,0:T(8,128)(2,1)S(1)}, u32[]{:S(2)}, u32[]{:S(2)}) collective-permute-start(bf16[2096,128]{1,0:T(8,128)(2,1)S(1)} %shard_map.40), channel_id=1, source_target_pairs={{0,1},{1,0},{2,3},{3,2},{4,5},{5,4},{6,7},{7,6},{8,9},{9,8},{10,11... | collective-permute-start | bytes 1609736 | tf_op jit(solution)/shard_map/ppermute | solution.py:439
  42.1 3.0 %shard_map.41 = (f32[128,2048]{1,0:T(8,128)S(1)}, f32[128,128]{1,0:T(8,128)S(1)}, f32[128,128]{1,0:T(8,128)S(1)}, f32[128,2048]{1,0:T(8,128)S(1)}) custom-call(bf16[2,2,128,2048]{3,2,1,0:T(8,128)(2,1)S(1)} %bitcast.6, bf16[2,2,64,2048]{3,2,1,0:T(8,128)(2,1)S(1)} %collective-permute-done.5.top_ref, ...), custom_call_target="tpu_custom_call" | custom-call | flops 1 | bytes 1 | tf_op jit(solution)/shard_map/pallas_call | solution.py:225
  45.1 4.3 %collective-permute-done.3.refs_2_ = bf16[2,64,2176]{2,1,0:T(8,128)(2,1)S(1)} collective-permute-done((bf16[2,64,2176]{2,1,0:T(8,128)(2,1)S(1)}, bf16[2,64,2176]{2,1,0:T(8,128)(2,1)S(1)}, u32[]{:S(2)}, u32[]{:S(2)}) %collective-permute-start.3) | collective-permute-done | bytes 557088 | tf_op jit(solution)/shard_map/ppermute | solution.py:429
  49.5 3.1 %shard_map.42 = bf16[2096,128]{1,0:T(8,128)(2,1)S(1)} custom-call(bf16[2,2,128,2048]{3,2,1,0:T(8,128)(2,1)S(1)} %bitcast.7, bf16[2,2,64,2048]{3,2,1,0:T(8,128)(2,1)S(1)} %collective-permute-done.5.top_ref, bf16[2,2,64,2048]{3,2,1,0:T(8,128)(2,1)S(1)} %collective-permute-done.4.bottom_ref, bf16[2,128,2048]{2,1,0:T(8,128)(2,1)S(1)} %collective-permute-done.1.frame_ref.refs_0_, ...), custom_call_target="tpu_custom_call" | custom-call | flops 1 | bytes 1 | tf_op jit(solution)/shard_map/pallas_call | solution.py:225
  52.6 1.6 %collective-permute-start.15 = (bf16[2096,128]{1,0:T(8,128)(2,1)S(1)}, bf16[2096,128]{1,0:T(8,128)(2,1)S(1)}, u32[]{:S(2)}, u32[]{:S(2)}) collective-permute-start(bf16[2096,128]{1,0:T(8,128)(2,1)S(1)} %shard_map.42), channel_id=1, source_target_pairs={{0,1},{1,0},{2,3},{3,2},{4,5},{5,4},{6,7},{7,6},{8,9},{9,8},{10,11... | collective-permute-start | bytes 1609736 | tf_op jit(solution)/shard_map/ppermute | solution.py:446
  54.3 0.6 collective-permute-start.13
  55.0 3.1 %shard_map.43 = (f32[128,2048]{1,0:T(8,128)S(1)}, f32[128,128]{1,0:T(8,128)S(1)}, f32[128,128]{1,0:T(8,128)S(1)}, f32[128,2048]{1,0:T(8,128)S(1)}) custom-call(bf16[2,2,128,2048]{3,2,1,0:T(8,128)(2,1)S(1)} %bitcast.8, bf16[2,2,64,2048]{3,2,1,0:T(8,128)(2,1)S(1)} %collective-permute-done.5.top_ref, ...), custom_call_target="tpu_custom_call" | custom-call | flops 30064771072 | bytes 1 | tf_op jit(solution)/shard_map/pallas_call | solution.py:225
  58.7 1.5 %collective-permute-done.12.refs_3_ = bf16[2,64,2048]{2,1,0:T(8,128)(2,1)S(1)} collective-permute-done((bf16[2,64,2048]{2,1,0:T(8,128)(2,1)S(1)}, bf16[2,64,2048]{2,1,0:T(8,128)(2,1)S(1)}, u32[]{:S(2)}, u32[]{:S(2)}) %collective-permute-start.12) | collective-permute-done | bytes 524320 | tf_op jit(solution)/shard_map/ppermute | solution.py:454
  60.2 5.2 %shard_map.46 = (f32[2,128,2048]{2,1,0:T(8,128)S(1)}, f32[2,128,128]{2,1,0:T(8,128)S(1)}, f32[2,128,128]{2,1,0:T(8,128)S(1)}) custom-call(s32[2,2,1,2]{3,2,1,0:T(1,128)S(1)} %copy-done.3, bf16[2,128,2048]{2,1,0:T(8,128)(2,1)S(1)} %bitcast.12, bf16[2,2,128,2048]{3,2,1,0:T(8,128)(2,1)S(1)} %collective-permute-done.refs_0_.core_ref, ...), custom_call_target="tpu_custom_call" | custom-call | flops 1 | bytes 1 | tf_op jit(solution)/shard_map/pallas_call | solution.py:312
  65.4 0.6 shard_map.47.refs_4_
  66.0 0.7 %collective-permute-done.15.refs_3_ = bf16[2096,128]{1,0:T(8,128)(2,1)S(1)} collective-permute-done((bf16[2096,128]{1,0:T(8,128)(2,1)S(1)}, bf16[2096,128]{1,0:T(8,128)(2,1)S(1)}, u32[]{:S(2)}, u32[]{:S(2)}) %collective-permute-start.15) | collective-permute-done | bytes 536608 | tf_op jit(solution)/shard_map/ppermute | solution.py:446
  66.7 1.3 %shard_map.48 = bf16[2,128,2048]{2,1,0:T(8,128)(2,1)} custom-call(f32[2,128,2048]{2,1,0:T(8,128)S(1)} %get-tuple-element.71.refs_0_, f32[2,128,128]{2,1,0:T(8,128)S(1)} %get-tuple-element.72.refs_1_, f32[2,128,128]{2,1,0:T(8,128)S(1)} %get-tuple-element.73.refs_2_, bf16[2096,128]{1,0:T(8,128)(2,1)S(1)} %collective-permute-done.15.refs_3_, ...), custom_call_target="tpu_custom_call" | custom-call | flops 1 | bytes 1 | tf_op jit(solution)/shard_map/pallas_call | solution.py:389
  (28 shorter events, 2.4 us)
Async XLA Ops:
  0.0 11.0 %collective-permute-start = (bf16[2,2,128,2048]{3,2,1,0:T(8,128)(2,1)}, bf16[2,2,128,2048]{3,2,1,0:T(8,128)(2,1)S(1)}, u32[]{:S(2)}, u32[]{:S(2)}) collective-permute-start(bf16[2,2,128,2048]{3,2,1,0:T(8,128)(2,1)} %bitcast.3), channel_id=1, source_target_pairs={{0,8},{8,0},{16,24},{24,16},{1,9},{9,1},{17,25},{25,17},{2,10},{10... | collective-permute-start | bytes 6291464 | tf_op jit(solution)/shard_map/ppermute | solution.py:420
  0.5 1.6 %copy-start = (bf16[2,2,16,8,2048]{4,3,2,1,0:T(8,128)(2,1)S(1)}, bf16[2,2,16,8,2048]{4,3,2,1,0:T(8,128)(2,1)}, u32[]{:S(2)}) copy-start(bf16[2,2,16,8,2048]{4,3,2,1,0:T(8,128)(2,1)} %param.4) | copy-start | bytes 6291460
  2.0 8.9 %copy-start.2 = (bf16[2,16,8,2048]{3,2,1,0:T(8,128)(2,1)S(1)}, bf16[2,16,8,2048]{3,2,1,0:T(8,128)(2,1)}, u32[]{:S(2)}) copy-start(bf16[2,16,8,2048]{3,2,1,0:T(8,128)(2,1)} %param.3) | copy-start | bytes 3145732
  2.4 35.1 %copy-start.1 = (bf16[2,2,16,8,2048]{4,3,2,1,0:T(8,128)(2,1)S(1)}, bf16[2,2,16,8,2048]{4,3,2,1,0:T(8,128)(2,1)}, u32[]{:S(2)}) copy-start(bf16[2,2,16,8,2048]{4,3,2,1,0:T(8,128)(2,1)} %param.4) | copy-start | bytes 6291460
  2.4 26.2 %collective-permute-start.1 = (bf16[2,128,2048]{2,1,0:T(8,128)(2,1)S(1)}, bf16[2,128,2048]{2,1,0:T(8,128)(2,1)S(1)}, u32[]{:S(2)}, u32[]{:S(2)}) collective-permute-start(bf16[2,128,2048]{2,1,0:T(8,128)(2,1)S(1)} %get-tuple-element.41), channel_id=1, source_target_pairs={{0,24},{8,16},{16,8},{24,0},{1,25},{9,17},{17,9},{25,1},{2,26},{10... | collective-permute-start | bytes 3145736 | tf_op jit(solution)/shard_map/ppermute | solution.py:422
  5.1 27.2 %collective-permute-start.4 = (bf16[2,2,64,2048]{3,2,1,0:T(8,128)(2,1)S(1)}, bf16[2,2,64,2048]{3,2,1,0:T(8,128)(2,1)S(1)}, u32[]{:S(2)}, u32[]{:S(2)}) collective-permute-start(bf16[2,2,64,2048]{3,2,1,0:T(8,128)(2,1)S(1)} %get-tuple-element.44), channel_id=1, source_target_pairs={{2,0},{4,2},{6,4},{3,1},{5,3},{7,5},{10,8},{12,10},{14,12},{11,9},... | collective-permute-start | bytes 3145736 | tf_op jit(solution)/shard_map/ppermute | solution.py:423
  6.3 27.2 %collective-permute-start.5 = (bf16[2,2,64,2048]{3,2,1,0:T(8,128)(2,1)S(1)}, bf16[2,2,64,2048]{3,2,1,0:T(8,128)(2,1)S(1)}, u32[]{:S(2)}, u32[]{:S(2)}) collective-permute-start(bf16[2,2,64,2048]{3,2,1,0:T(8,128)(2,1)S(1)} %get-tuple-element.45), channel_id=1, source_target_pairs={{0,2},{2,4},{4,6},{1,3},{3,5},{5,7},{8,10},{10,12},{12,14},{9,11},... | collective-permute-start | bytes 3145736 | tf_op jit(solution)/shard_map/ppermute | solution.py:424
  11.0 24.6 %collective-permute-start.6 = (bf16[2,128,2048]{2,1,0:T(8,128)(2,1)S(1)}, bf16[2,128,2048]{2,1,0:T(8,128)(2,1)S(1)}, u32[]{:S(2)}, u32[]{:S(2)}) collective-permute-start(bf16[2,128,2048]{2,1,0:T(8,128)(2,1)S(1)} %bitcast.9), channel_id=1, source_target_pairs={{0,1},{1,0},{2,3},{3,2},{4,5},{5,4},{6,7},{7,6},{8,9},{9,8},{10,11... | collective-permute-start | bytes 3145736 | tf_op jit(solution)/shard_map/ppermute | solution.py:426
  12.6 41.6 %collective-permute-start.9 = (bf16[2,128,2048]{2,1,0:T(8,128)(2,1)S(1)}, bf16[2,128,2048]{2,1,0:T(8,128)(2,1)S(1)}, u32[]{:S(2)}, u32[]{:S(2)}) collective-permute-start(bf16[2,128,2048]{2,1,0:T(8,128)(2,1)S(1)} %get-tuple-element.56), channel_id=1, source_target_pairs={{0,24},{8,16},{16,8},{24,0},{1,25},{9,17},{17,9},{25,1},{2,26},{10... | collective-permute-start | bytes 3145736 | tf_op jit(solution)/shard_map/ppermute | solution.py:430
  28.7 16.4 %collective-permute-start.2 = (bf16[2,64,2176]{2,1,0:T(8,128)(2,1)S(1)}, bf16[2,64,2176]{2,1,0:T(8,128)(2,1)S(1)}, u32[]{:S(2)}, u32[]{:S(2)}) collective-permute-start(bf16[2,64,2176]{2,1,0:T(8,128)(2,1)S(1)} %get-tuple-element.42), channel_id=1, source_target_pairs={{0,2},{2,4},{4,6},{1,3},{3,5},{5,7},{8,10},{10,12},{12,14},{9,11},... | collective-permute-start | bytes 1671176 | tf_op jit(solution)/shard_map/ppermute | solution.py:428
  32.2 17.3 %collective-permute-start.3 = (bf16[2,64,2176]{2,1,0:T(8,128)(2,1)S(1)}, bf16[2,64,2176]{2,1,0:T(8,128)(2,1)S(1)}, u32[]{:S(2)}, u32[]{:S(2)}) collective-permute-start(bf16[2,64,2176]{2,1,0:T(8,128)(2,1)S(1)} %get-tuple-element.59), channel_id=1, source_target_pairs={{2,0},{4,2},{6,4},{3,1},{5,3},{7,5},{10,8},{12,10},{14,12},{11,9},... | collective-permute-start | bytes 1671176 | tf_op jit(solution)/shard_map/ppermute | solution.py:429
  33.7 2.4 %collective-permute-start.8 = (bf16[2,64,2048]{2,1,0:T(8,128)(2,1)S(1)}, bf16[2,64,2048]{2,1,0:T(8,128)(2,1)S(1)}, u32[]{:S(2)}, u32[]{:S(2)}) collective-permute-start(bf16[2,64,2048]{2,1,0:T(8,128)(2,1)S(1)} %get-tuple-element.51), channel_id=1, source_target_pairs={{0,8},{8,0},{16,24},{24,16},{1,9},{9,1},{17,25},{25,17},{2,10},{10... | collective-permute-start | bytes 1572872 | tf_op jit(solution)/shard_map/ppermute | solution.py:433
  35.6 1.9 %collective-permute-start.7 = (bf16[2,64,2048]{2,1,0:T(8,128)(2,1)S(1)}, bf16[2,64,2048]{2,1,0:T(8,128)(2,1)S(1)}, u32[]{:S(2)}, u32[]{:S(2)}) collective-permute-start(bf16[2,64,2048]{2,1,0:T(8,128)(2,1)S(1)} %get-tuple-element.50), channel_id=1, source_target_pairs={{0,8},{8,0},{16,24},{24,16},{1,9},{9,1},{17,25},{25,17},{2,10},{10... | collective-permute-start | bytes 1572872 | tf_op jit(solution)/shard_map/ppermute | solution.py:435
  40.5 17.6 %collective-permute-start.11 = (bf16[2096,128]{1,0:T(8,128)(2,1)S(1)}, bf16[2096,128]{1,0:T(8,128)(2,1)S(1)}, u32[]{:S(2)}, u32[]{:S(2)}) collective-permute-start(bf16[2096,128]{1,0:T(8,128)(2,1)S(1)} %shard_map.40), channel_id=1, source_target_pairs={{0,1},{1,0},{2,3},{3,2},{4,5},{5,4},{6,7},{7,6},{8,9},{9,8},{10,11... | collective-permute-start | bytes 1609736 | tf_op jit(solution)/shard_map/ppermute | solution.py:439
  52.6 14.1 %collective-permute-start.15 = (bf16[2096,128]{1,0:T(8,128)(2,1)S(1)}, bf16[2096,128]{1,0:T(8,128)(2,1)S(1)}, u32[]{:S(2)}, u32[]{:S(2)}) collective-permute-start(bf16[2096,128]{1,0:T(8,128)(2,1)S(1)} %shard_map.42), channel_id=1, source_target_pairs={{0,1},{1,0},{2,3},{3,2},{4,5},{5,4},{6,7},{7,6},{8,9},{9,8},{10,11... | collective-permute-start | bytes 1609736 | tf_op jit(solution)/shard_map/ppermute | solution.py:446
  54.2 4.5 %collective-permute-start.10 = (bf16[2,64,2176]{2,1,0:T(8,128)(2,1)S(1)}, bf16[2,64,2176]{2,1,0:T(8,128)(2,1)S(1)}, u32[]{:S(2)}, u32[]{:S(2)}) collective-permute-start(bf16[2,64,2176]{2,1,0:T(8,128)(2,1)S(1)} %get-tuple-element.59), channel_id=1, source_target_pairs={{0,8},{8,0},{16,24},{24,16},{1,9},{9,1},{17,25},{25,17},{2,10},{10... | collective-permute-start | bytes 1671176 | tf_op jit(solution)/shard_map/ppermute | solution.py:452
  54.3 4.3 %collective-permute-start.13 = (bf16[2,64,2176]{2,1,0:T(8,128)(2,1)S(1)}, bf16[2,64,2176]{2,1,0:T(8,128)(2,1)S(1)}, u32[]{:S(2)}, u32[]{:S(2)}) collective-permute-start(bf16[2,64,2176]{2,1,0:T(8,128)(2,1)S(1)} %get-tuple-element.63), channel_id=1, source_target_pairs={{0,8},{8,0},{16,24},{24,16},{1,9},{9,1},{17,25},{25,17},{2,10},{10... | collective-permute-start | bytes 1671176 | tf_op jit(solution)/shard_map/ppermute | solution.py:450
  54.9 5.3 %copy-start.3 = (s32[2,2,1,2]{3,2,1,0:T(1,128)S(1)}, s32[2,2,1,2]{3,2,1,0:T(1,128)}, u32[]{:S(2)}) copy-start(s32[2,2,1,2]{3,2,1,0:T(1,128)} %far_ref.1) | copy-start | bytes 100
  54.9 3.8 %collective-permute-start.14 = (bf16[2,64,2176]{2,1,0:T(8,128)(2,1)S(1)}, bf16[2,64,2176]{2,1,0:T(8,128)(2,1)S(1)}, u32[]{:S(2)}, u32[]{:S(2)}) collective-permute-start(bf16[2,64,2176]{2,1,0:T(8,128)(2,1)S(1)} %get-tuple-element.64), channel_id=1, source_target_pairs={{0,8},{8,0},{16,24},{24,16},{1,9},{9,1},{17,25},{25,17},{2,10},{10... | collective-permute-start | bytes 1671176 | tf_op jit(solution)/shard_map/ppermute | solution.py:450
  58.2 2.0 %collective-permute-start.12 = (bf16[2,64,2048]{2,1,0:T(8,128)(2,1)S(1)}, bf16[2,64,2048]{2,1,0:T(8,128)(2,1)S(1)}, u32[]{:S(2)}, u32[]{:S(2)}) collective-permute-start(bf16[2,64,2048]{2,1,0:T(8,128)(2,1)S(1)} %shard_map.44), channel_id=1, source_target_pairs={{0,8},{8,0},{16,24},{24,16},{1,9},{9,1},{17,25},{25,17},{2,10},{10... | collective-permute-start | bytes 1572872 | tf_op jit(solution)/shard_map/ppermute | solution.py:454

commit v17 on v16

--- a/solution.py
+++ b/solution.py
@@ -16,6 +16,7 @@
 EXP_SCALE = HD ** (-0.5) * 1.4426950408889634
 VMEM_LIMIT = 16 * 1024 * 1024
 GROUP = 4
+NEAR_GROUP = 8
 FINISH_COST = 1
 LATE_COST = 28 << 30
 
@@ -136,6 +137,12 @@
     return copying_call(inner_rows_kernel, [top.shape[:1] + top.shape[2:]] * 2, 2, bottom, top)
 
 
+def corrected_reciprocal(value):
+    first = pl.reciprocal(value, approx=True)
+    second = first * (2.0 - value * first)
+    return second * (2.0 - value * second)
+
+
 def near_kernel(sides, home, early, has_rows, own_ref, top_ref, bottom_ref, *refs):
     parity = lax.axis_index("ta") % 2
     ha = lax.axis_index("ha")
@@ -158,8 +165,8 @@
 
     peaks = [jnp.zeros((half, HD), jnp.float32) for _ in range(2)]
     totals = [jnp.ones((half, HD), jnp.float32) for _ in range(2)]
-    for first in range(0, HEADS, GROUP):
-        members = [slice(h * HD, (h + 1) * HD) for h in range(first, first + GROUP)]
+    for first in range(0, HEADS, NEAR_GROUP):
+        members = [slice(h * HD, (h + 1) * HD) for h in range(first, first + NEAR_GROUP)]
         scores = []
         for lanes in members:
             queries = [
@@ -195,7 +202,7 @@
                     rows = slice(s * SPOT, (s + 1) * SPOT)
                     result = summed[rows, :HD]
                     if s < sides:
-                        result = result / total[rows]
+                        result = result * corrected_reciprocal(total[rows])
                     else:
                         filled = jnp.broadcast_to(peak[rows] * EXP_SCALE, (SPOT, HD))
                         out_refs[s + 3][a * SPOT : (a + 1) * SPOT, lanes] = filled

time: 68.4 us -> 68.5 us (level)
  transfers between devices with their start and end apart: 16 -> 16, of which waited for: 7 -> 8; matrix products, arithmetic and copies ran while one was open for 0% -> 0% of each run, Pallas kernels for 28% -> 27%
where the time goes in v17:
time: 68.5 us; the launch traced here: 68.3 us
  waiting for transfers between devices  25.8 us (38%)
  starting transfers between devices  20.5 us (30%)
  Pallas kernels  20 us (29%)
  local copies, waits for them, and re-layouts  1.6 us (2%)
    ppermute x1, waiting for transfers between devices, per_device(): cross = lax.ppermute(outer, 'ta', cross_pairs)  16 us
    pallas_call x4, Pallas kernels, near_attention(): pl.pallas_call(functools.partial(near_kernel, len(visitors), len(queries)...  12.2 us
    pallas_call x1, Pallas kernels, far_attention(): pl.pallas_call(functools.partial(far_kernel, members), out_shape=[jax.Sha...  5.14 us
    ppermute x1, starting transfers between devices, per_device(): top = lax.ppermute(last_rows, 'ha', up)  4.61 us
    ppermute x1, waiting for transfers between devices, per_device(): cross_bottom = lax.ppermute(cross_first, 'ha', down)  4.43 us
    ppermute x1, starting transfers between devices, per_device(): cross_top = lax.ppermute(cross_last, 'ha', up)  3.49 us
    ppermute x2, starting transfers between devices, per_device(): lax.ppermute(result, 'wa', back)  3.12 us
    ppermute x1, starting transfers between devices, per_device(): cross = lax.ppermute(outer, 'ta', cross_pairs)  2.67 us
  transfers between devices with their start and end apart: 16, of which 8 were waited for; matrix products, arithmetic and copies ran while one was open for 0% of the time, Pallas kernels for 27%

profile of v17, /device:TPU:0, one launch (start us, length us, event | category | flops | bytes accessed | tf_op | source)
XLA Modules:
  0.0 68.3 jit_solution(17167977046861218946)
XLA Ops:
  0.5 1.6 %copy-done = bf16[2,2,16,8,2048]{4,3,2,1,0:T(8,128)(2,1)S(1)} copy-done((bf16[2,2,16,8,2048]{4,3,2,1,0:T(8,128)(2,1)S(1)}, bf16[2,2,16,8,2048]{4,3,2,1,0:T(8,128)(2,1)}, u32[]{:S(2)}) %copy-start) | copy-done | bytes 2097176
  2.4 2.7 %collective-permute-start.1 = (bf16[2,128,2048]{2,1,0:T(8,128)(2,1)S(1)}, bf16[2,128,2048]{2,1,0:T(8,128)(2,1)S(1)}, u32[]{:S(2)}, u32[]{:S(2)}) collective-permute-start(bf16[2,128,2048]{2,1,0:T(8,128)(2,1)S(1)} %get-tuple-element.41), channel_id=1, source_target_pairs={{0,24},{8,16},{16,8},{24,0},{1,25},{9,17},{17,9},{25,1},{2,26},{10... | collective-permute-start | bytes 3145736 | tf_op jit(solution)/shard_map/ppermute | solution.py:429
  5.1 1.3 %collective-permute-start.4 = (bf16[2,2,64,2048]{3,2,1,0:T(8,128)(2,1)S(1)}, bf16[2,2,64,2048]{3,2,1,0:T(8,128)(2,1)S(1)}, u32[]{:S(2)}, u32[]{:S(2)}) collective-permute-start(bf16[2,2,64,2048]{3,2,1,0:T(8,128)(2,1)S(1)} %get-tuple-element.44), channel_id=1, source_target_pairs={{2,0},{4,2},{6,4},{3,1},{5,3},{7,5},{10,8},{12,10},{14,12},{11,9},... | collective-permute-start | bytes 3145736 | tf_op jit(solution)/shard_map/ppermute | solution.py:430
  6.3 4.6 %collective-permute-start.5 = (bf16[2,2,64,2048]{3,2,1,0:T(8,128)(2,1)S(1)}, bf16[2,2,64,2048]{3,2,1,0:T(8,128)(2,1)S(1)}, u32[]{:S(2)}, u32[]{:S(2)}) collective-permute-start(bf16[2,2,64,2048]{3,2,1,0:T(8,128)(2,1)S(1)} %get-tuple-element.45), channel_id=1, source_target_pairs={{0,2},{2,4},{4,6},{1,3},{3,5},{5,7},{8,10},{10,12},{12,14},{9,11},... | collective-permute-start | bytes 3145736 | tf_op jit(solution)/shard_map/ppermute | solution.py:431
  11.0 1.6 %collective-permute-start.6 = (bf16[2,128,2048]{2,1,0:T(8,128)(2,1)S(1)}, bf16[2,128,2048]{2,1,0:T(8,128)(2,1)S(1)}, u32[]{:S(2)}, u32[]{:S(2)}) collective-permute-start(bf16[2,128,2048]{2,1,0:T(8,128)(2,1)S(1)} %bitcast.9), channel_id=1, source_target_pairs={{0,1},{1,0},{2,3},{3,2},{4,5},{5,4},{6,7},{7,6},{8,9},{9,8},{10,11... | collective-permute-start | bytes 3145736 | tf_op jit(solution)/shard_map/ppermute | solution.py:433
  12.6 16.0 %collective-permute-done.1.frame_ref.refs_0_ = bf16[2,128,2048]{2,1,0:T(8,128)(2,1)S(1)} collective-permute-done((bf16[2,128,2048]{2,1,0:T(8,128)(2,1)S(1)}, bf16[2,128,2048]{2,1,0:T(8,128)(2,1)S(1)}, u32[]{:S(2)}, u32[]{:S(2)}) %collective-permute-start.1) | collective-permute-done | bytes 1048608 | tf_op jit(solution)/shard_map/ppermute | solution.py:429
  28.7 3.5 %collective-permute-start.2 = (bf16[2,64,2176]{2,1,0:T(8,128)(2,1)S(1)}, bf16[2,64,2176]{2,1,0:T(8,128)(2,1)S(1)}, u32[]{:S(2)}, u32[]{:S(2)}) collective-permute-start(bf16[2,64,2176]{2,1,0:T(8,128)(2,1)S(1)} %get-tuple-element.42), channel_id=1, source_target_pairs={{0,2},{2,4},{4,6},{1,3},{3,5},{5,7},{8,10},{10,12},{12,14},{9,11},... | collective-permute-start | bytes 1671176 | tf_op jit(solution)/shard_map/ppermute | solution.py:435
  32.2 1.3 %collective-permute-start.3 = (bf16[2,64,2176]{2,1,0:T(8,128)(2,1)S(1)}, bf16[2,64,2176]{2,1,0:T(8,128)(2,1)S(1)}, u32[]{:S(2)}, u32[]{:S(2)}) collective-permute-start(bf16[2,64,2176]{2,1,0:T(8,128)(2,1)S(1)} %get-tuple-element.59), channel_id=1, source_target_pairs={{2,0},{4,2},{6,4},{3,1},{5,3},{7,5},{10,8},{12,10},{14,12},{11,9},... | collective-permute-start | bytes 1671176 | tf_op jit(solution)/shard_map/ppermute | solution.py:436
  33.7 0.9 %collective-permute-start.8 = (bf16[2,64,2048]{2,1,0:T(8,128)(2,1)S(1)}, bf16[2,64,2048]{2,1,0:T(8,128)(2,1)S(1)}, u32[]{:S(2)}, u32[]{:S(2)}) collective-permute-start(bf16[2,64,2048]{2,1,0:T(8,128)(2,1)S(1)} %get-tuple-element.51), channel_id=1, source_target_pairs={{0,8},{8,0},{16,24},{24,16},{1,9},{9,1},{17,25},{25,17},{2,10},{10... | collective-permute-start | bytes 1572872 | tf_op jit(solution)/shard_map/ppermute | solution.py:440
  34.6 1.0 %collective-permute-done.6.refs_3_ = bf16[2,128,2048]{2,1,0:T(8,128)(2,1)S(1)} collective-permute-done((bf16[2,128,2048]{2,1,0:T(8,128)(2,1)S(1)}, bf16[2,128,2048]{2,1,0:T(8,128)(2,1)S(1)}, u32[]{:S(2)}, u32[]{:S(2)}) %collective-permute-start.6) | collective-permute-done | bytes 1048608 | tf_op jit(solution)/shard_map/ppermute | solution.py:433
  36.1 1.4 %collective-permute-done.7.refs_1_ = bf16[2,64,2048]{2,1,0:T(8,128)(2,1)S(1)} collective-permute-done((bf16[2,64,2048]{2,1,0:T(8,128)(2,1)S(1)}, bf16[2,64,2048]{2,1,0:T(8,128)(2,1)S(1)}, u32[]{:S(2)}, u32[]{:S(2)}) %collective-permute-start.7) | collective-permute-done | bytes 524320 | tf_op jit(solution)/shard_map/ppermute | solution.py:442
  37.5 2.9 %shard_map.40 = bf16[2096,128]{1,0:T(8,128)(2,1)S(1)} custom-call(bf16[2,2,128,2048]{3,2,1,0:T(8,128)(2,1)S(1)} %bitcast.5, bf16[2,2,64,2048]{3,2,1,0:T(8,128)(2,1)S(1)} %collective-permute-done.5.top_ref, bf16[2,2,64,2048]{3,2,1,0:T(8,128)(2,1)S(1)} %collective-permute-done.4.bottom_ref, ...), custom_call_target="tpu_custom_call" | custom-call | flops 1 | bytes 1 | tf_op jit(solution)/shard_map/pallas_call | solution.py:232
  40.4 1.6 %collective-permute-start.11 = (bf16[2096,128]{1,0:T(8,128)(2,1)S(1)}, bf16[2096,128]{1,0:T(8,128)(2,1)S(1)}, u32[]{:S(2)}, u32[]{:S(2)}) collective-permute-start(bf16[2096,128]{1,0:T(8,128)(2,1)S(1)} %shard_map.40), channel_id=1, source_target_pairs={{0,1},{1,0},{2,3},{3,2},{4,5},{5,4},{6,7},{7,6},{8,9},{9,8},{10,11... | collective-permute-start | bytes 1609736 | tf_op jit(solution)/shard_map/ppermute | solution.py:446
  41.9 2.9 %shard_map.41 = (f32[128,2048]{1,0:T(8,128)S(1)}, f32[128,128]{1,0:T(8,128)S(1)}, f32[128,128]{1,0:T(8,128)S(1)}, f32[128,2048]{1,0:T(8,128)S(1)}) custom-call(bf16[2,2,128,2048]{3,2,1,0:T(8,128)(2,1)S(1)} %bitcast.6, bf16[2,2,64,2048]{3,2,1,0:T(8,128)(2,1)S(1)} %collective-permute-done.5.top_ref, ...), custom_call_target="tpu_custom_call" | custom-call | flops 1 | bytes 1 | tf_op jit(solution)/shard_map/pallas_call | solution.py:232
  45.1 4.4 %collective-permute-done.3.refs_2_ = bf16[2,64,2176]{2,1,0:T(8,128)(2,1)S(1)} collective-permute-done((bf16[2,64,2176]{2,1,0:T(8,128)(2,1)S(1)}, bf16[2,64,2176]{2,1,0:T(8,128)(2,1)S(1)}, u32[]{:S(2)}, u32[]{:S(2)}) %collective-permute-start.3) | collective-permute-done | bytes 557088 | tf_op jit(solution)/shard_map/ppermute | solution.py:436
  49.5 3.2 %shard_map.42 = bf16[2096,128]{1,0:T(8,128)(2,1)S(1)} custom-call(bf16[2,2,128,2048]{3,2,1,0:T(8,128)(2,1)S(1)} %bitcast.7, bf16[2,2,64,2048]{3,2,1,0:T(8,128)(2,1)S(1)} %collective-permute-done.5.top_ref, bf16[2,2,64,2048]{3,2,1,0:T(8,128)(2,1)S(1)} %collective-permute-done.4.bottom_ref, bf16[2,128,2048]{2,1,0:T(8,128)(2,1)S(1)} %collective-permute-done.1.frame_ref.refs_0_, ...), custom_call_target="tpu_custom_call" | custom-call | flops 1 | bytes 1 | tf_op jit(solution)/shard_map/pallas_call | solution.py:232
  52.7 1.6 %collective-permute-start.15 = (bf16[2096,128]{1,0:T(8,128)(2,1)S(1)}, bf16[2096,128]{1,0:T(8,128)(2,1)S(1)}, u32[]{:S(2)}, u32[]{:S(2)}) collective-permute-start(bf16[2096,128]{1,0:T(8,128)(2,1)S(1)} %shard_map.42), channel_id=1, source_target_pairs={{0,1},{1,0},{2,3},{3,2},{4,5},{5,4},{6,7},{7,6},{8,9},{9,8},{10,11... | collective-permute-start | bytes 1609736 | tf_op jit(solution)/shard_map/ppermute | solution.py:453
  54.4 0.6 collective-permute-start.13
  55.1 3.2 %shard_map.43 = (f32[128,2048]{1,0:T(8,128)S(1)}, f32[128,128]{1,0:T(8,128)S(1)}, f32[128,128]{1,0:T(8,128)S(1)}, f32[128,2048]{1,0:T(8,128)S(1)}) custom-call(bf16[2,2,128,2048]{3,2,1,0:T(8,128)(2,1)S(1)} %bitcast.8, bf16[2,2,64,2048]{3,2,1,0:T(8,128)(2,1)S(1)} %collective-permute-done.5.top_ref, ...), custom_call_target="tpu_custom_call" | custom-call | flops 30064771072 | bytes 1 | tf_op jit(solution)/shard_map/pallas_call | solution.py:232
  58.9 1.5 %collective-permute-done.12.refs_3_ = bf16[2,64,2048]{2,1,0:T(8,128)(2,1)S(1)} collective-permute-done((bf16[2,64,2048]{2,1,0:T(8,128)(2,1)S(1)}, bf16[2,64,2048]{2,1,0:T(8,128)(2,1)S(1)}, u32[]{:S(2)}, u32[]{:S(2)}) %collective-permute-start.12) | collective-permute-done | bytes 524320 | tf_op jit(solution)/shard_map/ppermute | solution.py:461
  60.4 5.1 %shard_map.46 = (f32[2,128,2048]{2,1,0:T(8,128)S(1)}, f32[2,128,128]{2,1,0:T(8,128)S(1)}, f32[2,128,128]{2,1,0:T(8,128)S(1)}) custom-call(s32[2,2,1,2]{3,2,1,0:T(1,128)S(1)} %copy-done.3, bf16[2,128,2048]{2,1,0:T(8,128)(2,1)S(1)} %bitcast.12, bf16[2,2,128,2048]{3,2,1,0:T(8,128)(2,1)S(1)} %collective-permute-done.refs_0_.core_ref, ...), custom_call_target="tpu_custom_call" | custom-call | flops 1 | bytes 1 | tf_op jit(solution)/shard_map/pallas_call | solution.py:319
  65.5 0.6 shard_map.47.refs_4_
  66.2 0.7 collective-permute-done.15.refs_3_
  66.8 1.3 %shard_map.48 = bf16[2,128,2048]{2,1,0:T(8,128)(2,1)} custom-call(f32[2,128,2048]{2,1,0:T(8,128)S(1)} %get-tuple-element.71.refs_0_, f32[2,128,128]{2,1,0:T(8,128)S(1)} %get-tuple-element.72.refs_1_, f32[2,128,128]{2,1,0:T(8,128)S(1)} %get-tuple-element.73.refs_2_, bf16[2096,128]{1,0:T(8,128)(2,1)S(1)} %collective-permute-done.15.refs_3_, ...), custom_call_target="tpu_custom_call" | custom-call | flops 1 | bytes 1 | tf_op jit(solution)/shard_map/pallas_call | solution.py:396
  (28 shorter events, 2.6 us)
Async XLA Ops:
  0.0 11.0 %collective-permute-start = (bf16[2,2,128,2048]{3,2,1,0:T(8,128)(2,1)}, bf16[2,2,128,2048]{3,2,1,0:T(8,128)(2,1)S(1)}, u32[]{:S(2)}, u32[]{:S(2)}) collective-permute-start(bf16[2,2,128,2048]{3,2,1,0:T(8,128)(2,1)} %bitcast.3), channel_id=1, source_target_pairs={{0,8},{8,0},{16,24},{24,16},{1,9},{9,1},{17,25},{25,17},{2,10},{10... | collective-permute-start | bytes 6291464 | tf_op jit(solution)/shard_map/ppermute | solution.py:427
  0.5 1.6 %copy-start = (bf16[2,2,16,8,2048]{4,3,2,1,0:T(8,128)(2,1)S(1)}, bf16[2,2,16,8,2048]{4,3,2,1,0:T(8,128)(2,1)}, u32[]{:S(2)}) copy-start(bf16[2,2,16,8,2048]{4,3,2,1,0:T(8,128)(2,1)} %param.4) | copy-start | bytes 6291460
  2.0 8.9 %copy-start.2 = (bf16[2,16,8,2048]{3,2,1,0:T(8,128)(2,1)S(1)}, bf16[2,16,8,2048]{3,2,1,0:T(8,128)(2,1)}, u32[]{:S(2)}) copy-start(bf16[2,16,8,2048]{3,2,1,0:T(8,128)(2,1)} %param.3) | copy-start | bytes 3145732
  2.4 35.1 %copy-start.1 = (bf16[2,2,16,8,2048]{4,3,2,1,0:T(8,128)(2,1)S(1)}, bf16[2,2,16,8,2048]{4,3,2,1,0:T(8,128)(2,1)}, u32[]{:S(2)}) copy-start(bf16[2,2,16,8,2048]{4,3,2,1,0:T(8,128)(2,1)} %param.4) | copy-start | bytes 6291460
  2.4 26.2 %collective-permute-start.1 = (bf16[2,128,2048]{2,1,0:T(8,128)(2,1)S(1)}, bf16[2,128,2048]{2,1,0:T(8,128)(2,1)S(1)}, u32[]{:S(2)}, u32[]{:S(2)}) collective-permute-start(bf16[2,128,2048]{2,1,0:T(8,128)(2,1)S(1)} %get-tuple-element.41), channel_id=1, source_target_pairs={{0,24},{8,16},{16,8},{24,0},{1,25},{9,17},{17,9},{25,1},{2,26},{10... | collective-permute-start | bytes 3145736 | tf_op jit(solution)/shard_map/ppermute | solution.py:429
  5.1 27.2 %collective-permute-start.4 = (bf16[2,2,64,2048]{3,2,1,0:T(8,128)(2,1)S(1)}, bf16[2,2,64,2048]{3,2,1,0:T(8,128)(2,1)S(1)}, u32[]{:S(2)}, u32[]{:S(2)}) collective-permute-start(bf16[2,2,64,2048]{3,2,1,0:T(8,128)(2,1)S(1)} %get-tuple-element.44), channel_id=1, source_target_pairs={{2,0},{4,2},{6,4},{3,1},{5,3},{7,5},{10,8},{12,10},{14,12},{11,9},... | collective-permute-start | bytes 3145736 | tf_op jit(solution)/shard_map/ppermute | solution.py:430
  6.3 27.2 %collective-permute-start.5 = (bf16[2,2,64,2048]{3,2,1,0:T(8,128)(2,1)S(1)}, bf16[2,2,64,2048]{3,2,1,0:T(8,128)(2,1)S(1)}, u32[]{:S(2)}, u32[]{:S(2)}) collective-permute-start(bf16[2,2,64,2048]{3,2,1,0:T(8,128)(2,1)S(1)} %get-tuple-element.45), channel_id=1, source_target_pairs={{0,2},{2,4},{4,6},{1,3},{3,5},{5,7},{8,10},{10,12},{12,14},{9,11},... | collective-permute-start | bytes 3145736 | tf_op jit(solution)/shard_map/ppermute | solution.py:431
  11.0 24.6 %collective-permute-start.6 = (bf16[2,128,2048]{2,1,0:T(8,128)(2,1)S(1)}, bf16[2,128,2048]{2,1,0:T(8,128)(2,1)S(1)}, u32[]{:S(2)}, u32[]{:S(2)}) collective-permute-start(bf16[2,128,2048]{2,1,0:T(8,128)(2,1)S(1)} %bitcast.9), channel_id=1, source_target_pairs={{0,1},{1,0},{2,3},{3,2},{4,5},{5,4},{6,7},{7,6},{8,9},{9,8},{10,11... | collective-permute-start | bytes 3145736 | tf_op jit(solution)/shard_map/ppermute | solution.py:433
  12.6 41.7 %collective-permute-start.9 = (bf16[2,128,2048]{2,1,0:T(8,128)(2,1)S(1)}, bf16[2,128,2048]{2,1,0:T(8,128)(2,1)S(1)}, u32[]{:S(2)}, u32[]{:S(2)}) collective-permute-start(bf16[2,128,2048]{2,1,0:T(8,128)(2,1)S(1)} %get-tuple-element.56), channel_id=1, source_target_pairs={{0,24},{8,16},{16,8},{24,0},{1,25},{9,17},{17,9},{25,1},{2,26},{10... | collective-permute-start | bytes 3145736 | tf_op jit(solution)/shard_map/ppermute | solution.py:437
  28.7 16.3 %collective-permute-start.2 = (bf16[2,64,2176]{2,1,0:T(8,128)(2,1)S(1)}, bf16[2,64,2176]{2,1,0:T(8,128)(2,1)S(1)}, u32[]{:S(2)}, u32[]{:S(2)}) collective-permute-start(bf16[2,64,2176]{2,1,0:T(8,128)(2,1)S(1)} %get-tuple-element.42), channel_id=1, source_target_pairs={{0,2},{2,4},{4,6},{1,3},{3,5},{5,7},{8,10},{10,12},{12,14},{9,11},... | collective-permute-start | bytes 1671176 | tf_op jit(solution)/shard_map/ppermute | solution.py:435
  32.2 17.3 %collective-permute-start.3 = (bf16[2,64,2176]{2,1,0:T(8,128)(2,1)S(1)}, bf16[2,64,2176]{2,1,0:T(8,128)(2,1)S(1)}, u32[]{:S(2)}, u32[]{:S(2)}) collective-permute-start(bf16[2,64,2176]{2,1,0:T(8,128)(2,1)S(1)} %get-tuple-element.59), channel_id=1, source_target_pairs={{2,0},{4,2},{6,4},{3,1},{5,3},{7,5},{10,8},{12,10},{14,12},{11,9},... | collective-permute-start | bytes 1671176 | tf_op jit(solution)/shard_map/ppermute | solution.py:436
  33.7 2.4 %collective-permute-start.8 = (bf16[2,64,2048]{2,1,0:T(8,128)(2,1)S(1)}, bf16[2,64,2048]{2,1,0:T(8,128)(2,1)S(1)}, u32[]{:S(2)}, u32[]{:S(2)}) collective-permute-start(bf16[2,64,2048]{2,1,0:T(8,128)(2,1)S(1)} %get-tuple-element.51), channel_id=1, source_target_pairs={{0,8},{8,0},{16,24},{24,16},{1,9},{9,1},{17,25},{25,17},{2,10},{10... | collective-permute-start | bytes 1572872 | tf_op jit(solution)/shard_map/ppermute | solution.py:440
  35.6 1.9 %collective-permute-start.7 = (bf16[2,64,2048]{2,1,0:T(8,128)(2,1)S(1)}, bf16[2,64,2048]{2,1,0:T(8,128)(2,1)S(1)}, u32[]{:S(2)}, u32[]{:S(2)}) collective-permute-start(bf16[2,64,2048]{2,1,0:T(8,128)(2,1)S(1)} %get-tuple-element.50), channel_id=1, source_target_pairs={{0,8},{8,0},{16,24},{24,16},{1,9},{9,1},{17,25},{25,17},{2,10},{10... | collective-permute-start | bytes 1572872 | tf_op jit(solution)/shard_map/ppermute | solution.py:442
  40.4 17.9 %collective-permute-start.11 = (bf16[2096,128]{1,0:T(8,128)(2,1)S(1)}, bf16[2096,128]{1,0:T(8,128)(2,1)S(1)}, u32[]{:S(2)}, u32[]{:S(2)}) collective-permute-start(bf16[2096,128]{1,0:T(8,128)(2,1)S(1)} %shard_map.40), channel_id=1, source_target_pairs={{0,1},{1,0},{2,3},{3,2},{4,5},{5,4},{6,7},{7,6},{8,9},{9,8},{10,11... | collective-permute-start | bytes 1609736 | tf_op jit(solution)/shard_map/ppermute | solution.py:446
  52.7 14.1 %collective-permute-start.15 = (bf16[2096,128]{1,0:T(8,128)(2,1)S(1)}, bf16[2096,128]{1,0:T(8,128)(2,1)S(1)}, u32[]{:S(2)}, u32[]{:S(2)}) collective-permute-start(bf16[2096,128]{1,0:T(8,128)(2,1)S(1)} %shard_map.42), channel_id=1, source_target_pairs={{0,1},{1,0},{2,3},{3,2},{4,5},{5,4},{6,7},{7,6},{8,9},{9,8},{10,11... | collective-permute-start | bytes 1609736 | tf_op jit(solution)/shard_map/ppermute | solution.py:453
  54.3 4.5 %collective-permute-start.10 = (bf16[2,64,2176]{2,1,0:T(8,128)(2,1)S(1)}, bf16[2,64,2176]{2,1,0:T(8,128)(2,1)S(1)}, u32[]{:S(2)}, u32[]{:S(2)}) collective-permute-start(bf16[2,64,2176]{2,1,0:T(8,128)(2,1)S(1)} %get-tuple-element.59), channel_id=1, source_target_pairs={{0,8},{8,0},{16,24},{24,16},{1,9},{9,1},{17,25},{25,17},{2,10},{10... | collective-permute-start | bytes 1671176 | tf_op jit(solution)/shard_map/ppermute | solution.py:459
  54.4 4.4 %collective-permute-start.13 = (bf16[2,64,2176]{2,1,0:T(8,128)(2,1)S(1)}, bf16[2,64,2176]{2,1,0:T(8,128)(2,1)S(1)}, u32[]{:S(2)}, u32[]{:S(2)}) collective-permute-start(bf16[2,64,2176]{2,1,0:T(8,128)(2,1)S(1)} %get-tuple-element.63), channel_id=1, source_target_pairs={{0,8},{8,0},{16,24},{24,16},{1,9},{9,1},{17,25},{25,17},{2,10},{10... | collective-permute-start | bytes 1671176 | tf_op jit(solution)/shard_map/ppermute | solution.py:457
  55.0 5.4 %copy-start.3 = (s32[2,2,1,2]{3,2,1,0:T(1,128)S(1)}, s32[2,2,1,2]{3,2,1,0:T(1,128)}, u32[]{:S(2)}) copy-start(s32[2,2,1,2]{3,2,1,0:T(1,128)} %far_ref.1) | copy-start | bytes 100
  55.0 3.8 %collective-permute-start.14 = (bf16[2,64,2176]{2,1,0:T(8,128)(2,1)S(1)}, bf16[2,64,2176]{2,1,0:T(8,128)(2,1)S(1)}, u32[]{:S(2)}, u32[]{:S(2)}) collective-permute-start(bf16[2,64,2176]{2,1,0:T(8,128)(2,1)S(1)} %get-tuple-element.64), channel_id=1, source_target_pairs={{0,8},{8,0},{16,24},{24,16},{1,9},{9,1},{17,25},{25,17},{2,10},{10... | collective-permute-start | bytes 1671176 | tf_op jit(solution)/shard_map/ppermute | solution.py:457
  58.4 2.0 %collective-permute-start.12 = (bf16[2,64,2048]{2,1,0:T(8,128)(2,1)S(1)}, bf16[2,64,2048]{2,1,0:T(8,128)(2,1)S(1)}, u32[]{:S(2)}, u32[]{:S(2)}) collective-permute-start(bf16[2,64,2048]{2,1,0:T(8,128)(2,1)S(1)} %shard_map.44), channel_id=1, source_target_pairs={{0,8},{8,0},{16,24},{24,16},{1,9},{9,1},{17,25},{25,17},{2,10},{10... | collective-permute-start | bytes 1572872 | tf_op jit(solution)/shard_map/ppermute | solution.py:461

commit v18 on v17

--- a/solution.py
+++ b/solution.py
@@ -15,8 +15,8 @@
 NEGATIVE = -1e30
 EXP_SCALE = HD ** (-0.5) * 1.4426950408889634
 VMEM_LIMIT = 16 * 1024 * 1024
-GROUP = 4
-NEAR_GROUP = 8
+GROUP = 8
+NEAR_GROUP = 16
 FINISH_COST = 1
 LATE_COST = 28 << 30
 

time: 68.5 us -> 68.6 us (level)
  waiting for transfers between devices: 25.8 us -> 26.7 us
  Pallas kernels: 20 us -> 19.2 us
    pallas_call x1, Pallas kernels: 5.14 us -> 4.17 us  [far_attention(): pl.pallas_call(functools.partial(far_kernel, members), out_shape=[jax.Sha...]
    ppermute x2, waiting for transfers between devices: 0.67 us -> 1.55 us  [per_device(): lax.ppermute(result, 'wa', back)]
  transfers between devices with their start and end apart: 16 -> 16, of which waited for: 8 -> 8; matrix products, arithmetic and copies ran while one was open for 0% -> 0% of each run, Pallas kernels for 27% -> 26%
where the time goes in v18:
time: 68.6 us; the launch traced here: 68.4 us
  waiting for transfers between devices  26.7 us (39%)
  starting transfers between devices  20.5 us (30%)
  Pallas kernels  19.2 us (28%)
  local copies, waits for them, and re-layouts  1.6 us (2%)
    ppermute x1, waiting for transfers between devices, per_device(): cross = lax.ppermute(outer, 'ta', cross_pairs)  16 us
    pallas_call x4, Pallas kernels, near_attention(): pl.pallas_call(functools.partial(near_kernel, len(visitors), len(queries)...  12.3 us
    ppermute x1, starting transfers between devices, per_device(): top = lax.ppermute(last_rows, 'ha', up)  4.61 us
    ppermute x1, waiting for transfers between devices, per_device(): cross_bottom = lax.ppermute(cross_first, 'ha', down)  4.43 us
    pallas_call x1, Pallas kernels, far_attention(): pl.pallas_call(functools.partial(far_kernel, members), out_shape=[jax.Sha...  4.17 us
    ppermute x1, starting transfers between devices, per_device(): cross_top = lax.ppermute(cross_last, 'ha', up)  3.49 us
    ppermute x2, starting transfers between devices, per_device(): lax.ppermute(result, 'wa', back)  3.11 us
    ppermute x1, starting transfers between devices, per_device(): cross = lax.ppermute(outer, 'ta', cross_pairs)  2.67 us
  transfers between devices with their start and end apart: 16, of which 8 were waited for; matrix products, arithmetic and copies ran while one was open for 0% of the time, Pallas kernels for 26%

profile of v18, /device:TPU:0, one launch (start us, length us, event | category | flops | bytes accessed | tf_op | source)
XLA Modules:
  0.0 68.4 jit_solution(14356557500415845019)
XLA Ops:
  0.5 1.6 %copy-done = bf16[2,2,16,8,2048]{4,3,2,1,0:T(8,128)(2,1)S(1)} copy-done((bf16[2,2,16,8,2048]{4,3,2,1,0:T(8,128)(2,1)S(1)}, bf16[2,2,16,8,2048]{4,3,2,1,0:T(8,128)(2,1)}, u32[]{:S(2)}) %copy-start) | copy-done | bytes 2097176
  2.4 2.7 %collective-permute-start.1 = (bf16[2,128,2048]{2,1,0:T(8,128)(2,1)S(1)}, bf16[2,128,2048]{2,1,0:T(8,128)(2,1)S(1)}, u32[]{:S(2)}, u32[]{:S(2)}) collective-permute-start(bf16[2,128,2048]{2,1,0:T(8,128)(2,1)S(1)} %get-tuple-element.41), channel_id=1, source_target_pairs={{0,24},{8,16},{16,8},{24,0},{1,25},{9,17},{17,9},{25,1},{2,26},{10... | collective-permute-start | bytes 3145736 | tf_op jit(solution)/shard_map/ppermute | solution.py:429
  5.1 1.3 %collective-permute-start.4 = (bf16[2,2,64,2048]{3,2,1,0:T(8,128)(2,1)S(1)}, bf16[2,2,64,2048]{3,2,1,0:T(8,128)(2,1)S(1)}, u32[]{:S(2)}, u32[]{:S(2)}) collective-permute-start(bf16[2,2,64,2048]{3,2,1,0:T(8,128)(2,1)S(1)} %get-tuple-element.44), channel_id=1, source_target_pairs={{2,0},{4,2},{6,4},{3,1},{5,3},{7,5},{10,8},{12,10},{14,12},{11,9},... | collective-permute-start | bytes 3145736 | tf_op jit(solution)/shard_map/ppermute | solution.py:430
  6.3 4.6 %collective-permute-start.5 = (bf16[2,2,64,2048]{3,2,1,0:T(8,128)(2,1)S(1)}, bf16[2,2,64,2048]{3,2,1,0:T(8,128)(2,1)S(1)}, u32[]{:S(2)}, u32[]{:S(2)}) collective-permute-start(bf16[2,2,64,2048]{3,2,1,0:T(8,128)(2,1)S(1)} %get-tuple-element.45), channel_id=1, source_target_pairs={{0,2},{2,4},{4,6},{1,3},{3,5},{5,7},{8,10},{10,12},{12,14},{9,11},... | collective-permute-start | bytes 3145736 | tf_op jit(solution)/shard_map/ppermute | solution.py:431
  11.0 1.6 %collective-permute-start.6 = (bf16[2,128,2048]{2,1,0:T(8,128)(2,1)S(1)}, bf16[2,128,2048]{2,1,0:T(8,128)(2,1)S(1)}, u32[]{:S(2)}, u32[]{:S(2)}) collective-permute-start(bf16[2,128,2048]{2,1,0:T(8,128)(2,1)S(1)} %bitcast.9), channel_id=1, source_target_pairs={{0,1},{1,0},{2,3},{3,2},{4,5},{5,4},{6,7},{7,6},{8,9},{9,8},{10,11... | collective-permute-start | bytes 3145736 | tf_op jit(solution)/shard_map/ppermute | solution.py:433
  12.6 16.0 %collective-permute-done.1.frame_ref.refs_0_ = bf16[2,128,2048]{2,1,0:T(8,128)(2,1)S(1)} collective-permute-done((bf16[2,128,2048]{2,1,0:T(8,128)(2,1)S(1)}, bf16[2,128,2048]{2,1,0:T(8,128)(2,1)S(1)}, u32[]{:S(2)}, u32[]{:S(2)}) %collective-permute-start.1) | collective-permute-done | bytes 1048608 | tf_op jit(solution)/shard_map/ppermute | solution.py:429
  28.7 3.5 %collective-permute-start.2 = (bf16[2,64,2176]{2,1,0:T(8,128)(2,1)S(1)}, bf16[2,64,2176]{2,1,0:T(8,128)(2,1)S(1)}, u32[]{:S(2)}, u32[]{:S(2)}) collective-permute-start(bf16[2,64,2176]{2,1,0:T(8,128)(2,1)S(1)} %get-tuple-element.42), channel_id=1, source_target_pairs={{0,2},{2,4},{4,6},{1,3},{3,5},{5,7},{8,10},{10,12},{12,14},{9,11},... | collective-permute-start | bytes 1671176 | tf_op jit(solution)/shard_map/ppermute | solution.py:435
  32.2 1.3 %collective-permute-start.3 = (bf16[2,64,2176]{2,1,0:T(8,128)(2,1)S(1)}, bf16[2,64,2176]{2,1,0:T(8,128)(2,1)S(1)}, u32[]{:S(2)}, u32[]{:S(2)}) collective-permute-start(bf16[2,64,2176]{2,1,0:T(8,128)(2,1)S(1)} %get-tuple-element.59), channel_id=1, source_target_pairs={{2,0},{4,2},{6,4},{3,1},{5,3},{7,5},{10,8},{12,10},{14,12},{11,9},... | collective-permute-start | bytes 1671176 | tf_op jit(solution)/shard_map/ppermute | solution.py:436
  33.7 0.9 %collective-permute-start.8 = (bf16[2,64,2048]{2,1,0:T(8,128)(2,1)S(1)}, bf16[2,64,2048]{2,1,0:T(8,128)(2,1)S(1)}, u32[]{:S(2)}, u32[]{:S(2)}) collective-permute-start(bf16[2,64,2048]{2,1,0:T(8,128)(2,1)S(1)} %get-tuple-element.51), channel_id=1, source_target_pairs={{0,8},{8,0},{16,24},{24,16},{1,9},{9,1},{17,25},{25,17},{2,10},{10... | collective-permute-start | bytes 1572872 | tf_op jit(solution)/shard_map/ppermute | solution.py:440
  34.6 1.0 %collective-permute-done.6.refs_3_ = bf16[2,128,2048]{2,1,0:T(8,128)(2,1)S(1)} collective-permute-done((bf16[2,128,2048]{2,1,0:T(8,128)(2,1)S(1)}, bf16[2,128,2048]{2,1,0:T(8,128)(2,1)S(1)}, u32[]{:S(2)}, u32[]{:S(2)}) %collective-permute-start.6) | collective-permute-done | bytes 1048608 | tf_op jit(solution)/shard_map/ppermute | solution.py:433
  36.1 1.4 %collective-permute-done.7.refs_1_ = bf16[2,64,2048]{2,1,0:T(8,128)(2,1)S(1)} collective-permute-done((bf16[2,64,2048]{2,1,0:T(8,128)(2,1)S(1)}, bf16[2,64,2048]{2,1,0:T(8,128)(2,1)S(1)}, u32[]{:S(2)}, u32[]{:S(2)}) %collective-permute-start.7) | collective-permute-done | bytes 524320 | tf_op jit(solution)/shard_map/ppermute | solution.py:442
  37.5 2.9 %shard_map.40 = bf16[2096,128]{1,0:T(8,128)(2,1)S(1)} custom-call(bf16[2,2,128,2048]{3,2,1,0:T(8,128)(2,1)S(1)} %bitcast.5, bf16[2,2,64,2048]{3,2,1,0:T(8,128)(2,1)S(1)} %collective-permute-done.5.top_ref, bf16[2,2,64,2048]{3,2,1,0:T(8,128)(2,1)S(1)} %collective-permute-done.4.bottom_ref, ...), custom_call_target="tpu_custom_call" | custom-call | flops 1 | bytes 1 | tf_op jit(solution)/shard_map/pallas_call | solution.py:232
  40.4 1.6 %collective-permute-start.11 = (bf16[2096,128]{1,0:T(8,128)(2,1)S(1)}, bf16[2096,128]{1,0:T(8,128)(2,1)S(1)}, u32[]{:S(2)}, u32[]{:S(2)}) collective-permute-start(bf16[2096,128]{1,0:T(8,128)(2,1)S(1)} %shard_map.40), channel_id=1, source_target_pairs={{0,1},{1,0},{2,3},{3,2},{4,5},{5,4},{6,7},{7,6},{8,9},{9,8},{10,11... | collective-permute-start | bytes 1609736 | tf_op jit(solution)/shard_map/ppermute | solution.py:446
  41.9 2.9 %shard_map.41 = (f32[128,2048]{1,0:T(8,128)S(1)}, f32[128,128]{1,0:T(8,128)S(1)}, f32[128,128]{1,0:T(8,128)S(1)}, f32[128,2048]{1,0:T(8,128)S(1)}) custom-call(bf16[2,2,128,2048]{3,2,1,0:T(8,128)(2,1)S(1)} %bitcast.6, bf16[2,2,64,2048]{3,2,1,0:T(8,128)(2,1)S(1)} %collective-permute-done.5.top_ref, ...), custom_call_target="tpu_custom_call" | custom-call | flops 1 | bytes 1 | tf_op jit(solution)/shard_map/pallas_call | solution.py:232
  45.1 4.4 %collective-permute-done.3.refs_2_ = bf16[2,64,2176]{2,1,0:T(8,128)(2,1)S(1)} collective-permute-done((bf16[2,64,2176]{2,1,0:T(8,128)(2,1)S(1)}, bf16[2,64,2176]{2,1,0:T(8,128)(2,1)S(1)}, u32[]{:S(2)}, u32[]{:S(2)}) %collective-permute-start.3) | collective-permute-done | bytes 557088 | tf_op jit(solution)/shard_map/ppermute | solution.py:436
  49.5 3.3 %shard_map.42 = bf16[2096,128]{1,0:T(8,128)(2,1)S(1)} custom-call(bf16[2,2,128,2048]{3,2,1,0:T(8,128)(2,1)S(1)} %bitcast.7, bf16[2,2,64,2048]{3,2,1,0:T(8,128)(2,1)S(1)} %collective-permute-done.5.top_ref, bf16[2,2,64,2048]{3,2,1,0:T(8,128)(2,1)S(1)} %collective-permute-done.4.bottom_ref, bf16[2,128,2048]{2,1,0:T(8,128)(2,1)S(1)} %collective-permute-done.1.frame_ref.refs_0_, ...), custom_call_target="tpu_custom_call" | custom-call | flops 1 | bytes 1 | tf_op jit(solution)/shard_map/pallas_call | solution.py:232
  52.8 1.6 %collective-permute-start.15 = (bf16[2096,128]{1,0:T(8,128)(2,1)S(1)}, bf16[2096,128]{1,0:T(8,128)(2,1)S(1)}, u32[]{:S(2)}, u32[]{:S(2)}) collective-permute-start(bf16[2096,128]{1,0:T(8,128)(2,1)S(1)} %shard_map.42), channel_id=1, source_target_pairs={{0,1},{1,0},{2,3},{3,2},{4,5},{5,4},{6,7},{7,6},{8,9},{9,8},{10,11... | collective-permute-start | bytes 1609736 | tf_op jit(solution)/shard_map/ppermute | solution.py:453
  54.5 0.6 collective-permute-start.13
  55.1 3.3 %shard_map.43 = (f32[128,2048]{1,0:T(8,128)S(1)}, f32[128,128]{1,0:T(8,128)S(1)}, f32[128,128]{1,0:T(8,128)S(1)}, f32[128,2048]{1,0:T(8,128)S(1)}) custom-call(bf16[2,2,128,2048]{3,2,1,0:T(8,128)(2,1)S(1)} %bitcast.8, bf16[2,2,64,2048]{3,2,1,0:T(8,128)(2,1)S(1)} %collective-permute-done.5.top_ref, ...), custom_call_target="tpu_custom_call" | custom-call | flops 30064771072 | bytes 1 | tf_op jit(solution)/shard_map/pallas_call | solution.py:232
  59.0 1.5 %collective-permute-done.12.refs_3_ = bf16[2,64,2048]{2,1,0:T(8,128)(2,1)S(1)} collective-permute-done((bf16[2,64,2048]{2,1,0:T(8,128)(2,1)S(1)}, bf16[2,64,2048]{2,1,0:T(8,128)(2,1)S(1)}, u32[]{:S(2)}, u32[]{:S(2)}) %collective-permute-start.12) | collective-permute-done | bytes 524320 | tf_op jit(solution)/shard_map/ppermute | solution.py:461
  60.5 4.2 %shard_map.46 = (f32[2,128,2048]{2,1,0:T(8,128)S(1)}, f32[2,128,128]{2,1,0:T(8,128)S(1)}, f32[2,128,128]{2,1,0:T(8,128)S(1)}) custom-call(s32[2,2,1,2]{3,2,1,0:T(1,128)S(1)} %copy-done.3, bf16[2,128,2048]{2,1,0:T(8,128)(2,1)S(1)} %bitcast.12, bf16[2,2,128,2048]{3,2,1,0:T(8,128)(2,1)S(1)} %collective-permute-done.refs_0_.core_ref, ...), custom_call_target="tpu_custom_call" | custom-call | flops 1 | bytes 1 | tf_op jit(solution)/shard_map/pallas_call | solution.py:319
  64.7 0.6 shard_map.47.refs_4_
  65.3 1.5 %collective-permute-done.15.refs_3_ = bf16[2096,128]{1,0:T(8,128)(2,1)S(1)} collective-permute-done((bf16[2096,128]{1,0:T(8,128)(2,1)S(1)}, bf16[2096,128]{1,0:T(8,128)(2,1)S(1)}, u32[]{:S(2)}, u32[]{:S(2)}) %collective-permute-start.15) | collective-permute-done | bytes 536608 | tf_op jit(solution)/shard_map/ppermute | solution.py:453
  66.9 1.4 %shard_map.48 = bf16[2,128,2048]{2,1,0:T(8,128)(2,1)} custom-call(f32[2,128,2048]{2,1,0:T(8,128)S(1)} %get-tuple-element.71.refs_0_, f32[2,128,128]{2,1,0:T(8,128)S(1)} %get-tuple-element.72.refs_1_, f32[2,128,128]{2,1,0:T(8,128)S(1)} %get-tuple-element.73.refs_2_, bf16[2096,128]{1,0:T(8,128)(2,1)S(1)} %collective-permute-done.15.refs_3_, ...), custom_call_target="tpu_custom_call" | custom-call | flops 1 | bytes 1 | tf_op jit(solution)/shard_map/pallas_call | solution.py:396
  (28 shorter events, 2.6 us)
Async XLA Ops:
  0.0 11.0 %collective-permute-start = (bf16[2,2,128,2048]{3,2,1,0:T(8,128)(2,1)}, bf16[2,2,128,2048]{3,2,1,0:T(8,128)(2,1)S(1)}, u32[]{:S(2)}, u32[]{:S(2)}) collective-permute-start(bf16[2,2,128,2048]{3,2,1,0:T(8,128)(2,1)} %bitcast.3), channel_id=1, source_target_pairs={{0,8},{8,0},{16,24},{24,16},{1,9},{9,1},{17,25},{25,17},{2,10},{10... | collective-permute-start | bytes 6291464 | tf_op jit(solution)/shard_map/ppermute | solution.py:427
  0.5 1.6 %copy-start = (bf16[2,2,16,8,2048]{4,3,2,1,0:T(8,128)(2,1)S(1)}, bf16[2,2,16,8,2048]{4,3,2,1,0:T(8,128)(2,1)}, u32[]{:S(2)}) copy-start(bf16[2,2,16,8,2048]{4,3,2,1,0:T(8,128)(2,1)} %param.4) | copy-start | bytes 6291460
  2.0 8.9 %copy-start.2 = (bf16[2,16,8,2048]{3,2,1,0:T(8,128)(2,1)S(1)}, bf16[2,16,8,2048]{3,2,1,0:T(8,128)(2,1)}, u32[]{:S(2)}) copy-start(bf16[2,16,8,2048]{3,2,1,0:T(8,128)(2,1)} %param.3) | copy-start | bytes 3145732
  2.4 35.1 %copy-start.1 = (bf16[2,2,16,8,2048]{4,3,2,1,0:T(8,128)(2,1)S(1)}, bf16[2,2,16,8,2048]{4,3,2,1,0:T(8,128)(2,1)}, u32[]{:S(2)}) copy-start(bf16[2,2,16,8,2048]{4,3,2,1,0:T(8,128)(2,1)} %param.4) | copy-start | bytes 6291460
  2.4 26.2 %collective-permute-start.1 = (bf16[2,128,2048]{2,1,0:T(8,128)(2,1)S(1)}, bf16[2,128,2048]{2,1,0:T(8,128)(2,1)S(1)}, u32[]{:S(2)}, u32[]{:S(2)}) collective-permute-start(bf16[2,128,2048]{2,1,0:T(8,128)(2,1)S(1)} %get-tuple-element.41), channel_id=1, source_target_pairs={{0,24},{8,16},{16,8},{24,0},{1,25},{9,17},{17,9},{25,1},{2,26},{10... | collective-permute-start | bytes 3145736 | tf_op jit(solution)/shard_map/ppermute | solution.py:429
  5.1 27.2 %collective-permute-start.4 = (bf16[2,2,64,2048]{3,2,1,0:T(8,128)(2,1)S(1)}, bf16[2,2,64,2048]{3,2,1,0:T(8,128)(2,1)S(1)}, u32[]{:S(2)}, u32[]{:S(2)}) collective-permute-start(bf16[2,2,64,2048]{3,2,1,0:T(8,128)(2,1)S(1)} %get-tuple-element.44), channel_id=1, source_target_pairs={{2,0},{4,2},{6,4},{3,1},{5,3},{7,5},{10,8},{12,10},{14,12},{11,9},... | collective-permute-start | bytes 3145736 | tf_op jit(solution)/shard_map/ppermute | solution.py:430
  6.3 27.2 %collective-permute-start.5 = (bf16[2,2,64,2048]{3,2,1,0:T(8,128)(2,1)S(1)}, bf16[2,2,64,2048]{3,2,1,0:T(8,128)(2,1)S(1)}, u32[]{:S(2)}, u32[]{:S(2)}) collective-permute-start(bf16[2,2,64,2048]{3,2,1,0:T(8,128)(2,1)S(1)} %get-tuple-element.45), channel_id=1, source_target_pairs={{0,2},{2,4},{4,6},{1,3},{3,5},{5,7},{8,10},{10,12},{12,14},{9,11},... | collective-permute-start | bytes 3145736 | tf_op jit(solution)/shard_map/ppermute | solution.py:431
  11.0 24.6 %collective-permute-start.6 = (bf16[2,128,2048]{2,1,0:T(8,128)(2,1)S(1)}, bf16[2,128,2048]{2,1,0:T(8,128)(2,1)S(1)}, u32[]{:S(2)}, u32[]{:S(2)}) collective-permute-start(bf16[2,128,2048]{2,1,0:T(8,128)(2,1)S(1)} %bitcast.9), channel_id=1, source_target_pairs={{0,1},{1,0},{2,3},{3,2},{4,5},{5,4},{6,7},{7,6},{8,9},{9,8},{10,11... | collective-permute-start | bytes 3145736 | tf_op jit(solution)/shard_map/ppermute | solution.py:433
  12.6 41.7 %collective-permute-start.9 = (bf16[2,128,2048]{2,1,0:T(8,128)(2,1)S(1)}, bf16[2,128,2048]{2,1,0:T(8,128)(2,1)S(1)}, u32[]{:S(2)}, u32[]{:S(2)}) collective-permute-start(bf16[2,128,2048]{2,1,0:T(8,128)(2,1)S(1)} %get-tuple-element.56), channel_id=1, source_target_pairs={{0,24},{8,16},{16,8},{24,0},{1,25},{9,17},{17,9},{25,1},{2,26},{10... | collective-permute-start | bytes 3145736 | tf_op jit(solution)/shard_map/ppermute | solution.py:437
  28.7 16.3 %collective-permute-start.2 = (bf16[2,64,2176]{2,1,0:T(8,128)(2,1)S(1)}, bf16[2,64,2176]{2,1,0:T(8,128)(2,1)S(1)}, u32[]{:S(2)}, u32[]{:S(2)}) collective-permute-start(bf16[2,64,2176]{2,1,0:T(8,128)(2,1)S(1)} %get-tuple-element.42), channel_id=1, source_target_pairs={{0,2},{2,4},{4,6},{1,3},{3,5},{5,7},{8,10},{10,12},{12,14},{9,11},... | collective-permute-start | bytes 1671176 | tf_op jit(solution)/shard_map/ppermute | solution.py:435
  32.2 17.3 %collective-permute-start.3 = (bf16[2,64,2176]{2,1,0:T(8,128)(2,1)S(1)}, bf16[2,64,2176]{2,1,0:T(8,128)(2,1)S(1)}, u32[]{:S(2)}, u32[]{:S(2)}) collective-permute-start(bf16[2,64,2176]{2,1,0:T(8,128)(2,1)S(1)} %get-tuple-element.59), channel_id=1, source_target_pairs={{2,0},{4,2},{6,4},{3,1},{5,3},{7,5},{10,8},{12,10},{14,12},{11,9},... | collective-permute-start | bytes 1671176 | tf_op jit(solution)/shard_map/ppermute | solution.py:436
  33.7 2.4 %collective-permute-start.8 = (bf16[2,64,2048]{2,1,0:T(8,128)(2,1)S(1)}, bf16[2,64,2048]{2,1,0:T(8,128)(2,1)S(1)}, u32[]{:S(2)}, u32[]{:S(2)}) collective-permute-start(bf16[2,64,2048]{2,1,0:T(8,128)(2,1)S(1)} %get-tuple-element.51), channel_id=1, source_target_pairs={{0,8},{8,0},{16,24},{24,16},{1,9},{9,1},{17,25},{25,17},{2,10},{10... | collective-permute-start | bytes 1572872 | tf_op jit(solution)/shard_map/ppermute | solution.py:440
  35.6 1.9 %collective-permute-start.7 = (bf16[2,64,2048]{2,1,0:T(8,128)(2,1)S(1)}, bf16[2,64,2048]{2,1,0:T(8,128)(2,1)S(1)}, u32[]{:S(2)}, u32[]{:S(2)}) collective-permute-start(bf16[2,64,2048]{2,1,0:T(8,128)(2,1)S(1)} %get-tuple-element.50), channel_id=1, source_target_pairs={{0,8},{8,0},{16,24},{24,16},{1,9},{9,1},{17,25},{25,17},{2,10},{10... | collective-permute-start | bytes 1572872 | tf_op jit(solution)/shard_map/ppermute | solution.py:442
  40.4 18.0 %collective-permute-start.11 = (bf16[2096,128]{1,0:T(8,128)(2,1)S(1)}, bf16[2096,128]{1,0:T(8,128)(2,1)S(1)}, u32[]{:S(2)}, u32[]{:S(2)}) collective-permute-start(bf16[2096,128]{1,0:T(8,128)(2,1)S(1)} %shard_map.40), channel_id=1, source_target_pairs={{0,1},{1,0},{2,3},{3,2},{4,5},{5,4},{6,7},{7,6},{8,9},{9,8},{10,11... | collective-permute-start | bytes 1609736 | tf_op jit(solution)/shard_map/ppermute | solution.py:446
  52.8 14.1 %collective-permute-start.15 = (bf16[2096,128]{1,0:T(8,128)(2,1)S(1)}, bf16[2096,128]{1,0:T(8,128)(2,1)S(1)}, u32[]{:S(2)}, u32[]{:S(2)}) collective-permute-start(bf16[2096,128]{1,0:T(8,128)(2,1)S(1)} %shard_map.42), channel_id=1, source_target_pairs={{0,1},{1,0},{2,3},{3,2},{4,5},{5,4},{6,7},{7,6},{8,9},{9,8},{10,11... | collective-permute-start | bytes 1609736 | tf_op jit(solution)/shard_map/ppermute | solution.py:453
  54.3 4.7 %collective-permute-start.10 = (bf16[2,64,2176]{2,1,0:T(8,128)(2,1)S(1)}, bf16[2,64,2176]{2,1,0:T(8,128)(2,1)S(1)}, u32[]{:S(2)}, u32[]{:S(2)}) collective-permute-start(bf16[2,64,2176]{2,1,0:T(8,128)(2,1)S(1)} %get-tuple-element.59), channel_id=1, source_target_pairs={{0,8},{8,0},{16,24},{24,16},{1,9},{9,1},{17,25},{25,17},{2,10},{10... | collective-permute-start | bytes 1671176 | tf_op jit(solution)/shard_map/ppermute | solution.py:459
  54.5 4.5 %collective-permute-start.13 = (bf16[2,64,2176]{2,1,0:T(8,128)(2,1)S(1)}, bf16[2,64,2176]{2,1,0:T(8,128)(2,1)S(1)}, u32[]{:S(2)}, u32[]{:S(2)}) collective-permute-start(bf16[2,64,2176]{2,1,0:T(8,128)(2,1)S(1)} %get-tuple-element.63), channel_id=1, source_target_pairs={{0,8},{8,0},{16,24},{24,16},{1,9},{9,1},{17,25},{25,17},{2,10},{10... | collective-permute-start | bytes 1671176 | tf_op jit(solution)/shard_map/ppermute | solution.py:457
  55.0 5.5 %copy-start.3 = (s32[2,2,1,2]{3,2,1,0:T(1,128)S(1)}, s32[2,2,1,2]{3,2,1,0:T(1,128)}, u32[]{:S(2)}) copy-start(s32[2,2,1,2]{3,2,1,0:T(1,128)} %far_ref.1) | copy-start | bytes 100
  55.0 3.9 %collective-permute-start.14 = (bf16[2,64,2176]{2,1,0:T(8,128)(2,1)S(1)}, bf16[2,64,2176]{2,1,0:T(8,128)(2,1)S(1)}, u32[]{:S(2)}, u32[]{:S(2)}) collective-permute-start(bf16[2,64,2176]{2,1,0:T(8,128)(2,1)S(1)} %get-tuple-element.64), channel_id=1, source_target_pairs={{0,8},{8,0},{16,24},{24,16},{1,9},{9,1},{17,25},{25,17},{2,10},{10... | collective-permute-start | bytes 1671176 | tf_op jit(solution)/shard_map/ppermute | solution.py:457
  58.5 2.0 %collective-permute-start.12 = (bf16[2,64,2048]{2,1,0:T(8,128)(2,1)S(1)}, bf16[2,64,2048]{2,1,0:T(8,128)(2,1)S(1)}, u32[]{:S(2)}, u32[]{:S(2)}) collective-permute-start(bf16[2,64,2048]{2,1,0:T(8,128)(2,1)S(1)} %shard_map.44), channel_id=1, source_target_pairs={{0,8},{8,0},{16,24},{24,16},{1,9},{9,1},{17,25},{25,17},{2,10},{10... | collective-permute-start | bytes 1572872 | tf_op jit(solution)/shard_map/ppermute | solution.py:461

commit v19 on v18

--- a/solution.py
+++ b/solution.py
@@ -16,7 +16,7 @@
 EXP_SCALE = HD ** (-0.5) * 1.4426950408889634
 VMEM_LIMIT = 16 * 1024 * 1024
 GROUP = 8
-NEAR_GROUP = 16
+NEAR_GROUP = 8
 FINISH_COST = 1
 LATE_COST = 28 << 30
 

time: 68.6 us -> 68.6 us (level)
  no operation moved by 1% of the time
where the time goes in v19:
time: 68.6 us; the launch traced here: 68.3 us
  waiting for transfers between devices  26.8 us (39%)
  starting transfers between devices  20.5 us (30%)
  Pallas kernels  19.1 us (28%)
  local copies, waits for them, and re-layouts  1.6 us (2%)
    ppermute x1, waiting for transfers between devices, per_device(): cross = lax.ppermute(outer, 'ta', cross_pairs)  16 us
    pallas_call x4, Pallas kernels, near_attention(): pl.pallas_call(functools.partial(near_kernel, len(visitors), len(queries)...  12.2 us
    ppermute x1, starting transfers between devices, per_device(): top = lax.ppermute(last_rows, 'ha', up)  4.61 us
    ppermute x1, waiting for transfers between devices, per_device(): cross_bottom = lax.ppermute(cross_first, 'ha', down)  4.43 us
    pallas_call x1, Pallas kernels, far_attention(): pl.pallas_call(functools.partial(far_kernel, members), out_shape=[jax.Sha...  4.17 us
    ppermute x1, starting transfers between devices, per_device(): cross_top = lax.ppermute(cross_last, 'ha', up)  3.49 us
    ppermute x2, starting transfers between devices, per_device(): lax.ppermute(result, 'wa', back)  3.12 us
    ppermute x1, starting transfers between devices, per_device(): cross = lax.ppermute(outer, 'ta', cross_pairs)  2.67 us
  transfers between devices with their start and end apart: 16, of which 8 were waited for; matrix products, arithmetic and copies ran while one was open for 0% of the time, Pallas kernels for 26%

profile of v19, /device:TPU:0, one launch (start us, length us, event | category | flops | bytes accessed | tf_op | source)
XLA Modules:
  0.0 68.3 jit_solution(2636731315588145713)
XLA Ops:
  0.5 1.6 %copy-done = bf16[2,2,16,8,2048]{4,3,2,1,0:T(8,128)(2,1)S(1)} copy-done((bf16[2,2,16,8,2048]{4,3,2,1,0:T(8,128)(2,1)S(1)}, bf16[2,2,16,8,2048]{4,3,2,1,0:T(8,128)(2,1)}, u32[]{:S(2)}) %copy-start) | copy-done | bytes 2097176
  2.4 2.7 %collective-permute-start.1 = (bf16[2,128,2048]{2,1,0:T(8,128)(2,1)S(1)}, bf16[2,128,2048]{2,1,0:T(8,128)(2,1)S(1)}, u32[]{:S(2)}, u32[]{:S(2)}) collective-permute-start(bf16[2,128,2048]{2,1,0:T(8,128)(2,1)S(1)} %get-tuple-element.41), channel_id=1, source_target_pairs={{0,24},{8,16},{16,8},{24,0},{1,25},{9,17},{17,9},{25,1},{2,26},{10... | collective-permute-start | bytes 3145736 | tf_op jit(solution)/shard_map/ppermute | solution.py:429
  5.1 1.3 %collective-permute-start.4 = (bf16[2,2,64,2048]{3,2,1,0:T(8,128)(2,1)S(1)}, bf16[2,2,64,2048]{3,2,1,0:T(8,128)(2,1)S(1)}, u32[]{:S(2)}, u32[]{:S(2)}) collective-permute-start(bf16[2,2,64,2048]{3,2,1,0:T(8,128)(2,1)S(1)} %get-tuple-element.44), channel_id=1, source_target_pairs={{2,0},{4,2},{6,4},{3,1},{5,3},{7,5},{10,8},{12,10},{14,12},{11,9},... | collective-permute-start | bytes 3145736 | tf_op jit(solution)/shard_map/ppermute | solution.py:430
  6.3 4.6 %collective-permute-start.5 = (bf16[2,2,64,2048]{3,2,1,0:T(8,128)(2,1)S(1)}, bf16[2,2,64,2048]{3,2,1,0:T(8,128)(2,1)S(1)}, u32[]{:S(2)}, u32[]{:S(2)}) collective-permute-start(bf16[2,2,64,2048]{3,2,1,0:T(8,128)(2,1)S(1)} %get-tuple-element.45), channel_id=1, source_target_pairs={{0,2},{2,4},{4,6},{1,3},{3,5},{5,7},{8,10},{10,12},{12,14},{9,11},... | collective-permute-start | bytes 3145736 | tf_op jit(solution)/shard_map/ppermute | solution.py:431
  11.0 1.6 %collective-permute-start.6 = (bf16[2,128,2048]{2,1,0:T(8,128)(2,1)S(1)}, bf16[2,128,2048]{2,1,0:T(8,128)(2,1)S(1)}, u32[]{:S(2)}, u32[]{:S(2)}) collective-permute-start(bf16[2,128,2048]{2,1,0:T(8,128)(2,1)S(1)} %bitcast.9), channel_id=1, source_target_pairs={{0,1},{1,0},{2,3},{3,2},{4,5},{5,4},{6,7},{7,6},{8,9},{9,8},{10,11... | collective-permute-start | bytes 3145736 | tf_op jit(solution)/shard_map/ppermute | solution.py:433
  12.6 16.0 %collective-permute-done.1.frame_ref.refs_0_ = bf16[2,128,2048]{2,1,0:T(8,128)(2,1)S(1)} collective-permute-done((bf16[2,128,2048]{2,1,0:T(8,128)(2,1)S(1)}, bf16[2,128,2048]{2,1,0:T(8,128)(2,1)S(1)}, u32[]{:S(2)}, u32[]{:S(2)}) %collective-permute-start.1) | collective-permute-done | bytes 1048608 | tf_op jit(solution)/shard_map/ppermute | solution.py:429
  28.7 3.5 %collective-permute-start.2 = (bf16[2,64,2176]{2,1,0:T(8,128)(2,1)S(1)}, bf16[2,64,2176]{2,1,0:T(8,128)(2,1)S(1)}, u32[]{:S(2)}, u32[]{:S(2)}) collective-permute-start(bf16[2,64,2176]{2,1,0:T(8,128)(2,1)S(1)} %get-tuple-element.42), channel_id=1, source_target_pairs={{0,2},{2,4},{4,6},{1,3},{3,5},{5,7},{8,10},{10,12},{12,14},{9,11},... | collective-permute-start | bytes 1671176 | tf_op jit(solution)/shard_map/ppermute | solution.py:435
  32.2 1.3 %collective-permute-start.3 = (bf16[2,64,2176]{2,1,0:T(8,128)(2,1)S(1)}, bf16[2,64,2176]{2,1,0:T(8,128)(2,1)S(1)}, u32[]{:S(2)}, u32[]{:S(2)}) collective-permute-start(bf16[2,64,2176]{2,1,0:T(8,128)(2,1)S(1)} %get-tuple-element.59), channel_id=1, source_target_pairs={{2,0},{4,2},{6,4},{3,1},{5,3},{7,5},{10,8},{12,10},{14,12},{11,9},... | collective-permute-start | bytes 1671176 | tf_op jit(solution)/shard_map/ppermute | solution.py:436
  33.7 0.9 %collective-permute-start.8 = (bf16[2,64,2048]{2,1,0:T(8,128)(2,1)S(1)}, bf16[2,64,2048]{2,1,0:T(8,128)(2,1)S(1)}, u32[]{:S(2)}, u32[]{:S(2)}) collective-permute-start(bf16[2,64,2048]{2,1,0:T(8,128)(2,1)S(1)} %get-tuple-element.51), channel_id=1, source_target_pairs={{0,8},{8,0},{16,24},{24,16},{1,9},{9,1},{17,25},{25,17},{2,10},{10... | collective-permute-start | bytes 1572872 | tf_op jit(solution)/shard_map/ppermute | solution.py:440
  34.6 1.0 %collective-permute-done.6.refs_3_ = bf16[2,128,2048]{2,1,0:T(8,128)(2,1)S(1)} collective-permute-done((bf16[2,128,2048]{2,1,0:T(8,128)(2,1)S(1)}, bf16[2,128,2048]{2,1,0:T(8,128)(2,1)S(1)}, u32[]{:S(2)}, u32[]{:S(2)}) %collective-permute-start.6) | collective-permute-done | bytes 1048608 | tf_op jit(solution)/shard_map/ppermute | solution.py:433
  36.1 1.4 %collective-permute-done.7.refs_1_ = bf16[2,64,2048]{2,1,0:T(8,128)(2,1)S(1)} collective-permute-done((bf16[2,64,2048]{2,1,0:T(8,128)(2,1)S(1)}, bf16[2,64,2048]{2,1,0:T(8,128)(2,1)S(1)}, u32[]{:S(2)}, u32[]{:S(2)}) %collective-permute-start.7) | collective-permute-done | bytes 524320 | tf_op jit(solution)/shard_map/ppermute | solution.py:442
  37.5 2.9 %shard_map.40 = bf16[2096,128]{1,0:T(8,128)(2,1)S(1)} custom-call(bf16[2,2,128,2048]{3,2,1,0:T(8,128)(2,1)S(1)} %bitcast.5, bf16[2,2,64,2048]{3,2,1,0:T(8,128)(2,1)S(1)} %collective-permute-done.5.top_ref, bf16[2,2,64,2048]{3,2,1,0:T(8,128)(2,1)S(1)} %collective-permute-done.4.bottom_ref, ...), custom_call_target="tpu_custom_call" | custom-call | flops 1 | bytes 1 | tf_op jit(solution)/shard_map/pallas_call | solution.py:232
  40.4 1.6 %collective-permute-start.11 = (bf16[2096,128]{1,0:T(8,128)(2,1)S(1)}, bf16[2096,128]{1,0:T(8,128)(2,1)S(1)}, u32[]{:S(2)}, u32[]{:S(2)}) collective-permute-start(bf16[2096,128]{1,0:T(8,128)(2,1)S(1)} %shard_map.40), channel_id=1, source_target_pairs={{0,1},{1,0},{2,3},{3,2},{4,5},{5,4},{6,7},{7,6},{8,9},{9,8},{10,11... | collective-permute-start | bytes 1609736 | tf_op jit(solution)/shard_map/ppermute | solution.py:446
  41.9 2.9 %shard_map.41 = (f32[128,2048]{1,0:T(8,128)S(1)}, f32[128,128]{1,0:T(8,128)S(1)}, f32[128,128]{1,0:T(8,128)S(1)}, f32[128,2048]{1,0:T(8,128)S(1)}) custom-call(bf16[2,2,128,2048]{3,2,1,0:T(8,128)(2,1)S(1)} %bitcast.6, bf16[2,2,64,2048]{3,2,1,0:T(8,128)(2,1)S(1)} %collective-permute-done.5.top_ref, ...), custom_call_target="tpu_custom_call" | custom-call | flops 1 | bytes 1 | tf_op jit(solution)/shard_map/pallas_call | solution.py:232
  45.1 4.4 %collective-permute-done.3.refs_2_ = bf16[2,64,2176]{2,1,0:T(8,128)(2,1)S(1)} collective-permute-done((bf16[2,64,2176]{2,1,0:T(8,128)(2,1)S(1)}, bf16[2,64,2176]{2,1,0:T(8,128)(2,1)S(1)}, u32[]{:S(2)}, u32[]{:S(2)}) %collective-permute-start.3) | collective-permute-done | bytes 557088 | tf_op jit(solution)/shard_map/ppermute | solution.py:436
  49.5 3.2 %shard_map.42 = bf16[2096,128]{1,0:T(8,128)(2,1)S(1)} custom-call(bf16[2,2,128,2048]{3,2,1,0:T(8,128)(2,1)S(1)} %bitcast.7, bf16[2,2,64,2048]{3,2,1,0:T(8,128)(2,1)S(1)} %collective-permute-done.5.top_ref, bf16[2,2,64,2048]{3,2,1,0:T(8,128)(2,1)S(1)} %collective-permute-done.4.bottom_ref, bf16[2,128,2048]{2,1,0:T(8,128)(2,1)S(1)} %collective-permute-done.1.frame_ref.refs_0_, ...), custom_call_target="tpu_custom_call" | custom-call | flops 1 | bytes 1 | tf_op jit(solution)/shard_map/pallas_call | solution.py:232
  52.7 1.6 %collective-permute-start.15 = (bf16[2096,128]{1,0:T(8,128)(2,1)S(1)}, bf16[2096,128]{1,0:T(8,128)(2,1)S(1)}, u32[]{:S(2)}, u32[]{:S(2)}) collective-permute-start(bf16[2096,128]{1,0:T(8,128)(2,1)S(1)} %shard_map.42), channel_id=1, source_target_pairs={{0,1},{1,0},{2,3},{3,2},{4,5},{5,4},{6,7},{7,6},{8,9},{9,8},{10,11... | collective-permute-start | bytes 1609736 | tf_op jit(solution)/shard_map/ppermute | solution.py:453
  54.4 0.6 collective-permute-start.13
  55.1 3.2 %shard_map.43 = (f32[128,2048]{1,0:T(8,128)S(1)}, f32[128,128]{1,0:T(8,128)S(1)}, f32[128,128]{1,0:T(8,128)S(1)}, f32[128,2048]{1,0:T(8,128)S(1)}) custom-call(bf16[2,2,128,2048]{3,2,1,0:T(8,128)(2,1)S(1)} %bitcast.8, bf16[2,2,64,2048]{3,2,1,0:T(8,128)(2,1)S(1)} %collective-permute-done.5.top_ref, ...), custom_call_target="tpu_custom_call" | custom-call | flops 30064771072 | bytes 1 | tf_op jit(solution)/shard_map/pallas_call | solution.py:232
  58.9 1.5 %collective-permute-done.12.refs_3_ = bf16[2,64,2048]{2,1,0:T(8,128)(2,1)S(1)} collective-permute-done((bf16[2,64,2048]{2,1,0:T(8,128)(2,1)S(1)}, bf16[2,64,2048]{2,1,0:T(8,128)(2,1)S(1)}, u32[]{:S(2)}, u32[]{:S(2)}) %collective-permute-start.12) | collective-permute-done | bytes 524320 | tf_op jit(solution)/shard_map/ppermute | solution.py:461
  60.4 4.2 %shard_map.46 = (f32[2,128,2048]{2,1,0:T(8,128)S(1)}, f32[2,128,128]{2,1,0:T(8,128)S(1)}, f32[2,128,128]{2,1,0:T(8,128)S(1)}) custom-call(s32[2,2,1,2]{3,2,1,0:T(1,128)S(1)} %copy-done.3, bf16[2,128,2048]{2,1,0:T(8,128)(2,1)S(1)} %bitcast.12, bf16[2,2,128,2048]{3,2,1,0:T(8,128)(2,1)S(1)} %collective-permute-done.refs_0_.core_ref, ...), custom_call_target="tpu_custom_call" | custom-call | flops 1 | bytes 1 | tf_op jit(solution)/shard_map/pallas_call | solution.py:319
  64.6 0.6 shard_map.47.refs_4_
  65.2 1.6 %collective-permute-done.15.refs_3_ = bf16[2096,128]{1,0:T(8,128)(2,1)S(1)} collective-permute-done((bf16[2096,128]{1,0:T(8,128)(2,1)S(1)}, bf16[2096,128]{1,0:T(8,128)(2,1)S(1)}, u32[]{:S(2)}, u32[]{:S(2)}) %collective-permute-start.15) | collective-permute-done | bytes 536608 | tf_op jit(solution)/shard_map/ppermute | solution.py:453
  66.8 1.4 %shard_map.48 = bf16[2,128,2048]{2,1,0:T(8,128)(2,1)} custom-call(f32[2,128,2048]{2,1,0:T(8,128)S(1)} %get-tuple-element.71.refs_0_, f32[2,128,128]{2,1,0:T(8,128)S(1)} %get-tuple-element.72.refs_1_, f32[2,128,128]{2,1,0:T(8,128)S(1)} %get-tuple-element.73.refs_2_, bf16[2096,128]{1,0:T(8,128)(2,1)S(1)} %collective-permute-done.15.refs_3_, ...), custom_call_target="tpu_custom_call" | custom-call | flops 1 | bytes 1 | tf_op jit(solution)/shard_map/pallas_call | solution.py:396
  (28 shorter events, 2.6 us)
Async XLA Ops:
  0.0 11.0 %collective-permute-start = (bf16[2,2,128,2048]{3,2,1,0:T(8,128)(2,1)}, bf16[2,2,128,2048]{3,2,1,0:T(8,128)(2,1)S(1)}, u32[]{:S(2)}, u32[]{:S(2)}) collective-permute-start(bf16[2,2,128,2048]{3,2,1,0:T(8,128)(2,1)} %bitcast.3), channel_id=1, source_target_pairs={{0,8},{8,0},{16,24},{24,16},{1,9},{9,1},{17,25},{25,17},{2,10},{10... | collective-permute-start | bytes 6291464 | tf_op jit(solution)/shard_map/ppermute | solution.py:427
  0.5 1.6 %copy-start = (bf16[2,2,16,8,2048]{4,3,2,1,0:T(8,128)(2,1)S(1)}, bf16[2,2,16,8,2048]{4,3,2,1,0:T(8,128)(2,1)}, u32[]{:S(2)}) copy-start(bf16[2,2,16,8,2048]{4,3,2,1,0:T(8,128)(2,1)} %param.4) | copy-start | bytes 6291460
  2.0 8.9 %copy-start.2 = (bf16[2,16,8,2048]{3,2,1,0:T(8,128)(2,1)S(1)}, bf16[2,16,8,2048]{3,2,1,0:T(8,128)(2,1)}, u32[]{:S(2)}) copy-start(bf16[2,16,8,2048]{3,2,1,0:T(8,128)(2,1)} %param.3) | copy-start | bytes 3145732
  2.4 35.1 %copy-start.1 = (bf16[2,2,16,8,2048]{4,3,2,1,0:T(8,128)(2,1)S(1)}, bf16[2,2,16,8,2048]{4,3,2,1,0:T(8,128)(2,1)}, u32[]{:S(2)}) copy-start(bf16[2,2,16,8,2048]{4,3,2,1,0:T(8,128)(2,1)} %param.4) | copy-start | bytes 6291460
  2.4 26.2 %collective-permute-start.1 = (bf16[2,128,2048]{2,1,0:T(8,128)(2,1)S(1)}, bf16[2,128,2048]{2,1,0:T(8,128)(2,1)S(1)}, u32[]{:S(2)}, u32[]{:S(2)}) collective-permute-start(bf16[2,128,2048]{2,1,0:T(8,128)(2,1)S(1)} %get-tuple-element.41), channel_id=1, source_target_pairs={{0,24},{8,16},{16,8},{24,0},{1,25},{9,17},{17,9},{25,1},{2,26},{10... | collective-permute-start | bytes 3145736 | tf_op jit(solution)/shard_map/ppermute | solution.py:429
  5.1 27.2 %collective-permute-start.4 = (bf16[2,2,64,2048]{3,2,1,0:T(8,128)(2,1)S(1)}, bf16[2,2,64,2048]{3,2,1,0:T(8,128)(2,1)S(1)}, u32[]{:S(2)}, u32[]{:S(2)}) collective-permute-start(bf16[2,2,64,2048]{3,2,1,0:T(8,128)(2,1)S(1)} %get-tuple-element.44), channel_id=1, source_target_pairs={{2,0},{4,2},{6,4},{3,1},{5,3},{7,5},{10,8},{12,10},{14,12},{11,9},... | collective-permute-start | bytes 3145736 | tf_op jit(solution)/shard_map/ppermute | solution.py:430
  6.3 27.2 %collective-permute-start.5 = (bf16[2,2,64,2048]{3,2,1,0:T(8,128)(2,1)S(1)}, bf16[2,2,64,2048]{3,2,1,0:T(8,128)(2,1)S(1)}, u32[]{:S(2)}, u32[]{:S(2)}) collective-permute-start(bf16[2,2,64,2048]{3,2,1,0:T(8,128)(2,1)S(1)} %get-tuple-element.45), channel_id=1, source_target_pairs={{0,2},{2,4},{4,6},{1,3},{3,5},{5,7},{8,10},{10,12},{12,14},{9,11},... | collective-permute-start | bytes 3145736 | tf_op jit(solution)/shard_map/ppermute | solution.py:431
  11.0 24.6 %collective-permute-start.6 = (bf16[2,128,2048]{2,1,0:T(8,128)(2,1)S(1)}, bf16[2,128,2048]{2,1,0:T(8,128)(2,1)S(1)}, u32[]{:S(2)}, u32[]{:S(2)}) collective-permute-start(bf16[2,128,2048]{2,1,0:T(8,128)(2,1)S(1)} %bitcast.9), channel_id=1, source_target_pairs={{0,1},{1,0},{2,3},{3,2},{4,5},{5,4},{6,7},{7,6},{8,9},{9,8},{10,11... | collective-permute-start | bytes 3145736 | tf_op jit(solution)/shard_map/ppermute | solution.py:433
  12.6 41.7 %collective-permute-start.9 = (bf16[2,128,2048]{2,1,0:T(8,128)(2,1)S(1)}, bf16[2,128,2048]{2,1,0:T(8,128)(2,1)S(1)}, u32[]{:S(2)}, u32[]{:S(2)}) collective-permute-start(bf16[2,128,2048]{2,1,0:T(8,128)(2,1)S(1)} %get-tuple-element.56), channel_id=1, source_target_pairs={{0,24},{8,16},{16,8},{24,0},{1,25},{9,17},{17,9},{25,1},{2,26},{10... | collective-permute-start | bytes 3145736 | tf_op jit(solution)/shard_map/ppermute | solution.py:437
  28.7 16.3 %collective-permute-start.2 = (bf16[2,64,2176]{2,1,0:T(8,128)(2,1)S(1)}, bf16[2,64,2176]{2,1,0:T(8,128)(2,1)S(1)}, u32[]{:S(2)}, u32[]{:S(2)}) collective-permute-start(bf16[2,64,2176]{2,1,0:T(8,128)(2,1)S(1)} %get-tuple-element.42), channel_id=1, source_target_pairs={{0,2},{2,4},{4,6},{1,3},{3,5},{5,7},{8,10},{10,12},{12,14},{9,11},... | collective-permute-start | bytes 1671176 | tf_op jit(solution)/shard_map/ppermute | solution.py:435
  32.2 17.3 %collective-permute-start.3 = (bf16[2,64,2176]{2,1,0:T(8,128)(2,1)S(1)}, bf16[2,64,2176]{2,1,0:T(8,128)(2,1)S(1)}, u32[]{:S(2)}, u32[]{:S(2)}) collective-permute-start(bf16[2,64,2176]{2,1,0:T(8,128)(2,1)S(1)} %get-tuple-element.59), channel_id=1, source_target_pairs={{2,0},{4,2},{6,4},{3,1},{5,3},{7,5},{10,8},{12,10},{14,12},{11,9},... | collective-permute-start | bytes 1671176 | tf_op jit(solution)/shard_map/ppermute | solution.py:436
  33.7 2.4 %collective-permute-start.8 = (bf16[2,64,2048]{2,1,0:T(8,128)(2,1)S(1)}, bf16[2,64,2048]{2,1,0:T(8,128)(2,1)S(1)}, u32[]{:S(2)}, u32[]{:S(2)}) collective-permute-start(bf16[2,64,2048]{2,1,0:T(8,128)(2,1)S(1)} %get-tuple-element.51), channel_id=1, source_target_pairs={{0,8},{8,0},{16,24},{24,16},{1,9},{9,1},{17,25},{25,17},{2,10},{10... | collective-permute-start | bytes 1572872 | tf_op jit(solution)/shard_map/ppermute | solution.py:440
  35.6 1.9 %collective-permute-start.7 = (bf16[2,64,2048]{2,1,0:T(8,128)(2,1)S(1)}, bf16[2,64,2048]{2,1,0:T(8,128)(2,1)S(1)}, u32[]{:S(2)}, u32[]{:S(2)}) collective-permute-start(bf16[2,64,2048]{2,1,0:T(8,128)(2,1)S(1)} %get-tuple-element.50), channel_id=1, source_target_pairs={{0,8},{8,0},{16,24},{24,16},{1,9},{9,1},{17,25},{25,17},{2,10},{10... | collective-permute-start | bytes 1572872 | tf_op jit(solution)/shard_map/ppermute | solution.py:442
  40.4 17.9 %collective-permute-start.11 = (bf16[2096,128]{1,0:T(8,128)(2,1)S(1)}, bf16[2096,128]{1,0:T(8,128)(2,1)S(1)}, u32[]{:S(2)}, u32[]{:S(2)}) collective-permute-start(bf16[2096,128]{1,0:T(8,128)(2,1)S(1)} %shard_map.40), channel_id=1, source_target_pairs={{0,1},{1,0},{2,3},{3,2},{4,5},{5,4},{6,7},{7,6},{8,9},{9,8},{10,11... | collective-permute-start | bytes 1609736 | tf_op jit(solution)/shard_map/ppermute | solution.py:446
  52.7 14.1 %collective-permute-start.15 = (bf16[2096,128]{1,0:T(8,128)(2,1)S(1)}, bf16[2096,128]{1,0:T(8,128)(2,1)S(1)}, u32[]{:S(2)}, u32[]{:S(2)}) collective-permute-start(bf16[2096,128]{1,0:T(8,128)(2,1)S(1)} %shard_map.42), channel_id=1, source_target_pairs={{0,1},{1,0},{2,3},{3,2},{4,5},{5,4},{6,7},{7,6},{8,9},{9,8},{10,11... | collective-permute-start | bytes 1609736 | tf_op jit(solution)/shard_map/ppermute | solution.py:453
  54.3 4.5 %collective-permute-start.10 = (bf16[2,64,2176]{2,1,0:T(8,128)(2,1)S(1)}, bf16[2,64,2176]{2,1,0:T(8,128)(2,1)S(1)}, u32[]{:S(2)}, u32[]{:S(2)}) collective-permute-start(bf16[2,64,2176]{2,1,0:T(8,128)(2,1)S(1)} %get-tuple-element.59), channel_id=1, source_target_pairs={{0,8},{8,0},{16,24},{24,16},{1,9},{9,1},{17,25},{25,17},{2,10},{10... | collective-permute-start | bytes 1671176 | tf_op jit(solution)/shard_map/ppermute | solution.py:459
  54.4 4.4 %collective-permute-start.13 = (bf16[2,64,2176]{2,1,0:T(8,128)(2,1)S(1)}, bf16[2,64,2176]{2,1,0:T(8,128)(2,1)S(1)}, u32[]{:S(2)}, u32[]{:S(2)}) collective-permute-start(bf16[2,64,2176]{2,1,0:T(8,128)(2,1)S(1)} %get-tuple-element.63), channel_id=1, source_target_pairs={{0,8},{8,0},{16,24},{24,16},{1,9},{9,1},{17,25},{25,17},{2,10},{10... | collective-permute-start | bytes 1671176 | tf_op jit(solution)/shard_map/ppermute | solution.py:457
  55.0 5.4 %copy-start.3 = (s32[2,2,1,2]{3,2,1,0:T(1,128)S(1)}, s32[2,2,1,2]{3,2,1,0:T(1,128)}, u32[]{:S(2)}) copy-start(s32[2,2,1,2]{3,2,1,0:T(1,128)} %far_ref.1) | copy-start | bytes 100
  55.0 3.8 %collective-permute-start.14 = (bf16[2,64,2176]{2,1,0:T(8,128)(2,1)S(1)}, bf16[2,64,2176]{2,1,0:T(8,128)(2,1)S(1)}, u32[]{:S(2)}, u32[]{:S(2)}) collective-permute-start(bf16[2,64,2176]{2,1,0:T(8,128)(2,1)S(1)} %get-tuple-element.64), channel_id=1, source_target_pairs={{0,8},{8,0},{16,24},{24,16},{1,9},{9,1},{17,25},{25,17},{2,10},{10... | collective-permute-start | bytes 1671176 | tf_op jit(solution)/shard_map/ppermute | solution.py:457
  58.4 2.0 %collective-permute-start.12 = (bf16[2,64,2048]{2,1,0:T(8,128)(2,1)S(1)}, bf16[2,64,2048]{2,1,0:T(8,128)(2,1)S(1)}, u32[]{:S(2)}, u32[]{:S(2)}) collective-permute-start(bf16[2,64,2048]{2,1,0:T(8,128)(2,1)S(1)} %shard_map.44), channel_id=1, source_target_pairs={{0,8},{8,0},{16,24},{24,16},{1,9},{9,1},{17,25},{25,17},{2,10},{10... | collective-permute-start | bytes 1572872 | tf_op jit(solution)/shard_map/ppermute | solution.py:461
